TPU v7x, 32 devices: a whole 2x2x4 slice. The times are simulated.
32 devices in a mesh: dp: 4 (over z), ctx: 4 (over y, x), tp: 2 (over core).
Axes of the slice: x: 2, y: 2, z: 4, core: 2. Of those that a mesh axis runs over, the one named last changes fastest.
Arguments:
- tokens: bfloat16 [16384, 768], P(('dp', 'ctx')), may hold values from -6 to 6
- cotangent: bfloat16 [16384, 768], P(('dp', 'ctx')), may hold values from -6 to 6
- device_fill: int32 [4, 4], P('dp'), may hold values from 1 to 4, 12 in all within a row
- seq_lengths: int32 [4, 3], P('dp'), may hold values from 1 to 3070, as said below
- norm_gain: bfloat16 [768], P('dp'), may hold values from 0.5 to 1.5
- w_z: bfloat16 [768, 1536], P('dp', 'tp'), may hold values from -0.21875 to 0.21875
- w_x: bfloat16 [768, 1536], P('dp', 'tp'), may hold values from -0.21875 to 0.21875
- w_bc: bfloat16 [768, 256], P('dp'), may hold values from -0.21875 to 0.21875
- w_dt: bfloat16 [768, 24], P('dp', 'tp'), may hold values from -0.21875 to 0.21875
- conv_x: bfloat16 [4, 24, 64], P(None, 'tp', 'dp'), may hold values from -3 to 3
- conv_x_bias: bfloat16 [24, 64], P('tp', 'dp'), may hold values from -3 to 3
- conv_bc: bfloat16 [4, 256], P(None, 'dp'), may hold values from -3 to 3
- bias_bc: bfloat16 [256], P('dp'), may hold values from -3 to 3
- dt_bias: float32 [24], P('tp'), may hold values from -7.6 to -3
- a_log: float32 [24], P('tp'), may hold values from -3.9 to 1.4
- skip_d: float32 [24], P('tp'), may hold values from 0.5 to 1.5
- gate_gain: bfloat16 [24, 64], P('tp', 'dp'), may hold values from 0.5 to 1.5
- w_out: bfloat16 [1536, 768], P('tp', 'dp'), may hold values from -0.15625 to 0.15625
Outputs:
- layer_out: float32 [16384, 768], P(('dp', 'ctx'), 'tp')
- grad_tokens: float32 [16384, 768], P(('dp', 'ctx'))
- grad_norm_gain: float32 [768], P('dp')
- grad_w_z: float32 [768, 1536], P('dp', 'tp')
- grad_w_x: float32 [768, 1536], P('dp', 'tp')
- grad_w_bc: float32 [768, 256], P('dp')
- grad_w_dt: float32 [768, 24], P('dp', 'tp')
- grad_conv_x: float32 [4, 24, 64], P(None, 'tp', 'dp')
- grad_conv_x_bias: float32 [24, 64], P('tp', 'dp')
- grad_conv_bc: float32 [4, 256], P(None, 'dp')
- grad_bias_bc: float32 [256], P('dp')
- grad_dt_bias: float32 [24], P('tp')
- grad_a_log: float32 [24], P('tp')
- grad_skip_d: float32 [24], P('tp')
- grad_gate_gain: float32 [24, 64], P('tp', 'dp')
- grad_w_out: float32 [1536, 768], P('tp', 'dp')
Inputs may be any that keep to these rules, and one draw needn't show every extreme that they name: `device_fill`: A row sums to 12; used slots are a device's first ones. `seq_lengths`: A row's lengths sum to 3072; the first and the last are under 256.
All inputs are finite; a program needn't handle non-finite values.
Results may differ from a plain program's by a relative error of at most 0.029.
Values may be sent and summed in bfloat16 or wider, within the bound.
No kernel may reach another device: no remote copies, remote signals or barrier semaphores. Data moves between devices by JAX's collectives and lax.ppermute only.
A program may use at most 128 MiB of HBM per device.

v0:
```python
import jax
import jax.numpy as jnp
from jax import lax
from jax.sharding import PartitionSpec as P

CONV = 4
BLOCK = 256


epsilon = 1e-05


def from_behind(value, axis, steps):
    count = lax.axis_size(axis)
    first, last = (max(0, -steps), min(count, count - steps))
    return lax.ppermute(value, axis, [(source, source + steps) for source in range(first, last)])


def silu_slope(value):
    sigma = jax.nn.sigmoid(value)
    return sigma * (1.0 + value * (1.0 - sigma))


def segment_of(positions, seq_ends):
    found = jnp.sum((positions[:, None] >= seq_ends[None, :]).astype(jnp.int32), axis=1)
    return jnp.where(positions < 0, -1, found)


def product(left, right):
    return jnp.dot(left, right, preferred_element_type=jnp.float32)


def left_transposed(left, right):
    return lax.dot_general(
        left, right, (((0,), (0,)), ((), ())), preferred_element_type=jnp.float32
    )


def right_transposed(left, right):
    return lax.dot_general(
        left, right, (((1,), (1,)), ((), ())), preferred_element_type=jnp.float32
    )


def body(
    tokens,
    cotangent,
    device_fill,
    seq_lengths,
    norm_gain,
    w_z,
    w_x,
    w_bc,
    w_dt,
    conv_x,
    conv_x_bias,
    conv_bc,
    bias_bc,
    dt_bias,
    a_log,
    skip_d,
    gate_gain,
    w_out,
):
    row_count = tokens.shape[0]
    model_width = tokens.shape[1]
    heads_local = dt_bias.shape[0]
    (
        gain_norm,
        z_weight,
        x_weight,
        bc_weight,
        dt_weight,
        taps_inner,
        bias_inner,
        taps_state,
        bias_state,
        gain_gate,
        out_weight,
    ) = (
        lax.all_gather(norm_gain, "dp", axis=0, tiled=True),
        lax.all_gather(w_z, "dp", axis=0, tiled=True),
        lax.all_gather(w_x, "dp", axis=0, tiled=True),
        lax.all_gather(w_bc, "dp", axis=0, tiled=True),
        lax.all_gather(w_dt, "dp", axis=0, tiled=True),
        lax.all_gather(conv_x, "dp", axis=2, tiled=True),
        lax.all_gather(conv_x_bias, "dp", axis=1, tiled=True),
        lax.all_gather(conv_bc, "dp", axis=1, tiled=True),
        lax.all_gather(bias_bc, "dp", axis=0, tiled=True),
        lax.all_gather(gate_gain, "dp", axis=1, tiled=True),
        lax.all_gather(w_out, "dp", axis=1, tiled=True),
    )
    head_size = taps_inner.shape[2]
    inner_local = heads_local * head_size
    state_size = bc_weight.shape[1] // 2
    channels = inner_local + 2 * state_size
    nblocks = row_count // BLOCK
    margin = CONV - 1
    ctx_index = lax.axis_index("ctx")
    ctx_count = lax.axis_size("ctx")
    device_ids = jnp.arange(ctx_count)
    fill_all = device_fill[0] * BLOCK
    fill_rows = jnp.sum(jnp.where(device_ids == ctx_index, fill_all, 0))
    first_row = jnp.sum(jnp.where(device_ids < ctx_index, fill_all, 0))
    seq_ends = jnp.cumsum(seq_lengths[0])[:-1]
    row_ids = jnp.arange(row_count)
    valid_rows = (row_ids < fill_rows).astype(jnp.float32)
    segment = segment_of(first_row + jnp.minimum(row_ids, fill_rows - 1), seq_ends)
    halo_segment = segment_of(first_row - margin + jnp.arange(margin), seq_ends)
    inputs = tokens.astype(jnp.float32)
    inv_rms = lax.rsqrt(jnp.mean(inputs * inputs, axis=1, keepdims=True) + epsilon)
    gain_one = gain_norm.astype(jnp.float32)[None, :]
    normed = (inputs * inv_rms * gain_one).astype(jnp.bfloat16)
    z_raw = product(normed, z_weight).astype(jnp.bfloat16)
    x_raw = product(normed, x_weight).astype(jnp.bfloat16)
    bc_raw = product(normed, bc_weight).astype(jnp.bfloat16)
    dt_raw = product(normed, dt_weight).astype(jnp.bfloat16)
    conv_in = jnp.concatenate([x_raw, bc_raw], axis=1)
    tail_rows = lax.dynamic_slice_in_dim(conv_in, fill_rows - margin, margin, 0)
    halo_rows = from_behind(tail_rows, "ctx", 1)
    extended = jnp.concatenate([halo_rows, conv_in], axis=0).astype(jnp.float32)
    ext_segment = jnp.concatenate([halo_segment, segment])
    taps = jnp.concatenate([taps_inner.reshape(CONV, inner_local), taps_state], axis=1).astype(
        jnp.float32
    )
    shift_bias = jnp.concatenate([bias_inner.reshape(inner_local), bias_state]).astype(jnp.float32)
    same_masks = [
        (ext_segment[offset : offset + row_count] == segment).astype(jnp.float32)[:, None]
        for offset in range(CONV)
    ]
    pre_act = shift_bias[None, :] + sum(
        (
            taps[offset][None, :] * extended[offset : offset + row_count] * same_masks[offset]
            for offset in range(CONV)
        )
    )
    activated = jax.nn.silu(pre_act)
    x_conv = activated[:, :inner_local].astype(jnp.bfloat16)
    b_conv = activated[:, inner_local : inner_local + state_size].astype(jnp.bfloat16)
    c_conv = activated[:, inner_local + state_size :].astype(jnp.bfloat16)
    pre_step = dt_raw.astype(jnp.float32) + dt_bias[None, :]
    step_size = jax.nn.softplus(pre_step) * valid_rows[:, None]
    rates = jnp.exp(a_log)
    log_decay = -rates[None, :] * step_size
    x_blocks = x_conv.reshape(nblocks, BLOCK, heads_local, head_size)
    b_blocks = b_conv.reshape(nblocks, BLOCK, state_size)
    c_blocks = c_conv.reshape(nblocks, BLOCK, state_size)
    step_blocks = step_size.reshape(nblocks, BLOCK, heads_local)
    decay_blocks = log_decay.reshape(nblocks, BLOCK, heads_local)
    seg_blocks = segment.reshape(nblocks, BLOCK)
    seg_before = segment_of(
        first_row + jnp.minimum(jnp.arange(nblocks) * BLOCK, fill_rows) - 1, seq_ends
    )
    cum_decay = jnp.cumsum(decay_blocks, axis=1)
    gram = jnp.einsum("ctn,cjn->ctj", c_blocks, b_blocks, preferred_element_type=jnp.float32)
    in_block = jnp.arange(BLOCK)
    causal = in_block[:, None] >= in_block[None, :]
    keep = ((seg_blocks[:, :, None] == seg_blocks[:, None, :]) & causal[None]).astype(jnp.float32)
    cum_heads = jnp.swapaxes(cum_decay, 1, 2)
    diff = cum_heads[:, :, :, None] - cum_heads[:, :, None, :]
    kernel = jnp.exp(jnp.where(keep[:, None] > 0, diff, 0.0)) * keep[:, None]
    step_heads = jnp.swapaxes(step_blocks, 1, 2)
    weighting = kernel * step_heads[:, :, None, :]
    mixing = (gram[:, None] * weighting).astype(jnp.bfloat16)
    y_inner = jnp.einsum("chtj,cjhp->cthp", mixing, x_blocks, preferred_element_type=jnp.float32)
    end_keep = (seg_blocks == seg_blocks[:, -1:]).astype(jnp.float32)[:, :, None]
    end_kernel = jnp.exp(cum_decay[:, -1:, :] - cum_decay) * end_keep
    end_weight = end_kernel * step_blocks
    end_heads = jnp.swapaxes(end_weight, 1, 2)
    b_float = b_blocks.astype(jnp.float32)
    weighted_b = (end_heads[:, :, :, None] * b_float[:, None]).astype(jnp.bfloat16)
    block_state = jnp.einsum(
        "cjhp,chjn->chpn", x_blocks, weighted_b, preferred_element_type=jnp.float32
    )
    block_decay = (
        jnp.exp(cum_decay[:, -1, :])
        * (seg_blocks[:, -1] == seg_before).astype(jnp.float32)[:, None]
    )
    running = jnp.zeros_like(block_state[0])
    entry_local = []
    for block in range(nblocks):
        entry_local.append(running)
        running = block_decay[block][:, None, None] * running + block_state[block]
    device_decay = jnp.prod(block_decay, axis=0)
    device_state = running

    def relay_forward(turn_index, carry):
        incoming = from_behind(carry[1].astype(jnp.bfloat16), "ctx", 1).astype(jnp.float32)
        return (incoming, device_decay[:, None, None] * incoming + device_state)

    state_in = lax.fori_loop(
        0, ctx_count - 1, relay_forward, (jnp.zeros_like(device_state), device_state)
    )[0]
    factor = jnp.ones_like(device_decay)
    entries = []
    for block in range(nblocks):
        entries.append(entry_local[block] + factor[:, None, None] * state_in)
        factor = factor * block_decay[block]
    entry = jnp.stack(entries)
    entry_low = entry.astype(jnp.bfloat16)
    state_read = jnp.einsum(
        "ctn,chpn->cthp", c_blocks, entry_low, preferred_element_type=jnp.float32
    )
    enter_weight = (
        jnp.exp(cum_decay) * (seg_blocks == seg_before[:, None]).astype(jnp.float32)[:, :, None]
    )
    x_float = x_blocks.astype(jnp.float32)
    mixed = y_inner + enter_weight[..., None] * state_read + skip_d[None, None, :, None] * x_float
    mixed_rows = mixed.reshape(row_count, inner_local)
    z_float = z_raw.astype(jnp.float32)
    z_gate = jax.nn.silu(z_float)
    gated = mixed_rows * z_gate
    inner_all = inner_local * lax.axis_size("tp")
    squares = lax.psum(jnp.sum(gated * gated, axis=1), "tp")
    gate_inv = lax.rsqrt(squares / inner_all + epsilon)[:, None]
    gain_two = gain_gate.reshape(inner_local).astype(jnp.float32)[None, :]
    normal_out = (gated * gate_inv * gain_two).astype(jnp.bfloat16)
    branch = lax.psum_scatter(
        product(normal_out, out_weight).astype(jnp.bfloat16), "tp", scatter_dimension=1, tiled=True
    ).astype(jnp.float32)
    part_width = branch.shape[1]
    own_inputs = lax.dynamic_slice_in_dim(inputs, lax.axis_index("tp") * part_width, part_width, 1)
    layer_out = own_inputs + branch * valid_rows[:, None]
    grad_out = cotangent * valid_rows[:, None].astype(jnp.bfloat16)
    grad_out_weight = left_transposed(normal_out, grad_out)
    grad_normal = right_transposed(grad_out, out_weight)
    scaled = gain_two * grad_normal
    cross = lax.psum(jnp.sum(scaled * gated, axis=1), "tp")
    grad_gated = (
        gate_inv * scaled - gated * (gate_inv * gate_inv * gate_inv) * cross[:, None] / inner_all
    )
    grad_gain_gate = jnp.sum(grad_normal * gated * gate_inv, axis=0)
    grad_mixed = (grad_gated * z_gate).astype(jnp.bfloat16)
    grad_z = (grad_gated * mixed_rows * silu_slope(z_float)).astype(jnp.bfloat16)
    grad_blocks = grad_mixed.reshape(nblocks, BLOCK, heads_local, head_size)
    grad_float = grad_blocks.astype(jnp.float32)
    grad_read = (enter_weight[..., None] * grad_float).astype(jnp.bfloat16)
    grad_enter = jnp.sum(grad_float * state_read, axis=3)
    grad_skip = jnp.sum(grad_float * x_float, axis=(0, 1, 3))
    entry_grad = jnp.einsum(
        "ctn,cthp->chpn", c_blocks, grad_read, preferred_element_type=jnp.float32
    )
    running = jnp.zeros_like(device_state)
    exit_local = [running] * nblocks
    for block in reversed(range(nblocks)):
        exit_local[block] = running
        running = block_decay[block][:, None, None] * running + entry_grad[block]
    device_back = running

    def relay_backward(turn_index, carry):
        incoming = from_behind(carry[1].astype(jnp.bfloat16), "ctx", -1).astype(jnp.float32)
        return (incoming, device_decay[:, None, None] * incoming + device_back)

    grad_exit = lax.fori_loop(
        0, ctx_count - 1, relay_backward, (jnp.zeros_like(device_back), device_back)
    )[0]
    factor = jnp.ones_like(device_decay)
    exits = [running] * nblocks
    for block in reversed(range(nblocks)):
        exits[block] = exit_local[block] + factor[:, None, None] * grad_exit
        factor = factor * block_decay[block]
    grad_state = jnp.stack(exits)
    grad_state_low = grad_state.astype(jnp.bfloat16)
    grad_block_decay = jnp.sum(grad_state * entry, axis=(2, 3))
    grad_x = (
        jnp.einsum("chtj,cthp->cjhp", mixing, grad_blocks, preferred_element_type=jnp.float32)
        + jnp.einsum(
            "chjn,chpn->cjhp", weighted_b, grad_state_low, preferred_element_type=jnp.float32
        )
        + skip_d[None, None, :, None] * grad_float
    )
    grad_mixing = jnp.einsum(
        "cthp,cjhp->chtj", grad_blocks, x_blocks, preferred_element_type=jnp.float32
    )
    grad_gram = jnp.sum(grad_mixing * weighting, axis=1).astype(jnp.bfloat16)
    gram_kernel = grad_mixing * gram[:, None] * kernel
    grad_step = jnp.sum(gram_kernel, axis=2)
    gram_diff = gram_kernel * step_heads[:, :, None, :]
    grad_cum_heads = jnp.sum(gram_diff, axis=3) - jnp.sum(gram_diff, axis=2)
    grad_c = jnp.einsum(
        "ctj,cjn->ctn", grad_gram, b_blocks, preferred_element_type=jnp.float32
    ) + jnp.einsum("cthp,chpn->ctn", grad_read, entry_low, preferred_element_type=jnp.float32)
    grad_weighted = jnp.einsum(
        "cjhp,chpn->chjn", x_blocks, grad_state_low, preferred_element_type=jnp.float32
    )
    grad_b = jnp.einsum(
        "ctj,ctn->cjn", grad_gram, c_blocks, preferred_element_type=jnp.float32
    ) + jnp.einsum("chjn,chj->cjn", grad_weighted, end_heads)
    grad_end = jnp.swapaxes(jnp.einsum("chjn,cjn->chj", grad_weighted, b_float), 1, 2)
    end_part = grad_end * end_weight
    grad_cum = jnp.swapaxes(grad_cum_heads, 1, 2) - end_part + grad_enter * enter_weight
    grad_cum = grad_cum.at[:, -1, :].add(jnp.sum(end_part, axis=1) + grad_block_decay * block_decay)
    grad_log = jnp.flip(jnp.cumsum(jnp.flip(grad_cum, 1), axis=1), 1)
    grad_step_total = (
        jnp.swapaxes(grad_step, 1, 2) + grad_end * end_kernel - rates[None, None, :] * grad_log
    )
    grad_a_log = jnp.sum(grad_log * decay_blocks, axis=(0, 1))
    grad_pre_step = (
        grad_step_total.reshape(row_count, heads_local)
        * jax.nn.sigmoid(pre_step)
        * valid_rows[:, None]
    )
    grad_dt_bias = jnp.sum(grad_pre_step, axis=0)
    grad_dt = grad_pre_step.astype(jnp.bfloat16)
    grad_bc_act = lax.psum(
        jnp.concatenate([grad_b, grad_c], axis=2)
        .reshape(row_count, 2 * state_size)
        .astype(jnp.bfloat16),
        "tp",
    ).astype(jnp.float32)
    grad_act = jnp.concatenate([grad_x.reshape(row_count, inner_local), grad_bc_act], axis=1)
    grad_pre = grad_act * silu_slope(pre_act)
    grad_shift_bias = jnp.sum(grad_pre, axis=0)
    grad_taps = jnp.stack(
        [
            jnp.sum(grad_pre * extended[offset : offset + row_count] * same_masks[offset], axis=0)
            for offset in range(CONV)
        ]
    )
    grad_ext = sum(
        (
            jnp.pad(
                taps[offset][None, :] * grad_pre * same_masks[offset],
                ((offset, margin - offset), (0, 0)),
            )
            for offset in range(CONV)
        )
    )
    returned = from_behind(grad_ext[:margin], "ctx", -1)
    grad_conv_in = grad_ext[margin:] + lax.dynamic_update_slice_in_dim(
        jnp.zeros((row_count, channels), jnp.float32), returned, fill_rows - margin, 0
    )
    grad_x_raw = grad_conv_in[:, :inner_local].astype(jnp.bfloat16)
    grad_bc_raw = grad_conv_in[:, inner_local:].astype(jnp.bfloat16)
    grad_z_weight = left_transposed(normed, grad_z)
    grad_x_weight = left_transposed(normed, grad_x_raw)
    grad_bc_weight = left_transposed(normed, grad_bc_raw)
    grad_dt_weight = left_transposed(normed, grad_dt)
    leading = (lax.axis_index("tp") == 0).astype(jnp.float32)
    partial_normed = (
        right_transposed(grad_z, z_weight)
        + right_transposed(grad_x_raw, x_weight)
        + right_transposed(grad_dt, dt_weight)
        + leading * right_transposed(grad_bc_raw, bc_weight)
    )
    grad_normed = lax.psum(partial_normed.astype(jnp.bfloat16), "tp").astype(jnp.float32)
    scaled_in = gain_one * grad_normed
    inner_dot = jnp.sum(scaled_in * inputs, axis=1, keepdims=True)
    grad_inputs = (
        inv_rms * scaled_in
        - inputs * (inv_rms * inv_rms * inv_rms) * inner_dot / model_width
        + cotangent.astype(jnp.float32)
    )
    grad_gain_norm = jnp.sum(grad_normed * inputs * inv_rms, axis=0)
    heads_part = jnp.stack([grad_dt_bias, grad_a_log, grad_skip])
    spread = jnp.broadcast_to(heads_part[None], (lax.axis_size("dp"), 3, heads_local))
    shards = (
        lax.psum_scatter(
            grad_gain_norm.astype(jnp.bfloat16), "dp", scatter_dimension=0, tiled=True
        ).astype(jnp.float32),
        lax.psum_scatter(
            grad_z_weight.astype(jnp.bfloat16), "dp", scatter_dimension=0, tiled=True
        ).astype(jnp.float32),
        lax.psum_scatter(
            grad_x_weight.astype(jnp.bfloat16), "dp", scatter_dimension=0, tiled=True
        ).astype(jnp.float32),
        lax.psum_scatter(
            grad_bc_weight.astype(jnp.bfloat16), "dp", scatter_dimension=0, tiled=True
        ).astype(jnp.float32),
        lax.psum_scatter(
            grad_dt_weight.astype(jnp.bfloat16), "dp", scatter_dimension=0, tiled=True
        ).astype(jnp.float32),
        lax.psum_scatter(
            grad_taps[:, :inner_local].reshape(CONV, heads_local, head_size).astype(jnp.bfloat16),
            "dp",
            scatter_dimension=2,
            tiled=True,
        ).astype(jnp.float32),
        lax.psum_scatter(
            grad_shift_bias[:inner_local].reshape(heads_local, head_size).astype(jnp.bfloat16),
            "dp",
            scatter_dimension=1,
            tiled=True,
        ).astype(jnp.float32),
        lax.psum_scatter(
            grad_taps[:, inner_local:].astype(jnp.bfloat16), "dp", scatter_dimension=1, tiled=True
        ).astype(jnp.float32),
        lax.psum_scatter(
            grad_shift_bias[inner_local:].astype(jnp.bfloat16),
            "dp",
            scatter_dimension=0,
            tiled=True,
        ).astype(jnp.float32),
        lax.psum_scatter(
            grad_gain_gate.reshape(heads_local, head_size).astype(jnp.bfloat16),
            "dp",
            scatter_dimension=1,
            tiled=True,
        ).astype(jnp.float32),
        lax.psum_scatter(
            grad_out_weight.astype(jnp.bfloat16), "dp", scatter_dimension=1, tiled=True
        ).astype(jnp.float32),
        lax.psum_scatter(spread.astype(jnp.bfloat16), "dp", scatter_dimension=0, tiled=True).astype(
            jnp.float32
        ),
    )
    totals = (
        lax.psum(shards[0].astype(jnp.bfloat16), "ctx").astype(jnp.float32),
        lax.psum(shards[1].astype(jnp.bfloat16), "ctx").astype(jnp.float32),
        lax.psum(shards[2].astype(jnp.bfloat16), "ctx").astype(jnp.float32),
        lax.psum(shards[3].astype(jnp.bfloat16), "ctx").astype(jnp.float32),
        lax.psum(shards[4].astype(jnp.bfloat16), "ctx").astype(jnp.float32),
        lax.psum(shards[5].astype(jnp.bfloat16), "ctx").astype(jnp.float32),
        lax.psum(shards[6].astype(jnp.bfloat16), "ctx").astype(jnp.float32),
        lax.psum(shards[7].astype(jnp.bfloat16), "ctx").astype(jnp.float32),
        lax.psum(shards[8].astype(jnp.bfloat16), "ctx").astype(jnp.float32),
        lax.psum(shards[9].astype(jnp.bfloat16), "ctx").astype(jnp.float32),
        lax.psum(shards[10].astype(jnp.bfloat16), "ctx").astype(jnp.float32),
        lax.psum(shards[11].astype(jnp.bfloat16), "ctx").astype(jnp.float32),
    )
    return (
        layer_out,
        grad_inputs,
        totals[0],
        totals[1],
        totals[2],
        totals[3],
        totals[4],
        totals[5],
        totals[6],
        totals[7],
        totals[8],
        totals[11][0, 0],
        totals[11][0, 1],
        totals[11][0, 2],
        totals[9],
        totals[10],
    )


def solution(mesh):
    placed = (
        P(("dp", "ctx"), None),
        P(("dp", "ctx"), None),
        P("dp", None),
        P("dp", None),
        P("dp"),
        P("dp", "tp"),
        P("dp", "tp"),
        P("dp", None),
        P("dp", "tp"),
        P(None, "tp", "dp"),
        P("tp", "dp"),
        P(None, "dp"),
        P("dp"),
        P("tp"),
        P("tp"),
        P("tp"),
        P("tp", "dp"),
        P("tp", "dp"),
    )
    return jax.shard_map(
        body,
        mesh=mesh,
        in_specs=placed,
        out_specs=(
            P(("dp", "ctx"), "tp"),
            P(("dp", "ctx"), None),
            P("dp"),
            P("dp", "tp"),
            P("dp", "tp"),
            P("dp", None),
            P("dp", "tp"),
            P(None, "tp", "dp"),
            P("tp", "dp"),
            P(None, "dp"),
            P("dp"),
            P("tp"),
            P("tp"),
            P("tp"),
            P("tp", "dp"),
            P("tp", "dp"),
        ),
        check_vma=False,
    )
```

profile of v0, /device:TPU:0, one launch (start us, length us, event | category | flops | bytes accessed | tf_op | source)
XLA Modules:
  0.0 698.5 jit_solution(11256696687080779608)
XLA Ops:
  24.6 14.1 %all-reduce.12 = (bf16[768]{0:T(1024)(128)(2,1)S(1)}, bf16[256]{0:T(256)(128)(2,1)}) all-reduce(bf16[768]{0:T(1024)(128)(2,1)S(1)} %dynamic-update-slice.5, bf16[256]{0:T(256)(128)(2,1)S(1)} %dynamic-update-slice.4), channel_id=1, replica_groups=mesh['dp'=4,'ctx'=4,'tp'=2] {'dp'}, use_global_device_ids=true, to_apply=%add.5 | all-reduce | flops 1024 | bytes 4096
  43.5 13.4 %all-gather.1 = bf16[4,192,12]{1,2,0:T(8,128)(2,1)S(1)} all-gather(bf16[1,192,12]{1,2,0:T(8,128)(2,1)} %bitcast.348), channel_id=1, replica_groups=mesh['dp'=4,'ctx'=4,'tp'=2] {'dp'}, dimensions={0}, use_global_device_ids=true | all-gather | bytes 23040 | tf_op jit(solution)/shard_map/all_gather | solution.py:85
  65.6 7.7 %all-gather = bf16[4,64,4]{1,2,0:T(4,128)(2,1)S(1)} all-gather(bf16[1,64,4]{1,2,0:T(4,128)(2,1)S(1)} %bitcast.356), channel_id=1, replica_groups=mesh['dp'=4,'ctx'=4,'tp'=2] {'dp'}, dimensions={0}, use_global_device_ids=true | all-gather | bytes 2560 | tf_op jit(solution)/shard_map/all_gather | solution.py:88
  73.4 13.2 %all_gather.33 = bf16[12,64]{0,1:T(8,128)(2,1)S(1)} all-gather(bf16[12,16]{0,1:T(8,128)(2,1)S(1)} %copy.366), channel_id=1, replica_groups=mesh['dp'=4,'ctx'=4,'tp'=2] {'dp'}, dimensions={1}, use_global_device_ids=true | all-gather | bytes 1920 | tf_op jit(solution)/shard_map/all_gather | solution.py:87
  87.4 13.6 %all_gather.35 = bf16[4,12,64]{1,0,2:T(4,128)(2,1)S(1)} all-gather(bf16[4,12,16]{1,0,2:T(4,128)(2,1)S(1)} %copy.368), channel_id=1, replica_groups=mesh['dp'=4,'ctx'=4,'tp'=2] {'dp'}, dimensions={2}, use_global_device_ids=true | all-gather | bytes 7680 | tf_op jit(solution)/shard_map/all_gather | solution.py:86
  102.2 16.0 %all_gather.39 = bf16[768,256]{1,0:T(8,128)(2,1)S(1)} all-gather(bf16[192,256]{1,0:T(8,128)(2,1)S(1)} %copy-done.52), channel_id=1, replica_groups=mesh['dp'=4,'ctx'=4,'tp'=2] {'dp'}, dimensions={0}, use_global_device_ids=true | all-gather | bytes 491520 | tf_op jit(solution)/shard_map/all_gather | solution.py:84
  135.5 13.6 %all_gather.42 = bf16[12,64]{0,1:T(8,128)(2,1)S(1)} all-gather(bf16[12,16]{0,1:T(8,128)(2,1)S(1)} %copy.395), channel_id=1, replica_groups=mesh['dp'=4,'ctx'=4,'tp'=2] {'dp'}, dimensions={1}, use_global_device_ids=true | all-gather | bytes 1920 | tf_op jit(solution)/shard_map/all_gather | solution.py:90
  183.7 24.4 %while.25 = (s32[]{:T(128)}, f32[12,64,128]{2,1,0:T(8,128)}, bf16[12,64,128]{2,1,0:T(8,128)(2,1)S(1)}, f32[12]{0:T(128)S(1)}, f32[12,64,128]{2,1,0:T(8,128)S(1)}, /*index=5*/s32[]{:T(128)}) while((s32[]{:T(128)}, f32[12,64,128]{2,1,0:T(8,128)}, bf16[12,64,128]{2,1,0:T(8,128)(2,1)S(1)}, f32[12]{0:T(128)S(1)}, f32[12,64,128]{2,1,0:T(8,128)S(1)}, ...), condition=%wide.region_11.12_spmd, body=%wide.region_10.11_spmd.sunk | while | flops 393218 | bytes 1966237 | solution.py:191
  241.1 7.0 %multiply_reduce_fusion.8 = (f32[768]{0:T(1024)}, bf16[1024,768]{0,1:T(8,128)(2,1)}, bf16[1024,768]{0,1:T(8,128)(2,1)}) fusion(bf16[1024,1024]{0,1:T(8,128)(2,1)} %copy-done.5, f32[1024]{0:T(1024)S(1)} %psum.113, f32[1024]{0:T(1024)} %get-tuple-element.303, f32[1024,768]{0,1:T(8,128)} %bitcast.295, bf16[1024,768]{0,1:T(8,128)(2,1)} %get-tuple-element.322, ...), kind=kLoop, calls=%fused_computation.66 | loop fusion | flops 19660032 | bytes 12601344 | tf_op jit(solution)/shard_map/reduce_sum | solution.py:239
  256.5 11.1 %multiply_reduce_fusion.1 = (f32[4,12,256]{2,1,0:T(8,128)}, f32[4,12,256]{2,1,0:T(8,128)}, f32[4,12,256]{2,1,0:T(8,128)}, bf16[4,256,256]{2,1,0:T(8,128)(2,1)}) fusion(f32[4,12,256]{2,1,0:T(8,128)S(1)} %copy-done.62, f32[4,256,256]{2,1,0:T(8,128)S(1)} %copy-done.46, f32[4,12,256]{2,1,0:T(8,128)S(1)} %copy-done.60, pred[4,256,256]{2,1,0:T(8,128)(4,1)S(1)} %copy-done.50, ...), kind=kOutput, calls=%fused_computation.7 | convolution fusion | flops 440102912 | bytes 6275072 | tf_op jit(solution)/shard_map/cthp,cjhp->chtj/dot_general | solution.py:272
  276.5 35.2 %while.26 = (s32[]{:T(128)}, f32[12,64,128]{2,1,0:T(8,128)}, bf16[12,64,128]{2,1,0:T(8,128)(2,1)}, f32[12]{0:T(128)}, f32[12,64,128]{2,1,0:T(8,128)S(1)}, /*index=5*/s32[]{:T(128)}) while((s32[]{:T(128)}, f32[12,64,128]{2,1,0:T(8,128)}, bf16[12,64,128]{2,1,0:T(8,128)(2,1)}, f32[12]{0:T(128)}, f32[12,64,128]{2,1,0:T(8,128)S(1)}, ...), condition=%wide.region_18.19_spmd, body=%wide.region_17.18_spmd.sunk | while | flops 393218 | bytes 1966237 | solution.py:254
  277.8 9.5 %collective-permute-done.1 = bf16[12,64,128]{2,1,0:T(8,128)(2,1)} collective-permute-done((bf16[12,64,128]{2,1,0:T(8,128)(2,1)}, bf16[12,64,128]{2,1,0:T(8,128)(2,1)}, u32[]{:S(2)}, u32[]{:S(2)}) %collective-permute-start.1) | collective-permute-done | bytes 196640 | tf_op jit(solution)/shard_map/while/body/eval_jaxpr/ppermute | solution.py:16
  290.4 9.0 %collective-permute-done.1 = bf16[12,64,128]{2,1,0:T(8,128)(2,1)} collective-permute-done((bf16[12,64,128]{2,1,0:T(8,128)(2,1)}, bf16[12,64,128]{2,1,0:T(8,128)(2,1)}, u32[]{:S(2)}, u32[]{:S(2)}) %collective-permute-start.1) | collective-permute-done | bytes 196640 | tf_op jit(solution)/shard_map/while/body/eval_jaxpr/ppermute | solution.py:16
  302.5 7.4 %collective-permute-done.1 = bf16[12,64,128]{2,1,0:T(8,128)(2,1)} collective-permute-done((bf16[12,64,128]{2,1,0:T(8,128)(2,1)}, bf16[12,64,128]{2,1,0:T(8,128)(2,1)}, u32[]{:S(2)}, u32[]{:S(2)}) %collective-permute-start.1) | collective-permute-done | bytes 196640 | tf_op jit(solution)/shard_map/while/body/eval_jaxpr/ppermute | solution.py:16
  394.1 12.3 %multiply_reduce_fusion.6 = (f32[1024]{0:T(1024)S(1)}, f32[1024]{0:T(1024)S(1)}, f32[1024]{0:T(1024)S(1)}, f32[1024]{0:T(1024)S(1)}, bf16[1024]{0:T(1024)(128)(2,1)S(1)}, /*index=5*/f32[1024,1024]{0,1:T(8,128)S(1)}) fusion(f32[1027,1024]{0,1:T(8,128)} %copy-done, f32[1024]{0:T(1024)S(1)} %get-tuple-element.298, f32[1024]{0:T(1024)S(1)} %get-tuple-element.300, ...), kind=kLoop, calls=%fused_computation.27 | loop fusion | flops 22014976 | bytes 29390848 | tf_op jit(solution)/shard_map/reduce_sum | solution.py:316
  410.4 9.6 %pad_add_fusion = f32[1027,1024]{0,1:T(8,128)} fusion(f32[1024,1024]{0,1:T(8,128)S(1)} %get-tuple-element.275, f32[1024,1024]{0,1:T(8,128)} %get-tuple-element.276, f32[1024,1024]{0,1:T(8,128)} %get-tuple-element.277, f32[1024,1024]{0,1:T(8,128)S(1)} %get-tuple-element.274), kind=kLoop, calls=%fused_computation.20 | loop fusion | flops 3154944 | bytes 20983808 | tf_op jit(solution)/shard_map/add | solution.py:320
  482.4 19.9 %all-reduce.19.cloned.1.call-done = bf16[1024,768]{1,0:T(8,128)(2,1)} async-done(((bf16[1024,768]{1,0:T(8,128)(2,1)}), bf16[1024,768]{1,0:T(8,128)(2,1)}) %all-reduce.19.cloned.1.call-update) | async-done | bytes 1572880 | tf_op jit(solution)/shard_map/psum | solution.py:346
  505.1 12.1 %all-reduce.11 = (bf16[768]{0:T(1024)(128)(2,1)S(1)}, bf16[256]{0:T(256)(128)(2,1)S(1)}, bf16[4,3,12]{2,1,0:T(4,128)(2,1)S(1)}) all-reduce(bf16[768]{0:T(1024)(128)(2,1)S(1)} %get-tuple-element.205, bf16[256]{0:T(256)(128)(2,1)S(1)} %slice.239, ...), channel_id=3, replica_groups=mesh['dp'=4,'ctx'=4,'tp'=2] {'dp'}, use_global_device_ids=true, to_apply=%region_32.33.clone | all-reduce | flops 1168 | bytes 4672
  517.3 9.9 %reduce-scatter.27.cloned.1.call-done = bf16[192,256]{1,0:T(8,128)(2,1)} async-done(((bf16[768,256]{1,0:T(8,128)(2,1)}), bf16[192,256]{1,0:T(8,128)(2,1)}) %reduce-scatter.27.cloned.1.call-update) | async-done | bytes 98320 | tf_op jit(solution)/shard_map/reduce_scatter | solution.py:367
  527.2 29.6 %reduce-scatter.29.cloned.1.call-done = bf16[768,192]{0,1:T(8,128)(2,1)} async-done(((bf16[768,768]{0,1:T(8,128)(2,1)}), bf16[768,192]{0,1:T(8,128)(2,1)}) %reduce-scatter.29.cloned.1.call-update) | async-done | bytes 294928 | tf_op jit(solution)/shard_map/reduce_scatter | solution.py:400
  556.8 30.2 %reduce-scatter.23.cloned.1.call-done = bf16[192,768]{1,0:T(8,128)(2,1)} async-done(((bf16[768,768]{1,0:T(8,128)(2,1)}), bf16[192,768]{1,0:T(8,128)(2,1)}) %reduce-scatter.23.cloned.1.call-update) | async-done | bytes 294928 | tf_op jit(solution)/shard_map/reduce_scatter | solution.py:361
  587.0 30.1 %reduce-scatter.25.cloned.1.call-done = bf16[192,768]{1,0:T(8,128)(2,1)} async-done(((bf16[768,768]{1,0:T(8,128)(2,1)}), bf16[192,768]{1,0:T(8,128)(2,1)}) %reduce-scatter.25.cloned.1.call-update) | async-done | bytes 294928 | tf_op jit(solution)/shard_map/reduce_scatter | solution.py:364
  618.0 16.7 %all-reduce.9 = (bf16[4,12,16]{2,1,0:T(8,128)(2,1)S(1)}, bf16[192]{0:T(256)(128)(2,1)S(1)}, bf16[192,12]{0,1:T(8,128)(2,1)S(1)}, bf16[12,16]{1,0:T(8,128)(2,1)S(...) all-reduce(bf16[4,12,16]{2,1,0:T(8,128)(2,1)S(1)} %copy.446, ...), channel_id=1, replica_groups=mesh['dp'=4,'ctx'=4,'tp'=2] {'ctx'}, use_global_device_ids=true, to_apply=%region_47.48 | all-reduce | flops 4004 | bytes 16016 | tf_op jit(solution)/shard_map/psum | solution.py:413
  647.2 37.5 %all-reduce.21.cloned.1.call-done = (bf16[192,768]{1,0:T(8,128)(2,1)}, bf16[192,768]{1,0:T(8,128)(2,1)}, bf16[192,256]{1,0:T(8,128)(2,1)}, bf16[768,192]{0,1:T(8,128)(2,1)}) async-done(((bf16[192,768]{1,0:T(8,128)(2,1)}, bf16[192,768]{1,0:T(8,128)(2,1)}, bf16[192,256]{1,0:T(8,128)(2,1)}, bf16[768,192]{0,1:T(8,128)(2,1)}), (bf16[192,768]{1,0:T(8,128)(2,1)}, bf16[192,768]{1,0:T(8,128)(2,1)}, ...) | async-done | bytes 983056 | tf_op jit(solution)/shard_map/psum | solution.py:409
  (475 shorter events, 333.8 us)
Async XLA Ops:
  7.2 117.2 %all-gather.6.cloned.1.call-start = ((), (), s32[]{:S(2)}) async-start(), calls=%async_computation.10 | async-start | bytes 1474560 | tf_op jit(solution)/shard_map/all_gather | solution.py:83
  7.9 213.2 %all-gather.8.cloned.1.call-start = ((), (), s32[]{:S(2)}) async-start(), calls=%async_computation.11 | async-start | bytes 1474560 | tf_op jit(solution)/shard_map/all_gather | solution.py:82
  8.7 222.9 %all-gather.10.cloned.1.call-start = ((), (), s32[]{:S(2)}) async-start(), calls=%async_computation.12 | async-start | bytes 1474560 | tf_op jit(solution)/shard_map/all_gather | solution.py:91
  9.4 383.5 %all-reduce.17.cloned.1.call-start = ((), (), s32[]{:S(2)}) async-start(), calls=%async_computation.13 | async-start | bytes 1048576 | tf_op jit(solution)/shard_map/psum | solution.py:305
  128.5 25.2 %collective-permute-start.2 = (bf16[3,1024]{0,1:T(8,128)(2,1)}, bf16[3,1024]{0,1:T(8,128)(2,1)}, u32[]{:S(2)}, u32[]{:S(2)}) collective-permute-start(bf16[3,1024]{0,1:T(8,128)(2,1)} %fusion.83), channel_id=1, source_target_pairs={{0,2},{2,4},{4,6},{1,3},{3,5},{5,7},{8,10},{10,12},{12,14},{9,11},... | collective-permute-start | bytes 18440 | tf_op jit(solution)/shard_map/ppermute | solution.py:16
  183.7 5.9 collective-permute-start
  190.4 7.6 %collective-permute-start = (bf16[12,64,128]{2,1,0:T(8,128)(2,1)S(1)}, bf16[12,64,128]{2,1,0:T(8,128)(2,1)S(1)}, u32[]{:S(2)}, u32[]{:S(2)}) collective-permute-start(bf16[12,64,128]{2,1,0:T(8,128)(2,1)S(1)} %get-tuple-element.400), channel_id=1, source_target_pairs={{0,2},{2,4},{4,6},{1,3},{3,5},{5,7},{8,10},{10,12},{12,14},{9,11},... | collective-permute-start | bytes 589832 | tf_op jit(solution)/shard_map/while/body/eval_jaxpr/ppermute | solution.py:16
  198.7 8.4 %collective-permute-start = (bf16[12,64,128]{2,1,0:T(8,128)(2,1)S(1)}, bf16[12,64,128]{2,1,0:T(8,128)(2,1)S(1)}, u32[]{:S(2)}, u32[]{:S(2)}) collective-permute-start(bf16[12,64,128]{2,1,0:T(8,128)(2,1)S(1)} %get-tuple-element.400), channel_id=1, source_target_pairs={{0,2},{2,4},{4,6},{1,3},{3,5},{5,7},{8,10},{10,12},{12,14},{9,11},... | collective-permute-start | bytes 589832 | tf_op jit(solution)/shard_map/while/body/eval_jaxpr/ppermute | solution.py:16
  276.5 10.8 %collective-permute-start.1 = (bf16[12,64,128]{2,1,0:T(8,128)(2,1)}, bf16[12,64,128]{2,1,0:T(8,128)(2,1)}, u32[]{:S(2)}, u32[]{:S(2)}) collective-permute-start(bf16[12,64,128]{2,1,0:T(8,128)(2,1)} %get-tuple-element.418), channel_id=1, source_target_pairs={{2,0},{4,2},{6,4},{3,1},{5,3},{7,5},{10,8},{12,10},{14,12},{11,9},... | collective-permute-start | bytes 589832 | tf_op jit(solution)/shard_map/while/body/eval_jaxpr/ppermute | solution.py:16
  289.1 10.3 %collective-permute-start.1 = (bf16[12,64,128]{2,1,0:T(8,128)(2,1)}, bf16[12,64,128]{2,1,0:T(8,128)(2,1)}, u32[]{:S(2)}, u32[]{:S(2)}) collective-permute-start(bf16[12,64,128]{2,1,0:T(8,128)(2,1)} %get-tuple-element.418), channel_id=1, source_target_pairs={{2,0},{4,2},{6,4},{3,1},{5,3},{7,5},{10,8},{12,10},{14,12},{11,9},... | collective-permute-start | bytes 589832 | tf_op jit(solution)/shard_map/while/body/eval_jaxpr/ppermute | solution.py:16
  301.2 8.7 %collective-permute-start.1 = (bf16[12,64,128]{2,1,0:T(8,128)(2,1)}, bf16[12,64,128]{2,1,0:T(8,128)(2,1)}, u32[]{:S(2)}, u32[]{:S(2)}) collective-permute-start(bf16[12,64,128]{2,1,0:T(8,128)(2,1)} %get-tuple-element.418), channel_id=1, source_target_pairs={{2,0},{4,2},{6,4},{3,1},{5,3},{7,5},{10,8},{12,10},{14,12},{11,9},... | collective-permute-start | bytes 589832 | tf_op jit(solution)/shard_map/while/body/eval_jaxpr/ppermute | solution.py:16
  349.1 127.8 %reduce-scatter.41.cloned.1.call-start = ((), (), s32[]{:S(2)}) async-start(), calls=%async_computation.24 | async-start | bytes 20480
  381.2 96.5 %reduce-scatter.33.cloned.1.call-start = ((), (), s32[]{:S(2)}) async-start(), calls=%async_computation.20 | async-start | bytes 245760
  387.8 90.8 %reduce-scatter.37.cloned.1.call-start = ((), (), s32[]{:S(2)}) async-start(), calls=%async_computation.22 | async-start | bytes 20480
  422.4 57.0 %reduce-scatter.39.cloned.1.call-start = ((), (), s32[]{:S(2)}) async-start(), calls=%async_computation.23 | async-start | bytes 81920
  423.2 14.4 %collective-permute-start.3 = (f32[3,1024]{0,1:T(8,128)S(1)}, f32[3,1024]{0,1:T(8,128)S(1)}, u32[]{:S(2)}, u32[]{:S(2)}) collective-permute-start(f32[3,1024]{0,1:T(8,128)S(1)} %pad_add_fusion.1), channel_id=1, source_target_pairs={{2,0},{4,2},{6,4},{3,1},{5,3},{7,5},{10,8},{12,10},{14,12},{11,9},... | collective-permute-start | bytes 36872 | tf_op jit(solution)/shard_map/ppermute | solution.py:16
  424.5 57.0 %reduce-scatter.35.cloned.1.call-start = ((), (), s32[]{:S(2)}) async-start(), calls=%async_computation.21 | async-start | bytes 20480
  431.1 71.1 %all-reduce.19.cloned.1.call-start = ((), (), s32[]{:S(2)}) async-start(), calls=%async_computation.14 | async-start | bytes 3145728 | tf_op jit(solution)/shard_map/psum | solution.py:346
  450.5 76.7 %reduce-scatter.27.cloned.1.call-start = ((), (), s32[]{:S(2)}) async-start(), calls=%async_computation.17 | async-start | bytes 491520 | tf_op jit(solution)/shard_map/reduce_scatter | solution.py:367
  453.1 103.7 %reduce-scatter.29.cloned.1.call-start = ((), (), s32[]{:S(2)}) async-start(), calls=%async_computation.18 | async-start | bytes 1474560 | tf_op jit(solution)/shard_map/reduce_scatter | solution.py:400
  458.6 128.4 %reduce-scatter.23.cloned.1.call-start = ((), (), s32[]{:S(2)}) async-start(), calls=%async_computation.15 | async-start | bytes 1474560 | tf_op jit(solution)/shard_map/reduce_scatter | solution.py:361
  462.6 154.5 %reduce-scatter.25.cloned.1.call-start = ((), (), s32[]{:S(2)}) async-start(), calls=%async_computation.16 | async-start | bytes 1474560 | tf_op jit(solution)/shard_map/reduce_scatter | solution.py:364
  466.6 176.3 %reduce-scatter.31.cloned.1.call-start = ((), (), s32[]{:S(2)}) async-start(), calls=%async_computation.19 | async-start | bytes 2359296
  473.2 211.5 %all-reduce.21.cloned.1.call-start = ((), (), s32[]{:S(2)}) async-start(), calls=%async_computation.25 | async-start | bytes 1966080 | tf_op jit(solution)/shard_map/psum | solution.py:409
  (103 other events, 1512.1 us)
Sparse Core Ops, SparseCore 0:
  9.6 33.3 all-gather.5
  44.5 29.3 all-gather.7
  75.5 35.1 all-gather.9
  349.3 18.7 all-reduce.16
  381.3 18.9 reduce-scatter.40
  402.9 17.3 reduce-scatter.32
  423.3 18.1 reduce-scatter.36
  444.3 17.1 reduce-scatter.38
  464.4 17.0 reduce-scatter.34
  483.7 18.4 all-reduce.18
  505.2 21.9 reduce-scatter.26
  529.4 27.3 reduce-scatter.28
  559.1 27.8 reduce-scatter.22
  589.2 27.8 reduce-scatter.24
  619.8 7.7 reduce-scatter.30
  631.3 53.4 all-reduce.20
where the time goes:
time: 708 us; the launch traced here: 699 us
  waiting for transfers between devices  203 us (29%)
  other arithmetic  129 us (18%)
  blocking collectives  126 us (18%)
  matrix products  101 us (14%)
  local copies, waits for them, and re-layouts  95.9 us (14%)
  starting transfers between devices  22.9 us (3%)
  between operations  20.9 us (3%)
    ppermute x8, waiting for transfers between devices, from_behind(): lax.ppermute(value, axis, [(source, source + steps) for source in range(f...  41.7 us
    psum x1, waiting for transfers between devices, body(): lax.psum(shards[1].astype(jnp.bfloat16), 'ctx').astype(jnp.float32)  37.5 us
    reduce_scatter x1, waiting for transfers between devices, body(): lax.psum_scatter(grad_z_weight.astype(jnp.bfloat16), 'dp', scatter_dimens...  30.2 us
    reduce_scatter x1, waiting for transfers between devices, body(): lax.psum_scatter(grad_x_weight.astype(jnp.bfloat16), 'dp', scatter_dimens...  30.1 us
    reduce_scatter x1, waiting for transfers between devices, body(): lax.psum_scatter(grad_out_weight.astype(jnp.bfloat16), 'dp', scatter_dime...  29.6 us
    unnamed x238, local copies, waits for them, and re-layouts  28.6 us
    unnamed x2, blocking collectives  26.3 us
    ppermute x8, starting transfers between devices, from_behind(): lax.ppermute(value, axis, [(source, source + steps) for source in range(f...  21.6 us
  transfers between devices with their start and end apart: 24, of which 14 were waited for; matrix products, arithmetic and copies ran while one was open for 33% of the time, Pallas kernels for 0%

commit v1 on v0

v1 whole, which is shorter than its diff:
```python
import functools

import jax
import jax.numpy as jnp
from jax import lax
from jax.experimental import pallas as pl
from jax.experimental.pallas import tpu as pltpu
from jax.sharding import PartitionSpec as P

CONV = 4
BLOCK = 256
HEAD = 64
LANES = 128
EPS = 1e-05
VMEM = 56 * 1024 * 1024
F32 = jnp.float32
BF16 = jnp.bfloat16


def dot(left, right):
    return jnp.dot(left, right, preferred_element_type=F32)


def dot_tn(left, right):
    return lax.dot_general(left, right, (((0,), (0,)), ((), ())), preferred_element_type=F32)


def dot_nt(left, right):
    return lax.dot_general(left, right, (((1,), (1,)), ((), ())), preferred_element_type=F32)


def dot_exact(left, right):
    return jnp.dot(left, right, preferred_element_type=F32, precision=lax.Precision.HIGHEST)


def iota(shape, dim):
    return lax.broadcasted_iota(jnp.int32, shape, dim)


def sigmoid(value):
    return 1.0 / (1.0 + jnp.exp(-value))


def softplus(value):
    return jnp.maximum(value, 0.0) + jnp.log1p(jnp.exp(-jnp.abs(value)))


def split(value):
    high = value.astype(BF16)
    return high, (value - high.astype(F32)).astype(BF16)


def expand(value, spread):
    return dot(jnp.concatenate(split(value), axis=1), spread[...])


def reduce_heads(value, spread):
    high, low = split(value)
    pick = spread[:LANES, :]
    return dot_nt(high, pick) + dot_nt(low, pick)


def head_column(row, channels):
    shape = (channels, LANES)
    return jnp.sum(jnp.where(iota(shape, 0) // HEAD == iota(shape, 1), row, 0.0), axis=1, keepdims=True)


def xor(value, mask):
    return jnp.bitwise_xor(value, jnp.int32(mask))


class Place:
    def __init__(self, info, counts):
        devices, sequences = counts
        own = info[devices + sequences]
        self.ctx = own
        self.tp = info[devices + sequences + 1]
        self.dp = info[devices + sequences + 2]
        self.fill = jnp.int32(0)
        self.first = jnp.int32(0)
        for device in range(devices):
            rows = info[device] * BLOCK
            self.fill = self.fill + jnp.where(own == device, rows, 0)
            self.first = self.first + jnp.where(own > device, rows, 0)
        self.ends = []
        total = jnp.int32(0)
        for sequence in range(sequences - 1):
            total = total + info[devices + sequence]
            self.ends.append(total)

    def of(self, position):
        found = (position >= self.ends[0]).astype(jnp.int32)
        for end in self.ends[1:]:
            found = found + (position >= end).astype(jnp.int32)
        return jnp.where(position < 0, -1, found)

    def rows(self, index):
        return self.of(self.first + jnp.minimum(index, self.fill - 1))

    def before(self, block):
        position = self.first + jnp.minimum(block * BLOCK, self.fill) - 1
        found = jnp.int32(0)
        for end in self.ends:
            found = found + jnp.where(position >= end, 1, 0)
        return jnp.where(position < 0, -1, found)

    def last(self, block):
        position = self.first + jnp.minimum(block * BLOCK + BLOCK - 1, self.fill - 1)
        found = jnp.int32(0)
        for end in self.ends:
            found = found + jnp.where(position >= end, 1, 0)
        return found

    def column(self, block, shift=0):
        return self.rows(block * BLOCK + shift + iota((BLOCK, 1), 0))

    def valid(self, block):
        return (block * BLOCK + iota((BLOCK, 1), 0) < self.fill).astype(F32)

    def keep(self, block):
        down = self.rows(block * BLOCK + iota((BLOCK, BLOCK), 0))
        across = self.rows(block * BLOCK + iota((BLOCK, BLOCK), 1))
        return (down == across) & (iota((BLOCK, BLOCK), 0) >= iota((BLOCK, BLOCK), 1))


def step_sizes(place, block, pre_step, heads):
    lane = iota((BLOCK, LANES), 1)
    return jnp.where(lane < heads, softplus(pre_step), 0.0) * place.valid(block)


def end_weights(place, block, cum):
    same = (place.column(block) == place.last(block)).astype(F32)
    return jnp.exp(cum[BLOCK - 1 :, :] - cum) * same


def enter_weights(place, block, cum):
    return jnp.exp(cum) * (place.column(block) == place.before(block)).astype(F32)


def block_decay(place, block, cum):
    return jnp.exp(cum[BLOCK - 1 :, :]) * jnp.where(place.last(block) == place.before(block), 1.0, 0.0)


def decay_kernel(keep, cum, cum_rows, head):
    return jnp.exp(jnp.where(keep, cum[:, head : head + 1] - cum_rows[head : head + 1, :], -1e30))


def both_halves(pair):
    lane = iota(pair.shape, 1)
    zero = jnp.zeros_like(pair)
    return [jnp.where(lane < HEAD, pair, zero), jnp.where(lane >= HEAD, pair, zero)]


def same_mask(place, block, tap):
    return (place.column(block, tap - (CONV - 1)) == place.column(block)).astype(F32)


def conv_pre(place, block, ext, par, channels):
    total = par[4:5, :channels]
    for tap in range(CONV):
        first = 8 - (CONV - 1) + tap
        total = total + par[tap : tap + 1, :channels] * ext[first : first + BLOCK, :] * same_mask(
            place, block, tap
        )
    return total


def state_packet(state, decay):
    high, low = split(decay)
    row = iota((16, LANES), 0)
    tail = jnp.where(row == 0, high.astype(F32), jnp.where(row == 1, low.astype(F32), 0.0))
    return jnp.concatenate([state.astype(BF16), tail.astype(BF16)], axis=0)


def merge_packets(packets, inner):
    total = jnp.zeros((inner, LANES), F32)
    for packet in reversed(packets):
        tail = packet[inner : inner + 16, :].astype(F32)
        decay = tail[0:1, :] + tail[1:2, :]
        total = packet[:inner, :].astype(F32) + head_column(decay, inner) * total
    return total


def normalise(rows, gain):
    inv = lax.rsqrt(jnp.mean(rows * rows, axis=1, keepdims=True) + EPS)
    return rows * inv, inv, (rows * inv * gain).astype(BF16)


def piece_rows(place, dp_count, parts, rows):
    for part in range(parts):
        for block in range(dp_count):
            owner = xor(place.dp, block) * parts + (xor(place.ctx, part) if parts > 1 else 0)
            yield part, block, pl.multiple_of(owner * rows, rows)


def join_pieces(place, dp_count, parts, whole):
    if len(parts) == 1:
        whole[...] = parts[0][...]
        return
    rows = parts[0].shape[0] // dp_count
    for part, block, first in piece_rows(place, dp_count, len(parts), rows):
        whole[pl.ds(first, rows), :] = parts[part][block * rows : (block + 1) * rows, :]


def cut_pieces(place, dp_count, whole, parts, lanes):
    if len(parts) == 1:
        parts[0][:, lanes] = whole[...].astype(BF16)
        return
    rows = parts[0].shape[0] // dp_count
    for part, block, first in piece_rows(place, dp_count, len(parts), rows):
        parts[part][block * rows : (block + 1) * rows, lanes] = whole[pl.ds(first, rows), :].astype(BF16)


def join_parameters(place, vectors, skip, heads, par):
    shard = vectors[0].shape[1]
    each = HEAD // len(vectors)
    inner = heads * HEAD
    by_channel = jnp.zeros((16, inner), F32)
    in_order = jnp.zeros((16, shard * len(vectors)), F32)
    by_state = jnp.zeros((16, 2 * LANES), F32)
    states = 2 * LANES // len(vectors)
    for block, vector in enumerate(vectors):
        owner = xor(place.dp, block)
        source, target = iota((shard, inner), 0), iota((shard, inner), 1)
        pick = target == source // each * HEAD + owner * each + source % each
        by_channel = by_channel + dot(vector[...], pick.astype(BF16))
        source, target = iota((shard, in_order.shape[1]), 0), iota((shard, in_order.shape[1]), 1)
        in_order = in_order + dot(vector[...], (target == owner * shard + source).astype(BF16))
        source, target = iota((shard, 2 * LANES), 0), iota((shard, 2 * LANES), 1)
        pick = (target == owner * states + source) & (source < states)
        by_state = by_state + dot(vector[...], pick.astype(BF16))
    par[...] = jnp.zeros_like(par)
    par[0:5, :inner] = by_channel[0:5, :]
    par[0:5, inner:] = by_state[8:13, :]
    par[5:6, : in_order.shape[1]] = in_order[5:6, :]
    par[6:7, :inner] = by_channel[6:7, :]
    par[7:8, :inner] = skip


TAPS, NORM, GATE, STATE_TAPS, BY_HEAD = 12, 17, 18, 20, 25


def pack_parameters(dp_count, heads, small, gate, skip):
    inner = heads * HEAD
    each = HEAD // dp_count
    shard = inner // dp_count
    states = 2 * LANES // dp_count

    def lanes(pieces, columns):
        rows, at = [], 0
        for first, value in pieces:
            if first > at:
                rows.append(jnp.zeros((first - at, columns), F32))
            rows.append(value)
            at = first + value.shape[0]
        rows.append(jnp.zeros((LANES - at, columns), F32))
        return jnp.concatenate(rows, axis=0)

    source, target = iota((inner, inner), 0), iota((inner, inner), 1)
    inside = source % shard
    pick = target == inside // each * HEAD + source // shard * each + inside % each
    by_channel = lanes([(TAPS, small[0:5, :inner]), (GATE, gate)], inner)
    total = dot_nt(pick.astype(BF16), by_channel.astype(BF16))
    total = total + lanes([(NORM, small[5:6, :inner])], inner).T
    source, target = iota((inner, 2 * LANES), 0), iota((inner, 2 * LANES), 1)
    inside = source % shard
    pick = (target == source // shard * states + inside) & (inside < states)
    by_state = lanes([(STATE_TAPS, small[0:5, inner : inner + 2 * LANES])], 2 * LANES)
    total = total + dot_nt(pick.astype(BF16), by_state.astype(BF16))
    source, target = iota((inner, LANES), 0) % shard, iota((inner, LANES), 1)
    for index, row in enumerate((small[6:7, :LANES], small[7:8, :LANES], skip)):
        pick = (source == target + index * heads) & (target < heads)
        total = total + dot_nt(pick.astype(BF16), lanes([(BY_HEAD, row)], LANES).astype(BF16))
    return total


def forward_kernel(
    counts, heads, dp_count, part_count, info, *refs
):
    vectors = refs[:dp_count]
    parts = refs[dp_count : dp_count + part_count]
    (
        tok, halo, dtp, spread,
        w1, par, normed_o, halo_normed_o, halo_v_o, v_o, xc_o, bc_o, ypart_o, pre_o, cum_o, entry_o, decay_o,
        packet_o, ext, run, factor,
    ) = refs[dp_count + part_count :]
    forward_block(
        counts, heads, info, vectors, parts, tok, halo, w1, par, dtp, spread,
        normed_o, halo_normed_o, halo_v_o, v_o, xc_o, bc_o, ypart_o, pre_o, cum_o, entry_o, decay_o, packet_o,
        ext, run, factor,
    )


def forward_block(
    counts, heads, info, vectors, parts, tok, halo, w1, par, dtp, spread,
    normed_o, halo_normed_o, halo_v_o, v_o, xc_o, bc_o, ypart_o, pre_o, cum_o, entry_o, decay_o, packet_o,
    ext, run, factor,
):
    block = pl.program_id(0)
    place = Place(info, counts)
    inner = heads * HEAD
    state = LANES
    channels = inner + 2 * state
    width = tok.shape[1]

    @pl.when(block == 0)
    def _():
        join_pieces(place, len(vectors), parts, w1)
        join_parameters(place, vectors, expand(dtp[...], spread)[2:3, :], heads, par)

    gain = par[5:6, :width]
    _, _, normed = normalise(tok[...].astype(F32), gain)
    normed_o[...] = normed

    @pl.when(block == 0)
    def _():
        _, _, before = normalise(halo[...].astype(F32), gain)
        halo_normed_o[...] = before
        raw = dot(before, w1[:, :channels]).astype(BF16).astype(F32)
        ext[0:8, :] = raw[8:16, :]
        halo_v_o[...] = raw[8:16, :]
        run[...] = jnp.zeros_like(run)
        factor[...] = jnp.ones_like(factor)

    @pl.when(block > 0)
    def _():
        ext[0:8, :] = ext[BLOCK : BLOCK + 8, :]

    raw = dot(normed, w1[...])
    v = raw[:, :channels].astype(BF16)
    v_o[...] = v
    ext[8 : 8 + BLOCK, :] = v.astype(F32)
    pre = conv_pre(place, block, ext, par, channels)
    act = (pre * sigmoid(pre)).astype(BF16)
    xc = act[:, :inner]
    bq = act[:, inner : inner + state]
    cq = act[:, inner + state :]
    xc_o[...] = xc
    bc_o[...] = act[:, inner:]
    pre_step = raw[:, channels:].astype(BF16).astype(F32) + dtp[0:1, :]
    pre_o[...] = pre_step
    step = step_sizes(place, block, pre_step, heads)
    tri = (iota((BLOCK, BLOCK), 0) >= iota((BLOCK, BLOCK), 1)).astype(F32)
    cum = dot_exact(tri, -dtp[1:2, :] * step)
    cum_o[...] = cum
    cum_rows = cum.T
    step_rows = step.T
    gram = dot_nt(cq, bq)
    keep = place.keep(block)
    for pair in range(heads // 2):
        lanes = slice(pair * LANES, (pair + 1) * LANES)
        mixing = []
        for head in (2 * pair, 2 * pair + 1):
            weight = decay_kernel(keep, cum, cum_rows, head) * step_rows[head : head + 1, :]
            mixing.append((gram * weight).astype(BF16))
        x_pair = xc[:, lanes]
        y_pair = dot(jnp.concatenate(mixing, axis=1), jnp.concatenate(both_halves(x_pair), axis=0))
        ypart_o[:, lanes] = y_pair + par[7:8, lanes] * x_pair.astype(F32)
    weighted = (expand(end_weights(place, block, cum) * step, spread) * xc.astype(F32)).astype(BF16)
    block_state = dot_tn(weighted, bq)
    decay = block_decay(place, block, cum)
    entry_o[0] = run[...]
    total = head_column(decay, inner) * run[...] + block_state
    run[...] = total
    before = factor[0:1, :]
    row = iota((8, LANES), 0)
    decay_o[0] = jnp.where(row == 0, decay, jnp.where(row == 1, before, 0.0))
    after = before * decay
    factor[...] = jnp.broadcast_to(after, factor.shape)

    @pl.when(block == pl.num_programs(0) - 1)
    def _():
        packet_o[...] = state_packet(total, after)


def gate_matmul_kernel(counts, dp_count, info, *refs):
    shards = refs[:dp_count]
    normed, cot, w2, z_o, dn_o = refs[dp_count:]
    block = pl.program_id(0)
    place = Place(info, counts)
    inner = z_o.shape[1]
    shard = shards[0].shape[0]

    @pl.when(block == 0)
    def _():
        for offset in range(dp_count):
            first = pl.multiple_of(xor(place.dp, offset) * shard, shard)
            w2[pl.ds(first, shard), :] = shards[offset][...]

    z_o[...] = dot(normed[...], w2[:, :inner]).astype(BF16)
    grad = (cot[...].astype(F32) * place.valid(block)).astype(BF16)
    dn_o[...] = dot(grad, w2[:, inner:])


def apply_kernel(counts, packet_count, info, *refs):
    packets = refs[:packet_count]
    entry, decay, cum, bc, ypart, z, dn, par, spread, y_o, hb_o, h_o, stat_o, start = refs[packet_count:]
    block = pl.program_id(0)
    place = Place(info, counts)
    inner = z.shape[1]

    @pl.when(block == 0)
    def _():
        start[...] = merge_packets([packet[...] for packet in packets], inner)

    state = entry[0] + head_column(decay[0, 1:2, :], inner) * start[...]
    h_o[0] = state
    low = state.astype(BF16)
    hb_o[0] = low
    cq = bc[:, LANES:]
    y = ypart[...] + expand(enter_weights(place, block, cum[...]), spread) * dot_nt(cq, low)
    y_o[...] = y
    gate = z[...].astype(F32)
    gated = y * gate * sigmoid(gate)
    squares = jnp.sum(gated * gated, axis=1, keepdims=True)
    cross = jnp.sum(par[6:7, :inner] * dn[...] * gated, axis=1, keepdims=True)
    lane = iota((BLOCK, LANES), 1)
    both = jnp.where(lane == 0, squares, jnp.where(lane == 1, cross, 0.0))
    stat_o[...] = both.T[0:8, :]


def gate_back_kernel(
    counts, inner_all, info, stat, y, z, dn, cot, cum, bc, xc, hb, decay, wo, par, spread,
    keep_o, send_o, gwo_o, small_o, dy_o, dz_o, de_o, exit_o, packet_o,
    acc, run, factor,
):
    step = pl.program_id(0)
    block = pl.num_programs(0) - 1 - step
    place = Place(info, counts)
    inner = z.shape[1]
    width = cot.shape[1]
    half = width // 2

    @pl.when(step == 0)
    def _():
        acc[...] = jnp.zeros_like(acc)
        run[...] = jnp.zeros_like(run)
        factor[...] = jnp.ones_like(factor)
        small_o[...] = jnp.zeros_like(small_o)

    column = jnp.concatenate([stat[...], jnp.zeros((LANES - 8, BLOCK), F32)], axis=0).T
    inv = lax.rsqrt(column[:, 0:1] / inner_all + EPS)
    cross = column[:, 1:2]
    gain = par[6:7, :inner]
    gate = z[...].astype(F32)
    sig = sigmoid(gate)
    silu = gate * sig
    mixed = y[...]
    gated = mixed * silu
    normal = (gated * inv * gain).astype(BF16)
    own = pl.multiple_of(place.tp * half, half)
    other = pl.multiple_of((1 - place.tp) * half, half)
    keep_o[...] = dot_nt(normal, wo[pl.ds(own, half), :]).astype(BF16)
    send_o[...] = dot_nt(normal, wo[pl.ds(other, half), :]).astype(BF16)
    grad = (cot[...].astype(F32) * place.valid(block)).astype(BF16)
    acc[...] += dot_tn(grad, normal)
    back = dn[...]
    grad_gated = inv * (gain * back) - gated * (inv * inv * inv) * (cross / inner_all)
    dy = (grad_gated * silu).astype(BF16)
    dy_o[...] = dy
    dz_o[...] = (grad_gated * mixed * sig * (1.0 + gate * (1.0 - sig))).astype(BF16)
    dy_float = dy.astype(F32)
    cq = bc[:, LANES:]
    read = dot_nt(cq, hb[0])
    de_o[...] = reduce_heads(dy_float * read, spread)
    small_o[0:1, :] += jnp.sum(back * gated * inv, axis=0, keepdims=True)
    small_o[1:2, :] += jnp.sum(dy_float * xc[...].astype(F32), axis=0, keepdims=True)
    dq = (expand(enter_weights(place, block, cum[...]), spread) * dy_float).astype(BF16)
    exit_o[0] = run[...]
    here = decay[0, 0:1, :]
    total = head_column(here, inner) * run[...] + dot_tn(dq, cq)
    run[...] = total
    after = factor[0:1, :] * here
    factor[...] = jnp.broadcast_to(after, factor.shape)

    @pl.when(step == pl.num_programs(0) - 1)
    def _():
        packet_o[...] = state_packet(total, after)
        gwo_o[...] = acc[...].astype(BF16)


def intra_back_kernel(counts, heads, dp_count, info, *refs):
    dy, dz, xc, bc, cum, pre_step, hb, normed, wz, gwo, par, spread = refs[:12]
    dxc_o, dcq_o, dbq_o, rows_o, cols_o, dnz_o = refs[12:18]
    parts = refs[18:-2]
    acc, columns = refs[-2:]
    block = pl.program_id(0)
    place = Place(info, counts)
    inner = heads * HEAD

    @pl.when(block == 0)
    def _():
        acc[...] = jnp.zeros_like(acc)
        columns[...] = jnp.zeros_like(columns)

    bq = bc[:, :LANES]
    cq = bc[:, LANES:]
    cums = cum[...]
    step = step_sizes(place, block, pre_step[...], heads)
    cum_rows = cums.T
    step_rows = step.T
    gram = dot_nt(cq, bq)
    keep = place.keep(block)
    lane = iota((BLOCK, LANES), 1)
    grad_gram = jnp.zeros((BLOCK, BLOCK), F32)
    sums = jnp.zeros((BLOCK, LANES), F32)
    for pair in range(heads // 2):
        lanes = slice(pair * LANES, (pair + 1) * LANES)
        dy_pair = dy[:, lanes]
        x_pair = xc[:, lanes]
        halves = jnp.concatenate(both_halves(dy_pair), axis=0)
        grad_mixing = dot_nt(halves, x_pair)
        mixing = []
        for side in range(2):
            head = 2 * pair + side
            grad_m = grad_mixing[side * BLOCK : (side + 1) * BLOCK, :]
            kernel = decay_kernel(keep, cums, cum_rows, head)
            step_row = step_rows[head : head + 1, :]
            weight = kernel * step_row
            mixing.append((gram * weight).astype(BF16))
            grad_gram = grad_gram + grad_m * weight
            part = grad_m * gram * kernel
            columns[head : head + 1, :] = jnp.sum(part, axis=0, keepdims=True)
            sums = sums + jnp.where(lane == head, jnp.sum(part * step_row, axis=1, keepdims=True), 0.0)
        dx_pair = dot_tn(jnp.concatenate(mixing, axis=0), halves)
        dxc_o[:, lanes] = dx_pair + par[7:8, lanes] * dy_pair.astype(F32)
    grad_low = grad_gram.astype(BF16)
    dq = (expand(enter_weights(place, block, cums), spread) * dy[...].astype(F32)).astype(BF16)
    dcq_o[...] = dot(grad_low, bq) + dot(dq, hb[0])
    dbq_o[...] = dot_tn(grad_low, cq)
    rows_o[...] = sums
    cols_o[...] = columns[...].T
    dnz_o[...] = dot_nt(dz[...], wz[...])
    acc[...] += dot_tn(normed[...], dz[...])

    @pl.when(block == pl.num_programs(0) - 1)
    def _():
        cut_pieces(place, dp_count, acc, parts, slice(0, inner))
        cut_pieces(place, dp_count, gwo, parts, slice(inner, 2 * inner))


def state_back_kernel(counts, heads, dp_count, packet_count, part_count, info, *refs):
    packets = refs[:packet_count]
    (
        exits, h, xc, bc, cum, pre_step, de, dxc, dcq, dbq, rows, cols, decay, v, v_tail, halo_v, halo_normed,
        halo, tok, normed, dnz, small_gate, w1, par, dtp, spread,
        dn_o, dnh_o,
    ) = refs[packet_count : -6 - part_count]
    parts = refs[-6 - part_count : -6]
    start, factor, ext, grad_ext, acc, small_o = refs[-6:]
    step_id = pl.program_id(0)
    block = pl.num_programs(0) - 1 - step_id
    place = Place(info, counts)
    inner = heads * HEAD
    channels = inner + 2 * LANES
    width = tok.shape[1]

    @pl.when(step_id == 0)
    def _():
        start[...] = merge_packets([packet[...] for packet in packets], inner)
        factor[...] = jnp.ones_like(factor)
        acc[...] = jnp.zeros_like(acc)
        grad_ext[...] = jnp.zeros_like(grad_ext)
        small_o[...] = jnp.zeros_like(small_o)

    here = decay[0, 0:1, :]
    before = factor[0:1, :]
    grad_state = exits[0] + head_column(before, inner) * start[...]
    factor[...] = jnp.broadcast_to(before * here, factor.shape)
    shape = (inner, LANES)
    overlap = jnp.sum(grad_state * h[0], axis=1, keepdims=True)
    grad_decay = jnp.sum(
        jnp.where(iota(shape, 0) // HEAD == iota(shape, 1), overlap, 0.0), axis=0, keepdims=True
    )
    low = grad_state.astype(BF16)
    bq = bc[:, :LANES]
    cums = cum[...]
    x_float = xc[...].astype(F32)
    pre_dt = pre_step[...]
    valid = place.valid(block)
    step = step_sizes(place, block, pre_dt, heads)
    end_kernel = end_weights(place, block, cums)
    end_weight = end_kernel * step
    end_wide = expand(end_weight, spread)
    spread_b = dot_nt(bq, low)
    grad_x = dxc[...] + end_wide * spread_b
    grad_end = reduce_heads(x_float * spread_b, spread)
    grad_b = dbq[...] + dot((x_float * end_wide).astype(BF16), low)
    end_part = grad_end * end_weight
    last = iota((BLOCK, LANES), 0) == BLOCK - 1
    grad_cum = rows[...] - cols[...] * step - end_part + de[...] * enter_weights(place, block, cums)
    grad_cum = grad_cum + jnp.where(
        last, jnp.sum(end_part, axis=0, keepdims=True) + grad_decay * here, 0.0
    )
    upper = (iota((BLOCK, BLOCK), 0) <= iota((BLOCK, BLOCK), 1)).astype(F32)
    grad_log = dot_exact(upper, grad_cum)
    rates = dtp[1:2, :]
    grad_step = cols[...] + grad_end * end_kernel - rates * grad_log
    heads_lane = iota((BLOCK, LANES), 1) < heads
    grad_pre_dt = jnp.where(heads_lane, grad_step * sigmoid(pre_dt), 0.0) * valid
    small_o[6:7, :LANES] += jnp.sum(grad_pre_dt, axis=0, keepdims=True)
    small_o[7:8, :LANES] += jnp.sum(grad_log * (-rates * step), axis=0, keepdims=True)

    ext[8 : 8 + BLOCK, :] = v[...].astype(F32)

    @pl.when(block == 0)
    def _():
        ext[0:8, :] = halo_v[...]

    @pl.when(block > 0)
    def _():
        ext[0:8, :] = v_tail[...].astype(F32)[8:16, :]

    pre = conv_pre(place, block, ext, par, channels)
    sig = sigmoid(pre)
    slope = sig * (1.0 + pre * (1.0 - sig))
    grad_pre = jnp.concatenate([grad_x, grad_b, dcq[...]], axis=1) * slope
    small_o[4:5, :] += jnp.sum(grad_pre, axis=0, keepdims=True)
    carry = grad_ext[0:8, :]
    grad_ext[0 : BLOCK, :] = jnp.zeros((BLOCK, channels), F32)
    grad_ext[BLOCK : BLOCK + 8, :] = carry
    for tap in range(CONV):
        first = 8 - (CONV - 1) + tap
        masked = grad_pre * same_mask(place, block, tap)
        small_o[tap : tap + 1, :] += jnp.sum(masked * ext[first : first + BLOCK, :], axis=0, keepdims=True)
        grad_ext[first : first + BLOCK, :] += par[tap : tap + 1, :channels] * masked
    packed = jnp.concatenate([grad_ext[8 : 8 + BLOCK, :].astype(BF16), grad_pre_dt.astype(BF16)], axis=1)
    partial = dnz[...] + dot_nt(packed, w1[...])
    dn_o[...] = partial.astype(BF16)
    acc[...] += dot_tn(normed[...], packed)
    gain = par[5:6, :width]
    scaled, _, _ = normalise(tok[...].astype(F32), gain)
    small_o[5:6, :width] += jnp.sum(partial * scaled, axis=0, keepdims=True)

    @pl.when(block == 0)
    def _():
        back = jnp.concatenate([jnp.zeros((8, channels), F32), grad_ext[0:8, :]], axis=0).astype(BF16)
        halo_grad = dot_nt(back, w1[:, :channels])
        dnh_o[...] = halo_grad[8:16, :]
        halo_scaled, _, _ = normalise(halo[...].astype(F32), gain)
        small_o[5:6, :width] += jnp.sum(halo_grad * halo_scaled, axis=0, keepdims=True)
        acc[:, :channels] += dot_tn(halo_normed[...], back)
        skip = reduce_heads(jnp.broadcast_to(small_gate[1:2, :], (8, inner)), spread)[0:1, :]
        acc[:, channels:] += pack_parameters(dp_count, heads, small_o, small_gate[0:1, :], skip)
        cut_pieces(place, dp_count, acc, parts, slice(0, channels + LANES))


def finish_kernel(counts, info, own, other, halo_a, halo_b, tok, cot, par, grad_o):
    block = pl.program_id(0)
    place = Place(info, counts)
    width = tok.shape[1]
    grad = own[...].astype(F32) + other[...].astype(F32)
    is_last = jnp.where((block + 1) * BLOCK == place.fill, 1.0, 0.0)
    halo = (halo_a[...] + halo_b[...]) * is_last
    grad = jnp.concatenate([grad[: BLOCK - 8, :], grad[BLOCK - 8 :, :] + halo], axis=0)
    inputs = tok[...].astype(F32)
    inv = lax.rsqrt(jnp.mean(inputs * inputs, axis=1, keepdims=True) + EPS)
    scaled = par[5:6, :width] * grad
    inner_dot = jnp.sum(scaled * inputs, axis=1, keepdims=True)
    grad_o[...] = (
        inv * scaled - inputs * (inv * inv * inv) * (inner_dot / width) + cot[...].astype(F32)
    )


def unpack_gate_kernel(counts, part_count, info, *refs):
    parts = refs[:part_count]
    wz_o, wo_o, wide = refs[part_count:]
    place = Place(info, counts)
    shard, inner = wz_o.shape
    rows = shard // part_count
    for part in range(part_count):
        first = pl.multiple_of(xor(place.ctx, part) * rows, rows) if part_count > 1 else 0
        wz_o[pl.ds(first, rows), :] = parts[part][:, :inner].astype(F32)
        wide[pl.ds(first, rows), :] = parts[part][:, inner:].astype(F32)
    wo_o[...] = wide[...].T[:, :shard]


def unpack_input_kernel(counts, heads, part_count, info, *refs):
    parts = refs[:part_count]
    crosses = refs[part_count : 2 * part_count]
    (
        wx_o, wbc_o, wdt_o, norm_o, taps_o, bias_o, state_taps_o, state_bias_o, dt_bias_o, a_log_o, skip_o,
        gate_o, wide, cross,
    ) = refs[2 * part_count :]
    place = Place(info, counts)
    shard, inner = wx_o.shape
    channels = inner + 2 * LANES
    rows = shard // part_count
    for part in range(part_count):
        first = pl.multiple_of(xor(place.ctx, part) * rows, rows) if part_count > 1 else 0
        wide[pl.ds(first, rows), :] = parts[part][...].astype(F32)
        cross[pl.ds(first, rows), :] = crosses[part][...].astype(F32)
    wx_o[...] = wide[:shard, :inner]
    wbc_o[...] = wide[:shard, inner:channels] + cross[:shard, : 2 * LANES]
    wdt_o[...] = wide[:shard, channels : channels + heads]
    lane = iota((wide.shape[0], LANES), 1)
    both = (lane == NORM) | ((lane >= STATE_TAPS) & (lane < BY_HEAD))
    block = wide[:, channels:] + jnp.where(both, cross[:, 2 * LANES :], 0.0)
    lines = block.T
    each = gate_o.shape[1]
    size = lines.shape[1]
    source = iota((16, size), 1)
    inside = (source // each == iota((16, size), 0)) & (source < shard)
    place_in = (iota((size, LANES), 0) % each == iota((size, LANES), 1)).astype(BF16)

    def by_head(line):
        row = jnp.where(inside, lines[line : line + 1, :], 0.0).astype(BF16)
        return dot(row, place_in)[:heads, :each]

    for tap in range(CONV):
        taps_o[tap] = by_head(TAPS + tap)
    bias_o[...] = by_head(TAPS + CONV)
    gate_o[...] = by_head(GATE)
    norm_o[...] = lines[NORM : NORM + 1, :shard]
    states = state_bias_o.shape[1]
    state_taps_o[...] = lines[STATE_TAPS : STATE_TAPS + CONV, :states]
    state_bias_o[...] = lines[STATE_TAPS + CONV : STATE_TAPS + CONV + 1, :states]
    row = lines[BY_HEAD : BY_HEAD + 1, :]
    dt_bias_o[...] = row[:, :heads]
    a_log_o[...] = row[:, heads : 2 * heads]
    skip_o[...] = row[:, 2 * heads : 3 * heads]


def call(body, steps, info, operands, outputs, scratch=(), reverse=False):
    def at(index):
        return steps - 1 - index if reverse else index

    def spec(shape, kind):
        if kind == "rows":
            return pl.BlockSpec((BLOCK,) + tuple(shape[1:]), lambda i: (at(i), 0))
        if kind == "block":
            return pl.BlockSpec((1,) + tuple(shape[1:]), lambda i: (at(i), 0, 0))
        if kind == "lanes":
            return pl.BlockSpec((shape[0], BLOCK), lambda i: (0, at(i)))
        if kind == "tail":
            each = BLOCK // 16
            return pl.BlockSpec((16, shape[1]), lambda i: (jnp.maximum(at(i) * each - 1, 0), 0))
        if kind == "whole":
            return pl.BlockSpec(tuple(shape), lambda i: (0,) * len(shape))
        return kind

    return pl.pallas_call(
        body,
        grid=(steps,),
        in_specs=[pl.BlockSpec(memory_space=pltpu.SMEM)]
        + [spec(array.shape, kind) for array, kind in operands],
        out_specs=[spec(shape.shape, kind) for shape, kind in outputs],
        out_shape=[shape for shape, _ in outputs],
        scratch_shapes=list(scratch),
        compiler_params=pltpu.CompilerParams(
            dimension_semantics=("arbitrary",), vmem_limit_bytes=VMEM
        ),
    )(info, *[array for array, _ in operands])


def shifted(value, axis, steps):
    count = lax.axis_size(axis)
    first, last = max(0, -steps), min(count, count - steps)
    return lax.ppermute(value, axis, [(source, source + steps) for source in range(first, last)])


def swapped(value):
    return lax.ppermute(value, "tp", [(0, 1), (1, 0)])


def partnered(value, axis, mask):
    return lax.ppermute(value, axis, [(one, one ^ mask) for one in range(lax.axis_size(axis))])


def partnered_across(value, mask):
    size = 2 * lax.axis_size("ctx")
    return lax.ppermute(value, ("ctx", "tp"), [(one, one ^ (2 * mask + 1)) for one in range(size)])


def exchanged(value, axis):
    return [value] + [partnered(value, axis, mask) for mask in range(1, lax.axis_size(axis))]


def gather_rows(value, parts):
    if parts == 1:
        return [lax.all_gather(value, "dp", axis=0, tiled=True)]
    rows = value.shape[0] // parts
    own = lax.dynamic_slice_in_dim(value, lax.axis_index("ctx") * rows, rows, 0)
    return exchanged(jnp.concatenate(exchanged(own, "dp"), axis=0), "ctx")


def reduce_rows(pieces):
    if len(pieces) == 1:
        own = lax.psum_scatter(pieces[0], "dp", scatter_dimension=0, tiled=True)
        return lax.psum(own, "ctx")
    dp_count = lax.axis_size("dp")
    rows = pieces[0].shape[0] // dp_count
    total = pieces[0].astype(F32)
    for mask in range(1, len(pieces)):
        total = total + partnered(pieces[mask], "ctx", mask).astype(F32)
    own = total[:rows]
    for mask in range(1, dp_count):
        block = total[mask * rows : (mask + 1) * rows].astype(BF16)
        own = own + partnered(block, "dp", mask).astype(F32)
    return own.astype(BF16)


def body(
    tokens, cotangent, device_fill, seq_lengths, norm_gain, w_z, w_x, w_bc, w_dt,
    conv_x, conv_x_bias, conv_bc, bias_bc, dt_bias, a_log, skip_d, gate_gain, w_out,
):
    rows, width = tokens.shape
    heads = dt_bias.shape[0]
    inner = heads * HEAD
    channels = inner + 2 * LANES
    steps = rows // BLOCK
    shard = norm_gain.shape[0]
    dp_count = lax.axis_size("dp")
    ctx_count = lax.axis_size("ctx")
    tp_index = lax.axis_index("tp")
    counts = (ctx_count, seq_lengths.shape[1])

    parts = ctx_count if shard % (16 * ctx_count) == 0 else 1
    part_rows = shard // parts

    with jax.named_scope("gather_weights"):
        w1_parts = gather_rows(
            jnp.concatenate([w_x, w_bc, jnp.pad(w_dt, ((0, 0), (0, LANES - heads)))], axis=1), parts
        )
        vector = jnp.concatenate(
            [
                conv_x.reshape(CONV, shard),
                conv_x_bias.reshape(1, shard),
                norm_gain[None, :],
                gate_gain.reshape(1, shard),
                jnp.zeros((1, shard), BF16),
                jnp.pad(
                    jnp.concatenate([conv_bc, bias_bc[None, :]], axis=0),
                    ((0, 3), (0, shard - bias_bc.shape[0])),
                ),
            ],
            axis=0,
        )
        vectors = exchanged(vector, "dp")
        w2_shards = exchanged(jnp.concatenate([w_z, w_out.T], axis=1), "dp")

    dtp = jnp.pad(jnp.stack([dt_bias, jnp.exp(a_log), skip_d]), ((0, 5), (0, LANES - heads)))
    shape = (2 * LANES, inner)
    spread = (iota(shape, 0) % LANES == iota(shape, 1) // HEAD).astype(BF16)
    info = jnp.concatenate(
        [
            device_fill[0],
            seq_lengths[0],
            jnp.stack([lax.axis_index("ctx"), tp_index, lax.axis_index("dp")]).astype(jnp.int32),
        ]
    )
    fill = jnp.sum(jnp.where(jnp.arange(ctx_count) == lax.axis_index("ctx"), device_fill[0], 0)) * BLOCK
    halo = shifted(lax.dynamic_slice_in_dim(tokens, fill - 16, 16, 0), "ctx", 1)

    def out(shape, dtype, kind):
        return (jax.ShapeDtypeStruct(shape, dtype), kind)

    def row_out(columns, dtype):
        return out((rows, columns), dtype, "rows")

    state_out = out((steps, inner, LANES), F32, "block")
    packet_out = out((inner + 16, LANES), BF16, "whole")

    (w1, par, normed, halo_normed, halo_v, v, xc, bc, ypart, pre_step, cum, entry, decay, packet) = call(
        functools.partial(forward_kernel, counts, heads, dp_count, parts),
        steps,
        info,
        [(value, "whole") for value in vectors + w1_parts]
        + [(tokens, "rows"), (halo, "whole"), (dtp, "whole"), (spread, "whole")],
        [
            out((width, channels + LANES), BF16, "whole"),
            out((8, channels), F32, "whole"),
            row_out(width, BF16),
            out((16, width), BF16, "whole"),
            out((8, channels), F32, "whole"),
            row_out(channels, BF16),
            row_out(inner, BF16),
            row_out(2 * LANES, BF16),
            row_out(inner, F32),
            row_out(LANES, F32),
            row_out(LANES, F32),
            state_out,
            out((steps, 8, LANES), F32, "block"),
            packet_out,
        ],
        [
            pltpu.VMEM((8 + BLOCK, channels), F32),
            pltpu.VMEM((inner, LANES), F32),
            pltpu.VMEM((8, LANES), F32),
        ],
    )
    packets = [(shifted(packet, "ctx", step), "whole") for step in range(1, ctx_count)]
    wz_spec = pl.BlockSpec((width, inner), lambda i: (0, 0))
    wo_spec = pl.BlockSpec((width, inner), lambda i: (0, 1))
    w2, z, dn = call(
        functools.partial(gate_matmul_kernel, counts, dp_count),
        steps,
        info,
        [(value, "whole") for value in w2_shards] + [(normed, "rows"), (cotangent, "rows")],
        [out((width, 2 * inner), BF16, "whole"), row_out(inner, BF16), row_out(inner, F32)],
    )
    y, hb, h, stat = call(
        functools.partial(apply_kernel, counts, len(packets)),
        steps,
        info,
        packets
        + [
            (entry, "block"),
            (decay, "block"),
            (cum, "rows"),
            (bc, "rows"),
            (ypart, "rows"),
            (z, "rows"),
            (dn, "rows"),
            (par, "whole"),
            (spread, "whole"),
        ],
        [
            row_out(inner, F32),
            out((steps, inner, LANES), BF16, "block"),
            state_out,
            out((8, rows), F32, "lanes"),
        ],
        [pltpu.VMEM((inner, LANES), F32)],
    )
    stat = lax.psum(stat, "tp")
    inner_all = inner * lax.axis_size("tp")
    half = width // 2
    keep, send, gwo, small_gate, dy, dz, de, exits, packet = call(
        functools.partial(gate_back_kernel, counts, inner_all),
        steps,
        info,
        [
            (stat, "lanes"),
            (y, "rows"),
            (z, "rows"),
            (dn, "rows"),
            (cotangent, "rows"),
            (cum, "rows"),
            (bc, "rows"),
            (xc, "rows"),
            (hb, "block"),
            (decay, "block"),
            (w2, wo_spec),
            (par, "whole"),
            (spread, "whole"),
        ],
        [
            row_out(half, BF16),
            row_out(half, BF16),
            out((width, inner), BF16, "whole"),
            out((8, inner), F32, "whole"),
            row_out(inner, BF16),
            row_out(inner, BF16),
            row_out(LANES, F32),
            state_out,
            packet_out,
        ],
        [
            pltpu.VMEM((width, inner), F32),
            pltpu.VMEM((inner, LANES), F32),
            pltpu.VMEM((8, LANES), F32),
        ],
        reverse=True,
    )
    packets = [(shifted(packet, "ctx", -step), "whole") for step in range(1, ctx_count)]
    with jax.named_scope("layer_out"):
        received = swapped(send)
        own_inputs = lax.dynamic_slice_in_dim(tokens, tp_index * half, half, 1).astype(F32)
        valid = (jnp.arange(rows) < fill).astype(F32)[:, None]
        layer_out = own_inputs + (keep.astype(F32) + received.astype(F32)) * valid
    dxc, dcq, dbq, row_sums, col_sums, dnz, *g2 = call(
        functools.partial(intra_back_kernel, counts, heads, dp_count),
        steps,
        info,
        [
            (dy, "rows"),
            (dz, "rows"),
            (xc, "rows"),
            (bc, "rows"),
            (cum, "rows"),
            (pre_step, "rows"),
            (hb, "block"),
            (normed, "rows"),
            (w2, wz_spec),
            (gwo, "whole"),
            (par, "whole"),
            (spread, "whole"),
        ],
        [
            row_out(inner, F32),
            row_out(LANES, F32),
            row_out(LANES, F32),
            row_out(LANES, F32),
            row_out(LANES, F32),
            row_out(width, F32),
        ]
        + [out((width // parts, 2 * inner), BF16, "whole")] * parts,
        [pltpu.VMEM((width, inner), F32), pltpu.VMEM((LANES, BLOCK), F32)],
    )
    with jax.named_scope("reduce_gate_weights"):
        total2 = reduce_rows(g2)
        total2 = exchanged(total2, "ctx") if parts > 1 else [total2]
    partial, halo_grad, *g1 = call(
        functools.partial(state_back_kernel, counts, heads, dp_count, len(packets), parts),
        steps,
        info,
        packets
        + [
            (exits, "block"),
            (h, "block"),
            (xc, "rows"),
            (bc, "rows"),
            (cum, "rows"),
            (pre_step, "rows"),
            (de, "rows"),
            (dxc, "rows"),
            (dcq, "rows"),
            (dbq, "rows"),
            (row_sums, "rows"),
            (col_sums, "rows"),
            (decay, "block"),
            (v, "rows"),
            (v, "tail"),
            (halo_v, "whole"),
            (halo_normed, "whole"),
            (halo, "whole"),
            (tokens, "rows"),
            (normed, "rows"),
            (dnz, "rows"),
            (small_gate, "whole"),
            (w1, "whole"),
            (par, "whole"),
            (dtp, "whole"),
            (spread, "whole"),
        ],
        [
            row_out(width, BF16),
            out((8, width), F32, "whole"),
        ]
        + [out((width // parts, channels + LANES), BF16, "whole")] * parts,
        [
            pltpu.VMEM((inner, LANES), F32),
            pltpu.VMEM((8, LANES), F32),
            pltpu.VMEM((8 + BLOCK, channels), F32),
            pltpu.VMEM((8 + BLOCK, channels), F32),
            pltpu.VMEM((width, channels + LANES), F32),
            pltpu.VMEM((8, channels), F32),
        ],
        reverse=True,
    )
    other = swapped(partial)
    size = ctx_count * 2
    back = [(s, s - 2) for s in range(2, size)]
    cross = [(s, (s - 2) ^ 1) for s in range(2, size)]
    halo_a = lax.ppermute(halo_grad, ("ctx", "tp"), back)
    halo_b = lax.ppermute(halo_grad, ("ctx", "tp"), cross)
    with jax.named_scope("reduce_input_weights"):
        total1 = reduce_rows(g1)
        across = total1[:, inner:]
        if parts > 1:
            total1 = exchanged(total1, "ctx")
            across = [partnered_across(across, mask) for mask in range(parts)]
        else:
            total1, across = [total1], [swapped(across)]
    (grad_tokens,) = call(
        functools.partial(finish_kernel, counts),
        steps,
        info,
        [
            (partial, "rows"),
            (other, "rows"),
            (halo_a, "whole"),
            (halo_b, "whole"),
            (tokens, "rows"),
            (cotangent, "rows"),
            (par, "whole"),
        ],
        [row_out(width, F32)],
    )
    each = HEAD // dp_count
    part_bc = bias_bc.shape[0]
    tall = -(-shard // LANES) * LANES

    def final(*sizes):
        return out(sizes, F32, "whole")

    grad_wz, grad_wo = call(
        functools.partial(unpack_gate_kernel, counts, parts),
        1,
        info,
        [(value, "whole") for value in total2],
        [final(shard, inner), final(inner, shard)],
        [pltpu.VMEM((tall, inner), F32)],
    )
    (
        grad_wx, grad_wbc, grad_wdt, grad_norm, grad_taps, grad_bias, grad_state_taps, grad_state_bias,
        grad_dt_bias, grad_a_log, grad_skip, grad_gate,
    ) = call(
        functools.partial(unpack_input_kernel, counts, heads, parts),
        1,
        info,
        [(value, "whole") for value in total1 + across],
        [
            final(shard, inner),
            final(shard, 2 * LANES),
            final(shard, heads),
            final(1, shard),
            final(CONV, heads, each),
            final(heads, each),
            final(CONV, part_bc),
            final(1, part_bc),
            final(1, heads),
            final(1, heads),
            final(1, heads),
            final(heads, each),
        ],
        [pltpu.VMEM((tall, channels + LANES), F32), pltpu.VMEM((tall, 3 * LANES), F32)],
    )
    return (
        layer_out,
        grad_tokens,
        grad_norm[0],
        grad_wz,
        grad_wx,
        grad_wbc,
        grad_wdt,
        grad_taps,
        grad_bias,
        grad_state_taps,
        grad_state_bias[0],
        grad_dt_bias[0],
        grad_a_log[0],
        grad_skip[0],
        grad_gate,
        grad_wo,
    )


def solution(mesh):
    shards = P(("dp", "ctx"), None)
    return jax.shard_map(
        body,
        mesh=mesh,
        in_specs=(
            shards,
            shards,
            P("dp", None),
            P("dp", None),
            P("dp"),
            P("dp", "tp"),
            P("dp", "tp"),
            P("dp", None),
            P("dp", "tp"),
            P(None, "tp", "dp"),
            P("tp", "dp"),
            P(None, "dp"),
            P("dp"),
            P("tp"),
            P("tp"),
            P("tp"),
            P("tp", "dp"),
            P("tp", "dp"),
        ),
        out_specs=(
            P(("dp", "ctx"), "tp"),
            shards,
            P("dp"),
            P("dp", "tp"),
            P("dp", "tp"),
            P("dp", None),
            P("dp", "tp"),
            P(None, "tp", "dp"),
            P("tp", "dp"),
            P(None, "dp"),
            P("dp"),
            P("tp"),
            P("tp"),
            P("tp"),
            P("tp", "dp"),
            P("tp", "dp"),
        ),
        check_vma=False,
    )
```

time: 708 us -> 292 us (0.41); the launches traced: 699 us -> 291 us
  blocking collectives: 126 us -> 4.69 us
  other arithmetic: 129 us -> 8.5 us
  waiting for transfers between devices: 203 us -> 83.5 us
  Pallas kernels: 0 us -> 110 us
  matrix products: 101 us -> 0 us
  local copies, waits for them, and re-layouts: 95.9 us -> 16.1 us
  starting transfers between devices: 22.9 us -> 66 us
  between operations: 20.9 us -> 1.96 us
    pallas_call x0 -> x9, Pallas kernels: none -> 110 us  [call(): pl.pallas_call(body, grid=(steps,), in_specs=[pl.BlockSpec(memory_space=p...]
    dot_general x29 -> x0, matrix products: 101 us -> none  [the longest x5 18.1 us: right_transposed(): lax.dot_general(left, right, (((1,), (1,)), ((), ())), preferred_element_...]
    reduce_scatter x4 -> x0, waiting for transfers between devices: 99.8 us -> none  [the longest x1 30.2 us: body(): lax.psum_scatter(grad_z_weight.astype(jnp.bfloat16), 'dp', scatter_dimens...]
    all_gather x6 -> x0, blocking collectives: 77.5 us -> none  [the longest x1 16 us: body(): lax.all_gather(w_bc, 'dp', axis=0, tiled=True)]
    psum x3 -> x0, waiting for transfers between devices: 57.4 us -> none  [the longest x1 37.5 us: body(): lax.psum(shards[1].astype(jnp.bfloat16), 'ctx').astype(jnp.float32)]
    ppermute x8 -> x45, starting transfers between devices: 21.6 us -> 66 us  [the longest x30 44.8 us: partnered(): lax.ppermute(value, axis, [(one, one ^ mask) for one in range(lax.axis_si...]
    ppermute x8 -> x45, waiting for transfers between devices: 41.7 us -> 83.5 us  [the longest x30 48.8 us: partnered(): lax.ppermute(value, axis, [(one, one ^ mask) for one in range(lax.axis_si...]
    reduce_sum x14 -> x1, other arithmetic: 38.2 us -> 0.69 us  [body(): jnp.sum(jnp.where(jnp.arange(ctx_count) == lax.axis_index('ctx'), device_...]
  transfers between devices with their start and end apart: 24 -> 45, of which waited for: 14 -> 12; matrix products, arithmetic and copies ran while one was open for 33% -> 6% of each run, Pallas kernels for 0% -> 21%
where the time goes in v1:
time: 292 us; the launch traced here: 291 us
  Pallas kernels  110 us (38%)
  waiting for transfers between devices  83.5 us (29%)
  starting transfers between devices  66 us (23%)
  local copies, waits for them, and re-layouts  16.1 us (6%)
  other arithmetic  8.5 us (3%)
  blocking collectives  4.69 us (2%)
    pallas_call x9, Pallas kernels, call(): pl.pallas_call(body, grid=(steps,), in_specs=[pl.BlockSpec(memory_space=p...  110 us
    ppermute x30, waiting for transfers between devices, partnered(): lax.ppermute(value, axis, [(one, one ^ mask) for one in range(lax.axis_si...  48.8 us
    ppermute x30, starting transfers between devices, partnered(): lax.ppermute(value, axis, [(one, one ^ mask) for one in range(lax.axis_si...  44.8 us
    ppermute x7, waiting for transfers between devices, shifted(): lax.ppermute(value, axis, [(source, source + steps) for source in range(f...  34.6 us
    ppermute x7, starting transfers between devices, shifted(): lax.ppermute(value, axis, [(source, source + steps) for source in range(f...  15.2 us
    unnamed x73, local copies, waits for them, and re-layouts  11 us
  transfers between devices with their start and end apart: 45, of which 12 were waited for; matrix products, arithmetic and copies ran while one was open for 6% of the time, Pallas kernels for 21%

profile of v1, /device:TPU:0, one launch (start us, length us, event | category | flops | bytes accessed | tf_op | source)
XLA Modules:
  0.0 290.7 jit_solution(15438677635309314305)
XLA Ops:
  12.8 3.5 %collective-permute-start.1 = (bf16[16,192]{1,0:T(8,128)(2,1)S(1)}, bf16[16,192]{1,0:T(8,128)(2,1)S(1)}, u32[]{:S(2)}, u32[]{:S(2)}) collective-permute-start(bf16[16,192]{1,0:T(8,128)(2,1)S(1)} %concatenate.20.refs_0_), channel_id=1, source_target_pairs={{0,16},{8,24},{16,0},{24,8},{1,17},{9,25},{17,1},{25,9},{2,18},{10... | collective-permute-start | bytes 18440 | tf_op jit(solution)/shard_map/gather_weights/ppermute | solution.py:767
  25.6 3.9 %collective-permute-start.14 = (bf16[192,1536]{1,0:T(8,128)(2,1)S(1)}, bf16[192,1536]{1,0:T(8,128)(2,1)S(1)}, u32[]{:S(2)}, u32[]{:S(2)}) collective-permute-start(bf16[192,1536]{1,0:T(8,128)(2,1)S(1)} %pad_maximum_fusion.refs_0_), channel_id=1, source_target_pairs={{0,16},{8,24},{16,0},{24,8},{1,17},{9,25},{17,1},{25,9},{2,18},{10... | collective-permute-start | bytes 1769480 | tf_op jit(solution)/shard_map/gather_weights/ppermute | solution.py:767
  35.5 13.8 %collective-permute-done.7.refs_6_ = bf16[192,1152]{1,0:T(8,128)(2,1)} collective-permute-done((bf16[192,1152]{1,0:T(8,128)(2,1)S(1)}, bf16[192,1152]{1,0:T(8,128)(2,1)}, u32[]{:S(2)}, u32[]{:S(2)}) %collective-permute-start.7) | collective-permute-done | bytes 442400 | tf_op jit(solution)/shard_map/gather_weights/ppermute | solution.py:767
  49.4 20.6 %shard_map.297 = (bf16[768,1152]{1,0:T(8,128)(2,1)}, f32[8,1024]{1,0:T(8,128)}, bf16[1024,768]{1,0:T(8,128)(2,1)}, bf16[16,768]{1,0:T(8,128)(2,1)}, f32[8,1024]{...) custom-call(s32[10]{0:T(128)} %concatenate.18.info, ...), custom_call_target="tpu_custom_call" | custom-call | tf_op jit(solution)/shard_map/pallas_call | solution.py:742
  70.0 4.0 %collective-permute-start.10 = (bf16[784,128]{1,0:T(8,128)(2,1)}, bf16[784,128]{1,0:T(8,128)(2,1)S(1)}, u32[]{:S(2)}, u32[]{:S(2)}) collective-permute-start(bf16[784,128]{1,0:T(8,128)(2,1)} %get-tuple-element.76), channel_id=1, source_target_pairs={{0,2},{2,4},{4,6},{1,3},{3,5},{5,7},{8,10},{10,12},{12,14},{9,11},... | collective-permute-start | bytes 602120 | tf_op jit(solution)/shard_map/ppermute | solution.py:759
  74.0 3.4 %collective-permute-start.11 = (bf16[784,128]{1,0:T(8,128)(2,1)}, bf16[784,128]{1,0:T(8,128)(2,1)S(1)}, u32[]{:S(2)}, u32[]{:S(2)}) collective-permute-start(bf16[784,128]{1,0:T(8,128)(2,1)} %get-tuple-element.76), channel_id=1, source_target_pairs={{0,4},{2,6},{1,5},{3,7},{8,12},{10,14},{9,13},{11,15},{16,20},{18,... | collective-permute-start | bytes 602120 | tf_op jit(solution)/shard_map/ppermute | solution.py:759
  79.8 7.4 %shard_map.298 = (bf16[768,1536]{1,0:T(8,128)(2,1)}, bf16[1024,768]{1,0:T(8,128)(2,1)}, f32[1024,768]{1,0:T(8,128)}) custom-call(s32[10]{0:T(128)} %concatenate.18.info, bf16[192,1536]{1,0:T(8,128)(2,1)} %copy-done.1, bf16[192,1536]{1,0:T(8,128)(2,1)} %copy-done.7, bf16[192,1536]{1,0:T(8,128)(2,1)} %copy-done.9, bf16[192,1536]{1,0:T(8,128)(2,1)} %copy-done.10, ...), custom_call_target="tpu_custom_call" | custom-call | tf_op jit(solution)/shard_map/pallas_call | solution.py:742
  88.0 8.6 %shard_map.299 = (f32[1024,768]{1,0:T(8,128)}, bf16[4,768,128]{2,1,0:T(8,128)(2,1)}, f32[4,768,128]{2,1,0:T(8,128)}, f32[8,1024]{1,0:T(8,128)}) custom-call(s32[10]{0:T(128)} %concatenate.18.info, bf16[784,128]{1,0:T(8,128)(2,1)} %copy-done.13, bf16[784,128]{1,0:T(8,128)(2,1)} %copy-done.14, bf16[784,128]{1,0:T(8,128)(2,1)} %copy-done.15, ...), custom_call_target="tpu_custom_call" | custom-call | tf_op jit(solution)/shard_map/pallas_call | solution.py:742
  96.6 4.7 %psum.7.stat = f32[8,1024]{1,0:T(8,128)} all-reduce(f32[8,1024]{1,0:T(8,128)} %get-tuple-element.86), channel_id=1, replica_groups=mesh['dp'=4,'ctx'=4,'tp'=2] {'tp'}, use_global_device_ids=true, to_apply=%region_1.2 | all-reduce | flops 8192 | bytes 65536 | tf_op jit(solution)/shard_map/psum | solution.py:926
  101.3 15.2 %shard_map.300 = (bf16[1024,384]{1,0:T(8,128)(2,1)}, bf16[1024,384]{1,0:T(8,128)(2,1)}, bf16[768,768]{1,0:T(8,128)(2,1)}, f32[8,768]{1,0:T(8,128)}, bf16[1024,76...) custom-call(s32[10]{0:T(128)} %concatenate.18.info, ...), custom_call_target="tpu_custom_call" | custom-call | tf_op jit(solution)/shard_map/pallas_call | solution.py:742
  116.5 18.8 %shard_map.301 = (f32[1024,768]{1,0:T(8,128)}, f32[1024,128]{1,0:T(8,128)}, f32[1024,128]{1,0:T(8,128)}, f32[1024,128]{1,0:T(8,128)}, f32[1024,128]{1,0:T(8,128)...) custom-call(s32[10]{0:T(128)} %concatenate.18.info, ...), custom_call_target="tpu_custom_call" | custom-call | tf_op jit(solution)/shard_map/pallas_call | solution.py:742
  135.5 3.4 %collective-permute-start.38 = (bf16[192,1536]{1,0:T(8,128)(2,1)}, bf16[192,1536]{1,0:T(8,128)(2,1)S(1)}, u32[]{:S(2)}, u32[]{:S(2)}) collective-permute-start(bf16[192,1536]{1,0:T(8,128)(2,1)} %get-tuple-element.122), channel_id=1, source_target_pairs={{0,6},{2,4},{4,2},{6,0},{1,7},{3,5},{5,3},{7,1},{8,14},{10,12},{12... | collective-permute-start | bytes 1769480 | tf_op jit(solution)/shard_map/reduce_gate_weights/ppermute | solution.py:767
  141.5 26.6 %collective-permute-done.17.refs_0_ = bf16[784,128]{1,0:T(8,128)(2,1)S(1)} collective-permute-done((bf16[784,128]{1,0:T(8,128)(2,1)S(1)}, bf16[784,128]{1,0:T(8,128)(2,1)S(1)}, u32[]{:S(2)}, u32[]{:S(2)}) %collective-permute-start.17) | collective-permute-done | bytes 200736 | tf_op jit(solution)/shard_map/ppermute | solution.py:759
  169.7 7.6 %collective-permute-done.19.refs_2_ = bf16[784,128]{1,0:T(8,128)(2,1)S(1)} collective-permute-done((bf16[784,128]{1,0:T(8,128)(2,1)S(1)}, bf16[784,128]{1,0:T(8,128)(2,1)S(1)}, u32[]{:S(2)}, u32[]{:S(2)}) %collective-permute-start.19) | collective-permute-done | bytes 200736 | tf_op jit(solution)/shard_map/ppermute | solution.py:759
  177.9 29.1 %shard_map.302 = (bf16[1024,768]{1,0:T(8,128)(2,1)}, f32[8,768]{1,0:T(8,128)}, bf16[192,1152]{1,0:T(8,128)(2,1)}, bf16[192,1152]{1,0:T(8,128)(2,1)}, bf16[192,11...) custom-call(s32[10]{0:T(128)} %concatenate.18.info, bf16[784,128]{1,0:T(8,128)(2,1)} %copy-done.16, ...), custom_call_target="tpu_custom_call" | custom-call | tf_op jit(solution)/shard_map/pallas_call | solution.py:742
  207.2 3.4 %collective-permute-start.25 = (bf16[192,1152]{1,0:T(8,128)(2,1)}, bf16[192,1152]{1,0:T(8,128)(2,1)S(1)}, u32[]{:S(2)}, u32[]{:S(2)}) collective-permute-start(bf16[192,1152]{1,0:T(8,128)(2,1)} %get-tuple-element.117), channel_id=1, source_target_pairs={{0,6},{2,4},{4,2},{6,0},{1,7},{3,5},{5,3},{7,1},{8,14},{10,12},{12... | collective-permute-start | bytes 1327112 | tf_op jit(solution)/shard_map/reduce_input_weights/ppermute | solution.py:767
  210.9 9.5 %collective-permute-done.23 = bf16[192,1152]{1,0:T(8,128)(2,1)S(1)} collective-permute-done((bf16[192,1152]{1,0:T(8,128)(2,1)}, bf16[192,1152]{1,0:T(8,128)(2,1)S(1)}, u32[]{:S(2)}, u32[]{:S(2)}) %collective-permute-start.23) | collective-permute-done | bytes 442400 | tf_op jit(solution)/shard_map/reduce_input_weights/ppermute | solution.py:767
  220.4 7.1 %collective-permute-done.24 = bf16[192,1152]{1,0:T(8,128)(2,1)S(1)} collective-permute-done((bf16[192,1152]{1,0:T(8,128)(2,1)}, bf16[192,1152]{1,0:T(8,128)(2,1)S(1)}, u32[]{:S(2)}, u32[]{:S(2)}) %collective-permute-start.24) | collective-permute-done | bytes 442400 | tf_op jit(solution)/shard_map/reduce_input_weights/ppermute | solution.py:767
  232.6 3.8 %collective-permute-done.26 = bf16[48,1152]{1,0:T(8,128)(2,1)S(1)} collective-permute-done((bf16[48,1152]{1,0:T(8,128)(2,1)S(1)}, bf16[48,1152]{1,0:T(8,128)(2,1)S(1)}, u32[]{:S(2)}, u32[]{:S(2)}) %collective-permute-start.26) | collective-permute-done | bytes 110624 | tf_op jit(solution)/shard_map/reduce_input_weights/ppermute | solution.py:767
  236.4 4.8 %collective-permute-done.27 = bf16[48,1152]{1,0:T(8,128)(2,1)S(1)} collective-permute-done((bf16[48,1152]{1,0:T(8,128)(2,1)S(1)}, bf16[48,1152]{1,0:T(8,128)(2,1)S(1)}, u32[]{:S(2)}, u32[]{:S(2)}) %collective-permute-start.27) | collective-permute-done | bytes 110624 | tf_op jit(solution)/shard_map/reduce_input_weights/ppermute | solution.py:767
  245.3 5.1 %collective-permute-done.40 = bf16[48,1536]{1,0:T(8,128)(2,1)S(1)} collective-permute-done((bf16[48,1536]{1,0:T(8,128)(2,1)S(1)}, bf16[48,1536]{1,0:T(8,128)(2,1)S(1)}, u32[]{:S(2)}, u32[]{:S(2)}) %collective-permute-start.40) | collective-permute-done | bytes 147488 | tf_op jit(solution)/shard_map/reduce_gate_weights/ppermute | solution.py:767
  259.2 4.3 %collective-permute-done.29.refs_1_ = bf16[48,1152]{1,0:T(8,128)(2,1)S(1)} collective-permute-done((bf16[48,1152]{1,0:T(8,128)(2,1)S(1)}, bf16[48,1152]{1,0:T(8,128)(2,1)S(1)}, u32[]{:S(2)}, u32[]{:S(2)}) %collective-permute-start.29) | collective-permute-done | bytes 110624 | tf_op jit(solution)/shard_map/reduce_input_weights/ppermute | solution.py:767
  266.4 3.8 %collective-permute-start.43 = (bf16[48,1536]{1,0:T(8,128)(2,1)S(1)}, bf16[48,1536]{1,0:T(8,128)(2,1)}, u32[]{:S(2)}, u32[]{:S(2)}) collective-permute-start(bf16[48,1536]{1,0:T(8,128)(2,1)S(1)} %fusion.3.refs_0_), channel_id=1, source_target_pairs={{0,4},{2,6},{4,0},{6,2},{1,5},{3,7},{5,1},{7,3},{8,12},{10,14},{12... | collective-permute-start | bytes 442376 | tf_op jit(solution)/shard_map/reduce_gate_weights/ppermute | solution.py:767
  285.1 5.6 %shard_map.303 = f32[1024,768]{1,0:T(8,128)} custom-call(s32[10]{0:T(128)} %concatenate.18.info, bf16[1024,768]{1,0:T(8,128)(2,1)} %get-tuple-element.112.own, bf16[1024,768]{1,0:T(8,128)(2,1)} %copy-done.3, f32[8,768]{1,0:T(8,128)} %collective-permute-done.21.halo_a, f32[8,768]{1,0:T(8,128)} %collective-permute-done.22.halo_b, bf16[1024,768]{1,0:T(8,128)(2,1)} %tok.1, ...), custom_call_target="tpu_custom_call" | custom-call | tf_op jit(solution)/shard_map/pallas_call | solution.py:742
  (178 shorter events, 70.9 us)
Async XLA Ops:
  2.4 17.0 %collective-permute-start.3 = (bf16[48,1152]{1,0:T(8,128)(2,1)S(1)}, bf16[48,1152]{1,0:T(8,128)(2,1)S(1)}, u32[]{:S(2)}, u32[]{:S(2)}) collective-permute-start(bf16[48,1152]{1,0:T(8,128)(2,1)S(1)} %fusion.8), channel_id=1, source_target_pairs={{0,8},{8,0},{16,24},{24,16},{1,9},{9,1},{17,25},{25,17},{2,10},{10... | collective-permute-start | bytes 331784 | tf_op jit(solution)/shard_map/gather_weights/ppermute | solution.py:767
  5.5 14.0 %collective-permute-start.4 = (bf16[48,1152]{1,0:T(8,128)(2,1)S(1)}, bf16[48,1152]{1,0:T(8,128)(2,1)S(1)}, u32[]{:S(2)}, u32[]{:S(2)}) collective-permute-start(bf16[48,1152]{1,0:T(8,128)(2,1)S(1)} %fusion.8), channel_id=1, source_target_pairs={{0,16},{8,24},{16,0},{24,8},{1,17},{9,25},{17,1},{25,9},{2,18},{10... | collective-permute-start | bytes 331784 | tf_op jit(solution)/shard_map/gather_weights/ppermute | solution.py:767
  12.8 12.7 %collective-permute-start.1 = (bf16[16,192]{1,0:T(8,128)(2,1)S(1)}, bf16[16,192]{1,0:T(8,128)(2,1)S(1)}, u32[]{:S(2)}, u32[]{:S(2)}) collective-permute-start(bf16[16,192]{1,0:T(8,128)(2,1)S(1)} %concatenate.20.refs_0_), channel_id=1, source_target_pairs={{0,16},{8,24},{16,0},{24,8},{1,17},{9,25},{17,1},{25,9},{2,18},{10... | collective-permute-start | bytes 18440 | tf_op jit(solution)/shard_map/gather_weights/ppermute | solution.py:767
  19.6 57.9 %collective-permute-start.13 = (bf16[192,1536]{1,0:T(8,128)(2,1)S(1)}, bf16[192,1536]{1,0:T(8,128)(2,1)S(1)}, u32[]{:S(2)}, u32[]{:S(2)}) collective-permute-start(bf16[192,1536]{1,0:T(8,128)(2,1)S(1)} %pad_maximum_fusion.refs_0_), channel_id=1, source_target_pairs={{0,8},{8,0},{16,24},{24,16},{1,9},{9,1},{17,25},{25,17},{2,10},{10... | collective-permute-start | bytes 1769480 | tf_op jit(solution)/shard_map/gather_weights/ppermute | solution.py:767
  25.6 53.2 %collective-permute-start.14 = (bf16[192,1536]{1,0:T(8,128)(2,1)S(1)}, bf16[192,1536]{1,0:T(8,128)(2,1)S(1)}, u32[]{:S(2)}, u32[]{:S(2)}) collective-permute-start(bf16[192,1536]{1,0:T(8,128)(2,1)S(1)} %pad_maximum_fusion.refs_0_), channel_id=1, source_target_pairs={{0,16},{8,24},{16,0},{24,8},{1,17},{9,25},{17,1},{25,9},{2,18},{10... | collective-permute-start | bytes 1769480 | tf_op jit(solution)/shard_map/gather_weights/ppermute | solution.py:767
  29.5 49.3 %collective-permute-start.15 = (bf16[192,1536]{1,0:T(8,128)(2,1)S(1)}, bf16[192,1536]{1,0:T(8,128)(2,1)S(1)}, u32[]{:S(2)}, u32[]{:S(2)}) collective-permute-start(bf16[192,1536]{1,0:T(8,128)(2,1)S(1)} %pad_maximum_fusion.refs_0_), channel_id=1, source_target_pairs={{0,24},{8,16},{16,8},{24,0},{1,25},{9,17},{17,9},{25,1},{2,26},{10... | collective-permute-start | bytes 1769480 | tf_op jit(solution)/shard_map/gather_weights/ppermute | solution.py:767
  30.0 19.3 %collective-permute-start.7 = (bf16[192,1152]{1,0:T(8,128)(2,1)S(1)}, bf16[192,1152]{1,0:T(8,128)(2,1)}, u32[]{:S(2)}, u32[]{:S(2)}) collective-permute-start(bf16[192,1152]{1,0:T(8,128)(2,1)S(1)} %pad_maximum_fusion.1.refs_4_), channel_id=1, source_target_pairs={{0,4},{2,6},{4,0},{6,2},{1,5},{3,7},{5,1},{7,3},{8,12},{10,14},{12... | collective-permute-start | bytes 1327112 | tf_op jit(solution)/shard_map/gather_weights/ppermute | solution.py:767
  32.6 16.7 %collective-permute-start.8 = (bf16[192,1152]{1,0:T(8,128)(2,1)S(1)}, bf16[192,1152]{1,0:T(8,128)(2,1)}, u32[]{:S(2)}, u32[]{:S(2)}) collective-permute-start(bf16[192,1152]{1,0:T(8,128)(2,1)S(1)} %pad_maximum_fusion.1.refs_4_), channel_id=1, source_target_pairs={{0,6},{2,4},{4,2},{6,0},{1,7},{3,5},{5,3},{7,1},{8,14},{10,12},{12... | collective-permute-start | bytes 1327112 | tf_op jit(solution)/shard_map/gather_weights/ppermute | solution.py:767
  70.0 17.2 %collective-permute-start.10 = (bf16[784,128]{1,0:T(8,128)(2,1)}, bf16[784,128]{1,0:T(8,128)(2,1)S(1)}, u32[]{:S(2)}, u32[]{:S(2)}) collective-permute-start(bf16[784,128]{1,0:T(8,128)(2,1)} %get-tuple-element.76), channel_id=1, source_target_pairs={{0,2},{2,4},{4,6},{1,3},{3,5},{5,7},{8,10},{10,12},{12,14},{9,11},... | collective-permute-start | bytes 602120 | tf_op jit(solution)/shard_map/ppermute | solution.py:759
  74.0 13.3 %collective-permute-start.11 = (bf16[784,128]{1,0:T(8,128)(2,1)}, bf16[784,128]{1,0:T(8,128)(2,1)S(1)}, u32[]{:S(2)}, u32[]{:S(2)}) collective-permute-start(bf16[784,128]{1,0:T(8,128)(2,1)} %get-tuple-element.76), channel_id=1, source_target_pairs={{0,4},{2,6},{1,5},{3,7},{8,12},{10,14},{9,13},{11,15},{16,20},{18,... | collective-permute-start | bytes 602120 | tf_op jit(solution)/shard_map/ppermute | solution.py:759
  135.3 71.8 %collective-permute-start.36 = (bf16[192,1536]{1,0:T(8,128)(2,1)}, bf16[192,1536]{1,0:T(8,128)(2,1)S(1)}, u32[]{:S(2)}, u32[]{:S(2)}) collective-permute-start(bf16[192,1536]{1,0:T(8,128)(2,1)} %get-tuple-element.120), channel_id=1, source_target_pairs={{0,2},{2,0},{4,6},{6,4},{1,3},{3,1},{5,7},{7,5},{8,10},{10,8},{12,... | collective-permute-start | bytes 1769480 | tf_op jit(solution)/shard_map/reduce_gate_weights/ppermute | solution.py:767
  135.4 71.8 %collective-permute-start.37 = (bf16[192,1536]{1,0:T(8,128)(2,1)}, bf16[192,1536]{1,0:T(8,128)(2,1)S(1)}, u32[]{:S(2)}, u32[]{:S(2)}) collective-permute-start(bf16[192,1536]{1,0:T(8,128)(2,1)} %get-tuple-element.121), channel_id=1, source_target_pairs={{0,4},{2,6},{4,0},{6,2},{1,5},{3,7},{5,1},{7,3},{8,12},{10,14},{12... | collective-permute-start | bytes 1769480 | tf_op jit(solution)/shard_map/reduce_gate_weights/ppermute | solution.py:767
  135.5 75.1 %collective-permute-start.38 = (bf16[192,1536]{1,0:T(8,128)(2,1)}, bf16[192,1536]{1,0:T(8,128)(2,1)S(1)}, u32[]{:S(2)}, u32[]{:S(2)}) collective-permute-start(bf16[192,1536]{1,0:T(8,128)(2,1)} %get-tuple-element.122), channel_id=1, source_target_pairs={{0,6},{2,4},{4,2},{6,0},{1,7},{3,5},{5,3},{7,1},{8,14},{10,12},{12... | collective-permute-start | bytes 1769480 | tf_op jit(solution)/shard_map/reduce_gate_weights/ppermute | solution.py:767
  138.9 29.2 %collective-permute-start.17 = (bf16[784,128]{1,0:T(8,128)(2,1)S(1)}, bf16[784,128]{1,0:T(8,128)(2,1)S(1)}, u32[]{:S(2)}, u32[]{:S(2)}) collective-permute-start(bf16[784,128]{1,0:T(8,128)(2,1)S(1)} %copy-done.33), channel_id=1, source_target_pairs={{2,0},{4,2},{6,4},{3,1},{5,3},{7,5},{10,8},{12,10},{14,12},{11,9},... | collective-permute-start | bytes 602120 | tf_op jit(solution)/shard_map/ppermute | solution.py:759
  140.2 29.4 %collective-permute-start.18 = (bf16[784,128]{1,0:T(8,128)(2,1)S(1)}, bf16[784,128]{1,0:T(8,128)(2,1)S(1)}, u32[]{:S(2)}, u32[]{:S(2)}) collective-permute-start(bf16[784,128]{1,0:T(8,128)(2,1)S(1)} %copy-done.33), channel_id=1, source_target_pairs={{4,0},{6,2},{5,1},{7,3},{12,8},{14,10},{13,9},{15,11},{20,16},{22,... | collective-permute-start | bytes 602120 | tf_op jit(solution)/shard_map/ppermute | solution.py:759
  169.6 83.1 %collective-permute-start.16 = (bf16[1024,384]{1,0:T(8,128)(2,1)}, bf16[1024,384]{1,0:T(8,128)(2,1)S(1)}, u32[]{:S(2)}, u32[]{:S(2)}) collective-permute-start(bf16[1024,384]{1,0:T(8,128)(2,1)} %get-tuple-element.92), channel_id=1, source_target_pairs={{0,1},{1,0},{2,3},{3,2},{4,5},{5,4},{6,7},{7,6},{8,9},{9,8},{10,11... | collective-permute-start | bytes 2359304 | tf_op jit(solution)/shard_map/layer_out/ppermute | solution.py:763
  207.0 13.4 %collective-permute-start.23 = (bf16[192,1152]{1,0:T(8,128)(2,1)}, bf16[192,1152]{1,0:T(8,128)(2,1)S(1)}, u32[]{:S(2)}, u32[]{:S(2)}) collective-permute-start(bf16[192,1152]{1,0:T(8,128)(2,1)} %get-tuple-element.115), channel_id=1, source_target_pairs={{0,2},{2,0},{4,6},{6,4},{1,3},{3,1},{5,7},{7,5},{8,10},{10,8},{12,... | collective-permute-start | bytes 1327112 | tf_op jit(solution)/shard_map/reduce_input_weights/ppermute | solution.py:767
  207.1 20.4 %collective-permute-start.24 = (bf16[192,1152]{1,0:T(8,128)(2,1)}, bf16[192,1152]{1,0:T(8,128)(2,1)S(1)}, u32[]{:S(2)}, u32[]{:S(2)}) collective-permute-start(bf16[192,1152]{1,0:T(8,128)(2,1)} %get-tuple-element.116), channel_id=1, source_target_pairs={{0,4},{2,6},{4,0},{6,2},{1,5},{3,7},{5,1},{7,3},{8,12},{10,14},{12... | collective-permute-start | bytes 1327112 | tf_op jit(solution)/shard_map/reduce_input_weights/ppermute | solution.py:767
  207.2 20.3 %collective-permute-start.25 = (bf16[192,1152]{1,0:T(8,128)(2,1)}, bf16[192,1152]{1,0:T(8,128)(2,1)S(1)}, u32[]{:S(2)}, u32[]{:S(2)}) collective-permute-start(bf16[192,1152]{1,0:T(8,128)(2,1)} %get-tuple-element.117), channel_id=1, source_target_pairs={{0,6},{2,4},{4,2},{6,0},{1,7},{3,5},{5,3},{7,1},{8,14},{10,12},{12... | collective-permute-start | bytes 1327112 | tf_op jit(solution)/shard_map/reduce_input_weights/ppermute | solution.py:767
  210.6 73.4 %collective-permute-start.20 = (bf16[1024,768]{1,0:T(8,128)(2,1)}, bf16[1024,768]{1,0:T(8,128)(2,1)S(1)}, u32[]{:S(2)}, u32[]{:S(2)}) collective-permute-start(bf16[1024,768]{1,0:T(8,128)(2,1)} %get-tuple-element.112.own), channel_id=1, source_target_pairs={{0,1},{1,0},{2,3},{3,2},{4,5},{5,4},{6,7},{7,6},{8,9},{9,8},{10,11... | collective-permute-start | bytes 4718600 | tf_op jit(solution)/shard_map/ppermute | solution.py:763
  254.5 15.8 %collective-permute-start.42 = (bf16[48,1536]{1,0:T(8,128)(2,1)S(1)}, bf16[48,1536]{1,0:T(8,128)(2,1)S(1)}, u32[]{:S(2)}, u32[]{:S(2)}) collective-permute-start(bf16[48,1536]{1,0:T(8,128)(2,1)S(1)} %fusion.3.refs_0_), channel_id=1, source_target_pairs={{0,2},{2,0},{4,6},{6,4},{1,3},{3,1},{5,7},{7,5},{8,10},{10,8},{12,... | collective-permute-start | bytes 442376 | tf_op jit(solution)/shard_map/reduce_gate_weights/ppermute | solution.py:767
  263.5 20.5 %collective-permute-start.21 = (f32[8,768]{1,0:T(8,128)}, f32[8,768]{1,0:T(8,128)}, u32[]{:S(2)}, u32[]{:S(2)}) collective-permute-start(f32[8,768]{1,0:T(8,128)} %get-tuple-element.113), channel_id=1, source_target_pairs={{2,0},{3,1},{4,2},{5,3},{6,4},{7,5},{10,8},{11,9},{12,10},{13,11},... | collective-permute-start | bytes 73736 | tf_op jit(solution)/shard_map/ppermute | solution.py:1056
  264.8 19.2 %collective-permute-start.22 = (f32[8,768]{1,0:T(8,128)}, f32[8,768]{1,0:T(8,128)}, u32[]{:S(2)}, u32[]{:S(2)}) collective-permute-start(f32[8,768]{1,0:T(8,128)} %get-tuple-element.113), channel_id=1, source_target_pairs={{2,1},{3,0},{4,3},{5,2},{6,5},{7,4},{10,9},{11,8},{12,11},{13,10},... | collective-permute-start | bytes 73736 | tf_op jit(solution)/shard_map/ppermute | solution.py:1057
  266.4 12.8 %collective-permute-start.43 = (bf16[48,1536]{1,0:T(8,128)(2,1)S(1)}, bf16[48,1536]{1,0:T(8,128)(2,1)}, u32[]{:S(2)}, u32[]{:S(2)}) collective-permute-start(bf16[48,1536]{1,0:T(8,128)(2,1)S(1)} %fusion.3.refs_0_), channel_id=1, source_target_pairs={{0,4},{2,6},{4,0},{6,2},{1,5},{3,7},{5,1},{7,3},{8,12},{10,14},{12... | collective-permute-start | bytes 442376 | tf_op jit(solution)/shard_map/reduce_gate_weights/ppermute | solution.py:767
  (55 other events, 726.7 us)

commit v2 on v1

--- a/solution.py
+++ b/solution.py
@@ -118,9 +118,8 @@
         return (block * BLOCK + iota((BLOCK, 1), 0) < self.fill).astype(F32)
 
     def keep(self, block):
-        down = self.rows(block * BLOCK + iota((BLOCK, BLOCK), 0))
-        across = self.rows(block * BLOCK + iota((BLOCK, BLOCK), 1))
-        return (down == across) & (iota((BLOCK, BLOCK), 0) >= iota((BLOCK, BLOCK), 1))
+        across = self.rows(block * BLOCK + iota((1, BLOCK), 1))
+        return (self.column(block) == across) & (iota((BLOCK, BLOCK), 0) >= iota((BLOCK, BLOCK), 1))
 
 
 def step_sizes(place, block, pre_step, heads):
@@ -194,12 +193,13 @@
 
 
 def join_pieces(place, dp_count, parts, whole):
+    columns = parts[0].shape[1]
     if len(parts) == 1:
-        whole[...] = parts[0][...]
+        whole[:, :columns] = parts[0][...]
         return
     rows = parts[0].shape[0] // dp_count
     for part, block, first in piece_rows(place, dp_count, len(parts), rows):
-        whole[pl.ds(first, rows), :] = parts[part][block * rows : (block + 1) * rows, :]
+        whole[pl.ds(first, rows), :columns] = parts[part][block * rows : (block + 1) * rows, :]
 
 
 def cut_pieces(place, dp_count, whole, parts, lanes):
@@ -211,7 +211,7 @@
         parts[part][block * rows : (block + 1) * rows, lanes] = whole[pl.ds(first, rows), :].astype(BF16)
 
 
-def join_parameters(place, vectors, skip, heads, par):
+def join_parameters(place, vectors, skip, heads, par, w1):
     shard = vectors[0].shape[1]
     each = HEAD // len(vectors)
     inner = heads * HEAD
@@ -219,16 +219,19 @@
     in_order = jnp.zeros((16, shard * len(vectors)), F32)
     by_state = jnp.zeros((16, 2 * LANES), F32)
     states = 2 * LANES // len(vectors)
+    eye = (iota((16, LANES), 0) == iota((16, LANES), 1)).astype(BF16)
     for block, vector in enumerate(vectors):
         owner = xor(place.dp, block)
+        first = pl.multiple_of(owner * shard, shard)
+        w1[pl.ds(first, shard), inner + 2 * LANES :] = dot_tn(vector[16:32, :], eye).astype(BF16)
         source, target = iota((shard, inner), 0), iota((shard, inner), 1)
         pick = target == source // each * HEAD + owner * each + source % each
-        by_channel = by_channel + dot(vector[...], pick.astype(BF16))
+        by_channel = by_channel + dot(vector[0:16, :], pick.astype(BF16))
         source, target = iota((shard, in_order.shape[1]), 0), iota((shard, in_order.shape[1]), 1)
-        in_order = in_order + dot(vector[...], (target == owner * shard + source).astype(BF16))
+        in_order = in_order + dot(vector[0:16, :], (target == owner * shard + source).astype(BF16))
         source, target = iota((shard, 2 * LANES), 0), iota((shard, 2 * LANES), 1)
         pick = (target == owner * states + source) & (source < states)
-        by_state = by_state + dot(vector[...], pick.astype(BF16))
+        by_state = by_state + dot(vector[0:16, :], pick.astype(BF16))
     par[...] = jnp.zeros_like(par)
     par[0:5, :inner] = by_channel[0:5, :]
     par[0:5, inner:] = by_state[8:13, :]
@@ -306,7 +309,7 @@
     @pl.when(block == 0)
     def _():
         join_pieces(place, len(vectors), parts, w1)
-        join_parameters(place, vectors, expand(dtp[...], spread)[2:3, :], heads, par)
+        join_parameters(place, vectors, expand(dtp[...], spread)[2:3, :], heads, par, w1)
 
     gain = par[5:6, :width]
     _, _, normed = normalise(tok[...].astype(F32), gain)
@@ -664,24 +667,22 @@
 
 def unpack_gate_kernel(counts, part_count, info, *refs):
     parts = refs[:part_count]
-    wz_o, wo_o, wide = refs[part_count:]
+    wz_o, wo_o = refs[part_count:]
     place = Place(info, counts)
     shard, inner = wz_o.shape
     rows = shard // part_count
     for part in range(part_count):
         first = pl.multiple_of(xor(place.ctx, part) * rows, rows) if part_count > 1 else 0
         wz_o[pl.ds(first, rows), :] = parts[part][:, :inner].astype(F32)
-        wide[pl.ds(first, rows), :] = parts[part][:, inner:].astype(F32)
-    wo_o[...] = wide[...].T[:, :shard]
+        wo_o[pl.ds(first, rows), :] = parts[part][:, inner:].astype(F32)
 
 
 def unpack_input_kernel(counts, heads, part_count, info, *refs):
     parts = refs[:part_count]
-    crosses = refs[part_count : 2 * part_count]
     (
         wx_o, wbc_o, wdt_o, norm_o, taps_o, bias_o, state_taps_o, state_bias_o, dt_bias_o, a_log_o, skip_o,
-        gate_o, wide, cross,
-    ) = refs[2 * part_count :]
+        gate_o, wide,
+    ) = refs[part_count:]
     place = Place(info, counts)
     shard, inner = wx_o.shape
     channels = inner + 2 * LANES
@@ -689,14 +690,10 @@
     for part in range(part_count):
         first = pl.multiple_of(xor(place.ctx, part) * rows, rows) if part_count > 1 else 0
         wide[pl.ds(first, rows), :] = parts[part][...].astype(F32)
-        cross[pl.ds(first, rows), :] = crosses[part][...].astype(F32)
     wx_o[...] = wide[:shard, :inner]
-    wbc_o[...] = wide[:shard, inner:channels] + cross[:shard, : 2 * LANES]
-    wdt_o[...] = wide[:shard, channels : channels + heads]
-    lane = iota((wide.shape[0], LANES), 1)
-    both = (lane == NORM) | ((lane >= STATE_TAPS) & (lane < BY_HEAD))
-    block = wide[:, channels:] + jnp.where(both, cross[:, 2 * LANES :], 0.0)
-    lines = block.T
+    wbc_o[...] = wide[:shard, inner:channels]
+    lines = wide[:, channels:].T
+    wdt_o[...] = lines[:heads, :shard]
     each = gate_o.shape[1]
     size = lines.shape[1]
     source = iota((16, size), 1)
@@ -708,7 +705,7 @@
         return dot(row, place_in)[:heads, :each]
 
     for tap in range(CONV):
-        taps_o[tap] = by_head(TAPS + tap)
+        taps_o[:, tap, :] = by_head(TAPS + tap)
     bias_o[...] = by_head(TAPS + CONV)
     gate_o[...] = by_head(GATE)
     norm_o[...] = lines[NORM : NORM + 1, :shard]
@@ -721,7 +718,7 @@
     skip_o[...] = row[:, 2 * heads : 3 * heads]
 
 
-def call(body, steps, info, operands, outputs, scratch=(), reverse=False):
+def call(body, steps, info, operands, outputs, scratch=(), reverse=False, micros=1):
     def at(index):
         return steps - 1 - index if reverse else index
 
@@ -750,6 +747,9 @@
         compiler_params=pltpu.CompilerParams(
             dimension_semantics=("arbitrary",), vmem_limit_bytes=VMEM
         ),
+        cost_estimate=pl.CostEstimate(
+            flops=micros * 1_100_000_000, bytes_accessed=micros * 3_500_000, transcendentals=0
+        ),
     )(info, *[array for array, _ in operands])
 
 
@@ -767,21 +767,17 @@
     return lax.ppermute(value, axis, [(one, one ^ mask) for one in range(lax.axis_size(axis))])
 
 
-def partnered_across(value, mask):
-    size = 2 * lax.axis_size("ctx")
-    return lax.ppermute(value, ("ctx", "tp"), [(one, one ^ (2 * mask + 1)) for one in range(size)])
-
-
 def exchanged(value, axis):
     return [value] + [partnered(value, axis, mask) for mask in range(1, lax.axis_size(axis))]
 
 
 def gather_rows(value, parts):
     if parts == 1:
-        return [lax.all_gather(value, "dp", axis=0, tiled=True)]
+        return [lax.all_gather(value, "dp", axis=0, tiled=True)], ()
     rows = value.shape[0] // parts
     own = lax.dynamic_slice_in_dim(value, lax.axis_index("ctx") * rows, rows, 0)
-    return exchanged(jnp.concatenate(exchanged(own, "dp"), axis=0), "ctx")
+    joined = jnp.concatenate(exchanged(own, "dp"), axis=0)
+    return exchanged(joined, "ctx"), joined
 
 
 def reduce_rows(pieces):
@@ -819,9 +815,7 @@
     part_rows = shard // parts
 
     with jax.named_scope("gather_weights"):
-        w1_parts = gather_rows(
-            jnp.concatenate([w_x, w_bc, jnp.pad(w_dt, ((0, 0), (0, LANES - heads)))], axis=1), parts
-        )
+        w1_parts, arrived = gather_rows(jnp.concatenate([w_x, w_bc], axis=1), parts)
         vector = jnp.concatenate(
             [
                 conv_x.reshape(CONV, shard),
@@ -833,11 +827,14 @@
                     jnp.concatenate([conv_bc, bias_bc[None, :]], axis=0),
                     ((0, 3), (0, shard - bias_bc.shape[0])),
                 ),
+                jnp.pad(w_dt.T, ((0, 16 - heads), (0, 0))),
             ],
             axis=0,
         )
         vectors = exchanged(vector, "dp")
-        w2_shards = exchanged(jnp.concatenate([w_z, w_out.T], axis=1), "dp")
+        shard2 = jnp.concatenate([w_z, w_out.T], axis=1)
+        shard2, _ = lax.optimization_barrier((shard2, arrived))
+        w2_shards = exchanged(shard2, "dp")
 
     dtp = jnp.pad(jnp.stack([dt_bias, jnp.exp(a_log), skip_d]), ((0, 5), (0, LANES - heads)))
     shape = (2 * LANES, inner)
@@ -888,6 +885,7 @@
             pltpu.VMEM((inner, LANES), F32),
             pltpu.VMEM((8, LANES), F32),
         ],
+        micros=20,
     )
     packets = [(shifted(packet, "ctx", step), "whole") for step in range(1, ctx_count)]
     wz_spec = pl.BlockSpec((width, inner), lambda i: (0, 0))
@@ -898,6 +896,7 @@
         info,
         [(value, "whole") for value in w2_shards] + [(normed, "rows"), (cotangent, "rows")],
         [out((width, 2 * inner), BF16, "whole"), row_out(inner, BF16), row_out(inner, F32)],
+        micros=7,
     )
     y, hb, h, stat = call(
         functools.partial(apply_kernel, counts, len(packets)),
@@ -922,6 +921,7 @@
             out((8, rows), F32, "lanes"),
         ],
         [pltpu.VMEM((inner, LANES), F32)],
+        micros=8,
     )
     stat = lax.psum(stat, "tp")
     inner_all = inner * lax.axis_size("tp")
@@ -962,6 +962,7 @@
             pltpu.VMEM((8, LANES), F32),
         ],
         reverse=True,
+        micros=15,
     )
     packets = [(shifted(packet, "ctx", -step), "whole") for step in range(1, ctx_count)]
     with jax.named_scope("layer_out"):
@@ -997,6 +998,7 @@
         ]
         + [out((width // parts, 2 * inner), BF16, "whole")] * parts,
         [pltpu.VMEM((width, inner), F32), pltpu.VMEM((LANES, BLOCK), F32)],
+        micros=18,
     )
     with jax.named_scope("reduce_gate_weights"):
         total2 = reduce_rows(g2)
@@ -1048,6 +1050,7 @@
             pltpu.VMEM((8, channels), F32),
         ],
         reverse=True,
+        micros=28,
     )
     other = swapped(partial)
     size = ctx_count * 2
@@ -1057,12 +1060,12 @@
     halo_b = lax.ppermute(halo_grad, ("ctx", "tp"), cross)
     with jax.named_scope("reduce_input_weights"):
         total1 = reduce_rows(g1)
-        across = total1[:, inner:]
-        if parts > 1:
-            total1 = exchanged(total1, "ctx")
-            across = [partnered_across(across, mask) for mask in range(parts)]
-        else:
-            total1, across = [total1], [swapped(across)]
+        across = swapped(total1[:, inner:])
+        lane = jnp.arange(3 * LANES) - 2 * LANES
+        both = (lane < 0) | (lane == NORM) | ((lane >= STATE_TAPS) & (lane < BY_HEAD))
+        summed = total1[:, inner:] + jnp.where(both[None, :], across, 0)
+        total1 = jnp.concatenate([total1[:, :inner], summed], axis=1)
+        total1 = exchanged(total1, "ctx") if parts > 1 else [total1]
     (grad_tokens,) = call(
         functools.partial(finish_kernel, counts),
         steps,
@@ -1077,6 +1080,7 @@
             (par, "whole"),
         ],
         [row_out(width, F32)],
+        micros=5,
     )
     each = HEAD // dp_count
     part_bc = bias_bc.shape[0]
@@ -1090,8 +1094,8 @@
         1,
         info,
         [(value, "whole") for value in total2],
-        [final(shard, inner), final(inner, shard)],
-        [pltpu.VMEM((tall, inner), F32)],
+        [final(shard, inner), final(shard, inner)],
+        micros=2,
     )
     (
         grad_wx, grad_wbc, grad_wdt, grad_norm, grad_taps, grad_bias, grad_state_taps, grad_state_bias,
@@ -1100,13 +1104,13 @@
         functools.partial(unpack_input_kernel, counts, heads, parts),
         1,
         info,
-        [(value, "whole") for value in total1 + across],
+        [(value, "whole") for value in total1],
         [
             final(shard, inner),
             final(shard, 2 * LANES),
-            final(shard, heads),
+            final(heads, shard),
             final(1, shard),
-            final(CONV, heads, each),
+            final(heads, CONV, each),
             final(heads, each),
             final(CONV, part_bc),
             final(1, part_bc),
@@ -1115,7 +1119,8 @@
             final(1, heads),
             final(heads, each),
         ],
-        [pltpu.VMEM((tall, channels + LANES), F32), pltpu.VMEM((tall, 3 * LANES), F32)],
+        [pltpu.VMEM((tall, channels + LANES), F32)],
+        micros=2,
     )
     return (
         layer_out,
@@ -1124,8 +1129,8 @@
         grad_wz,
         grad_wx,
         grad_wbc,
-        grad_wdt,
-        grad_taps,
+        grad_wdt.T,
+        grad_taps.transpose(1, 0, 2),
         grad_bias,
         grad_state_taps,
         grad_state_bias[0],
@@ -1133,7 +1138,7 @@
         grad_a_log[0],
         grad_skip[0],
         grad_gate,
-        grad_wo,
+        grad_wo.T,
     )
 
 

time: 292 us -> 260 us (0.89)
  waiting for transfers between devices: 83.5 us -> 41.3 us
  starting transfers between devices: 66 us -> 80.2 us
  local copies, waits for them, and re-layouts: 16.1 us -> 12.2 us
    ppermute x7, waiting for transfers between devices: 34.6 us -> 6.99 us  [shifted(): lax.ppermute(value, axis, [(source, source + steps) for source in range(f...]
    ppermute x30, starting transfers between devices: 44.8 us -> 60.7 us  [partnered(): lax.ppermute(value, axis, [(one, one ^ mask) for one in range(lax.axis_si...]
    ppermute x30, waiting for transfers between devices: 48.8 us -> 33.9 us  [partnered(): lax.ppermute(value, axis, [(one, one ^ mask) for one in range(lax.axis_si...]
    unnamed x73 -> x81, local copies, waits for them, and re-layouts: 11 us -> 7.13 us
    ppermute x4 -> x0, starting transfers between devices: 3.26 us -> none  [partnered_across(): lax.ppermute(value, ('ctx', 'tp'), [(one, one ^ 2 * mask + 1) for one in...]
  transfers between devices with their start and end apart: 45 -> 42, of which waited for: 12 -> 10; matrix products, arithmetic and copies ran while one was open for 6% -> 5% of each run, Pallas kernels for 21% -> 31%
where the time goes in v2:
time: 260 us; the launch traced here: 257 us
  Pallas kernels  110 us (42%)
  starting transfers between devices  80.2 us (31%)
  waiting for transfers between devices  41.3 us (16%)
  local copies, waits for them, and re-layouts  12.2 us (5%)
  other arithmetic  7.15 us (3%)
  blocking collectives  4.65 us (2%)
    pallas_call x9, Pallas kernels, call(): pl.pallas_call(body, grid=(steps,), in_specs=[pl.BlockSpec(memory_space=p...  110 us
    ppermute x30, starting transfers between devices, partnered(): lax.ppermute(value, axis, [(one, one ^ mask) for one in range(lax.axis_si...  60.7 us
    ppermute x30, waiting for transfers between devices, partnered(): lax.ppermute(value, axis, [(one, one ^ mask) for one in range(lax.axis_si...  33.9 us
    ppermute x7, starting transfers between devices, shifted(): lax.ppermute(value, axis, [(source, source + steps) for source in range(f...  16.7 us
    unnamed x81, local copies, waits for them, and re-layouts  7.13 us
    ppermute x7, waiting for transfers between devices, shifted(): lax.ppermute(value, axis, [(source, source + steps) for source in range(f...  6.99 us
  transfers between devices with their start and end apart: 42, of which 10 were waited for; matrix products, arithmetic and copies ran while one was open for 5% of the time, Pallas kernels for 31%

profile of v2, /device:TPU:0, one launch (start us, length us, event | category | flops | bytes accessed | tf_op | source)
XLA Modules:
  0.0 257.1 jit_solution(4492706306782381397)
XLA Ops:
  1.6 3.1 %collective-permute-start.3 = (bf16[48,1024]{1,0:T(8,128)(2,1)S(1)}, bf16[48,1024]{1,0:T(8,128)(2,1)S(1)}, u32[]{:S(2)}, u32[]{:S(2)}) collective-permute-start(bf16[48,1024]{1,0:T(8,128)(2,1)S(1)} %fusion.7), channel_id=1, source_target_pairs={{0,8},{8,0},{16,24},{24,16},{1,9},{9,1},{17,25},{25,17},{2,10},{10... | collective-permute-start | bytes 294920 | tf_op jit(solution)/shard_map/gather_weights/ppermute | solution.py:767
  12.7 3.5 %collective-permute-start.1 = (bf16[32,192]{1,0:T(8,128)(2,1)S(1)}, bf16[32,192]{1,0:T(8,128)(2,1)S(1)}, u32[]{:S(2)}, u32[]{:S(2)}) collective-permute-start(bf16[32,192]{1,0:T(8,128)(2,1)S(1)} %concatenate.23.refs_0_), channel_id=1, source_target_pairs={{0,16},{8,24},{16,0},{24,8},{1,17},{9,25},{17,1},{25,9},{2,18},{10... | collective-permute-start | bytes 36872 | tf_op jit(solution)/shard_map/gather_weights/ppermute | solution.py:767
  25.3 3.6 %collective-permute-start.9 = (bf16[16,768]{1,0:T(8,128)(2,1)S(1)}, bf16[16,768]{1,0:T(8,128)(2,1)S(1)}, u32[]{:S(2)}, u32[]{:S(2)}) collective-permute-start(bf16[16,768]{1,0:T(8,128)(2,1)S(1)} %constant_dynamic-slice_fusion), channel_id=1, source_target_pairs={{0,2},{2,4},{4,6},{1,3},{3,5},{5,7},{8,10},{10,12},{12,14},{9,11},... | collective-permute-start | bytes 73736 | tf_op jit(solution)/shard_map/ppermute | solution.py:759
  30.9 7.0 %collective-permute-done.9.refs_9_.refs_20_ = bf16[16,768]{1,0:T(8,128)(2,1)S(1)} collective-permute-done((bf16[16,768]{1,0:T(8,128)(2,1)S(1)}, bf16[16,768]{1,0:T(8,128)(2,1)S(1)}, u32[]{:S(2)}, u32[]{:S(2)}) %collective-permute-start.9) | collective-permute-done | bytes 24608 | tf_op jit(solution)/shard_map/ppermute | solution.py:759
  42.1 20.5 %shard_map.297 = (bf16[768,1152]{1,0:T(8,128)(2,1)}, f32[8,1024]{1,0:T(8,128)}, bf16[1024,768]{1,0:T(8,128)(2,1)}, bf16[16,768]{1,0:T(8,128)(2,1)}, f32[8,1024]{...) custom-call(s32[10]{0:T(128)} %concatenate.21.info, ...), custom_call_target="tpu_custom_call" | custom-call | flops 22000001024 | bytes 70000000 | tf_op jit(solution)/shard_map/pallas_call | solution.py:739
  62.6 4.4 %collective-permute-start.10 = (bf16[784,128]{1,0:T(8,128)(2,1)}, bf16[784,128]{1,0:T(8,128)(2,1)S(1)}, u32[]{:S(2)}, u32[]{:S(2)}) collective-permute-start(bf16[784,128]{1,0:T(8,128)(2,1)} %get-tuple-element.77), channel_id=1, source_target_pairs={{0,2},{2,4},{4,6},{1,3},{3,5},{5,7},{8,10},{10,12},{12,14},{9,11},... | collective-permute-start | bytes 602120 | tf_op jit(solution)/shard_map/ppermute | solution.py:759
  67.0 3.4 %collective-permute-start.11 = (bf16[784,128]{1,0:T(8,128)(2,1)}, bf16[784,128]{1,0:T(8,128)(2,1)S(1)}, u32[]{:S(2)}, u32[]{:S(2)}) collective-permute-start(bf16[784,128]{1,0:T(8,128)(2,1)} %get-tuple-element.77), channel_id=1, source_target_pairs={{0,4},{2,6},{1,5},{3,7},{8,12},{10,14},{9,13},{11,15},{16,20},{18,... | collective-permute-start | bytes 602120 | tf_op jit(solution)/shard_map/ppermute | solution.py:759
  71.8 7.3 %collective-permute-done.14.refs_2_ = bf16[192,1536]{1,0:T(8,128)(2,1)S(1)} collective-permute-done((bf16[192,1536]{1,0:T(8,128)(2,1)S(1)}, bf16[192,1536]{1,0:T(8,128)(2,1)S(1)}, u32[]{:S(2)}, u32[]{:S(2)}) %collective-permute-start.14) | collective-permute-done | bytes 589856 | tf_op jit(solution)/shard_map/gather_weights/ppermute | solution.py:767
  80.1 7.4 %shard_map.298 = (bf16[768,1536]{1,0:T(8,128)(2,1)}, bf16[1024,768]{1,0:T(8,128)(2,1)}, f32[1024,768]{1,0:T(8,128)}) custom-call(s32[10]{0:T(128)} %concatenate.21.info, bf16[192,1536]{1,0:T(8,128)(2,1)} %copy-done.1, bf16[192,1536]{1,0:T(8,128)(2,1)} %copy-done.15, bf16[192,1536]{1,0:T(8,128)(2,1)} %copy-done.16, bf16[192,1536]{1,0:T(8,128)(2,1)} %copy-done.17, ...), custom_call_target="tpu_custom_call" | custom-call | flops 7699999744 | bytes 24500000 | tf_op jit(solution)/shard_map/pallas_call | solution.py:739
  88.4 8.5 %shard_map.299 = (f32[1024,768]{1,0:T(8,128)}, bf16[4,768,128]{2,1,0:T(8,128)(2,1)}, f32[4,768,128]{2,1,0:T(8,128)}, f32[8,1024]{1,0:T(8,128)}) custom-call(s32[10]{0:T(128)} %concatenate.21.info, bf16[784,128]{1,0:T(8,128)(2,1)} %copy-done.24, bf16[784,128]{1,0:T(8,128)(2,1)} %copy-done.25, bf16[784,128]{1,0:T(8,128)(2,1)} %copy-done.26, ...), custom_call_target="tpu_custom_call" | custom-call | flops 8800000000 | bytes 28000000 | tf_op jit(solution)/shard_map/pallas_call | solution.py:739
  96.9 4.6 %psum.7.stat = f32[8,1024]{1,0:T(8,128)} all-reduce(f32[8,1024]{1,0:T(8,128)} %get-tuple-element.88), channel_id=1, replica_groups=mesh['dp'=4,'ctx'=4,'tp'=2] {'tp'}, use_global_device_ids=true, to_apply=%region_1.2 | all-reduce | flops 8192 | bytes 65536 | tf_op jit(solution)/shard_map/psum | solution.py:926
  101.6 15.2 %shard_map.300 = (bf16[1024,384]{1,0:T(8,128)(2,1)}, bf16[1024,384]{1,0:T(8,128)(2,1)}, bf16[768,768]{1,0:T(8,128)(2,1)}, f32[8,768]{1,0:T(8,128)}, bf16[1024,76...) custom-call(s32[10]{0:T(128)} %concatenate.21.info, ...), custom_call_target="tpu_custom_call" | custom-call | flops 16499999744 | bytes 52500000 | tf_op jit(solution)/shard_map/pallas_call | solution.py:739
  120.8 18.8 %shard_map.301 = (f32[1024,768]{1,0:T(8,128)}, f32[1024,128]{1,0:T(8,128)}, f32[1024,128]{1,0:T(8,128)}, f32[1024,128]{1,0:T(8,128)}, f32[1024,128]{1,0:T(8,128)...) custom-call(s32[10]{0:T(128)} %concatenate.21.info, ...), custom_call_target="tpu_custom_call" | custom-call | flops 19800000512 | bytes 63000000 | tf_op jit(solution)/shard_map/pallas_call | solution.py:739
  141.8 3.3 %collective-permute-start.34 = (bf16[192,1536]{1,0:T(8,128)(2,1)}, bf16[192,1536]{1,0:T(8,128)(2,1)S(1)}, u32[]{:S(2)}, u32[]{:S(2)}) collective-permute-start(bf16[192,1536]{1,0:T(8,128)(2,1)} %get-tuple-element.123), channel_id=1, source_target_pairs={{0,4},{2,6},{4,0},{6,2},{1,5},{3,7},{5,1},{7,3},{8,12},{10,14},{12... | collective-permute-start | bytes 1769480 | tf_op jit(solution)/shard_map/reduce_gate_weights/ppermute | solution.py:767
  145.9 29.2 %shard_map.302 = (bf16[1024,768]{1,0:T(8,128)(2,1)}, f32[8,768]{1,0:T(8,128)}, bf16[192,1152]{1,0:T(8,128)(2,1)}, bf16[192,1152]{1,0:T(8,128)(2,1)}, bf16[192,11...) custom-call(s32[10]{0:T(128)} %concatenate.21.info, bf16[784,128]{1,0:T(8,128)(2,1)} %copy-done.21, ...), custom_call_target="tpu_custom_call" | custom-call | flops 30799998976 | bytes 98000000 | tf_op jit(solution)/shard_map/pallas_call | solution.py:739
  179.0 9.3 %collective-permute-done.23 = bf16[192,1152]{1,0:T(8,128)(2,1)S(1)} collective-permute-done((bf16[192,1152]{1,0:T(8,128)(2,1)}, bf16[192,1152]{1,0:T(8,128)(2,1)S(1)}, u32[]{:S(2)}, u32[]{:S(2)}) %collective-permute-start.23) | collective-permute-done | bytes 442400 | tf_op jit(solution)/shard_map/reduce_input_weights/ppermute | solution.py:767
  188.3 11.2 %collective-permute-start.36 = (bf16[48,1536]{1,0:T(8,128)(2,1)S(1)}, bf16[48,1536]{1,0:T(8,128)(2,1)S(1)}, u32[]{:S(2)}, u32[]{:S(2)}) collective-permute-start(bf16[48,1536]{1,0:T(8,128)(2,1)S(1)} %get-tuple-element.142), channel_id=1, source_target_pairs={{0,8},{8,0},{16,24},{24,16},{1,9},{9,1},{17,25},{25,17},{2,10},{10... | collective-permute-start | bytes 442376 | tf_op jit(solution)/shard_map/reduce_gate_weights/ppermute | solution.py:767
  199.5 9.5 %collective-permute-start.37 = (bf16[48,1536]{1,0:T(8,128)(2,1)S(1)}, bf16[48,1536]{1,0:T(8,128)(2,1)S(1)}, u32[]{:S(2)}, u32[]{:S(2)}) collective-permute-start(bf16[48,1536]{1,0:T(8,128)(2,1)S(1)} %get-tuple-element.144), channel_id=1, source_target_pairs={{0,16},{8,24},{16,0},{24,8},{1,17},{9,25},{17,1},{25,9},{2,18},{10... | collective-permute-start | bytes 442376 | tf_op jit(solution)/shard_map/reduce_gate_weights/ppermute | solution.py:767
  208.9 3.4 %collective-permute-start.38 = (bf16[48,1536]{1,0:T(8,128)(2,1)S(1)}, bf16[48,1536]{1,0:T(8,128)(2,1)S(1)}, u32[]{:S(2)}, u32[]{:S(2)}) collective-permute-start(bf16[48,1536]{1,0:T(8,128)(2,1)S(1)} %get-tuple-element.143), channel_id=1, source_target_pairs={{0,24},{8,16},{16,8},{24,0},{1,25},{9,17},{17,9},{25,1},{2,26},{10... | collective-permute-start | bytes 442376 | tf_op jit(solution)/shard_map/reduce_gate_weights/ppermute | solution.py:767
  212.7 4.9 %collective-permute-done.37 = bf16[48,1536]{1,0:T(8,128)(2,1)S(1)} collective-permute-done((bf16[48,1536]{1,0:T(8,128)(2,1)S(1)}, bf16[48,1536]{1,0:T(8,128)(2,1)S(1)}, u32[]{:S(2)}, u32[]{:S(2)}) %collective-permute-start.37) | collective-permute-done | bytes 147488 | tf_op jit(solution)/shard_map/reduce_gate_weights/ppermute | solution.py:767
  219.3 3.8 %collective-permute-start.28 = (bf16[48,1152]{1,0:T(8,128)(2,1)S(1)}, bf16[48,1152]{1,0:T(8,128)(2,1)S(1)}, u32[]{:S(2)}, u32[]{:S(2)}) collective-permute-start(bf16[48,1152]{1,0:T(8,128)(2,1)S(1)} %get-tuple-element.146), channel_id=1, source_target_pairs={{0,24},{8,16},{16,8},{24,0},{1,25},{9,17},{17,9},{25,1},{2,26},{10... | collective-permute-start | bytes 331784 | tf_op jit(solution)/shard_map/reduce_input_weights/ppermute | solution.py:767
  224.4 4.8 %collective-permute-done.27 = bf16[48,1152]{1,0:T(8,128)(2,1)S(1)} collective-permute-done((bf16[48,1152]{1,0:T(8,128)(2,1)S(1)}, bf16[48,1152]{1,0:T(8,128)(2,1)S(1)}, u32[]{:S(2)}, u32[]{:S(2)}) %collective-permute-start.27) | collective-permute-done | bytes 110624 | tf_op jit(solution)/shard_map/reduce_input_weights/ppermute | solution.py:767
  237.1 3.9 %collective-permute-done.41.refs_3_ = bf16[48,1536]{1,0:T(8,128)(2,1)S(1)} collective-permute-done((bf16[48,1536]{1,0:T(8,128)(2,1)S(1)}, bf16[48,1536]{1,0:T(8,128)(2,1)S(1)}, u32[]{:S(2)}, u32[]{:S(2)}) %collective-permute-start.41) | collective-permute-done | bytes 147488 | tf_op jit(solution)/shard_map/reduce_gate_weights/ppermute | solution.py:767
  251.6 5.6 %shard_map.303 = f32[1024,768]{1,0:T(8,128)} custom-call(s32[10]{0:T(128)} %concatenate.21.info, bf16[1024,768]{1,0:T(8,128)(2,1)} %get-tuple-element.114.own, bf16[1024,768]{1,0:T(8,128)(2,1)} %copy-done.13, f32[8,768]{1,0:T(8,128)} %copy-done.35, f32[8,768]{1,0:T(8,128)} %copy-done.36, bf16[1024,768]{1,0:T(8,128)(2,1)} %tok.1, bf16[1024,768]{1,0:T(8,128)(2,1)} %cot.3, ...), custom_call_target="tpu_custom_call" | custom-call | flops 5500000256 | bytes 17500000 | tf_op jit(solution)/shard_map/pallas_call | solution.py:739
  (185 shorter events, 59.2 us)
Async XLA Ops:
  1.6 18.7 %collective-permute-start.3 = (bf16[48,1024]{1,0:T(8,128)(2,1)S(1)}, bf16[48,1024]{1,0:T(8,128)(2,1)S(1)}, u32[]{:S(2)}, u32[]{:S(2)}) collective-permute-start(bf16[48,1024]{1,0:T(8,128)(2,1)S(1)} %fusion.7), channel_id=1, source_target_pairs={{0,8},{8,0},{16,24},{24,16},{1,9},{9,1},{17,25},{25,17},{2,10},{10... | collective-permute-start | bytes 294920 | tf_op jit(solution)/shard_map/gather_weights/ppermute | solution.py:767
  4.7 15.6 %collective-permute-start.4 = (bf16[48,1024]{1,0:T(8,128)(2,1)S(1)}, bf16[48,1024]{1,0:T(8,128)(2,1)S(1)}, u32[]{:S(2)}, u32[]{:S(2)}) collective-permute-start(bf16[48,1024]{1,0:T(8,128)(2,1)S(1)} %fusion.7), channel_id=1, source_target_pairs={{0,16},{8,24},{16,0},{24,8},{1,17},{9,25},{17,1},{25,9},{2,18},{10... | collective-permute-start | bytes 294920 | tf_op jit(solution)/shard_map/gather_weights/ppermute | solution.py:767
  20.3 17.8 %collective-permute-start.6 = (bf16[192,1024]{1,0:T(8,128)(2,1)S(1)}, bf16[192,1024]{1,0:T(8,128)(2,1)S(1)}, u32[]{:S(2)}, u32[]{:S(2)}) collective-permute-start(bf16[192,1024]{1,0:T(8,128)(2,1)S(1)} %pad_maximum_fusion.1.refs_4_), channel_id=1, source_target_pairs={{0,2},{2,0},{4,6},{6,4},{1,3},{3,1},{5,7},{7,5},{8,10},{10,8},{12,... | collective-permute-start | bytes 1179656 | tf_op jit(solution)/shard_map/gather_weights/ppermute | solution.py:767
  21.9 18.7 %collective-permute-start.7 = (bf16[192,1024]{1,0:T(8,128)(2,1)S(1)}, bf16[192,1024]{1,0:T(8,128)(2,1)S(1)}, u32[]{:S(2)}, u32[]{:S(2)}) collective-permute-start(bf16[192,1024]{1,0:T(8,128)(2,1)S(1)} %pad_maximum_fusion.1.refs_4_), channel_id=1, source_target_pairs={{0,4},{2,6},{4,0},{6,2},{1,5},{3,7},{5,1},{7,3},{8,12},{10,14},{12... | collective-permute-start | bytes 1179656 | tf_op jit(solution)/shard_map/gather_weights/ppermute | solution.py:767
  23.4 17.2 %collective-permute-start.8 = (bf16[192,1024]{1,0:T(8,128)(2,1)S(1)}, bf16[192,1024]{1,0:T(8,128)(2,1)S(1)}, u32[]{:S(2)}, u32[]{:S(2)}) collective-permute-start(bf16[192,1024]{1,0:T(8,128)(2,1)S(1)} %pad_maximum_fusion.1.refs_4_), channel_id=1, source_target_pairs={{0,6},{2,4},{4,2},{6,0},{1,7},{3,5},{5,3},{7,1},{8,14},{10,12},{12... | collective-permute-start | bytes 1179656 | tf_op jit(solution)/shard_map/gather_weights/ppermute | solution.py:767
  30.9 39.5 %collective-permute-start.13 = (bf16[192,1536]{1,0:T(8,128)(2,1)S(1)}, bf16[192,1536]{1,0:T(8,128)(2,1)S(1)}, u32[]{:S(2)}, u32[]{:S(2)}) collective-permute-start(bf16[192,1536]{1,0:T(8,128)(2,1)S(1)} %pad_maximum_fusion.refs_0_), channel_id=1, source_target_pairs={{0,8},{8,0},{16,24},{24,16},{1,9},{9,1},{17,25},{25,17},{2,10},{10... | collective-permute-start | bytes 1769480 | tf_op jit(solution)/shard_map/gather_weights/ppermute | solution.py:767
  37.9 41.2 %collective-permute-start.14 = (bf16[192,1536]{1,0:T(8,128)(2,1)S(1)}, bf16[192,1536]{1,0:T(8,128)(2,1)S(1)}, u32[]{:S(2)}, u32[]{:S(2)}) collective-permute-start(bf16[192,1536]{1,0:T(8,128)(2,1)S(1)} %pad_maximum_fusion.refs_0_), channel_id=1, source_target_pairs={{0,16},{8,24},{16,0},{24,8},{1,17},{9,25},{17,1},{25,9},{2,18},{10... | collective-permute-start | bytes 1769480 | tf_op jit(solution)/shard_map/gather_weights/ppermute | solution.py:767
  38.2 40.9 %collective-permute-start.15 = (bf16[192,1536]{1,0:T(8,128)(2,1)S(1)}, bf16[192,1536]{1,0:T(8,128)(2,1)S(1)}, u32[]{:S(2)}, u32[]{:S(2)}) collective-permute-start(bf16[192,1536]{1,0:T(8,128)(2,1)S(1)} %pad_maximum_fusion.refs_0_), channel_id=1, source_target_pairs={{0,24},{8,16},{16,8},{24,0},{1,25},{9,17},{17,9},{25,1},{2,26},{10... | collective-permute-start | bytes 1769480 | tf_op jit(solution)/shard_map/gather_weights/ppermute | solution.py:767
  62.6 24.9 %collective-permute-start.10 = (bf16[784,128]{1,0:T(8,128)(2,1)}, bf16[784,128]{1,0:T(8,128)(2,1)S(1)}, u32[]{:S(2)}, u32[]{:S(2)}) collective-permute-start(bf16[784,128]{1,0:T(8,128)(2,1)} %get-tuple-element.77), channel_id=1, source_target_pairs={{0,2},{2,4},{4,6},{1,3},{3,5},{5,7},{8,10},{10,12},{12,14},{9,11},... | collective-permute-start | bytes 602120 | tf_op jit(solution)/shard_map/ppermute | solution.py:759
  67.0 20.5 %collective-permute-start.11 = (bf16[784,128]{1,0:T(8,128)(2,1)}, bf16[784,128]{1,0:T(8,128)(2,1)S(1)}, u32[]{:S(2)}, u32[]{:S(2)}) collective-permute-start(bf16[784,128]{1,0:T(8,128)(2,1)} %get-tuple-element.77), channel_id=1, source_target_pairs={{0,4},{2,6},{1,5},{3,7},{8,12},{10,14},{9,13},{11,15},{16,20},{18,... | collective-permute-start | bytes 602120 | tf_op jit(solution)/shard_map/ppermute | solution.py:759
  70.5 17.1 %collective-permute-start.12 = (bf16[784,128]{1,0:T(8,128)(2,1)}, bf16[784,128]{1,0:T(8,128)(2,1)S(1)}, u32[]{:S(2)}, u32[]{:S(2)}) collective-permute-start(bf16[784,128]{1,0:T(8,128)(2,1)} %get-tuple-element.77), channel_id=1, source_target_pairs={{0,6},{1,7},{8,14},{9,15},{16,22},{17,23},{24,30},{25,31}} | collective-permute-start | bytes 602120 | tf_op jit(solution)/shard_map/ppermute | solution.py:759
  116.7 28.3 %collective-permute-start.17 = (bf16[784,128]{1,0:T(8,128)(2,1)}, bf16[784,128]{1,0:T(8,128)(2,1)S(1)}, u32[]{:S(2)}, u32[]{:S(2)}) collective-permute-start(bf16[784,128]{1,0:T(8,128)(2,1)} %get-tuple-element.95), channel_id=1, source_target_pairs={{2,0},{4,2},{6,4},{3,1},{5,3},{7,5},{10,8},{12,10},{14,12},{11,9},... | collective-permute-start | bytes 602120 | tf_op jit(solution)/shard_map/ppermute | solution.py:759
  118.0 27.0 %collective-permute-start.18 = (bf16[784,128]{1,0:T(8,128)(2,1)}, bf16[784,128]{1,0:T(8,128)(2,1)S(1)}, u32[]{:S(2)}, u32[]{:S(2)}) collective-permute-start(bf16[784,128]{1,0:T(8,128)(2,1)} %get-tuple-element.95), channel_id=1, source_target_pairs={{4,0},{6,2},{5,1},{7,3},{12,8},{14,10},{13,9},{15,11},{20,16},{22,... | collective-permute-start | bytes 602120 | tf_op jit(solution)/shard_map/ppermute | solution.py:759
  119.3 25.8 %collective-permute-start.19 = (bf16[784,128]{1,0:T(8,128)(2,1)}, bf16[784,128]{1,0:T(8,128)(2,1)S(1)}, u32[]{:S(2)}, u32[]{:S(2)}) collective-permute-start(bf16[784,128]{1,0:T(8,128)(2,1)} %get-tuple-element.95), channel_id=1, source_target_pairs={{6,0},{7,1},{14,8},{15,9},{22,16},{23,17},{30,24},{31,25}} | collective-permute-start | bytes 602120 | tf_op jit(solution)/shard_map/ppermute | solution.py:759
  139.7 36.9 %collective-permute-start.33 = (bf16[192,1536]{1,0:T(8,128)(2,1)}, bf16[192,1536]{1,0:T(8,128)(2,1)S(1)}, u32[]{:S(2)}, u32[]{:S(2)}) collective-permute-start(bf16[192,1536]{1,0:T(8,128)(2,1)} %get-tuple-element.122), channel_id=1, source_target_pairs={{0,2},{2,0},{4,6},{6,4},{1,3},{3,1},{5,7},{7,5},{8,10},{10,8},{12,... | collective-permute-start | bytes 1769480 | tf_op jit(solution)/shard_map/reduce_gate_weights/ppermute | solution.py:767
  141.8 36.8 %collective-permute-start.34 = (bf16[192,1536]{1,0:T(8,128)(2,1)}, bf16[192,1536]{1,0:T(8,128)(2,1)S(1)}, u32[]{:S(2)}, u32[]{:S(2)}) collective-permute-start(bf16[192,1536]{1,0:T(8,128)(2,1)} %get-tuple-element.123), channel_id=1, source_target_pairs={{0,4},{2,6},{4,0},{6,2},{1,5},{3,7},{5,1},{7,3},{8,12},{10,14},{12... | collective-permute-start | bytes 1769480 | tf_op jit(solution)/shard_map/reduce_gate_weights/ppermute | solution.py:767
  145.1 33.6 %collective-permute-start.35 = (bf16[192,1536]{1,0:T(8,128)(2,1)}, bf16[192,1536]{1,0:T(8,128)(2,1)S(1)}, u32[]{:S(2)}, u32[]{:S(2)}) collective-permute-start(bf16[192,1536]{1,0:T(8,128)(2,1)} %get-tuple-element.124), channel_id=1, source_target_pairs={{0,6},{2,4},{4,2},{6,0},{1,7},{3,5},{5,3},{7,1},{8,14},{10,12},{12... | collective-permute-start | bytes 1769480 | tf_op jit(solution)/shard_map/reduce_gate_weights/ppermute | solution.py:767
  145.1 86.6 %collective-permute-start.16 = (bf16[1024,384]{1,0:T(8,128)(2,1)S(1)}, bf16[1024,384]{1,0:T(8,128)(2,1)S(1)}, u32[]{:S(2)}, u32[]{:S(2)}) collective-permute-start(bf16[1024,384]{1,0:T(8,128)(2,1)S(1)} %copy-done.14), channel_id=1, source_target_pairs={{0,1},{1,0},{2,3},{3,2},{4,5},{5,4},{6,7},{7,6},{8,9},{9,8},{10,11... | collective-permute-start | bytes 2359304 | tf_op jit(solution)/shard_map/layer_out/ppermute | solution.py:763
  176.6 22.8 %collective-permute-start.24 = (bf16[192,1152]{1,0:T(8,128)(2,1)}, bf16[192,1152]{1,0:T(8,128)(2,1)S(1)}, u32[]{:S(2)}, u32[]{:S(2)}) collective-permute-start(bf16[192,1152]{1,0:T(8,128)(2,1)} %get-tuple-element.118), channel_id=1, source_target_pairs={{0,4},{2,6},{4,0},{6,2},{1,5},{3,7},{5,1},{7,3},{8,12},{10,14},{12... | collective-permute-start | bytes 1327112 | tf_op jit(solution)/shard_map/reduce_input_weights/ppermute | solution.py:767
  178.6 30.3 %collective-permute-start.25 = (bf16[192,1152]{1,0:T(8,128)(2,1)}, bf16[192,1152]{1,0:T(8,128)(2,1)S(1)}, u32[]{:S(2)}, u32[]{:S(2)}) collective-permute-start(bf16[192,1152]{1,0:T(8,128)(2,1)} %get-tuple-element.119), channel_id=1, source_target_pairs={{0,6},{2,4},{4,2},{6,0},{1,7},{3,5},{5,3},{7,1},{8,14},{10,12},{12... | collective-permute-start | bytes 1327112 | tf_op jit(solution)/shard_map/reduce_input_weights/ppermute | solution.py:767
  178.6 71.2 %collective-permute-start.20 = (bf16[1024,768]{1,0:T(8,128)(2,1)}, bf16[1024,768]{1,0:T(8,128)(2,1)S(1)}, u32[]{:S(2)}, u32[]{:S(2)}) collective-permute-start(bf16[1024,768]{1,0:T(8,128)(2,1)} %get-tuple-element.114.own), channel_id=1, source_target_pairs={{0,1},{1,0},{2,3},{3,2},{4,5},{5,4},{6,7},{7,6},{8,9},{9,8},{10,11... | collective-permute-start | bytes 4718600 | tf_op jit(solution)/shard_map/ppermute | solution.py:763
  188.3 24.3 %collective-permute-start.36 = (bf16[48,1536]{1,0:T(8,128)(2,1)S(1)}, bf16[48,1536]{1,0:T(8,128)(2,1)S(1)}, u32[]{:S(2)}, u32[]{:S(2)}) collective-permute-start(bf16[48,1536]{1,0:T(8,128)(2,1)S(1)} %get-tuple-element.142), channel_id=1, source_target_pairs={{0,8},{8,0},{16,24},{24,16},{1,9},{9,1},{17,25},{25,17},{2,10},{10... | collective-permute-start | bytes 442376 | tf_op jit(solution)/shard_map/reduce_gate_weights/ppermute | solution.py:767
  199.5 18.2 %collective-permute-start.37 = (bf16[48,1536]{1,0:T(8,128)(2,1)S(1)}, bf16[48,1536]{1,0:T(8,128)(2,1)S(1)}, u32[]{:S(2)}, u32[]{:S(2)}) collective-permute-start(bf16[48,1536]{1,0:T(8,128)(2,1)S(1)} %get-tuple-element.144), channel_id=1, source_target_pairs={{0,16},{8,24},{16,0},{24,8},{1,17},{9,25},{17,1},{25,9},{2,18},{10... | collective-permute-start | bytes 442376 | tf_op jit(solution)/shard_map/reduce_gate_weights/ppermute | solution.py:767
  223.1 26.3 %collective-permute-start.21 = (f32[8,768]{1,0:T(8,128)S(1)}, f32[8,768]{1,0:T(8,128)S(1)}, u32[]{:S(2)}, u32[]{:S(2)}) collective-permute-start(f32[8,768]{1,0:T(8,128)S(1)} %copy-done.33), channel_id=1, source_target_pairs={{2,0},{3,1},{4,2},{5,3},{6,4},{7,5},{10,8},{11,9},{12,10},{13,11},... | collective-permute-start | bytes 73736 | tf_op jit(solution)/shard_map/ppermute | solution.py:1059
  (58 other events, 596.8 us)

commit v3 on v2

--- a/solution.py
+++ b/solution.py
@@ -376,20 +376,10 @@
         packet_o[...] = state_packet(total, after)
 
 
-def gate_matmul_kernel(counts, dp_count, info, *refs):
-    shards = refs[:dp_count]
-    normed, cot, w2, z_o, dn_o = refs[dp_count:]
+def gate_matmul_kernel(counts, info, normed, cot, w2, z_o, dn_o):
     block = pl.program_id(0)
     place = Place(info, counts)
     inner = z_o.shape[1]
-    shard = shards[0].shape[0]
-
-    @pl.when(block == 0)
-    def _():
-        for offset in range(dp_count):
-            first = pl.multiple_of(xor(place.dp, offset) * shard, shard)
-            w2[pl.ds(first, shard), :] = shards[offset][...]
-
     z_o[...] = dot(normed[...], w2[:, :inner]).astype(BF16)
     grad = (cot[...].astype(F32) * place.valid(block)).astype(BF16)
     dn_o[...] = dot(grad, w2[:, inner:])
@@ -423,8 +413,8 @@
 
 
 def gate_back_kernel(
-    counts, inner_all, info, stat, y, z, dn, cot, cum, bc, xc, hb, decay, wo, par, spread,
-    keep_o, send_o, gwo_o, small_o, dy_o, dz_o, de_o, exit_o, packet_o,
+    counts, inner_all, info, stat, y, z, dn, cot, cum, bc, xc, hb, decay, normed, wo, par, spread,
+    keep_o, send_o, g2_o, small_o, dy_o, dz_o, de_o, exit_o, packet_o,
     acc, run, factor,
 ):
     step = pl.program_id(0)
@@ -456,12 +446,14 @@
     keep_o[...] = dot_nt(normal, wo[pl.ds(own, half), :]).astype(BF16)
     send_o[...] = dot_nt(normal, wo[pl.ds(other, half), :]).astype(BF16)
     grad = (cot[...].astype(F32) * place.valid(block)).astype(BF16)
-    acc[...] += dot_tn(grad, normal)
+    acc[:, inner:] += dot_tn(grad, normal)
     back = dn[...]
     grad_gated = inv * (gain * back) - gated * (inv * inv * inv) * (cross / inner_all)
     dy = (grad_gated * silu).astype(BF16)
     dy_o[...] = dy
-    dz_o[...] = (grad_gated * mixed * sig * (1.0 + gate * (1.0 - sig))).astype(BF16)
+    dz = (grad_gated * mixed * sig * (1.0 + gate * (1.0 - sig))).astype(BF16)
+    dz_o[...] = dz
+    acc[:, :inner] += dot_tn(normed[...], dz)
     dy_float = dy.astype(F32)
     cq = bc[:, LANES:]
     read = dot_nt(cq, hb[0])
@@ -479,21 +471,19 @@
     @pl.when(step == pl.num_programs(0) - 1)
     def _():
         packet_o[...] = state_packet(total, after)
-        gwo_o[...] = acc[...].astype(BF16)
-
-
-def intra_back_kernel(counts, heads, dp_count, info, *refs):
-    dy, dz, xc, bc, cum, pre_step, hb, normed, wz, gwo, par, spread = refs[:12]
-    dxc_o, dcq_o, dbq_o, rows_o, cols_o, dnz_o = refs[12:18]
-    parts = refs[18:-2]
-    acc, columns = refs[-2:]
+        g2_o[...] = acc[...].astype(BF16)
+
+
+def intra_back_kernel(
+    counts, heads, info, dy, dz, xc, bc, cum, pre_step, hb, wz, par, spread,
+    dxc_o, dcq_o, dbq_o, rows_o, cols_o, dnz_o,
+    columns,
+):
     block = pl.program_id(0)
     place = Place(info, counts)
-    inner = heads * HEAD
 
     @pl.when(block == 0)
     def _():
-        acc[...] = jnp.zeros_like(acc)
         columns[...] = jnp.zeros_like(columns)
 
     bq = bc[:, :LANES]
@@ -534,12 +524,6 @@
     rows_o[...] = sums
     cols_o[...] = columns[...].T
     dnz_o[...] = dot_nt(dz[...], wz[...])
-    acc[...] += dot_tn(normed[...], dz[...])
-
-    @pl.when(block == pl.num_programs(0) - 1)
-    def _():
-        cut_pieces(place, dp_count, acc, parts, slice(0, inner))
-        cut_pieces(place, dp_count, gwo, parts, slice(inner, 2 * inner))
 
 
 def state_back_kernel(counts, heads, dp_count, packet_count, part_count, info, *refs):
@@ -663,18 +647,6 @@
     grad_o[...] = (
         inv * scaled - inputs * (inv * inv * inv) * (inner_dot / width) + cot[...].astype(F32)
     )
-
-
-def unpack_gate_kernel(counts, part_count, info, *refs):
-    parts = refs[:part_count]
-    wz_o, wo_o = refs[part_count:]
-    place = Place(info, counts)
-    shard, inner = wz_o.shape
-    rows = shard // part_count
-    for part in range(part_count):
-        first = pl.multiple_of(xor(place.ctx, part) * rows, rows) if part_count > 1 else 0
-        wz_o[pl.ds(first, rows), :] = parts[part][:, :inner].astype(F32)
-        wo_o[pl.ds(first, rows), :] = parts[part][:, inner:].astype(F32)
 
 
 def unpack_input_kernel(counts, heads, part_count, info, *refs):
@@ -773,11 +745,11 @@
 
 def gather_rows(value, parts):
     if parts == 1:
-        return [lax.all_gather(value, "dp", axis=0, tiled=True)], ()
+        return [lax.all_gather(value, "dp", axis=0, tiled=True)]
     rows = value.shape[0] // parts
     own = lax.dynamic_slice_in_dim(value, lax.axis_index("ctx") * rows, rows, 0)
     joined = jnp.concatenate(exchanged(own, "dp"), axis=0)
-    return exchanged(joined, "ctx"), joined
+    return exchanged(joined, "ctx")
 
 
 def reduce_rows(pieces):
@@ -815,7 +787,7 @@
     part_rows = shard // parts
 
     with jax.named_scope("gather_weights"):
-        w1_parts, arrived = gather_rows(jnp.concatenate([w_x, w_bc], axis=1), parts)
+        w1_parts = gather_rows(jnp.concatenate([w_x, w_bc], axis=1), parts)
         vector = jnp.concatenate(
             [
                 conv_x.reshape(CONV, shard),
@@ -832,9 +804,7 @@
             axis=0,
         )
         vectors = exchanged(vector, "dp")
-        shard2 = jnp.concatenate([w_z, w_out.T], axis=1)
-        shard2, _ = lax.optimization_barrier((shard2, arrived))
-        w2_shards = exchanged(shard2, "dp")
+        w2 = lax.all_gather(jnp.concatenate([w_z, w_out.T], axis=1), "dp", axis=0, tiled=True)
 
     dtp = jnp.pad(jnp.stack([dt_bias, jnp.exp(a_log), skip_d]), ((0, 5), (0, LANES - heads)))
     shape = (2 * LANES, inner)
@@ -890,12 +860,12 @@
     packets = [(shifted(packet, "ctx", step), "whole") for step in range(1, ctx_count)]
     wz_spec = pl.BlockSpec((width, inner), lambda i: (0, 0))
     wo_spec = pl.BlockSpec((width, inner), lambda i: (0, 1))
-    w2, z, dn = call(
-        functools.partial(gate_matmul_kernel, counts, dp_count),
+    z, dn = call(
+        functools.partial(gate_matmul_kernel, counts),
         steps,
         info,
-        [(value, "whole") for value in w2_shards] + [(normed, "rows"), (cotangent, "rows")],
-        [out((width, 2 * inner), BF16, "whole"), row_out(inner, BF16), row_out(inner, F32)],
+        [(normed, "rows"), (cotangent, "rows"), (w2, "whole")],
+        [row_out(inner, BF16), row_out(inner, F32)],
         micros=7,
     )
     y, hb, h, stat = call(
@@ -926,7 +896,7 @@
     stat = lax.psum(stat, "tp")
     inner_all = inner * lax.axis_size("tp")
     half = width // 2
-    keep, send, gwo, small_gate, dy, dz, de, exits, packet = call(
+    keep, send, g2, small_gate, dy, dz, de, exits, packet = call(
         functools.partial(gate_back_kernel, counts, inner_all),
         steps,
         info,
@@ -941,6 +911,7 @@
             (xc, "rows"),
             (hb, "block"),
             (decay, "block"),
+            (normed, "rows"),
             (w2, wo_spec),
             (par, "whole"),
             (spread, "whole"),
@@ -948,7 +919,7 @@
         [
             row_out(half, BF16),
             row_out(half, BF16),
-            out((width, inner), BF16, "whole"),
+            out((width, 2 * inner), BF16, "whole"),
             out((8, inner), F32, "whole"),
             row_out(inner, BF16),
             row_out(inner, BF16),
@@ -957,21 +928,24 @@
             packet_out,
         ],
         [
-            pltpu.VMEM((width, inner), F32),
+            pltpu.VMEM((width, 2 * inner), F32),
             pltpu.VMEM((inner, LANES), F32),
             pltpu.VMEM((8, LANES), F32),
         ],
         reverse=True,
-        micros=15,
-    )
+        micros=16,
+    )
+    with jax.named_scope("reduce_gate_weights"):
+        total2 = lax.psum_scatter(g2, "dp", scatter_dimension=0, tiled=True)
+        total2 = lax.psum(total2, "ctx").astype(F32)
     packets = [(shifted(packet, "ctx", -step), "whole") for step in range(1, ctx_count)]
     with jax.named_scope("layer_out"):
         received = swapped(send)
         own_inputs = lax.dynamic_slice_in_dim(tokens, tp_index * half, half, 1).astype(F32)
         valid = (jnp.arange(rows) < fill).astype(F32)[:, None]
         layer_out = own_inputs + (keep.astype(F32) + received.astype(F32)) * valid
-    dxc, dcq, dbq, row_sums, col_sums, dnz, *g2 = call(
-        functools.partial(intra_back_kernel, counts, heads, dp_count),
+    dxc, dcq, dbq, row_sums, col_sums, dnz = call(
+        functools.partial(intra_back_kernel, counts, heads),
         steps,
         info,
         [
@@ -982,9 +956,7 @@
             (cum, "rows"),
             (pre_step, "rows"),
             (hb, "block"),
-            (normed, "rows"),
             (w2, wz_spec),
-            (gwo, "whole"),
             (par, "whole"),
             (spread, "whole"),
         ],
@@ -995,14 +967,10 @@
             row_out(LANES, F32),
             row_out(LANES, F32),
             row_out(width, F32),
-        ]
-        + [out((width // parts, 2 * inner), BF16, "whole")] * parts,
-        [pltpu.VMEM((width, inner), F32), pltpu.VMEM((LANES, BLOCK), F32)],
-        micros=18,
-    )
-    with jax.named_scope("reduce_gate_weights"):
-        total2 = reduce_rows(g2)
-        total2 = exchanged(total2, "ctx") if parts > 1 else [total2]
+        ],
+        [pltpu.VMEM((LANES, BLOCK), F32)],
+        micros=17,
+    )
     partial, halo_grad, *g1 = call(
         functools.partial(state_back_kernel, counts, heads, dp_count, len(packets), parts),
         steps,
@@ -1089,14 +1057,6 @@
     def final(*sizes):
         return out(sizes, F32, "whole")
 
-    grad_wz, grad_wo = call(
-        functools.partial(unpack_gate_kernel, counts, parts),
-        1,
-        info,
-        [(value, "whole") for value in total2],
-        [final(shard, inner), final(shard, inner)],
-        micros=2,
-    )
     (
         grad_wx, grad_wbc, grad_wdt, grad_norm, grad_taps, grad_bias, grad_state_taps, grad_state_bias,
         grad_dt_bias, grad_a_log, grad_skip, grad_gate,
@@ -1126,7 +1086,7 @@
         layer_out,
         grad_tokens,
         grad_norm[0],
-        grad_wz,
+        total2[:, :inner],
         grad_wx,
         grad_wbc,
         grad_wdt.T,
@@ -1138,7 +1098,7 @@
         grad_a_log[0],
         grad_skip[0],
         grad_gate,
-        grad_wo.T,
+        total2[:, inner:].T,
     )
 
 

time: 260 us -> 275 us (1.058)
  waiting for transfers between devices: 41.3 us -> 79 us
  starting transfers between devices: 80.2 us -> 49.9 us
  between operations: 2.03 us -> 14.9 us
  Pallas kernels: 110 us -> 106 us
    psum x0 -> x1, waiting for transfers between devices: none -> 33.3 us  [body(): total2 = lax.psum(total2, 'ctx').astype(F32)]
    ppermute x30 -> x18, starting transfers between devices: 60.7 us -> 32.2 us  [partnered(): lax.ppermute(value, axis, [(one, one ^ mask) for one in range(lax.axis_si...]
    pallas_call x9 -> x8, Pallas kernels: 110 us -> 106 us  [call(): pl.pallas_call(body, grid=(steps,), in_specs=[pl.BlockSpec(memory_space=p...]
    ppermute x30 -> x18, waiting for transfers between devices: 33.9 us -> 36.8 us  [partnered(): lax.ppermute(value, axis, [(one, one ^ mask) for one in range(lax.axis_si...]
    unnamed x81 -> x59, local copies, waits for them, and re-layouts: 7.13 us -> 4.24 us
  transfers between devices with their start and end apart: 42 -> 33, of which waited for: 10 -> 14; matrix products, arithmetic and copies ran while one was open for 5% -> 3% of each run, Pallas kernels for 31% -> 29%
where the time goes in v3:
time: 275 us; the launch traced here: 274 us
  Pallas kernels  106 us (39%)
  waiting for transfers between devices  79 us (29%)
  starting transfers between devices  49.9 us (18%)
  between operations  14.9 us (5%)
  local copies, waits for them, and re-layouts  10.5 us (4%)
  other arithmetic  9.08 us (3%)
  blocking collectives  4.65 us (2%)
    pallas_call x8, Pallas kernels, call(): pl.pallas_call(body, grid=(steps,), in_specs=[pl.BlockSpec(memory_space=p...  106 us
    ppermute x18, waiting for transfers between devices, partnered(): lax.ppermute(value, axis, [(one, one ^ mask) for one in range(lax.axis_si...  36.8 us
    psum x1, waiting for transfers between devices, body(): total2 = lax.psum(total2, 'ctx').astype(F32)  33.3 us
    ppermute x18, starting transfers between devices, partnered(): lax.ppermute(value, axis, [(one, one ^ mask) for one in range(lax.axis_si...  32.2 us
    ppermute x7, starting transfers between devices, shifted(): lax.ppermute(value, axis, [(source, source + steps) for source in range(f...  14.9 us
    ppermute x7, waiting for transfers between devices, shifted(): lax.ppermute(value, axis, [(source, source + steps) for source in range(f...  7.99 us
  transfers between devices with their start and end apart: 33, of which 14 were waited for; matrix products, arithmetic and copies ran while one was open for 3% of the time, Pallas kernels for 29%

profile of v3, /device:TPU:0, one launch (start us, length us, event | category | flops | bytes accessed | tf_op | source)
XLA Modules:
  0.0 274.0 jit_solution(3335693493285305923)
XLA Ops:
  11.8 5.1 %collective-permute-start.2 = (bf16[32,192]{1,0:T(8,128)(2,1)S(1)}, bf16[32,192]{1,0:T(8,128)(2,1)S(1)}, u32[]{:S(2)}, u32[]{:S(2)}) collective-permute-start(bf16[32,192]{1,0:T(8,128)(2,1)S(1)} %concatenate.23.refs_0_), channel_id=1, source_target_pairs={{0,24},{8,16},{16,8},{24,0},{1,25},{9,17},{17,9},{25,1},{2,26},{10... | collective-permute-start | bytes 36872 | tf_op jit(solution)/shard_map/gather_weights/ppermute | solution.py:739
  26.5 4.1 %collective-permute-done.4 = bf16[48,1024]{1,0:T(8,128)(2,1)S(1)} collective-permute-done((bf16[48,1024]{1,0:T(8,128)(2,1)S(1)}, bf16[48,1024]{1,0:T(8,128)(2,1)S(1)}, u32[]{:S(2)}, u32[]{:S(2)}) %collective-permute-start.4) | collective-permute-done | bytes 98336 | tf_op jit(solution)/shard_map/gather_weights/ppermute | solution.py:739
  30.6 2.5 collective-permute-start.8
  37.2 3.0 %collective-permute-start.9 = (bf16[16,768]{1,0:T(8,128)(2,1)S(1)}, bf16[16,768]{1,0:T(8,128)(2,1)S(1)}, u32[]{:S(2)}, u32[]{:S(2)}) collective-permute-start(bf16[16,768]{1,0:T(8,128)(2,1)S(1)} %constant_dynamic-slice_fusion), channel_id=1, source_target_pairs={{0,2},{2,4},{4,6},{1,3},{3,5},{5,7},{8,10},{10,12},{12,14},{9,11},... | collective-permute-start | bytes 73736 | tf_op jit(solution)/shard_map/ppermute | solution.py:731
  41.4 8.0 %collective-permute-done.9.refs_9_.refs_20_ = bf16[16,768]{1,0:T(8,128)(2,1)S(1)} collective-permute-done((bf16[16,768]{1,0:T(8,128)(2,1)S(1)}, bf16[16,768]{1,0:T(8,128)(2,1)S(1)}, u32[]{:S(2)}, u32[]{:S(2)}) %collective-permute-start.9) | collective-permute-done | bytes 24608 | tf_op jit(solution)/shard_map/ppermute | solution.py:731
  51.2 20.5 %shard_map.297 = (bf16[768,1152]{1,0:T(8,128)(2,1)}, f32[8,1024]{1,0:T(8,128)}, bf16[1024,768]{1,0:T(8,128)(2,1)}, bf16[16,768]{1,0:T(8,128)(2,1)}, f32[8,1024]{...) custom-call(s32[10]{0:T(128)} %concatenate.21.info, ...), custom_call_target="tpu_custom_call" | custom-call | flops 22000001024 | bytes 70000000 | tf_op jit(solution)/shard_map/pallas_call | solution.py:711
  71.8 4.1 %collective-permute-start.12 = (bf16[784,128]{1,0:T(8,128)(2,1)}, bf16[784,128]{1,0:T(8,128)(2,1)S(1)}, u32[]{:S(2)}, u32[]{:S(2)}) collective-permute-start(bf16[784,128]{1,0:T(8,128)(2,1)} %get-tuple-element.69), channel_id=1, source_target_pairs={{0,6},{1,7},{8,14},{9,15},{16,22},{17,23},{24,30},{25,31}} | collective-permute-start | bytes 602120 | tf_op jit(solution)/shard_map/ppermute | solution.py:731
  79.7 6.7 %shard_map.298 = (bf16[1024,768]{1,0:T(8,128)(2,1)}, f32[1024,768]{1,0:T(8,128)}) custom-call(s32[10]{0:T(128)} %concatenate.21.info, bf16[1024,768]{1,0:T(8,128)(2,1)} %get-tuple-element.75.normed.refs_22_, bf16[1024,768]{1,0:T(8,128)(2,1)} %cot.5, bf16[768,1536]{1,0:T(8,128)(2,1)} %all-gather.2.cloned.1.call-done.w2.wo.wz), custom_call_target="tpu_custom_call" | custom-call | flops 7699999744 | bytes 24500000 | tf_op jit(solution)/shard_map/pallas_call | solution.py:711
  87.2 8.6 %shard_map.299 = (f32[1024,768]{1,0:T(8,128)}, bf16[4,768,128]{2,1,0:T(8,128)(2,1)}, f32[4,768,128]{2,1,0:T(8,128)}, f32[8,1024]{1,0:T(8,128)}) custom-call(s32[10]{0:T(128)} %concatenate.21.info, bf16[784,128]{1,0:T(8,128)(2,1)} %copy-done.20, bf16[784,128]{1,0:T(8,128)(2,1)} %copy-done.19, bf16[784,128]{1,0:T(8,128)(2,1)} %copy-done.18, ...), custom_call_target="tpu_custom_call" | custom-call | flops 8800000000 | bytes 28000000 | tf_op jit(solution)/shard_map/pallas_call | solution.py:711
  95.8 4.6 %psum.14.stat = f32[8,1024]{1,0:T(8,128)} all-reduce(f32[8,1024]{1,0:T(8,128)} %get-tuple-element.79), channel_id=1, replica_groups=mesh['dp'=4,'ctx'=4,'tp'=2] {'tp'}, use_global_device_ids=true, to_apply=%region_1.2 | all-reduce | flops 8192 | bytes 65536 | tf_op jit(solution)/shard_map/psum | solution.py:896
  100.5 16.8 %shard_map.300 = (bf16[1024,384]{1,0:T(8,128)(2,1)}, bf16[1024,384]{1,0:T(8,128)(2,1)}, bf16[768,1536]{1,0:T(8,128)(2,1)}, f32[8,768]{1,0:T(8,128)}, bf16[1024,7...) custom-call(s32[10]{0:T(128)} %concatenate.21.info, ...), custom_call_target="tpu_custom_call" | custom-call | flops 17600000000 | bytes 56000000 | tf_op jit(solution)/shard_map/pallas_call | solution.py:711
  121.4 16.5 %shard_map.301 = (f32[1024,768]{1,0:T(8,128)}, f32[1024,128]{1,0:T(8,128)}, f32[1024,128]{1,0:T(8,128)}, f32[1024,128]{1,0:T(8,128)}, f32[1024,128]{1,0:T(8,128)}, /*index=5*/f32[1024,768]{1,0:T(8,128)}) custom-call(s32[10]{0:T(128)} %concatenate.21.info, bf16[1024,768]{1,0:T(8,128)(2,1)} %get-tuple-element.90.dy, bf16[1024,768]{1,0:T(8,128)(2,1)} %get-tuple-element.91.dz, ...), custom_call_target="tpu_custom_call" | custom-call | flops 18699999232 | bytes 59500000 | tf_op jit(solution)/shard_map/pallas_call | solution.py:711
  138.9 29.1 %shard_map.302 = (bf16[1024,768]{1,0:T(8,128)(2,1)}, f32[8,768]{1,0:T(8,128)}, bf16[192,1152]{1,0:T(8,128)(2,1)}, bf16[192,1152]{1,0:T(8,128)(2,1)}, bf16[192,11...) custom-call(s32[10]{0:T(128)} %concatenate.21.info, bf16[784,128]{1,0:T(8,128)(2,1)} %copy-done.17, ...), custom_call_target="tpu_custom_call" | custom-call | flops 30799998976 | bytes 98000000 | tf_op jit(solution)/shard_map/pallas_call | solution.py:711
  168.0 2.7 collective-permute-start.20
  170.7 2.7 collective-permute-start.21
  173.3 8.5 %collective-permute-done.20 = bf16[192,1152]{1,0:T(8,128)(2,1)S(1)} collective-permute-done((bf16[192,1152]{1,0:T(8,128)(2,1)}, bf16[192,1152]{1,0:T(8,128)(2,1)S(1)}, u32[]{:S(2)}, u32[]{:S(2)}) %collective-permute-start.20) | collective-permute-done | bytes 442400 | tf_op jit(solution)/shard_map/reduce_input_weights/ppermute | solution.py:739
  181.8 11.0 %collective-permute-done.21 = bf16[192,1152]{1,0:T(8,128)(2,1)S(1)} collective-permute-done((bf16[192,1152]{1,0:T(8,128)(2,1)}, bf16[192,1152]{1,0:T(8,128)(2,1)S(1)}, u32[]{:S(2)}, u32[]{:S(2)}) %collective-permute-start.21) | collective-permute-done | bytes 442400 | tf_op jit(solution)/shard_map/reduce_input_weights/ppermute | solution.py:739
  194.3 2.7 collective-permute-start.23
  196.9 3.2 %collective-permute-start.25 = (bf16[48,1152]{1,0:T(8,128)(2,1)S(1)}, bf16[48,1152]{1,0:T(8,128)(2,1)S(1)}, u32[]{:S(2)}, u32[]{:S(2)}) collective-permute-start(bf16[48,1152]{1,0:T(8,128)(2,1)S(1)} %get-tuple-element.125), channel_id=1, source_target_pairs={{0,24},{8,16},{16,8},{24,0},{1,25},{9,17},{17,9},{25,1},{2,26},{10... | collective-permute-start | bytes 331784 | tf_op jit(solution)/shard_map/reduce_input_weights/ppermute | solution.py:739
  200.7 5.2 %collective-permute-done.25 = bf16[48,1152]{1,0:T(8,128)(2,1)S(1)} collective-permute-done((bf16[48,1152]{1,0:T(8,128)(2,1)S(1)}, bf16[48,1152]{1,0:T(8,128)(2,1)S(1)}, u32[]{:S(2)}, u32[]{:S(2)}) %collective-permute-start.25) | collective-permute-done | bytes 110624 | tf_op jit(solution)/shard_map/reduce_input_weights/ppermute | solution.py:739
  205.8 3.8 %collective-permute-done.24 = bf16[48,1152]{1,0:T(8,128)(2,1)S(1)} collective-permute-done((bf16[48,1152]{1,0:T(8,128)(2,1)S(1)}, bf16[48,1152]{1,0:T(8,128)(2,1)S(1)}, u32[]{:S(2)}, u32[]{:S(2)}) %collective-permute-start.24) | collective-permute-done | bytes 110624 | tf_op jit(solution)/shard_map/reduce_input_weights/ppermute | solution.py:739
  211.2 4.2 %collective-permute-start.29 = (bf16[48,1152]{1,0:T(8,128)(2,1)S(1)}, bf16[48,1152]{1,0:T(8,128)(2,1)S(1)}, u32[]{:S(2)}, u32[]{:S(2)}) collective-permute-start(bf16[48,1152]{1,0:T(8,128)(2,1)S(1)} %pad_maximum_fusion.2.refs_0_), channel_id=1, source_target_pairs={{0,6},{2,4},{4,2},{6,0},{1,7},{3,5},{5,3},{7,1},{8,14},{10,12},{12... | collective-permute-start | bytes 331784 | tf_op jit(solution)/shard_map/reduce_input_weights/ppermute | solution.py:739
  225.5 5.6 %shard_map.303 = f32[1024,768]{1,0:T(8,128)} custom-call(s32[10]{0:T(128)} %concatenate.21.info, bf16[1024,768]{1,0:T(8,128)(2,1)} %get-tuple-element.103.own, bf16[1024,768]{1,0:T(8,128)(2,1)} %collective-permute-done.17.other, f32[8,768]{1,0:T(8,128)} %copy-done.24, f32[8,768]{1,0:T(8,128)} %collective-permute-done.19.halo_b, bf16[1024,768]{1,0:T(8,128)(2,1)} %tok.1, ...), custom_call_target="tpu_custom_call" | custom-call | flops 5500000256 | bytes 17500000 | tf_op jit(solution)/shard_map/pallas_call | solution.py:711
  231.2 33.3 %all-reduce.5.cloned.1.call-done = bf16[192,1536]{1,0:T(8,128)(2,1)} async-done(((bf16[192,1536]{1,0:T(8,128)(2,1)}), bf16[192,1536]{1,0:T(8,128)(2,1)}) %all-reduce.5.cloned.1.call-update) | async-done | bytes 589840 | tf_op jit(solution)/shard_map/reduce_gate_weights/psum | solution.py:940
  (147 shorter events, 46.5 us)
Async XLA Ops:
  7.2 72.5 %all-gather.2.cloned.1.call-start = ((), (), s32[]{:S(2)}) async-start(), calls=%async_computation.1 | async-start | bytes 2949120 | tf_op jit(solution)/shard_map/gather_weights/all_gather | solution.py:807
  11.8 23.1 %collective-permute-start.2 = (bf16[32,192]{1,0:T(8,128)(2,1)S(1)}, bf16[32,192]{1,0:T(8,128)(2,1)S(1)}, u32[]{:S(2)}, u32[]{:S(2)}) collective-permute-start(bf16[32,192]{1,0:T(8,128)(2,1)S(1)} %concatenate.23.refs_0_), channel_id=1, source_target_pairs={{0,24},{8,16},{16,8},{24,0},{1,25},{9,17},{17,9},{25,1},{2,26},{10... | collective-permute-start | bytes 36872 | tf_op jit(solution)/shard_map/gather_weights/ppermute | solution.py:739
  16.9 20.3 %collective-permute-start.1 = (bf16[32,192]{1,0:T(8,128)(2,1)S(1)}, bf16[32,192]{1,0:T(8,128)(2,1)S(1)}, u32[]{:S(2)}, u32[]{:S(2)}) collective-permute-start(bf16[32,192]{1,0:T(8,128)(2,1)S(1)} %concatenate.23.refs_0_), channel_id=1, source_target_pairs={{0,16},{8,24},{16,0},{24,8},{1,17},{9,25},{17,1},{25,9},{2,18},{10... | collective-permute-start | bytes 36872 | tf_op jit(solution)/shard_map/gather_weights/ppermute | solution.py:739
  18.9 198.9 %reduce-scatter.2.cloned.1.call-start = ((), (), s32[]{:S(2)}) async-start(), calls=%async_computation.2 | async-start | bytes 2949120 | tf_op jit(solution)/shard_map/reduce_gate_weights/reduce_scatter | solution.py:939
  21.0 9.6 %collective-permute-start.4 = (bf16[48,1024]{1,0:T(8,128)(2,1)S(1)}, bf16[48,1024]{1,0:T(8,128)(2,1)S(1)}, u32[]{:S(2)}, u32[]{:S(2)}) collective-permute-start(bf16[48,1024]{1,0:T(8,128)(2,1)S(1)} %fusion.4), channel_id=1, source_target_pairs={{0,16},{8,24},{16,0},{24,8},{1,17},{9,25},{17,1},{25,9},{2,18},{10... | collective-permute-start | bytes 294920 | tf_op jit(solution)/shard_map/gather_weights/ppermute | solution.py:739
  30.6 18.8 %collective-permute-start.8 = (bf16[192,1024]{1,0:T(8,128)(2,1)S(1)}, bf16[192,1024]{1,0:T(8,128)(2,1)S(1)}, u32[]{:S(2)}, u32[]{:S(2)}) collective-permute-start(bf16[192,1024]{1,0:T(8,128)(2,1)S(1)} %pad_maximum_fusion.1.refs_4_), channel_id=1, source_target_pairs={{0,6},{2,4},{4,2},{6,0},{1,7},{3,5},{5,3},{7,1},{8,14},{10,12},{12... | collective-permute-start | bytes 1179656 | tf_op jit(solution)/shard_map/gather_weights/ppermute | solution.py:739
  33.1 16.6 %collective-permute-start.7 = (bf16[192,1024]{1,0:T(8,128)(2,1)S(1)}, bf16[192,1024]{1,0:T(8,128)(2,1)S(1)}, u32[]{:S(2)}, u32[]{:S(2)}) collective-permute-start(bf16[192,1024]{1,0:T(8,128)(2,1)S(1)} %pad_maximum_fusion.1.refs_4_), channel_id=1, source_target_pairs={{0,4},{2,6},{4,0},{6,2},{1,5},{3,7},{5,1},{7,3},{8,12},{10,14},{12... | collective-permute-start | bytes 1179656 | tf_op jit(solution)/shard_map/gather_weights/ppermute | solution.py:739
  33.6 16.5 %collective-permute-start.6 = (bf16[192,1024]{1,0:T(8,128)(2,1)S(1)}, bf16[192,1024]{1,0:T(8,128)(2,1)S(1)}, u32[]{:S(2)}, u32[]{:S(2)}) collective-permute-start(bf16[192,1024]{1,0:T(8,128)(2,1)S(1)} %pad_maximum_fusion.1.refs_4_), channel_id=1, source_target_pairs={{0,2},{2,0},{4,6},{6,4},{1,3},{3,1},{5,7},{7,5},{8,10},{10,8},{12,... | collective-permute-start | bytes 1179656 | tf_op jit(solution)/shard_map/gather_weights/ppermute | solution.py:739
  37.2 12.2 %collective-permute-start.9 = (bf16[16,768]{1,0:T(8,128)(2,1)S(1)}, bf16[16,768]{1,0:T(8,128)(2,1)S(1)}, u32[]{:S(2)}, u32[]{:S(2)}) collective-permute-start(bf16[16,768]{1,0:T(8,128)(2,1)S(1)} %constant_dynamic-slice_fusion), channel_id=1, source_target_pairs={{0,2},{2,4},{4,6},{1,3},{3,5},{5,7},{8,10},{10,12},{12,14},{9,11},... | collective-permute-start | bytes 73736 | tf_op jit(solution)/shard_map/ppermute | solution.py:731
  71.8 14.6 %collective-permute-start.12 = (bf16[784,128]{1,0:T(8,128)(2,1)}, bf16[784,128]{1,0:T(8,128)(2,1)S(1)}, u32[]{:S(2)}, u32[]{:S(2)}) collective-permute-start(bf16[784,128]{1,0:T(8,128)(2,1)} %get-tuple-element.69), channel_id=1, source_target_pairs={{0,6},{1,7},{8,14},{9,15},{16,22},{17,23},{24,30},{25,31}} | collective-permute-start | bytes 602120 | tf_op jit(solution)/shard_map/ppermute | solution.py:731
  75.9 10.5 %collective-permute-start.11 = (bf16[784,128]{1,0:T(8,128)(2,1)}, bf16[784,128]{1,0:T(8,128)(2,1)S(1)}, u32[]{:S(2)}, u32[]{:S(2)}) collective-permute-start(bf16[784,128]{1,0:T(8,128)(2,1)} %get-tuple-element.69), channel_id=1, source_target_pairs={{0,4},{2,6},{1,5},{3,7},{8,12},{10,14},{9,13},{11,15},{16,20},{18,... | collective-permute-start | bytes 602120 | tf_op jit(solution)/shard_map/ppermute | solution.py:731
  77.2 9.2 %collective-permute-start.10 = (bf16[784,128]{1,0:T(8,128)(2,1)}, bf16[784,128]{1,0:T(8,128)(2,1)S(1)}, u32[]{:S(2)}, u32[]{:S(2)}) collective-permute-start(bf16[784,128]{1,0:T(8,128)(2,1)} %get-tuple-element.69), channel_id=1, source_target_pairs={{0,2},{2,4},{4,6},{1,3},{3,5},{5,7},{8,10},{10,12},{12,14},{9,11},... | collective-permute-start | bytes 602120 | tf_op jit(solution)/shard_map/ppermute | solution.py:731
  117.3 20.7 %collective-permute-start.16 = (bf16[784,128]{1,0:T(8,128)(2,1)}, bf16[784,128]{1,0:T(8,128)(2,1)S(1)}, u32[]{:S(2)}, u32[]{:S(2)}) collective-permute-start(bf16[784,128]{1,0:T(8,128)(2,1)} %get-tuple-element.85), channel_id=1, source_target_pairs={{6,0},{7,1},{14,8},{15,9},{22,16},{23,17},{30,24},{31,25}} | collective-permute-start | bytes 602120 | tf_op jit(solution)/shard_map/ppermute | solution.py:731
  118.6 19.4 %collective-permute-start.15 = (bf16[784,128]{1,0:T(8,128)(2,1)}, bf16[784,128]{1,0:T(8,128)(2,1)S(1)}, u32[]{:S(2)}, u32[]{:S(2)}) collective-permute-start(bf16[784,128]{1,0:T(8,128)(2,1)} %get-tuple-element.85), channel_id=1, source_target_pairs={{4,0},{6,2},{5,1},{7,3},{12,8},{14,10},{13,9},{15,11},{20,16},{22,... | collective-permute-start | bytes 602120 | tf_op jit(solution)/shard_map/ppermute | solution.py:731
  120.1 17.9 %collective-permute-start.14 = (bf16[784,128]{1,0:T(8,128)(2,1)}, bf16[784,128]{1,0:T(8,128)(2,1)S(1)}, u32[]{:S(2)}, u32[]{:S(2)}) collective-permute-start(bf16[784,128]{1,0:T(8,128)(2,1)} %get-tuple-element.85), channel_id=1, source_target_pairs={{2,0},{4,2},{6,4},{3,1},{5,3},{7,5},{10,8},{12,10},{14,12},{11,9},... | collective-permute-start | bytes 602120 | tf_op jit(solution)/shard_map/ppermute | solution.py:731
  121.4 143.1 %all-reduce.5.cloned.1.call-start = ((), (), s32[]{:S(2)}) async-start(), calls=%async_computation.3 | async-start | bytes 1179648 | tf_op jit(solution)/shard_map/reduce_gate_weights/psum | solution.py:940
  168.0 13.9 %collective-permute-start.20 = (bf16[192,1152]{1,0:T(8,128)(2,1)}, bf16[192,1152]{1,0:T(8,128)(2,1)S(1)}, u32[]{:S(2)}, u32[]{:S(2)}) collective-permute-start(bf16[192,1152]{1,0:T(8,128)(2,1)} %get-tuple-element.106), channel_id=1, source_target_pairs={{0,2},{2,0},{4,6},{6,4},{1,3},{3,1},{5,7},{7,5},{8,10},{10,8},{12,... | collective-permute-start | bytes 1327112 | tf_op jit(solution)/shard_map/reduce_input_weights/ppermute | solution.py:739
  170.7 22.2 %collective-permute-start.21 = (bf16[192,1152]{1,0:T(8,128)(2,1)}, bf16[192,1152]{1,0:T(8,128)(2,1)S(1)}, u32[]{:S(2)}, u32[]{:S(2)}) collective-permute-start(bf16[192,1152]{1,0:T(8,128)(2,1)} %get-tuple-element.107), channel_id=1, source_target_pairs={{0,4},{2,6},{4,0},{6,2},{1,5},{3,7},{5,1},{7,3},{8,12},{10,14},{12... | collective-permute-start | bytes 1327112 | tf_op jit(solution)/shard_map/reduce_input_weights/ppermute | solution.py:739
  173.3 19.5 %collective-permute-start.22 = (bf16[192,1152]{1,0:T(8,128)(2,1)}, bf16[192,1152]{1,0:T(8,128)(2,1)S(1)}, u32[]{:S(2)}, u32[]{:S(2)}) collective-permute-start(bf16[192,1152]{1,0:T(8,128)(2,1)} %get-tuple-element.108), channel_id=1, source_target_pairs={{0,6},{2,4},{4,2},{6,0},{1,7},{3,5},{5,3},{7,1},{8,14},{10,12},{12... | collective-permute-start | bytes 1327112 | tf_op jit(solution)/shard_map/reduce_input_weights/ppermute | solution.py:739
  173.3 51.6 %collective-permute-start.17 = (bf16[1024,768]{1,0:T(8,128)(2,1)}, bf16[1024,768]{1,0:T(8,128)(2,1)}, u32[]{:S(2)}, u32[]{:S(2)}) collective-permute-start(bf16[1024,768]{1,0:T(8,128)(2,1)} %get-tuple-element.103.own), channel_id=1, source_target_pairs={{0,1},{1,0},{2,3},{3,2},{4,5},{5,4},{6,7},{7,6},{8,9},{9,8},{10,11... | collective-permute-start | bytes 4718600 | tf_op jit(solution)/shard_map/ppermute | solution.py:735
  196.9 8.9 %collective-permute-start.25 = (bf16[48,1152]{1,0:T(8,128)(2,1)S(1)}, bf16[48,1152]{1,0:T(8,128)(2,1)S(1)}, u32[]{:S(2)}, u32[]{:S(2)}) collective-permute-start(bf16[48,1152]{1,0:T(8,128)(2,1)S(1)} %get-tuple-element.125), channel_id=1, source_target_pairs={{0,24},{8,16},{16,8},{24,0},{1,25},{9,17},{17,9},{25,1},{2,26},{10... | collective-permute-start | bytes 331784 | tf_op jit(solution)/shard_map/reduce_input_weights/ppermute | solution.py:739
  200.2 9.5 %collective-permute-start.24 = (bf16[48,1152]{1,0:T(8,128)(2,1)S(1)}, bf16[48,1152]{1,0:T(8,128)(2,1)S(1)}, u32[]{:S(2)}, u32[]{:S(2)}) collective-permute-start(bf16[48,1152]{1,0:T(8,128)(2,1)S(1)} %get-tuple-element.126), channel_id=1, source_target_pairs={{0,16},{8,24},{16,0},{24,8},{1,17},{9,25},{17,1},{25,9},{2,18},{10... | collective-permute-start | bytes 331784 | tf_op jit(solution)/shard_map/reduce_input_weights/ppermute | solution.py:739
  200.6 14.8 %collective-permute-start.13 = (bf16[1024,384]{1,0:T(8,128)(2,1)}, bf16[1024,384]{1,0:T(8,128)(2,1)S(1)}, u32[]{:S(2)}, u32[]{:S(2)}) collective-permute-start(bf16[1024,384]{1,0:T(8,128)(2,1)} %get-tuple-element.84), channel_id=1, source_target_pairs={{0,1},{1,0},{2,3},{3,2},{4,5},{5,4},{6,7},{7,6},{8,9},{9,8},{10,11... | collective-permute-start | bytes 2359304 | tf_op jit(solution)/shard_map/layer_out/ppermute | solution.py:735
  209.8 14.2 %collective-permute-start.19 = (f32[8,768]{1,0:T(8,128)}, f32[8,768]{1,0:T(8,128)}, u32[]{:S(2)}, u32[]{:S(2)}) collective-permute-start(f32[8,768]{1,0:T(8,128)} %get-tuple-element.104), channel_id=1, source_target_pairs={{2,1},{3,0},{4,3},{5,2},{6,5},{7,4},{10,9},{11,8},{12,11},{13,10},... | collective-permute-start | bytes 73736 | tf_op jit(solution)/shard_map/ppermute | solution.py:1028
  (38 other events, 330.1 us)
Sparse Core Ops, SparseCore 0:
  19.0 51.0 all-gather.1
  121.5 53.7 reduce-scatter.1
  218.0 46.4 all-reduce.4

commit v4 on v2

--- a/solution.py
+++ b/solution.py
@@ -212,7 +212,7 @@
 
 
 def join_parameters(place, vectors, skip, heads, par, w1):
-    shard = vectors[0].shape[1]
+    shard = vectors[0].shape[1] // 2
     each = HEAD // len(vectors)
     inner = heads * HEAD
     by_channel = jnp.zeros((16, inner), F32)
@@ -223,15 +223,15 @@
     for block, vector in enumerate(vectors):
         owner = xor(place.dp, block)
         first = pl.multiple_of(owner * shard, shard)
-        w1[pl.ds(first, shard), inner + 2 * LANES :] = dot_tn(vector[16:32, :], eye).astype(BF16)
+        w1[pl.ds(first, shard), inner + 2 * LANES :] = dot_tn(vector[:, shard:], eye).astype(BF16)
         source, target = iota((shard, inner), 0), iota((shard, inner), 1)
         pick = target == source // each * HEAD + owner * each + source % each
-        by_channel = by_channel + dot(vector[0:16, :], pick.astype(BF16))
+        by_channel = by_channel + dot(vector[:, :shard], pick.astype(BF16))
         source, target = iota((shard, in_order.shape[1]), 0), iota((shard, in_order.shape[1]), 1)
-        in_order = in_order + dot(vector[0:16, :], (target == owner * shard + source).astype(BF16))
+        in_order = in_order + dot(vector[:, :shard], (target == owner * shard + source).astype(BF16))
         source, target = iota((shard, 2 * LANES), 0), iota((shard, 2 * LANES), 1)
         pick = (target == owner * states + source) & (source < states)
-        by_state = by_state + dot(vector[0:16, :], pick.astype(BF16))
+        by_state = by_state + dot(vector[:, :shard], pick.astype(BF16))
     par[...] = jnp.zeros_like(par)
     par[0:5, :inner] = by_channel[0:5, :]
     par[0:5, inner:] = by_state[8:13, :]
@@ -240,7 +240,33 @@
     par[7:8, :inner] = skip
 
 
-TAPS, NORM, GATE, STATE_TAPS, BY_HEAD = 12, 17, 18, 20, 25
+TAPS, GATE, STATE_TAPS, BY_HEAD, NORM = 12, 18, 20, 25, 26
+
+
+def lanes(pieces, columns):
+    rows, at = [], 0
+    for first, value in pieces:
+        if first > at:
+            rows.append(jnp.zeros((first - at, columns), F32))
+        rows.append(value)
+        at = first + value.shape[0]
+    rows.append(jnp.zeros((LANES - at, columns), F32))
+    return jnp.concatenate(rows, axis=0)
+
+
+def pack_norm(place, dp_count, part_count, row, rows):
+    columns = row.shape[1]
+    shard = columns // dp_count
+    size = shard // rows
+    total = jnp.zeros((dp_count * rows, LANES), F32)
+    source, target = iota((dp_count * rows, columns), 0), iota((dp_count * rows, columns), 1)
+    owner = source // rows
+    if part_count > 1:
+        owner = jnp.bitwise_xor(owner, place.dp)
+    for lane in range(size):
+        pick = target == owner * shard + lane * rows + source % rows
+        total = total + dot_nt(pick.astype(BF16), lanes([(NORM + lane, row)], columns).astype(BF16))
+    return total
 
 
 def pack_parameters(dp_count, heads, small, gate, skip):
@@ -249,22 +275,11 @@
     shard = inner // dp_count
     states = 2 * LANES // dp_count
 
-    def lanes(pieces, columns):
-        rows, at = [], 0
-        for first, value in pieces:
-            if first > at:
-                rows.append(jnp.zeros((first - at, columns), F32))
-            rows.append(value)
-            at = first + value.shape[0]
-        rows.append(jnp.zeros((LANES - at, columns), F32))
-        return jnp.concatenate(rows, axis=0)
-
     source, target = iota((inner, inner), 0), iota((inner, inner), 1)
     inside = source % shard
     pick = target == inside // each * HEAD + source // shard * each + inside % each
     by_channel = lanes([(TAPS, small[0:5, :inner]), (GATE, gate)], inner)
     total = dot_nt(pick.astype(BF16), by_channel.astype(BF16))
-    total = total + lanes([(NORM, small[5:6, :inner])], inner).T
     source, target = iota((inner, 2 * LANES), 0), iota((inner, 2 * LANES), 1)
     inside = source % shard
     pick = (target == source // shard * states + inside) & (inside < states)
@@ -376,19 +391,16 @@
         packet_o[...] = state_packet(total, after)
 
 
-def gate_matmul_kernel(counts, dp_count, info, *refs):
-    shards = refs[:dp_count]
-    normed, cot, w2, z_o, dn_o = refs[dp_count:]
+def gate_matmul_kernel(counts, dp_count, part_count, info, *refs):
+    parts = refs[:part_count]
+    normed, cot, w2, z_o, dn_o = refs[part_count:]
     block = pl.program_id(0)
     place = Place(info, counts)
     inner = z_o.shape[1]
-    shard = shards[0].shape[0]
 
     @pl.when(block == 0)
     def _():
-        for offset in range(dp_count):
-            first = pl.multiple_of(xor(place.dp, offset) * shard, shard)
-            w2[pl.ds(first, shard), :] = shards[offset][...]
+        join_pieces(place, dp_count, parts, w2)
 
     z_o[...] = dot(normed[...], w2[:, :inner]).astype(BF16)
     grad = (cot[...].astype(F32) * place.valid(block)).astype(BF16)
@@ -542,28 +554,22 @@
         cut_pieces(place, dp_count, gwo, parts, slice(inner, 2 * inner))
 
 
-def state_back_kernel(counts, heads, dp_count, packet_count, part_count, info, *refs):
+def state_back_kernel(counts, heads, packet_count, info, *refs):
     packets = refs[:packet_count]
     (
-        exits, h, xc, bc, cum, pre_step, de, dxc, dcq, dbq, rows, cols, decay, v, v_tail, halo_v, halo_normed,
-        halo, tok, normed, dnz, small_gate, w1, par, dtp, spread,
-        dn_o, dnh_o,
-    ) = refs[packet_count : -6 - part_count]
-    parts = refs[-6 - part_count : -6]
-    start, factor, ext, grad_ext, acc, small_o = refs[-6:]
+        exits, h, xc, bc, cum, pre_step, de, dxc, dcq, dbq, rows, cols, decay, dtp, spread,
+        act_o, ddt_o, small_o,
+        start, factor,
+    ) = refs[packet_count:]
     step_id = pl.program_id(0)
     block = pl.num_programs(0) - 1 - step_id
     place = Place(info, counts)
     inner = heads * HEAD
-    channels = inner + 2 * LANES
-    width = tok.shape[1]
 
     @pl.when(step_id == 0)
     def _():
         start[...] = merge_packets([packet[...] for packet in packets], inner)
         factor[...] = jnp.ones_like(factor)
-        acc[...] = jnp.zeros_like(acc)
-        grad_ext[...] = jnp.zeros_like(grad_ext)
         small_o[...] = jnp.zeros_like(small_o)
 
     here = decay[0, 0:1, :]
@@ -586,9 +592,10 @@
     end_weight = end_kernel * step
     end_wide = expand(end_weight, spread)
     spread_b = dot_nt(bq, low)
-    grad_x = dxc[...] + end_wide * spread_b
+    act_o[:, :inner] = dxc[...] + end_wide * spread_b
     grad_end = reduce_heads(x_float * spread_b, spread)
-    grad_b = dbq[...] + dot((x_float * end_wide).astype(BF16), low)
+    act_o[:, inner : inner + LANES] = dbq[...] + dot((x_float * end_wide).astype(BF16), low)
+    act_o[:, inner + LANES :] = dcq[...]
     end_part = grad_end * end_weight
     last = iota((BLOCK, LANES), 0) == BLOCK - 1
     grad_cum = rows[...] - cols[...] * step - end_part + de[...] * enter_weights(place, block, cums)
@@ -601,8 +608,27 @@
     grad_step = cols[...] + grad_end * end_kernel - rates * grad_log
     heads_lane = iota((BLOCK, LANES), 1) < heads
     grad_pre_dt = jnp.where(heads_lane, grad_step * sigmoid(pre_dt), 0.0) * valid
-    small_o[6:7, :LANES] += jnp.sum(grad_pre_dt, axis=0, keepdims=True)
-    small_o[7:8, :LANES] += jnp.sum(grad_log * (-rates * step), axis=0, keepdims=True)
+    ddt_o[...] = grad_pre_dt.astype(BF16)
+    small_o[0:1, :] += jnp.sum(grad_pre_dt, axis=0, keepdims=True)
+    small_o[1:2, :] += jnp.sum(grad_log * (-rates * step), axis=0, keepdims=True)
+
+
+def conv_back_kernel(counts, heads, dp_count, part_count, info, *refs):
+    act, ddt, v, v_tail, halo_v, halo_normed, normed, small_gate, small_state, par, spread = refs[:11]
+    packed_o, back_o = refs[11:13]
+    parts = refs[13 : 13 + part_count]
+    ext, grad_ext, acc, small_o = refs[13 + part_count :]
+    step_id = pl.program_id(0)
+    block = pl.num_programs(0) - 1 - step_id
+    place = Place(info, counts)
+    inner = heads * HEAD
+    channels = inner + 2 * LANES
+
+    @pl.when(step_id == 0)
+    def _():
+        acc[...] = jnp.zeros_like(acc)
+        grad_ext[...] = jnp.zeros_like(grad_ext)
+        small_o[...] = jnp.zeros_like(small_o)
 
     ext[8 : 8 + BLOCK, :] = v[...].astype(F32)
 
@@ -617,35 +643,60 @@
     pre = conv_pre(place, block, ext, par, channels)
     sig = sigmoid(pre)
     slope = sig * (1.0 + pre * (1.0 - sig))
-    grad_pre = jnp.concatenate([grad_x, grad_b, dcq[...]], axis=1) * slope
+    grad_pre = act[...] * slope
     small_o[4:5, :] += jnp.sum(grad_pre, axis=0, keepdims=True)
     carry = grad_ext[0:8, :]
-    grad_ext[0 : BLOCK, :] = jnp.zeros((BLOCK, channels), F32)
+    grad_ext[0:BLOCK, :] = jnp.zeros((BLOCK, channels), F32)
     grad_ext[BLOCK : BLOCK + 8, :] = carry
     for tap in range(CONV):
         first = 8 - (CONV - 1) + tap
         masked = grad_pre * same_mask(place, block, tap)
         small_o[tap : tap + 1, :] += jnp.sum(masked * ext[first : first + BLOCK, :], axis=0, keepdims=True)
         grad_ext[first : first + BLOCK, :] += par[tap : tap + 1, :channels] * masked
-    packed = jnp.concatenate([grad_ext[8 : 8 + BLOCK, :].astype(BF16), grad_pre_dt.astype(BF16)], axis=1)
-    partial = dnz[...] + dot_nt(packed, w1[...])
-    dn_o[...] = partial.astype(BF16)
+    packed = jnp.concatenate([grad_ext[8 : 8 + BLOCK, :].astype(BF16), ddt[...]], axis=1)
+    packed_o[...] = packed
     acc[...] += dot_tn(normed[...], packed)
-    gain = par[5:6, :width]
-    scaled, _, _ = normalise(tok[...].astype(F32), gain)
-    small_o[5:6, :width] += jnp.sum(partial * scaled, axis=0, keepdims=True)
 
     @pl.when(block == 0)
     def _():
         back = jnp.concatenate([jnp.zeros((8, channels), F32), grad_ext[0:8, :]], axis=0).astype(BF16)
-        halo_grad = dot_nt(back, w1[:, :channels])
-        dnh_o[...] = halo_grad[8:16, :]
-        halo_scaled, _, _ = normalise(halo[...].astype(F32), gain)
-        small_o[5:6, :width] += jnp.sum(halo_grad * halo_scaled, axis=0, keepdims=True)
+        back_o[...] = back
         acc[:, :channels] += dot_tn(halo_normed[...], back)
+        small_o[6:7, :LANES] = small_state[0:1, :]
+        small_o[7:8, :LANES] = small_state[1:2, :]
         skip = reduce_heads(jnp.broadcast_to(small_gate[1:2, :], (8, inner)), spread)[0:1, :]
         acc[:, channels:] += pack_parameters(dp_count, heads, small_o, small_gate[0:1, :], skip)
         cut_pieces(place, dp_count, acc, parts, slice(0, channels + LANES))
+
+
+def input_back_kernel(
+    counts, dp_count, part_count, info, packed, back, dnz, tok, halo, w1, par,
+    dn_o, dnh_o, norm_o, total,
+):
+    block = pl.program_id(0)
+    place = Place(info, counts)
+    width = tok.shape[1]
+    channels = back.shape[1]
+    gain = par[5:6, :width]
+
+    @pl.when(block == 0)
+    def _():
+        halo_grad = dot_nt(back[...], w1[:, :channels])
+        dnh_o[...] = halo_grad[8:16, :]
+        halo_scaled, _, _ = normalise(halo[...].astype(F32), gain)
+        total[...] = jnp.broadcast_to(
+            jnp.sum(halo_grad * halo_scaled, axis=0, keepdims=True), total.shape
+        )
+
+    partial = dnz[...] + dot_nt(packed[...], w1[...])
+    dn_o[...] = partial.astype(BF16)
+    scaled, _, _ = normalise(tok[...].astype(F32), gain)
+    total[0:1, :] += jnp.sum(partial * scaled, axis=0, keepdims=True)
+
+    @pl.when(block == pl.num_programs(0) - 1)
+    def _():
+        rows = norm_o.shape[0] // dp_count
+        norm_o[...] = pack_norm(place, dp_count, part_count, total[0:1, :], rows)
 
 
 def finish_kernel(counts, info, own, other, halo_a, halo_b, tok, cot, par, grad_o):
@@ -708,7 +759,16 @@
         taps_o[:, tap, :] = by_head(TAPS + tap)
     bias_o[...] = by_head(TAPS + CONV)
     gate_o[...] = by_head(GATE)
-    norm_o[...] = lines[NORM : NORM + 1, :shard]
+    gain = wide[:rows, channels:]
+    for part in range(1, part_count):
+        gain = gain + wide[part * rows : (part + 1) * rows, channels:]
+    gain = jnp.concatenate([gain, jnp.zeros((LANES - rows, LANES), F32)], axis=0).T
+    source, target = iota((LANES, size), 0), iota((LANES, size), 1)
+    total = jnp.zeros((8, size), F32)
+    for lane in range(shard // rows):
+        pick = ((target == lane * rows + source) & (source < rows)).astype(F32)
+        total = total + dot_exact(jnp.broadcast_to(gain[NORM + lane : NORM + lane + 1, :], (8, LANES)), pick)
+    norm_o[...] = total[0:1, :shard]
     states = state_bias_o.shape[1]
     state_taps_o[...] = lines[STATE_TAPS : STATE_TAPS + CONV, :states]
     state_bias_o[...] = lines[STATE_TAPS + CONV : STATE_TAPS + CONV + 1, :states]
@@ -771,29 +831,33 @@
     return [value] + [partnered(value, axis, mask) for mask in range(1, lax.axis_size(axis))]
 
 
-def gather_rows(value, parts):
-    if parts == 1:
-        return [lax.all_gather(value, "dp", axis=0, tiled=True)], ()
-    rows = value.shape[0] // parts
-    own = lax.dynamic_slice_in_dim(value, lax.axis_index("ctx") * rows, rows, 0)
-    joined = jnp.concatenate(exchanged(own, "dp"), axis=0)
-    return exchanged(joined, "ctx"), joined
-
-
-def reduce_rows(pieces):
-    if len(pieces) == 1:
-        own = lax.psum_scatter(pieces[0], "dp", scatter_dimension=0, tiled=True)
-        return lax.psum(own, "ctx")
-    dp_count = lax.axis_size("dp")
-    rows = pieces[0].shape[0] // dp_count
+def own_rows(value, rows):
+    return lax.dynamic_slice_in_dim(value, lax.axis_index("ctx") * rows, rows, 0)
+
+
+def joined_rows(values):
+    return jnp.concatenate(values, axis=0)
+
+
+def ctx_sum(pieces):
     total = pieces[0].astype(F32)
     for mask in range(1, len(pieces)):
         total = total + partnered(pieces[mask], "ctx", mask).astype(F32)
-    own = total[:rows]
+    return total
+
+
+def dp_sum(total):
+    dp_count = lax.axis_size("dp")
+    rows = total.shape[0] // dp_count
+    own = total[:rows].astype(F32)
     for mask in range(1, dp_count):
         block = total[mask * rows : (mask + 1) * rows].astype(BF16)
         own = own + partnered(block, "dp", mask).astype(F32)
     return own.astype(BF16)
+
+
+def whole_sum(value):
+    return lax.psum(lax.psum_scatter(value, "dp", scatter_dimension=0, tiled=True), "ctx")
 
 
 def body(
@@ -815,26 +879,42 @@
     part_rows = shard // parts
 
     with jax.named_scope("gather_weights"):
-        w1_parts, arrived = gather_rows(jnp.concatenate([w_x, w_bc], axis=1), parts)
         vector = jnp.concatenate(
             [
-                conv_x.reshape(CONV, shard),
-                conv_x_bias.reshape(1, shard),
-                norm_gain[None, :],
-                gate_gain.reshape(1, shard),
-                jnp.zeros((1, shard), BF16),
-                jnp.pad(
-                    jnp.concatenate([conv_bc, bias_bc[None, :]], axis=0),
-                    ((0, 3), (0, shard - bias_bc.shape[0])),
+                jnp.concatenate(
+                    [
+                        conv_x.reshape(CONV, shard),
+                        conv_x_bias.reshape(1, shard),
+                        norm_gain[None, :],
+                        gate_gain.reshape(1, shard),
+                        jnp.zeros((1, shard), BF16),
+                        jnp.pad(
+                            jnp.concatenate([conv_bc, bias_bc[None, :]], axis=0),
+                            ((0, 3), (0, shard - bias_bc.shape[0])),
+                        ),
+                    ],
+                    axis=0,
                 ),
                 jnp.pad(w_dt.T, ((0, 16 - heads), (0, 0))),
             ],
-            axis=0,
+            axis=1,
         )
-        vectors = exchanged(vector, "dp")
-        shard2 = jnp.concatenate([w_z, w_out.T], axis=1)
-        shard2, _ = lax.optimization_barrier((shard2, arrived))
-        w2_shards = exchanged(shard2, "dp")
+        input_rows = jnp.concatenate([w_x, w_bc], axis=1)
+        gate_rows = jnp.concatenate([w_z, w_out.T], axis=1)
+        if parts > 1:
+            w1_parts = joined_rows(exchanged(own_rows(input_rows, part_rows), "dp"))
+            vector = jnp.pad(vector, ((0, 0), (0, 2 * inner - 2 * shard)))
+            block = jnp.concatenate([own_rows(gate_rows, part_rows), vector], axis=0)
+            block, _ = lax.optimization_barrier((block, w1_parts))
+            vectors = exchanged(block, "dp")
+            w2_parts = exchanged(joined_rows([value[:part_rows] for value in vectors]), "ctx")
+            w1_parts = exchanged(w1_parts, "ctx")
+        else:
+            w1_parts = [lax.all_gather(input_rows, "dp", axis=0, tiled=True)]
+            w2_parts = [lax.all_gather(gate_rows, "dp", axis=0, tiled=True)]
+            vectors = exchanged(vector, "dp")
+    first_vector = part_rows // 16 if parts > 1 else 0
+    vector_spec = pl.BlockSpec((16, 2 * shard), lambda i: (first_vector, 0))
 
     dtp = jnp.pad(jnp.stack([dt_bias, jnp.exp(a_log), skip_d]), ((0, 5), (0, LANES - heads)))
     shape = (2 * LANES, inner)
@@ -862,7 +942,8 @@
         functools.partial(forward_kernel, counts, heads, dp_count, parts),
         steps,
         info,
-        [(value, "whole") for value in vectors + w1_parts]
+        [(value, vector_spec) for value in vectors]
+        + [(value, "whole") for value in w1_parts]
         + [(tokens, "rows"), (halo, "whole"), (dtp, "whole"), (spread, "whole")],
         [
             out((width, channels + LANES), BF16, "whole"),
@@ -891,10 +972,10 @@
     wz_spec = pl.BlockSpec((width, inner), lambda i: (0, 0))
     wo_spec = pl.BlockSpec((width, inner), lambda i: (0, 1))
     w2, z, dn = call(
-        functools.partial(gate_matmul_kernel, counts, dp_count),
+        functools.partial(gate_matmul_kernel, counts, dp_count, parts),
         steps,
         info,
-        [(value, "whole") for value in w2_shards] + [(normed, "rows"), (cotangent, "rows")],
+        [(value, "whole") for value in w2_parts] + [(normed, "rows"), (cotangent, "rows")],
         [out((width, 2 * inner), BF16, "whole"), row_out(inner, BF16), row_out(inner, F32)],
         micros=7,
     )
@@ -1001,10 +1082,9 @@
         micros=18,
     )
     with jax.named_scope("reduce_gate_weights"):
-        total2 = reduce_rows(g2)
-        total2 = exchanged(total2, "ctx") if parts > 1 else [total2]
-    partial, halo_grad, *g1 = call(
-        functools.partial(state_back_kernel, counts, heads, dp_count, len(packets), parts),
+        total2 = ctx_sum(g2) if parts > 1 else g2[0]
+    grad_act, ddt, small_state = call(
+        functools.partial(state_back_kernel, counts, heads, len(packets)),
         steps,
         info,
         packets
@@ -1022,35 +1102,68 @@
             (row_sums, "rows"),
             (col_sums, "rows"),
             (decay, "block"),
+            (dtp, "whole"),
+            (spread, "whole"),
+        ],
+        [row_out(channels, F32), row_out(LANES, BF16), out((8, LANES), F32, "whole")],
+        [pltpu.VMEM((inner, LANES), F32), pltpu.VMEM((8, LANES), F32)],
+        reverse=True,
+        micros=11,
+    )
+    with jax.named_scope("reduce_gate_weights"):
+        if parts > 1:
+            total2 = dp_sum(total2)
+        else:
+            total2 = whole_sum(total2)
+    packed, back, *g1 = call(
+        functools.partial(conv_back_kernel, counts, heads, dp_count, parts),
+        steps,
+        info,
+        [
+            (grad_act, "rows"),
+            (ddt, "rows"),
             (v, "rows"),
             (v, "tail"),
             (halo_v, "whole"),
             (halo_normed, "whole"),
-            (halo, "whole"),
-            (tokens, "rows"),
             (normed, "rows"),
-            (dnz, "rows"),
             (small_gate, "whole"),
-            (w1, "whole"),
+            (small_state, "whole"),
             (par, "whole"),
-            (dtp, "whole"),
             (spread, "whole"),
         ],
-        [
-            row_out(width, BF16),
-            out((8, width), F32, "whole"),
-        ]
+        [row_out(channels + LANES, BF16), out((16, channels), BF16, "whole")]
         + [out((width // parts, channels + LANES), BF16, "whole")] * parts,
         [
-            pltpu.VMEM((inner, LANES), F32),
-            pltpu.VMEM((8, LANES), F32),
             pltpu.VMEM((8 + BLOCK, channels), F32),
             pltpu.VMEM((8 + BLOCK, channels), F32),
             pltpu.VMEM((width, channels + LANES), F32),
             pltpu.VMEM((8, channels), F32),
         ],
         reverse=True,
-        micros=28,
+        micros=18,
+    )
+    norm_rows = part_rows * dp_count
+    partial, halo_grad, norm_part = call(
+        functools.partial(input_back_kernel, counts, dp_count, parts),
+        steps,
+        info,
+        [
+            (packed, "rows"),
+            (back, "whole"),
+            (dnz, "rows"),
+            (tokens, "rows"),
+            (halo, "whole"),
+            (w1, "whole"),
+            (par, "whole"),
+        ],
+        [
+            row_out(width, BF16),
+            out((8, width), F32, "whole"),
+            out((norm_rows, LANES), F32, "whole"),
+        ],
+        [pltpu.VMEM((8, width), F32)],
+        micros=5,
     )
     other = swapped(partial)
     size = ctx_count * 2
@@ -1059,13 +1172,17 @@
     halo_a = lax.ppermute(halo_grad, ("ctx", "tp"), back)
     halo_b = lax.ppermute(halo_grad, ("ctx", "tp"), cross)
     with jax.named_scope("reduce_input_weights"):
-        total1 = reduce_rows(g1)
+        norm_part = jnp.pad(norm_part, ((0, 0), (channels, 0)))
+        if parts > 1:
+            total1 = dp_sum(ctx_sum(g1) + norm_part)
+        else:
+            total1 = whole_sum((g1[0].astype(F32) + norm_part).astype(BF16))
         across = swapped(total1[:, inner:])
         lane = jnp.arange(3 * LANES) - 2 * LANES
-        both = (lane < 0) | (lane == NORM) | ((lane >= STATE_TAPS) & (lane < BY_HEAD))
+        both = (lane < 0) | ((lane >= STATE_TAPS) & (lane < BY_HEAD))
+        both = both | ((lane >= NORM) & (lane < NORM + shard // part_rows))
         summed = total1[:, inner:] + jnp.where(both[None, :], across, 0)
         total1 = jnp.concatenate([total1[:, :inner], summed], axis=1)
-        total1 = exchanged(total1, "ctx") if parts > 1 else [total1]
     (grad_tokens,) = call(
         functools.partial(finish_kernel, counts),
         steps,
@@ -1082,6 +1199,13 @@
         [row_out(width, F32)],
         micros=5,
     )
+    with jax.named_scope("last_hop"):
+        if parts > 1:
+            total2 = exchanged(total2, "ctx")
+            total1, grad_tokens = lax.optimization_barrier((total1, grad_tokens))
+            total1 = exchanged(total1, "ctx")
+        else:
+            total1, total2 = [total1], [total2]
     each = HEAD // dp_count
     part_bc = bias_bc.shape[0]
     tall = -(-shard // LANES) * LANES

time: 260 us -> 255 us (0.981)
  starting transfers between devices: 80.2 us -> 63.2 us
  Pallas kernels: 110 us -> 119 us
    ppermute x30, starting transfers between devices: 60.7 us -> 43.4 us  [partnered(): lax.ppermute(value, axis, [(one, one ^ mask) for one in range(lax.axis_si...]
    pallas_call x9 -> x11, Pallas kernels: 110 us -> 119 us  [call(): pl.pallas_call(body, grid=(steps,), in_specs=[pl.BlockSpec(memory_space=p...]
    ppermute x30, waiting for transfers between devices: 33.9 us -> 42 us  [partnered(): lax.ppermute(value, axis, [(one, one ^ mask) for one in range(lax.axis_si...]
    ppermute x7, waiting for transfers between devices: 6.99 us -> 1.33 us  [shifted(): lax.ppermute(value, axis, [(source, source + steps) for source in range(f...]
    ppermute x3, starting transfers between devices: 0.19 us -> 2.86 us  [swapped(): return lax.ppermute(value, 'tp', [(0, 1), (1, 0)])]
    unnamed x81 -> x89, local copies, waits for them, and re-layouts: 7.13 us -> 8.44 us
  transfers between devices with their start and end apart: 42 -> 42, of which waited for: 10 -> 8; matrix products, arithmetic and copies ran while one was open for 5% -> 5% of each run, Pallas kernels for 31% -> 37%
where the time goes in v4:
time: 255 us; the launch traced here: 253 us
  Pallas kernels  119 us (47%)
  starting transfers between devices  63.2 us (25%)
  waiting for transfers between devices  43.3 us (17%)
  local copies, waits for them, and re-layouts  13 us (5%)
  other arithmetic  8.46 us (3%)
  blocking collectives  4.65 us (2%)
    pallas_call x11, Pallas kernels, call(): pl.pallas_call(body, grid=(steps,), in_specs=[pl.BlockSpec(memory_space=p...  119 us
    ppermute x30, starting transfers between devices, partnered(): lax.ppermute(value, axis, [(one, one ^ mask) for one in range(lax.axis_si...  43.4 us
    ppermute x30, waiting for transfers between devices, partnered(): lax.ppermute(value, axis, [(one, one ^ mask) for one in range(lax.axis_si...  42 us
    ppermute x7, starting transfers between devices, shifted(): lax.ppermute(value, axis, [(source, source + steps) for source in range(f...  14.3 us
    unnamed x89, local copies, waits for them, and re-layouts  8.44 us
  transfers between devices with their start and end apart: 42, of which 8 were waited for; matrix products, arithmetic and copies ran while one was open for 5% of the time, Pallas kernels for 37%

profile of v4, /device:TPU:0, one launch (start us, length us, event | category | flops | bytes accessed | tf_op | source)
XLA Modules:
  0.0 253.4 jit_solution(11675371467321554135)
XLA Ops:
  1.6 3.1 %collective-permute-start = (bf16[48,1024]{1,0:T(8,128)(2,1)S(1)}, bf16[48,1024]{1,0:T(8,128)(2,1)S(1)}, u32[]{:S(2)}, u32[]{:S(2)}) collective-permute-start(bf16[48,1024]{1,0:T(8,128)(2,1)S(1)} %fusion.10), channel_id=1, source_target_pairs={{0,8},{8,0},{16,24},{24,16},{1,9},{9,1},{17,25},{25,17},{2,10},{10... | collective-permute-start | bytes 294920 | tf_op jit(solution)/shard_map/gather_weights/ppermute | solution.py:827
  4.7 2.6 %collective-permute-start.1 = (bf16[48,1024]{1,0:T(8,128)(2,1)S(1)}, bf16[48,1024]{1,0:T(8,128)(2,1)S(1)}, u32[]{:S(2)}, u32[]{:S(2)}) collective-permute-start(bf16[48,1024]{1,0:T(8,128)(2,1)S(1)} %fusion.10), channel_id=1, source_target_pairs={{0,16},{8,24},{16,0},{24,8},{1,17},{9,25},{17,1},{25,9},{2,18},{10... | collective-permute-start | bytes 294920 | tf_op jit(solution)/shard_map/gather_weights/ppermute | solution.py:827
  18.0 3.5 %collective-permute-start.4 = (bf16[64,1536]{1,0:T(8,128)(2,1)S(1)}, bf16[64,1536]{1,0:T(8,128)(2,1)S(1)}, u32[]{:S(2)}, u32[]{:S(2)}) collective-permute-start(bf16[64,1536]{1,0:T(8,128)(2,1)S(1)} %fusion.8.refs_0_), channel_id=1, source_target_pairs={{0,16},{8,24},{16,0},{24,8},{1,17},{9,25},{17,1},{25,9},{2,18},{10... | collective-permute-start | bytes 589832 | tf_op jit(solution)/shard_map/gather_weights/ppermute | solution.py:827
  28.6 6.8 %collective-permute-done.4.refs_2_ = bf16[64,1536]{1,0:T(8,128)(2,1)S(1)} collective-permute-done((bf16[64,1536]{1,0:T(8,128)(2,1)S(1)}, bf16[64,1536]{1,0:T(8,128)(2,1)S(1)}, u32[]{:S(2)}, u32[]{:S(2)}) %collective-permute-start.4) | collective-permute-done | bytes 196640 | tf_op jit(solution)/shard_map/gather_weights/ppermute | solution.py:827
  35.4 3.4 %collective-permute-start.9 = (bf16[16,768]{1,0:T(8,128)(2,1)S(1)}, bf16[16,768]{1,0:T(8,128)(2,1)S(1)}, u32[]{:S(2)}, u32[]{:S(2)}) collective-permute-start(bf16[16,768]{1,0:T(8,128)(2,1)S(1)} %constant_dynamic-slice_fusion), channel_id=1, source_target_pairs={{0,2},{2,4},{4,6},{1,3},{3,5},{5,7},{8,10},{10,12},{12,14},{9,11},... | collective-permute-start | bytes 73736 | tf_op jit(solution)/shard_map/ppermute | solution.py:819
  47.3 20.8 %shard_map.297 = (bf16[768,1152]{1,0:T(8,128)(2,1)}, f32[8,1024]{1,0:T(8,128)}, bf16[1024,768]{1,0:T(8,128)(2,1)}, bf16[16,768]{1,0:T(8,128)(2,1)}, f32[8,1024]{...) custom-call(s32[10]{0:T(128)} %concatenate.30.info, ...), custom_call_target="tpu_custom_call" | custom-call | flops 22000001024 | bytes 70000000 | tf_op jit(solution)/shard_map/pallas_call | solution.py:799
  70.2 3.6 %collective-permute-start.11 = (bf16[784,128]{1,0:T(8,128)(2,1)}, bf16[784,128]{1,0:T(8,128)(2,1)S(1)}, u32[]{:S(2)}, u32[]{:S(2)}) collective-permute-start(bf16[784,128]{1,0:T(8,128)(2,1)} %get-tuple-element.86), channel_id=1, source_target_pairs={{0,4},{2,6},{1,5},{3,7},{8,12},{10,14},{9,13},{11,15},{16,20},{18,... | collective-permute-start | bytes 602120 | tf_op jit(solution)/shard_map/ppermute | solution.py:819
  76.1 7.3 %shard_map.298 = (bf16[768,1536]{1,0:T(8,128)(2,1)}, bf16[1024,768]{1,0:T(8,128)(2,1)}, f32[1024,768]{1,0:T(8,128)}) custom-call(s32[10]{0:T(128)} %concatenate.30.info, bf16[192,1536]{1,0:T(8,128)(2,1)} %copy-done.2, bf16[192,1536]{1,0:T(8,128)(2,1)} %copy-done.19, bf16[192,1536]{1,0:T(8,128)(2,1)} %copy-done.20, bf16[192,1536]{1,0:T(8,128)(2,1)} %copy-done.21, ...), custom_call_target="tpu_custom_call" | custom-call | flops 7699999744 | bytes 24500000 | tf_op jit(solution)/shard_map/pallas_call | solution.py:799
  84.3 8.6 %shard_map.299 = (f32[1024,768]{1,0:T(8,128)}, bf16[4,768,128]{2,1,0:T(8,128)(2,1)}, f32[4,768,128]{2,1,0:T(8,128)}, f32[8,1024]{1,0:T(8,128)}) custom-call(s32[10]{0:T(128)} %concatenate.30.info, bf16[784,128]{1,0:T(8,128)(2,1)} %copy-done.31, bf16[784,128]{1,0:T(8,128)(2,1)} %copy-done.32, bf16[784,128]{1,0:T(8,128)(2,1)} %copy-done.33, ...), custom_call_target="tpu_custom_call" | custom-call | flops 8800000000 | bytes 28000000 | tf_op jit(solution)/shard_map/pallas_call | solution.py:799
  92.9 4.6 %psum.7.stat = f32[8,1024]{1,0:T(8,128)} all-reduce(f32[8,1024]{1,0:T(8,128)} %get-tuple-element.96), channel_id=1, replica_groups=mesh['dp'=4,'ctx'=4,'tp'=2] {'tp'}, use_global_device_ids=true, to_apply=%region_1.2 | all-reduce | flops 8192 | bytes 65536 | tf_op jit(solution)/shard_map/psum | solution.py:1007
  97.5 15.1 %shard_map.300 = (bf16[1024,384]{1,0:T(8,128)(2,1)}, bf16[1024,384]{1,0:T(8,128)(2,1)}, bf16[768,768]{1,0:T(8,128)(2,1)}, f32[8,768]{1,0:T(8,128)}, bf16[1024,76...) custom-call(s32[10]{0:T(128)} %concatenate.30.info, ...), custom_call_target="tpu_custom_call" | custom-call | flops 16499999744 | bytes 52500000 | tf_op jit(solution)/shard_map/pallas_call | solution.py:799
  116.8 18.8 %shard_map.301 = (f32[1024,768]{1,0:T(8,128)}, f32[1024,128]{1,0:T(8,128)}, f32[1024,128]{1,0:T(8,128)}, f32[1024,128]{1,0:T(8,128)}, f32[1024,128]{1,0:T(8,128)...) custom-call(s32[10]{0:T(128)} %concatenate.30.info, ...), custom_call_target="tpu_custom_call" | custom-call | flops 19800000512 | bytes 63000000 | tf_op jit(solution)/shard_map/pallas_call | solution.py:799
  137.7 3.3 %collective-permute-start.34 = (bf16[192,1536]{1,0:T(8,128)(2,1)}, bf16[192,1536]{1,0:T(8,128)(2,1)S(1)}, u32[]{:S(2)}, u32[]{:S(2)}) collective-permute-start(bf16[192,1536]{1,0:T(8,128)(2,1)} %get-tuple-element.139), channel_id=1, source_target_pairs={{0,4},{2,6},{4,0},{6,2},{1,5},{3,7},{5,1},{7,3},{8,12},{10,14},{12... | collective-permute-start | bytes 1769480 | tf_op jit(solution)/shard_map/reduce_gate_weights/ppermute | solution.py:827
  141.8 10.7 %shard_map.302 = (f32[1024,1024]{1,0:T(8,128)}, bf16[1024,128]{1,0:T(8,128)(2,1)}, f32[8,128]{1,0:T(8,128)}) custom-call(s32[10]{0:T(128)} %concatenate.30.info, bf16[784,128]{1,0:T(8,128)(2,1)} %copy-done.28, bf16[784,128]{1,0:T(8,128)(2,1)} %copy-done.29, bf16[784,128]{1,0:T(8,128)(2,1)} %copy-done.30, f32[4,768,128]{2,1,0:T(8,128)} %get-tuple-element.104.refs_3_, ...), custom_call_target="tpu_custom_call" | custom-call | flops 12099999744 | bytes 38500000 | tf_op jit(solution)/shard_map/pallas_call | solution.py:799
  152.5 18.5 %shard_map.303 = (bf16[1024,1152]{1,0:T(8,128)(2,1)}, bf16[16,1024]{1,0:T(8,128)(2,1)}, bf16[192,1152]{1,0:T(8,128)(2,1)}, bf16[192,1152]{1,0:T(8,128)(2,1)}, bf...) custom-call(s32[10]{0:T(128)} %concatenate.30.info, f32[1024,1024]{1,0:T(8,128)} %get-tuple-element.116.refs_0_, ...), custom_call_target="tpu_custom_call" | custom-call | flops 19800000512 | bytes 63000000 | tf_op jit(solution)/shard_map/pallas_call | solution.py:799
  171.1 8.5 %shard_map.304 = (bf16[1024,768]{1,0:T(8,128)(2,1)}, f32[8,768]{1,0:T(8,128)}, f32[192,128]{1,0:T(8,128)}) custom-call(s32[10]{0:T(128)} %concatenate.30.info, bf16[1024,1152]{1,0:T(8,128)(2,1)} %get-tuple-element.127.packed, bf16[16,1024]{1,0:T(8,128)(2,1)} %get-tuple-element.128.back, f32[1024,768]{1,0:T(8,128)} %get-tuple-element.129.dnz, ...), custom_call_target="tpu_custom_call" | custom-call | flops 5500000256 | bytes 17500000 | tf_op jit(solution)/shard_map/pallas_call | solution.py:799
  183.9 9.2 %collective-permute-done.20 = bf16[192,1152]{1,0:T(8,128)(2,1)S(1)} collective-permute-done((bf16[192,1152]{1,0:T(8,128)(2,1)S(1)}, bf16[192,1152]{1,0:T(8,128)(2,1)S(1)}, u32[]{:S(2)}, u32[]{:S(2)}) %collective-permute-start.20) | collective-permute-done | bytes 442400 | tf_op jit(solution)/shard_map/reduce_input_weights/ppermute | solution.py:827
  193.1 10.1 %collective-permute-done.21 = bf16[192,1152]{1,0:T(8,128)(2,1)S(1)} collective-permute-done((bf16[192,1152]{1,0:T(8,128)(2,1)S(1)}, bf16[192,1152]{1,0:T(8,128)(2,1)S(1)}, u32[]{:S(2)}, u32[]{:S(2)}) %collective-permute-start.21) | collective-permute-done | bytes 442400 | tf_op jit(solution)/shard_map/reduce_input_weights/ppermute | solution.py:827
  203.2 3.5 %collective-permute-start.38 = (bf16[48,1536]{1,0:T(8,128)(2,1)S(1)}, bf16[48,1536]{1,0:T(8,128)(2,1)S(1)}, u32[]{:S(2)}, u32[]{:S(2)}) collective-permute-start(bf16[48,1536]{1,0:T(8,128)(2,1)S(1)} %get-tuple-element.159), channel_id=1, source_target_pairs={{0,24},{8,16},{16,8},{24,0},{1,25},{9,17},{17,9},{25,1},{2,26},{10... | collective-permute-start | bytes 442376 | tf_op jit(solution)/shard_map/reduce_gate_weights/ppermute | solution.py:827
  207.6 7.6 %collective-permute-done.37 = bf16[48,1536]{1,0:T(8,128)(2,1)S(1)} collective-permute-done((bf16[48,1536]{1,0:T(8,128)(2,1)S(1)}, bf16[48,1536]{1,0:T(8,128)(2,1)S(1)}, u32[]{:S(2)}, u32[]{:S(2)}) %collective-permute-start.37) | collective-permute-done | bytes 147488 | tf_op jit(solution)/shard_map/reduce_gate_weights/ppermute | solution.py:827
  215.3 2.7 %collective-permute-start.25 = (bf16[48,1152]{1,0:T(8,128)(2,1)S(1)}, bf16[48,1152]{1,0:T(8,128)(2,1)S(1)}, u32[]{:S(2)}, u32[]{:S(2)}) collective-permute-start(bf16[48,1152]{1,0:T(8,128)(2,1)S(1)} %get-tuple-element.162), channel_id=1, source_target_pairs={{0,24},{8,16},{16,8},{24,0},{1,25},{9,17},{17,9},{25,1},{2,26},{10... | collective-permute-start | bytes 331784 | tf_op jit(solution)/shard_map/reduce_input_weights/ppermute | solution.py:827
  219.3 6.2 %collective-permute-done.24 = bf16[48,1152]{1,0:T(8,128)(2,1)S(1)} collective-permute-done((bf16[48,1152]{1,0:T(8,128)(2,1)S(1)}, bf16[48,1152]{1,0:T(8,128)(2,1)S(1)}, u32[]{:S(2)}, u32[]{:S(2)}) %collective-permute-start.24) | collective-permute-done | bytes 110624 | tf_op jit(solution)/shard_map/reduce_input_weights/ppermute | solution.py:827
  231.1 2.6 %collective-permute-start.40 = (bf16[48,1536]{1,0:T(8,128)(2,1)S(1)}, bf16[48,1536]{1,0:T(8,128)(2,1)S(1)}, u32[]{:S(2)}, u32[]{:S(2)}) collective-permute-start(bf16[48,1536]{1,0:T(8,128)(2,1)S(1)} %fusion.4.refs_0_), channel_id=1, source_target_pairs={{0,4},{2,6},{4,0},{6,2},{1,5},{3,7},{5,1},{7,3},{8,12},{10,14},{12... | collective-permute-start | bytes 442376 | tf_op jit(solution)/shard_map/last_hop/ppermute | solution.py:827
  235.6 5.6 %shard_map.305 = f32[1024,768]{1,0:T(8,128)} custom-call(s32[10]{0:T(128)} %concatenate.30.info, bf16[1024,768]{1,0:T(8,128)(2,1)} %get-tuple-element.132.own, bf16[1024,768]{1,0:T(8,128)(2,1)} %copy-done.17, f32[8,768]{1,0:T(8,128)} %copy-done.42, f32[8,768]{1,0:T(8,128)} %copy-done.43, bf16[1024,768]{1,0:T(8,128)(2,1)} %tok.3, bf16[1024,768]{1,0:T(8,128)(2,1)} %cot.3, ...), custom_call_target="tpu_custom_call" | custom-call | flops 5500000256 | bytes 17500000 | tf_op jit(solution)/shard_map/pallas_call | solution.py:799
  (201 shorter events, 64.5 us)
Async XLA Ops:
  1.6 14.5 %collective-permute-start = (bf16[48,1024]{1,0:T(8,128)(2,1)S(1)}, bf16[48,1024]{1,0:T(8,128)(2,1)S(1)}, u32[]{:S(2)}, u32[]{:S(2)}) collective-permute-start(bf16[48,1024]{1,0:T(8,128)(2,1)S(1)} %fusion.10), channel_id=1, source_target_pairs={{0,8},{8,0},{16,24},{24,16},{1,9},{9,1},{17,25},{25,17},{2,10},{10... | collective-permute-start | bytes 294920 | tf_op jit(solution)/shard_map/gather_weights/ppermute | solution.py:827
  18.0 17.4 %collective-permute-start.4 = (bf16[64,1536]{1,0:T(8,128)(2,1)S(1)}, bf16[64,1536]{1,0:T(8,128)(2,1)S(1)}, u32[]{:S(2)}, u32[]{:S(2)}) collective-permute-start(bf16[64,1536]{1,0:T(8,128)(2,1)S(1)} %fusion.8.refs_0_), channel_id=1, source_target_pairs={{0,16},{8,24},{16,0},{24,8},{1,17},{9,25},{17,1},{25,9},{2,18},{10... | collective-permute-start | bytes 589832 | tf_op jit(solution)/shard_map/gather_weights/ppermute | solution.py:827
  21.5 17.3 %collective-permute-start.5 = (bf16[64,1536]{1,0:T(8,128)(2,1)S(1)}, bf16[64,1536]{1,0:T(8,128)(2,1)S(1)}, u32[]{:S(2)}, u32[]{:S(2)}) collective-permute-start(bf16[64,1536]{1,0:T(8,128)(2,1)S(1)} %fusion.8.refs_0_), channel_id=1, source_target_pairs={{0,24},{8,16},{16,8},{24,0},{1,25},{9,17},{17,9},{25,1},{2,26},{10... | collective-permute-start | bytes 589832 | tf_op jit(solution)/shard_map/gather_weights/ppermute | solution.py:827
  21.5 22.5 %collective-permute-start.6 = (bf16[192,1024]{1,0:T(8,128)(2,1)S(1)}, bf16[192,1024]{1,0:T(8,128)(2,1)S(1)}, u32[]{:S(2)}, u32[]{:S(2)}) collective-permute-start(bf16[192,1024]{1,0:T(8,128)(2,1)S(1)} %pad_maximum_fusion.1.refs_4_), channel_id=1, source_target_pairs={{0,2},{2,0},{4,6},{6,4},{1,3},{3,1},{5,7},{7,5},{8,10},{10,8},{12,... | collective-permute-start | bytes 1179656 | tf_op jit(solution)/shard_map/gather_weights/ppermute | solution.py:827
  23.2 22.5 %collective-permute-start.7 = (bf16[192,1024]{1,0:T(8,128)(2,1)S(1)}, bf16[192,1024]{1,0:T(8,128)(2,1)S(1)}, u32[]{:S(2)}, u32[]{:S(2)}) collective-permute-start(bf16[192,1024]{1,0:T(8,128)(2,1)S(1)} %pad_maximum_fusion.1.refs_4_), channel_id=1, source_target_pairs={{0,4},{2,6},{4,0},{6,2},{1,5},{3,7},{5,1},{7,3},{8,12},{10,14},{12... | collective-permute-start | bytes 1179656 | tf_op jit(solution)/shard_map/gather_weights/ppermute | solution.py:827
  24.8 21.0 %collective-permute-start.8 = (bf16[192,1024]{1,0:T(8,128)(2,1)S(1)}, bf16[192,1024]{1,0:T(8,128)(2,1)S(1)}, u32[]{:S(2)}, u32[]{:S(2)}) collective-permute-start(bf16[192,1024]{1,0:T(8,128)(2,1)S(1)} %pad_maximum_fusion.1.refs_4_), channel_id=1, source_target_pairs={{0,6},{2,4},{4,2},{6,0},{1,7},{3,5},{5,3},{7,1},{8,14},{10,12},{12... | collective-permute-start | bytes 1179656 | tf_op jit(solution)/shard_map/gather_weights/ppermute | solution.py:827
  38.9 34.8 %collective-permute-start.13 = (bf16[192,1536]{1,0:T(8,128)(2,1)S(1)}, bf16[192,1536]{1,0:T(8,128)(2,1)S(1)}, u32[]{:S(2)}, u32[]{:S(2)}) collective-permute-start(bf16[192,1536]{1,0:T(8,128)(2,1)S(1)} %pad_maximum_fusion.refs_0_), channel_id=1, source_target_pairs={{0,2},{2,0},{4,6},{6,4},{1,3},{3,1},{5,7},{7,5},{8,10},{10,8},{12,... | collective-permute-start | bytes 1769480 | tf_op jit(solution)/shard_map/gather_weights/ppermute | solution.py:827
  41.8 33.3 %collective-permute-start.14 = (bf16[192,1536]{1,0:T(8,128)(2,1)S(1)}, bf16[192,1536]{1,0:T(8,128)(2,1)S(1)}, u32[]{:S(2)}, u32[]{:S(2)}) collective-permute-start(bf16[192,1536]{1,0:T(8,128)(2,1)S(1)} %pad_maximum_fusion.refs_0_), channel_id=1, source_target_pairs={{0,4},{2,6},{4,0},{6,2},{1,5},{3,7},{5,1},{7,3},{8,12},{10,14},{12... | collective-permute-start | bytes 1769480 | tf_op jit(solution)/shard_map/gather_weights/ppermute | solution.py:827
  44.1 31.1 %collective-permute-start.15 = (bf16[192,1536]{1,0:T(8,128)(2,1)S(1)}, bf16[192,1536]{1,0:T(8,128)(2,1)S(1)}, u32[]{:S(2)}, u32[]{:S(2)}) collective-permute-start(bf16[192,1536]{1,0:T(8,128)(2,1)S(1)} %pad_maximum_fusion.refs_0_), channel_id=1, source_target_pairs={{0,6},{2,4},{4,2},{6,0},{1,7},{3,5},{5,3},{7,1},{8,14},{10,12},{12... | collective-permute-start | bytes 1769480 | tf_op jit(solution)/shard_map/gather_weights/ppermute | solution.py:827
  68.1 15.3 %collective-permute-start.10 = (bf16[784,128]{1,0:T(8,128)(2,1)}, bf16[784,128]{1,0:T(8,128)(2,1)S(1)}, u32[]{:S(2)}, u32[]{:S(2)}) collective-permute-start(bf16[784,128]{1,0:T(8,128)(2,1)} %get-tuple-element.86), channel_id=1, source_target_pairs={{0,2},{2,4},{4,6},{1,3},{3,5},{5,7},{8,10},{10,12},{12,14},{9,11},... | collective-permute-start | bytes 602120 | tf_op jit(solution)/shard_map/ppermute | solution.py:819
  112.7 28.3 %collective-permute-start.17 = (bf16[784,128]{1,0:T(8,128)(2,1)}, bf16[784,128]{1,0:T(8,128)(2,1)S(1)}, u32[]{:S(2)}, u32[]{:S(2)}) collective-permute-start(bf16[784,128]{1,0:T(8,128)(2,1)} %get-tuple-element.103), channel_id=1, source_target_pairs={{2,0},{4,2},{6,4},{3,1},{5,3},{7,5},{10,8},{12,10},{14,12},{11,9},... | collective-permute-start | bytes 602120 | tf_op jit(solution)/shard_map/ppermute | solution.py:819
  114.0 27.0 %collective-permute-start.18 = (bf16[784,128]{1,0:T(8,128)(2,1)}, bf16[784,128]{1,0:T(8,128)(2,1)S(1)}, u32[]{:S(2)}, u32[]{:S(2)}) collective-permute-start(bf16[784,128]{1,0:T(8,128)(2,1)} %get-tuple-element.103), channel_id=1, source_target_pairs={{4,0},{6,2},{5,1},{7,3},{12,8},{14,10},{13,9},{15,11},{20,16},{22,... | collective-permute-start | bytes 602120 | tf_op jit(solution)/shard_map/ppermute | solution.py:819
  115.4 25.6 %collective-permute-start.19 = (bf16[784,128]{1,0:T(8,128)(2,1)}, bf16[784,128]{1,0:T(8,128)(2,1)S(1)}, u32[]{:S(2)}, u32[]{:S(2)}) collective-permute-start(bf16[784,128]{1,0:T(8,128)(2,1)} %get-tuple-element.103), channel_id=1, source_target_pairs={{6,0},{7,1},{14,8},{15,9},{22,16},{23,17},{30,24},{31,25}} | collective-permute-start | bytes 602120 | tf_op jit(solution)/shard_map/ppermute | solution.py:819
  135.6 44.5 %collective-permute-start.33 = (bf16[192,1536]{1,0:T(8,128)(2,1)}, bf16[192,1536]{1,0:T(8,128)(2,1)S(1)}, u32[]{:S(2)}, u32[]{:S(2)}) collective-permute-start(bf16[192,1536]{1,0:T(8,128)(2,1)} %get-tuple-element.138), channel_id=1, source_target_pairs={{0,2},{2,0},{4,6},{6,4},{1,3},{3,1},{5,7},{7,5},{8,10},{10,8},{12,... | collective-permute-start | bytes 1769480 | tf_op jit(solution)/shard_map/reduce_gate_weights/ppermute | solution.py:827
  137.7 43.9 %collective-permute-start.34 = (bf16[192,1536]{1,0:T(8,128)(2,1)}, bf16[192,1536]{1,0:T(8,128)(2,1)S(1)}, u32[]{:S(2)}, u32[]{:S(2)}) collective-permute-start(bf16[192,1536]{1,0:T(8,128)(2,1)} %get-tuple-element.139), channel_id=1, source_target_pairs={{0,4},{2,6},{4,0},{6,2},{1,5},{3,7},{5,1},{7,3},{8,12},{10,14},{12... | collective-permute-start | bytes 1769480 | tf_op jit(solution)/shard_map/reduce_gate_weights/ppermute | solution.py:827
  141.0 42.6 %collective-permute-start.35 = (bf16[192,1536]{1,0:T(8,128)(2,1)}, bf16[192,1536]{1,0:T(8,128)(2,1)S(1)}, u32[]{:S(2)}, u32[]{:S(2)}) collective-permute-start(bf16[192,1536]{1,0:T(8,128)(2,1)} %get-tuple-element.140), channel_id=1, source_target_pairs={{0,6},{2,4},{4,2},{6,0},{1,7},{3,5},{5,3},{7,1},{8,14},{10,12},{12... | collective-permute-start | bytes 1769480 | tf_op jit(solution)/shard_map/reduce_gate_weights/ppermute | solution.py:827
  141.0 86.3 %collective-permute-start.16 = (bf16[1024,384]{1,0:T(8,128)(2,1)S(1)}, bf16[1024,384]{1,0:T(8,128)(2,1)S(1)}, u32[]{:S(2)}, u32[]{:S(2)}) collective-permute-start(bf16[1024,384]{1,0:T(8,128)(2,1)S(1)} %copy-done.18), channel_id=1, source_target_pairs={{0,1},{1,0},{2,3},{3,2},{4,5},{5,4},{6,7},{7,6},{8,9},{9,8},{10,11... | collective-permute-start | bytes 2359304 | tf_op jit(solution)/shard_map/layer_out/ppermute | solution.py:823
  179.6 54.3 %collective-permute-start.27 = (bf16[1024,768]{1,0:T(8,128)(2,1)}, bf16[1024,768]{1,0:T(8,128)(2,1)S(1)}, u32[]{:S(2)}, u32[]{:S(2)}) collective-permute-start(bf16[1024,768]{1,0:T(8,128)(2,1)} %get-tuple-element.132.own), channel_id=1, source_target_pairs={{0,1},{1,0},{2,3},{3,2},{4,5},{5,4},{6,7},{7,6},{8,9},{9,8},{10,11... | collective-permute-start | bytes 4718600 | tf_op jit(solution)/shard_map/ppermute | solution.py:823
  181.6 21.6 %collective-permute-start.21 = (bf16[192,1152]{1,0:T(8,128)(2,1)S(1)}, bf16[192,1152]{1,0:T(8,128)(2,1)S(1)}, u32[]{:S(2)}, u32[]{:S(2)}) collective-permute-start(bf16[192,1152]{1,0:T(8,128)(2,1)S(1)} %copy-done.23), channel_id=1, source_target_pairs={{0,4},{2,6},{4,0},{6,2},{1,5},{3,7},{5,1},{7,3},{8,12},{10,14},{12... | collective-permute-start | bytes 1327112 | tf_op jit(solution)/shard_map/reduce_input_weights/ppermute | solution.py:827
  183.5 19.6 %collective-permute-start.22 = (bf16[192,1152]{1,0:T(8,128)(2,1)S(1)}, bf16[192,1152]{1,0:T(8,128)(2,1)S(1)}, u32[]{:S(2)}, u32[]{:S(2)}) collective-permute-start(bf16[192,1152]{1,0:T(8,128)(2,1)S(1)} %copy-done.22), channel_id=1, source_target_pairs={{0,6},{2,4},{4,2},{6,0},{1,7},{3,5},{5,3},{7,1},{8,14},{10,12},{12... | collective-permute-start | bytes 1327112 | tf_op jit(solution)/shard_map/reduce_input_weights/ppermute | solution.py:827
  193.1 13.9 %collective-permute-start.36 = (bf16[48,1536]{1,0:T(8,128)(2,1)S(1)}, bf16[48,1536]{1,0:T(8,128)(2,1)S(1)}, u32[]{:S(2)}, u32[]{:S(2)}) collective-permute-start(bf16[48,1536]{1,0:T(8,128)(2,1)S(1)} %get-tuple-element.158), channel_id=1, source_target_pairs={{0,8},{8,0},{16,24},{24,16},{1,9},{9,1},{17,25},{25,17},{2,10},{10... | collective-permute-start | bytes 442376 | tf_op jit(solution)/shard_map/reduce_gate_weights/ppermute | solution.py:827
  218.0 15.6 %collective-permute-start.28 = (f32[8,768]{1,0:T(8,128)S(1)}, f32[8,768]{1,0:T(8,128)S(1)}, u32[]{:S(2)}, u32[]{:S(2)}) collective-permute-start(f32[8,768]{1,0:T(8,128)S(1)} %copy-done.41), channel_id=1, source_target_pairs={{2,0},{3,1},{4,2},{5,3},{6,4},{7,5},{10,8},{11,9},{12,10},{13,11},... | collective-permute-start | bytes 73736 | tf_op jit(solution)/shard_map/ppermute | solution.py:1172
  226.8 17.8 %collective-permute-start.39 = (bf16[48,1536]{1,0:T(8,128)(2,1)S(1)}, bf16[48,1536]{1,0:T(8,128)(2,1)S(1)}, u32[]{:S(2)}, u32[]{:S(2)}) collective-permute-start(bf16[48,1536]{1,0:T(8,128)(2,1)S(1)} %fusion.4.refs_0_), channel_id=1, source_target_pairs={{0,2},{2,0},{4,6},{6,4},{1,3},{3,1},{5,7},{7,5},{8,10},{10,8},{12,... | collective-permute-start | bytes 442376 | tf_op jit(solution)/shard_map/last_hop/ppermute | solution.py:827
  231.1 13.6 %collective-permute-start.40 = (bf16[48,1536]{1,0:T(8,128)(2,1)S(1)}, bf16[48,1536]{1,0:T(8,128)(2,1)S(1)}, u32[]{:S(2)}, u32[]{:S(2)}) collective-permute-start(bf16[48,1536]{1,0:T(8,128)(2,1)S(1)} %fusion.4.refs_0_), channel_id=1, source_target_pairs={{0,4},{2,6},{4,0},{6,2},{1,5},{3,7},{5,1},{7,3},{8,12},{10,14},{12... | collective-permute-start | bytes 442376 | tf_op jit(solution)/shard_map/last_hop/ppermute | solution.py:827
  (62 other events, 595.2 us)

commit v5 on v4

--- a/solution.py
+++ b/solution.py
@@ -39,6 +39,23 @@
 
 def sigmoid(value):
     return 1.0 / (1.0 + jnp.exp(-value))
+
+
+def gate_sigmoid(value):
+    return 0.5 * jnp.tanh(0.5 * value) + 0.5
+
+
+def chunks(columns, rows=BLOCK):
+    for column in range(0, columns, LANES):
+        for row in range(0, rows, LANES):
+            yield slice(row, row + LANES), slice(column, column + LANES)
+
+
+TILES = ((0, 0), (LANES, 0), (LANES, LANES))
+
+
+def tile_slices(tile):
+    return slice(tile[0], tile[0] + LANES), slice(tile[1], tile[1] + LANES)
 
 
 def softplus(value):
@@ -140,8 +157,10 @@
     return jnp.exp(cum[BLOCK - 1 :, :]) * jnp.where(place.last(block) == place.before(block), 1.0, 0.0)
 
 
-def decay_kernel(keep, cum, cum_rows, head):
-    return jnp.exp(jnp.where(keep, cum[:, head : head + 1] - cum_rows[head : head + 1, :], -1e30))
+def decay_tile(neg, cum, cum_rows, head, tile):
+    rows, columns = tile_slices(tile)
+    diff = cum[rows, head : head + 1] - cum_rows[head : head + 1, columns]
+    return jnp.exp(diff + neg[rows, columns])
 
 
 def both_halves(pair):
@@ -154,13 +173,21 @@
     return (place.column(block, tap - (CONV - 1)) == place.column(block)).astype(F32)
 
 
-def conv_pre(place, block, ext, par, channels):
-    total = par[4:5, :channels]
+def fill_masks(place, block, masks):
+    for tap in range(CONV - 1):
+        masks[tap] = jnp.broadcast_to(same_mask(place, block, tap), (BLOCK, LANES))
+
+
+def shifted_rows(ext, masks, tap, rows, columns):
+    first = 8 - (CONV - 1) + tap + rows.start
+    value = ext[first : first + LANES, columns]
+    return value if tap == CONV - 1 else value * masks[tap, rows, :]
+
+
+def conv_chunk(shifts, par, columns):
+    total = par[CONV : CONV + 1, columns]
     for tap in range(CONV):
-        first = 8 - (CONV - 1) + tap
-        total = total + par[tap : tap + 1, :channels] * ext[first : first + BLOCK, :] * same_mask(
-            place, block, tap
-        )
+        total = total + par[tap : tap + 1, columns] * shifts[tap]
     return total
 
 
@@ -300,19 +327,19 @@
     (
         tok, halo, dtp, spread,
         w1, par, normed_o, halo_normed_o, halo_v_o, v_o, xc_o, bc_o, ypart_o, pre_o, cum_o, entry_o, decay_o,
-        packet_o, ext, run, factor,
+        packet_o, ext, run, factor, masks, gram, neg, mix,
     ) = refs[dp_count + part_count :]
     forward_block(
         counts, heads, info, vectors, parts, tok, halo, w1, par, dtp, spread,
         normed_o, halo_normed_o, halo_v_o, v_o, xc_o, bc_o, ypart_o, pre_o, cum_o, entry_o, decay_o, packet_o,
-        ext, run, factor,
+        ext, run, factor, masks, gram, neg, mix,
     )
 
 
 def forward_block(
     counts, heads, info, vectors, parts, tok, halo, w1, par, dtp, spread,
     normed_o, halo_normed_o, halo_v_o, v_o, xc_o, bc_o, ypart_o, pre_o, cum_o, entry_o, decay_o, packet_o,
-    ext, run, factor,
+    ext, run, factor, masks, gram, neg, mix,
 ):
     block = pl.program_id(0)
     place = Place(info, counts)
@@ -348,13 +375,17 @@
     v = raw[:, :channels].astype(BF16)
     v_o[...] = v
     ext[8 : 8 + BLOCK, :] = v.astype(F32)
-    pre = conv_pre(place, block, ext, par, channels)
-    act = (pre * sigmoid(pre)).astype(BF16)
-    xc = act[:, :inner]
-    bq = act[:, inner : inner + state]
-    cq = act[:, inner + state :]
-    xc_o[...] = xc
-    bc_o[...] = act[:, inner:]
+    fill_masks(place, block, masks)
+    for rows, columns in chunks(channels):
+        pre = conv_chunk([shifted_rows(ext, masks, tap, rows, columns) for tap in range(CONV)], par, columns)
+        act = (pre * gate_sigmoid(pre)).astype(BF16)
+        if columns.start < inner:
+            xc_o[rows, columns] = act
+        else:
+            bc_o[rows, columns.start - inner : columns.stop - inner] = act
+    xc = xc_o[...]
+    bq = bc_o[:, :state]
+    cq = bc_o[:, state:]
     pre_step = raw[:, channels:].astype(BF16).astype(F32) + dtp[0:1, :]
     pre_o[...] = pre_step
     step = step_sizes(place, block, pre_step, heads)
@@ -363,16 +394,25 @@
     cum_o[...] = cum
     cum_rows = cum.T
     step_rows = step.T
-    gram = dot_nt(cq, bq)
-    keep = place.keep(block)
+    gram[...] = dot_nt(cq, bq)
+    neg[...] = jnp.where(place.keep(block), 0.0, -1e30)
+
+    @pl.when(block == 0)
+    def _():
+        mix[...] = jnp.zeros_like(mix)
+
     for pair in range(heads // 2):
         lanes = slice(pair * LANES, (pair + 1) * LANES)
-        mixing = []
-        for head in (2 * pair, 2 * pair + 1):
-            weight = decay_kernel(keep, cum, cum_rows, head) * step_rows[head : head + 1, :]
-            mixing.append((gram * weight).astype(BF16))
+        slot = pair % 2
+        for side in range(2):
+            head = 2 * pair + side
+            for tile in TILES:
+                rows, columns = tile_slices(tile)
+                weight = decay_tile(neg, cum, cum_rows, head, tile) * step_rows[head : head + 1, columns]
+                first = side * BLOCK + columns.start
+                mix[slot, rows, first : first + LANES] = (gram[rows, columns] * weight).astype(BF16)
         x_pair = xc[:, lanes]
-        y_pair = dot(jnp.concatenate(mixing, axis=1), jnp.concatenate(both_halves(x_pair), axis=0))
+        y_pair = dot(mix[slot], jnp.concatenate(both_halves(x_pair), axis=0))
         ypart_o[:, lanes] = y_pair + par[7:8, lanes] * x_pair.astype(F32)
     weighted = (expand(end_weights(place, block, cum) * step, spread) * xc.astype(F32)).astype(BF16)
     block_state = dot_tn(weighted, bq)
@@ -423,12 +463,22 @@
     low = state.astype(BF16)
     hb_o[0] = low
     cq = bc[:, LANES:]
-    y = ypart[...] + expand(enter_weights(place, block, cum[...]), spread) * dot_nt(cq, low)
-    y_o[...] = y
-    gate = z[...].astype(F32)
-    gated = y * gate * sigmoid(gate)
-    squares = jnp.sum(gated * gated, axis=1, keepdims=True)
-    cross = jnp.sum(par[6:7, :inner] * dn[...] * gated, axis=1, keepdims=True)
+    enter = jnp.concatenate(split(enter_weights(place, block, cum[...])), axis=1)
+    squares, cross = [0.0, 0.0], [0.0, 0.0]
+    for column in range(0, inner, LANES):
+        columns = slice(column, column + LANES)
+        read = dot_nt(cq, low[columns, :])
+        wide = dot(enter, spread[:, columns])
+        for half in range(2):
+            rows = slice(half * LANES, (half + 1) * LANES)
+            mixed = ypart[rows, columns] + wide[rows, :] * read[rows, :]
+            y_o[rows, columns] = mixed
+            gate = z[rows, columns].astype(F32)
+            gated = mixed * gate * gate_sigmoid(gate)
+            squares[half] = squares[half] + gated * gated
+            cross[half] = cross[half] + par[6:7, columns] * dn[rows, columns] * gated
+    squares = jnp.sum(jnp.concatenate(squares, axis=0), axis=1, keepdims=True)
+    cross = jnp.sum(jnp.concatenate(cross, axis=0), axis=1, keepdims=True)
     lane = iota((BLOCK, LANES), 1)
     both = jnp.where(lane == 0, squares, jnp.where(lane == 1, cross, 0.0))
     stat_o[...] = both.T[0:8, :]
@@ -437,7 +487,7 @@
 def gate_back_kernel(
     counts, inner_all, info, stat, y, z, dn, cot, cum, bc, xc, hb, decay, wo, par, spread,
     keep_o, send_o, gwo_o, small_o, dy_o, dz_o, de_o, exit_o, packet_o,
-    acc, run, factor,
+    normals, grads, dq, high, low, run, factor,
 ):
     step = pl.program_id(0)
     block = pl.num_programs(0) - 1 - step
@@ -448,42 +498,50 @@
 
     @pl.when(step == 0)
     def _():
-        acc[...] = jnp.zeros_like(acc)
         run[...] = jnp.zeros_like(run)
         factor[...] = jnp.ones_like(factor)
         small_o[...] = jnp.zeros_like(small_o)
 
     column = jnp.concatenate([stat[...], jnp.zeros((LANES - 8, BLOCK), F32)], axis=0).T
     inv = lax.rsqrt(column[:, 0:1] / inner_all + EPS)
-    cross = column[:, 1:2]
-    gain = par[6:7, :inner]
-    gate = z[...].astype(F32)
-    sig = sigmoid(gate)
-    silu = gate * sig
-    mixed = y[...]
-    gated = mixed * silu
-    normal = (gated * inv * gain).astype(BF16)
+    cross = column[:, 1:2] / inner_all * (inv * inv * inv)
+    mine = pl.ds(pl.multiple_of(block * BLOCK, BLOCK), BLOCK)
+    grads[mine, :] = (cot[...].astype(F32) * place.valid(block)).astype(BF16)
+    cq = bc[:, LANES:]
+    read = dot_nt(cq, hb[0])
+    enter = jnp.concatenate(split(enter_weights(place, block, cum[...])), axis=1)
+    wide = dot(enter, spread[...])
+    for rows, columns in chunks(inner):
+        gain = par[6:7, columns]
+        inv_rows = inv[rows, :]
+        gate = z[rows, columns].astype(F32)
+        sig = gate_sigmoid(gate)
+        silu = gate * sig
+        mixed = y[rows, columns]
+        gated = mixed * silu
+        scaled = gated * inv_rows
+        lines = pl.ds(pl.multiple_of(block * BLOCK + rows.start, LANES), LANES)
+        normals[lines, columns] = (scaled * gain).astype(BF16)
+        back = dn[rows, columns]
+        grad_gated = inv_rows * (gain * back) - gated * cross[rows, :]
+        dy = (grad_gated * silu).astype(BF16)
+        dy_o[rows, columns] = dy
+        dz_o[rows, columns] = (grad_gated * mixed * (sig + silu * (1.0 - sig))).astype(BF16)
+        dy_float = dy.astype(F32)
+        high[rows, columns], low[rows, columns] = split(dy_float * read[rows, columns])
+        small_o[0:1, columns] += jnp.sum(back * scaled, axis=0, keepdims=True)
+        small_o[1:2, columns] += jnp.sum(dy_float * xc[rows, columns].astype(F32), axis=0, keepdims=True)
+        dq[rows, columns] = (wide[rows, columns] * dy_float).astype(BF16)
+    normal = normals[mine, :]
     own = pl.multiple_of(place.tp * half, half)
     other = pl.multiple_of((1 - place.tp) * half, half)
     keep_o[...] = dot_nt(normal, wo[pl.ds(own, half), :]).astype(BF16)
     send_o[...] = dot_nt(normal, wo[pl.ds(other, half), :]).astype(BF16)
-    grad = (cot[...].astype(F32) * place.valid(block)).astype(BF16)
-    acc[...] += dot_tn(grad, normal)
-    back = dn[...]
-    grad_gated = inv * (gain * back) - gated * (inv * inv * inv) * (cross / inner_all)
-    dy = (grad_gated * silu).astype(BF16)
-    dy_o[...] = dy
-    dz_o[...] = (grad_gated * mixed * sig * (1.0 + gate * (1.0 - sig))).astype(BF16)
-    dy_float = dy.astype(F32)
-    cq = bc[:, LANES:]
-    read = dot_nt(cq, hb[0])
-    de_o[...] = reduce_heads(dy_float * read, spread)
-    small_o[0:1, :] += jnp.sum(back * gated * inv, axis=0, keepdims=True)
-    small_o[1:2, :] += jnp.sum(dy_float * xc[...].astype(F32), axis=0, keepdims=True)
-    dq = (expand(enter_weights(place, block, cum[...]), spread) * dy_float).astype(BF16)
+    pick = spread[:LANES, :]
+    de_o[...] = dot_nt(high[...], pick) + dot_nt(low[...], pick)
     exit_o[0] = run[...]
     here = decay[0, 0:1, :]
-    total = head_column(here, inner) * run[...] + dot_tn(dq, cq)
+    total = head_column(here, inner) * run[...] + dot_tn(dq[...], cq)
     run[...] = total
     after = factor[0:1, :] * here
     factor[...] = jnp.broadcast_to(after, factor.shape)
@@ -491,22 +549,25 @@
     @pl.when(step == pl.num_programs(0) - 1)
     def _():
         packet_o[...] = state_packet(total, after)
-        gwo_o[...] = acc[...].astype(BF16)
+        gwo_o[...] = dot_tn(grads[...], normals[...]).astype(BF16)
 
 
 def intra_back_kernel(counts, heads, dp_count, info, *refs):
-    dy, dz, xc, bc, cum, pre_step, hb, normed, wz, gwo, par, spread = refs[:12]
-    dxc_o, dcq_o, dbq_o, rows_o, cols_o, dnz_o = refs[12:18]
-    parts = refs[18:-2]
-    acc, columns = refs[-2:]
+    dy, dz, xc, bc, cum, pre_step, hb, normed, all_dz, wz, gwo, par, spread = refs[:13]
+    dxc_o, dcq_o, dbq_o, rows_o, cols_o, dnz_o = refs[13:19]
+    parts = refs[19:-6]
+    acc, columns, neg, gram, grad_gram, mix = refs[-6:]
     block = pl.program_id(0)
     place = Place(info, counts)
     inner = heads * HEAD
 
     @pl.when(block == 0)
     def _():
-        acc[...] = jnp.zeros_like(acc)
         columns[...] = jnp.zeros_like(columns)
+        mix[...] = jnp.zeros_like(mix)
+        acc[...] = dot_tn(normed[...], all_dz[...])
+        cut_pieces(place, dp_count, acc, parts, slice(0, inner))
+        cut_pieces(place, dp_count, gwo, parts, slice(inner, 2 * inner))
 
     bq = bc[:, :LANES]
     cq = bc[:, LANES:]
@@ -514,44 +575,46 @@
     step = step_sizes(place, block, pre_step[...], heads)
     cum_rows = cums.T
     step_rows = step.T
-    gram = dot_nt(cq, bq)
-    keep = place.keep(block)
-    lane = iota((BLOCK, LANES), 1)
-    grad_gram = jnp.zeros((BLOCK, BLOCK), F32)
-    sums = jnp.zeros((BLOCK, LANES), F32)
+    gram[...] = dot_nt(cq, bq)
+    neg[...] = jnp.where(place.keep(block), 0.0, -1e30)
+    lane = iota((LANES, LANES), 1)
+    grad_gram[...] = jnp.zeros_like(grad_gram)
+    rows_o[...] = jnp.zeros_like(rows_o)
     for pair in range(heads // 2):
-        lanes = slice(pair * LANES, (pair + 1) * LANES)
-        dy_pair = dy[:, lanes]
-        x_pair = xc[:, lanes]
+        lanes_here = slice(pair * LANES, (pair + 1) * LANES)
+        slot = pair % 2
+        dy_pair = dy[:, lanes_here]
+        x_pair = xc[:, lanes_here]
         halves = jnp.concatenate(both_halves(dy_pair), axis=0)
         grad_mixing = dot_nt(halves, x_pair)
-        mixing = []
         for side in range(2):
             head = 2 * pair + side
-            grad_m = grad_mixing[side * BLOCK : (side + 1) * BLOCK, :]
-            kernel = decay_kernel(keep, cums, cum_rows, head)
-            step_row = step_rows[head : head + 1, :]
-            weight = kernel * step_row
-            mixing.append((gram * weight).astype(BF16))
-            grad_gram = grad_gram + grad_m * weight
-            part = grad_m * gram * kernel
-            columns[head : head + 1, :] = jnp.sum(part, axis=0, keepdims=True)
-            sums = sums + jnp.where(lane == head, jnp.sum(part * step_row, axis=1, keepdims=True), 0.0)
-        dx_pair = dot_tn(jnp.concatenate(mixing, axis=0), halves)
-        dxc_o[:, lanes] = dx_pair + par[7:8, lanes] * dy_pair.astype(F32)
-    grad_low = grad_gram.astype(BF16)
+            row_sums, column_sums = [0.0, 0.0], [0.0, 0.0]
+            for tile in TILES:
+                rows, across = tile_slices(tile)
+                first = side * BLOCK + rows.start
+                grad_m = grad_mixing[first : first + LANES, across]
+                kernel = decay_tile(neg, cums, cum_rows, head, tile)
+                step_row = step_rows[head : head + 1, across]
+                weighted = gram[rows, across] * kernel
+                mixing = weighted * step_row
+                mix[slot, first : first + LANES, across] = mixing.astype(BF16)
+                grad_gram[rows, across] += grad_m * (kernel * step_row)
+                row, column = rows.start // LANES, across.start // LANES
+                column_sums[column] = column_sums[column] + jnp.sum(grad_m * weighted, axis=0, keepdims=True)
+                row_sums[row] = row_sums[row] + grad_m * mixing
+            columns[head : head + 1, :] = jnp.concatenate(column_sums, axis=1)
+            for row in range(2):
+                total = jnp.sum(row_sums[row], axis=1, keepdims=True)
+                rows_o[row * LANES : (row + 1) * LANES, :] += jnp.where(lane == head, total, 0.0)
+        dx_pair = dot_tn(mix[slot], halves)
+        dxc_o[:, lanes_here] = dx_pair + par[7:8, lanes_here] * dy_pair.astype(F32)
+    grad_low = grad_gram[...].astype(BF16)
     dq = (expand(enter_weights(place, block, cums), spread) * dy[...].astype(F32)).astype(BF16)
     dcq_o[...] = dot(grad_low, bq) + dot(dq, hb[0])
     dbq_o[...] = dot_tn(grad_low, cq)
-    rows_o[...] = sums
     cols_o[...] = columns[...].T
     dnz_o[...] = dot_nt(dz[...], wz[...])
-    acc[...] += dot_tn(normed[...], dz[...])
-
-    @pl.when(block == pl.num_programs(0) - 1)
-    def _():
-        cut_pieces(place, dp_count, acc, parts, slice(0, inner))
-        cut_pieces(place, dp_count, gwo, parts, slice(inner, 2 * inner))
 
 
 def state_back_kernel(counts, heads, packet_count, info, *refs):
@@ -584,17 +647,26 @@
     low = grad_state.astype(BF16)
     bq = bc[:, :LANES]
     cums = cum[...]
-    x_float = xc[...].astype(F32)
     pre_dt = pre_step[...]
     valid = place.valid(block)
     step = step_sizes(place, block, pre_dt, heads)
     end_kernel = end_weights(place, block, cums)
     end_weight = end_kernel * step
-    end_wide = expand(end_weight, spread)
-    spread_b = dot_nt(bq, low)
-    act_o[:, :inner] = dxc[...] + end_wide * spread_b
-    grad_end = reduce_heads(x_float * spread_b, spread)
-    act_o[:, inner : inner + LANES] = dbq[...] + dot((x_float * end_wide).astype(BF16), low)
+    end_split = jnp.concatenate(split(end_weight), axis=1)
+    grad_end = jnp.zeros((BLOCK, LANES), F32)
+    grad_b = dbq[...]
+    for column in range(0, inner, LANES):
+        columns = slice(column, column + LANES)
+        low_part = low[columns, :]
+        spread_b = dot_nt(bq, low_part)
+        wide = dot(end_split, spread[:, columns])
+        x_part = xc[:, columns].astype(F32)
+        act_o[:, columns] = dxc[:, columns] + wide * spread_b
+        high, rest = split(x_part * spread_b)
+        pick = spread[:LANES, columns]
+        grad_end = grad_end + dot_nt(high, pick) + dot_nt(rest, pick)
+        grad_b = grad_b + dot((x_part * wide).astype(BF16), low_part)
+    act_o[:, inner : inner + LANES] = grad_b
     act_o[:, inner + LANES :] = dcq[...]
     end_part = grad_end * end_weight
     last = iota((BLOCK, LANES), 0) == BLOCK - 1
@@ -617,7 +689,7 @@
     act, ddt, v, v_tail, halo_v, halo_normed, normed, small_gate, small_state, par, spread = refs[:11]
     packed_o, back_o = refs[11:13]
     parts = refs[13 : 13 + part_count]
-    ext, grad_ext, acc, small_o = refs[13 + part_count :]
+    ext, grads, masks, ahead, acc, small_o = refs[13 + part_count :]
     step_id = pl.program_id(0)
     block = pl.num_programs(0) - 1 - step_id
     place = Place(info, counts)
@@ -626,11 +698,11 @@
 
     @pl.when(step_id == 0)
     def _():
-        acc[...] = jnp.zeros_like(acc)
-        grad_ext[...] = jnp.zeros_like(grad_ext)
+        grads[...] = jnp.zeros_like(grads)
         small_o[...] = jnp.zeros_like(small_o)
 
     ext[8 : 8 + BLOCK, :] = v[...].astype(F32)
+    grads[8 + BLOCK :, :] = grads[8:16, :]
 
     @pl.when(block == 0)
     def _():
@@ -640,27 +712,43 @@
     def _():
         ext[0:8, :] = v_tail[...].astype(F32)[8:16, :]
 
-    pre = conv_pre(place, block, ext, par, channels)
-    sig = sigmoid(pre)
-    slope = sig * (1.0 + pre * (1.0 - sig))
-    grad_pre = act[...] * slope
-    small_o[4:5, :] += jnp.sum(grad_pre, axis=0, keepdims=True)
-    carry = grad_ext[0:8, :]
-    grad_ext[0:BLOCK, :] = jnp.zeros((BLOCK, channels), F32)
-    grad_ext[BLOCK : BLOCK + 8, :] = carry
-    for tap in range(CONV):
-        first = 8 - (CONV - 1) + tap
-        masked = grad_pre * same_mask(place, block, tap)
-        small_o[tap : tap + 1, :] += jnp.sum(masked * ext[first : first + BLOCK, :], axis=0, keepdims=True)
-        grad_ext[first : first + BLOCK, :] += par[tap : tap + 1, :channels] * masked
-    packed = jnp.concatenate([grad_ext[8 : 8 + BLOCK, :].astype(BF16), ddt[...]], axis=1)
-    packed_o[...] = packed
-    acc[...] += dot_tn(normed[...], packed)
+    fill_masks(place, block, masks)
+    here = place.rows(block * BLOCK - 8 + iota((8 + BLOCK, 1), 0))
+    for step in range(1, CONV):
+        later = place.rows(block * BLOCK - 8 + step + iota((8 + BLOCK, 1), 0))
+        ahead[step - 1] = jnp.broadcast_to((here == later).astype(F32), (8 + BLOCK, LANES))
+    for rows, columns in chunks(channels):
+        shifts = [shifted_rows(ext, masks, tap, rows, columns) for tap in range(CONV)]
+        pre = conv_chunk(shifts, par, columns)
+        sig = gate_sigmoid(pre)
+        grad_pre = act[rows, columns] * (sig * (1.0 + pre * (1.0 - sig)))
+        grads[8 + rows.start : 8 + rows.stop, columns] = grad_pre
+        small_o[4:5, columns] += jnp.sum(grad_pre, axis=0, keepdims=True)
+        for tap in range(CONV):
+            small_o[tap : tap + 1, columns] += jnp.sum(grad_pre * shifts[tap], axis=0, keepdims=True)
+
+    def behind(first, size, columns):
+        total = par[CONV - 1 : CONV, columns] * grads[first : first + size, columns]
+        for step in range(1, CONV):
+            value = grads[first + step : first + step + size, columns] * ahead[step - 1, first : first + size, :]
+            total = total + par[CONV - 1 - step : CONV - step, columns] * value
+        return total
+
+    first_line = pl.multiple_of(block * BLOCK, BLOCK)
+    for rows, columns in chunks(channels):
+        lines = pl.ds(pl.multiple_of(first_line + rows.start, LANES), LANES)
+        packed_o[lines, columns] = behind(8 + rows.start, LANES, columns).astype(BF16)
+    packed_o[pl.ds(first_line, BLOCK), channels:] = ddt[...]
 
     @pl.when(block == 0)
     def _():
-        back = jnp.concatenate([jnp.zeros((8, channels), F32), grad_ext[0:8, :]], axis=0).astype(BF16)
+        grads[0:8, :] = jnp.zeros((8, channels), F32)
+        halo_part = jnp.concatenate(
+            [behind(0, 8, slice(column, column + LANES)) for column in range(0, channels, LANES)], axis=1
+        )
+        back = jnp.concatenate([jnp.zeros((8, channels), F32), halo_part], axis=0).astype(BF16)
         back_o[...] = back
+        acc[...] = dot_tn(normed[...], packed_o[...])
         acc[:, :channels] += dot_tn(halo_normed[...], back)
         small_o[6:7, :LANES] = small_state[0:1, :]
         small_o[7:8, :LANES] = small_state[1:2, :]
@@ -671,7 +759,7 @@
 
 def input_back_kernel(
     counts, dp_count, part_count, info, packed, back, dnz, tok, halo, w1, par,
-    dn_o, dnh_o, norm_o, total,
+    dn_o, dnh_o, norm_o, total, turned,
 ):
     block = pl.program_id(0)
     place = Place(info, counts)
@@ -681,14 +769,15 @@
 
     @pl.when(block == 0)
     def _():
-        halo_grad = dot_nt(back[...], w1[:, :channels])
+        turned[...] = w1[...].T
+        halo_grad = dot(back[...], turned[:channels, :])
         dnh_o[...] = halo_grad[8:16, :]
         halo_scaled, _, _ = normalise(halo[...].astype(F32), gain)
         total[...] = jnp.broadcast_to(
             jnp.sum(halo_grad * halo_scaled, axis=0, keepdims=True), total.shape
         )
 
-    partial = dnz[...] + dot_nt(packed[...], w1[...])
+    partial = dnz[...] + dot(packed[...], turned[...])
     dn_o[...] = partial.astype(BF16)
     scaled, _, _ = normalise(tok[...].astype(F32), gain)
     total[0:1, :] += jnp.sum(partial * scaled, axis=0, keepdims=True)
@@ -965,6 +1054,10 @@
             pltpu.VMEM((8 + BLOCK, channels), F32),
             pltpu.VMEM((inner, LANES), F32),
             pltpu.VMEM((8, LANES), F32),
+            pltpu.VMEM((CONV - 1, BLOCK, LANES), F32),
+            pltpu.VMEM((BLOCK, BLOCK), F32),
+            pltpu.VMEM((BLOCK, BLOCK), F32),
+            pltpu.VMEM((2, BLOCK, 2 * BLOCK), BF16),
         ],
         micros=20,
     )
@@ -1038,7 +1131,11 @@
             packet_out,
         ],
         [
-            pltpu.VMEM((width, inner), F32),
+            pltpu.VMEM((rows, inner), BF16),
+            pltpu.VMEM((rows, width), BF16),
+            pltpu.VMEM((BLOCK, inner), BF16),
+            pltpu.VMEM((BLOCK, inner), BF16),
+            pltpu.VMEM((BLOCK, inner), BF16),
             pltpu.VMEM((inner, LANES), F32),
             pltpu.VMEM((8, LANES), F32),
         ],
@@ -1063,7 +1160,8 @@
             (cum, "rows"),
             (pre_step, "rows"),
             (hb, "block"),
-            (normed, "rows"),
+            (normed, "whole"),
+            (dz, "whole"),
             (w2, wz_spec),
             (gwo, "whole"),
             (par, "whole"),
@@ -1078,7 +1176,14 @@
             row_out(width, F32),
         ]
         + [out((width // parts, 2 * inner), BF16, "whole")] * parts,
-        [pltpu.VMEM((width, inner), F32), pltpu.VMEM((LANES, BLOCK), F32)],
+        [
+            pltpu.VMEM((width, inner), F32),
+            pltpu.VMEM((LANES, BLOCK), F32),
+            pltpu.VMEM((BLOCK, BLOCK), F32),
+            pltpu.VMEM((BLOCK, BLOCK), F32),
+            pltpu.VMEM((BLOCK, BLOCK), F32),
+            pltpu.VMEM((2, 2 * BLOCK, BLOCK), BF16),
+        ],
         micros=18,
     )
     with jax.named_scope("reduce_gate_weights"):
@@ -1126,17 +1231,19 @@
             (v, "tail"),
             (halo_v, "whole"),
             (halo_normed, "whole"),
-            (normed, "rows"),
+            (normed, "whole"),
             (small_gate, "whole"),
             (small_state, "whole"),
             (par, "whole"),
             (spread, "whole"),
         ],
-        [row_out(channels + LANES, BF16), out((16, channels), BF16, "whole")]
+        [out((rows, channels + LANES), BF16, "whole"), out((16, channels), BF16, "whole")]
         + [out((width // parts, channels + LANES), BF16, "whole")] * parts,
         [
             pltpu.VMEM((8 + BLOCK, channels), F32),
-            pltpu.VMEM((8 + BLOCK, channels), F32),
+            pltpu.VMEM((16 + BLOCK, channels), F32),
+            pltpu.VMEM((CONV - 1, BLOCK, LANES), F32),
+            pltpu.VMEM((CONV - 1, 8 + BLOCK, LANES), F32),
             pltpu.VMEM((width, channels + LANES), F32),
             pltpu.VMEM((8, channels), F32),
         ],
@@ -1144,6 +1251,9 @@
         micros=18,
     )
     norm_rows = part_rows * dp_count
+    if parts > 1:
+        g1 = [g1[0]] + [partnered(g1[mask], "ctx", mask) for mask in range(1, parts)]
+        packed, g1[1] = lax.optimization_barrier((packed, g1[1]))
     partial, halo_grad, norm_part = call(
         functools.partial(input_back_kernel, counts, dp_count, parts),
         steps,
@@ -1162,8 +1272,8 @@
             out((8, width), F32, "whole"),
             out((norm_rows, LANES), F32, "whole"),
         ],
-        [pltpu.VMEM((8, width), F32)],
-        micros=5,
+        [pltpu.VMEM((8, width), F32), pltpu.VMEM((channels + LANES, width), BF16)],
+        micros=8,
     )
     other = swapped(partial)
     size = ctx_count * 2
@@ -1174,7 +1284,7 @@
     with jax.named_scope("reduce_input_weights"):
         norm_part = jnp.pad(norm_part, ((0, 0), (channels, 0)))
         if parts > 1:
-            total1 = dp_sum(ctx_sum(g1) + norm_part)
+            total1 = dp_sum(sum(piece.astype(F32) for piece in g1) + norm_part)
         else:
             total1 = whole_sum((g1[0].astype(F32) + norm_part).astype(BF16))
         across = swapped(total1[:, inner:])

time: 255 us -> 247 us (0.969)
  waiting for transfers between devices: 43.3 us -> 27.4 us
  Pallas kernels: 119 us -> 126 us
    ppermute x30, waiting for transfers between devices: 42 us -> 26 us  [partnered(): lax.ppermute(value, axis, [(one, one ^ mask) for one in range(lax.axis_si...]
    pallas_call x11, Pallas kernels: 119 us -> 126 us  [call(): pl.pallas_call(body, grid=(steps,), in_specs=[pl.BlockSpec(memory_space=p...]
    ppermute x30, starting transfers between devices: 43.4 us -> 46 us  [partnered(): lax.ppermute(value, axis, [(one, one ^ mask) for one in range(lax.axis_si...]
    unnamed x89 -> x81, local copies, waits for them, and re-layouts: 8.44 us -> 8.4 us
  transfers between devices with their start and end apart: 42 -> 42, of which waited for: 8 -> 9; matrix products, arithmetic and copies ran while one was open for 5% -> 6% of each run, Pallas kernels for 37% -> 40%
where the time goes in v5:
time: 247 us; the launch traced here: 246 us
  Pallas kernels  126 us (51%)
  starting transfers between devices  63.5 us (26%)
  waiting for transfers between devices  27.4 us (11%)
  local copies, waits for them, and re-layouts  12.9 us (5%)
  other arithmetic  9.36 us (4%)
  blocking collectives  4.69 us (2%)
    pallas_call x11, Pallas kernels, call(): pl.pallas_call(body, grid=(steps,), in_specs=[pl.BlockSpec(memory_space=p...  126 us
    ppermute x30, starting transfers between devices, partnered(): lax.ppermute(value, axis, [(one, one ^ mask) for one in range(lax.axis_si...  46 us
    ppermute x30, waiting for transfers between devices, partnered(): lax.ppermute(value, axis, [(one, one ^ mask) for one in range(lax.axis_si...  26 us
    ppermute x7, starting transfers between devices, shifted(): lax.ppermute(value, axis, [(source, source + steps) for source in range(f...  14.2 us
    unnamed x81, local copies, waits for them, and re-layouts  8.4 us
  transfers between devices with their start and end apart: 42, of which 9 were waited for; matrix products, arithmetic and copies ran while one was open for 6% of the time, Pallas kernels for 40%

profile of v5, /device:TPU:0, one launch (start us, length us, event | category | flops | bytes accessed | tf_op | source)
XLA Modules:
  0.0 245.7 jit_solution(13753759253041148024)
XLA Ops:
  1.6 3.1 %collective-permute-start = (bf16[48,1024]{1,0:T(8,128)(2,1)S(1)}, bf16[48,1024]{1,0:T(8,128)(2,1)S(1)}, u32[]{:S(2)}, u32[]{:S(2)}) collective-permute-start(bf16[48,1024]{1,0:T(8,128)(2,1)S(1)} %fusion.10), channel_id=1, source_target_pairs={{0,8},{8,0},{16,24},{24,16},{1,9},{9,1},{17,25},{25,17},{2,10},{10... | collective-permute-start | bytes 294920 | tf_op jit(solution)/shard_map/gather_weights/ppermute | solution.py:916
  4.7 2.6 %collective-permute-start.1 = (bf16[48,1024]{1,0:T(8,128)(2,1)S(1)}, bf16[48,1024]{1,0:T(8,128)(2,1)S(1)}, u32[]{:S(2)}, u32[]{:S(2)}) collective-permute-start(bf16[48,1024]{1,0:T(8,128)(2,1)S(1)} %fusion.10), channel_id=1, source_target_pairs={{0,16},{8,24},{16,0},{24,8},{1,17},{9,25},{17,1},{25,9},{2,18},{10... | collective-permute-start | bytes 294920 | tf_op jit(solution)/shard_map/gather_weights/ppermute | solution.py:916
  18.0 3.5 %collective-permute-start.4 = (bf16[64,1536]{1,0:T(8,128)(2,1)S(1)}, bf16[64,1536]{1,0:T(8,128)(2,1)S(1)}, u32[]{:S(2)}, u32[]{:S(2)}) collective-permute-start(bf16[64,1536]{1,0:T(8,128)(2,1)S(1)} %fusion.8.refs_0_), channel_id=1, source_target_pairs={{0,16},{8,24},{16,0},{24,8},{1,17},{9,25},{17,1},{25,9},{2,18},{10... | collective-permute-start | bytes 589832 | tf_op jit(solution)/shard_map/gather_weights/ppermute | solution.py:916
  24.8 2.4 collective-permute-start.8
  28.6 6.8 %collective-permute-done.4.refs_2_ = bf16[64,1536]{1,0:T(8,128)(2,1)S(1)} collective-permute-done((bf16[64,1536]{1,0:T(8,128)(2,1)S(1)}, bf16[64,1536]{1,0:T(8,128)(2,1)S(1)}, u32[]{:S(2)}, u32[]{:S(2)}) %collective-permute-start.4) | collective-permute-done | bytes 196640 | tf_op jit(solution)/shard_map/gather_weights/ppermute | solution.py:916
  35.4 3.4 %collective-permute-start.9 = (bf16[16,768]{1,0:T(8,128)(2,1)S(1)}, bf16[16,768]{1,0:T(8,128)(2,1)S(1)}, u32[]{:S(2)}, u32[]{:S(2)}) collective-permute-start(bf16[16,768]{1,0:T(8,128)(2,1)S(1)} %constant_dynamic-slice_fusion), channel_id=1, source_target_pairs={{0,2},{2,4},{4,6},{1,3},{3,5},{5,7},{8,10},{10,12},{12,14},{9,11},... | collective-permute-start | bytes 73736 | tf_op jit(solution)/shard_map/ppermute | solution.py:908
  47.3 22.7 %shard_map.297 = (bf16[768,1152]{1,0:T(8,128)(2,1)}, f32[8,1024]{1,0:T(8,128)}, bf16[1024,768]{1,0:T(8,128)(2,1)}, bf16[16,768]{1,0:T(8,128)(2,1)}, f32[8,1024]{...) custom-call(s32[10]{0:T(128)} %concatenate.30.info, ...), custom_call_target="tpu_custom_call" | custom-call | flops 22000001024 | bytes 70000000 | tf_op jit(solution)/shard_map/pallas_call | solution.py:888
  72.1 3.6 %collective-permute-start.11 = (bf16[784,128]{1,0:T(8,128)(2,1)}, bf16[784,128]{1,0:T(8,128)(2,1)S(1)}, u32[]{:S(2)}, u32[]{:S(2)}) collective-permute-start(bf16[784,128]{1,0:T(8,128)(2,1)} %get-tuple-element.88), channel_id=1, source_target_pairs={{0,4},{2,6},{1,5},{3,7},{8,12},{10,14},{9,13},{11,15},{16,20},{18,... | collective-permute-start | bytes 602120 | tf_op jit(solution)/shard_map/ppermute | solution.py:908
  78.0 7.4 %shard_map.298 = (bf16[768,1536]{1,0:T(8,128)(2,1)}, bf16[1024,768]{1,0:T(8,128)(2,1)}, f32[1024,768]{1,0:T(8,128)}) custom-call(s32[10]{0:T(128)} %concatenate.30.info, bf16[192,1536]{1,0:T(8,128)(2,1)} %copy-done.2, bf16[192,1536]{1,0:T(8,128)(2,1)} %copy-done.18, bf16[192,1536]{1,0:T(8,128)(2,1)} %copy-done.19, bf16[192,1536]{1,0:T(8,128)(2,1)} %copy-done.20, ...), custom_call_target="tpu_custom_call" | custom-call | flops 7699999744 | bytes 24500000 | tf_op jit(solution)/shard_map/pallas_call | solution.py:888
  86.2 8.6 %shard_map.299 = (f32[1024,768]{1,0:T(8,128)}, bf16[4,768,128]{2,1,0:T(8,128)(2,1)}, f32[4,768,128]{2,1,0:T(8,128)}, f32[8,1024]{1,0:T(8,128)}) custom-call(s32[10]{0:T(128)} %concatenate.30.info, bf16[784,128]{1,0:T(8,128)(2,1)} %copy-done.27, bf16[784,128]{1,0:T(8,128)(2,1)} %copy-done.28, bf16[784,128]{1,0:T(8,128)(2,1)} %copy-done.29, ...), custom_call_target="tpu_custom_call" | custom-call | flops 8800000000 | bytes 28000000 | tf_op jit(solution)/shard_map/pallas_call | solution.py:888
  94.8 4.7 %psum.7.stat = f32[8,1024]{1,0:T(8,128)} all-reduce(f32[8,1024]{1,0:T(8,128)} %get-tuple-element.98), channel_id=1, replica_groups=mesh['dp'=4,'ctx'=4,'tp'=2] {'tp'}, use_global_device_ids=true, to_apply=%region_1.2 | all-reduce | flops 8192 | bytes 65536 | tf_op jit(solution)/shard_map/psum | solution.py:1100
  99.5 15.3 %shard_map.300 = (bf16[1024,384]{1,0:T(8,128)(2,1)}, bf16[1024,384]{1,0:T(8,128)(2,1)}, bf16[768,768]{1,0:T(8,128)(2,1)}, f32[8,768]{1,0:T(8,128)}, bf16[1024,76...) custom-call(s32[10]{0:T(128)} %concatenate.30.info, ...), custom_call_target="tpu_custom_call" | custom-call | flops 16499999744 | bytes 52500000 | tf_op jit(solution)/shard_map/pallas_call | solution.py:888
  118.7 19.9 %shard_map.301 = (f32[1024,768]{1,0:T(8,128)}, f32[1024,128]{1,0:T(8,128)}, f32[1024,128]{1,0:T(8,128)}, f32[1024,128]{1,0:T(8,128)}, f32[1024,128]{1,0:T(8,128)...) custom-call(s32[10]{0:T(128)} %concatenate.30.info, ...), custom_call_target="tpu_custom_call" | custom-call | flops 19800000512 | bytes 63000000 | tf_op jit(solution)/shard_map/pallas_call | solution.py:888
  140.6 3.3 %collective-permute-start.34 = (bf16[192,1536]{1,0:T(8,128)(2,1)}, bf16[192,1536]{1,0:T(8,128)(2,1)S(1)}, u32[]{:S(2)}, u32[]{:S(2)}) collective-permute-start(bf16[192,1536]{1,0:T(8,128)(2,1)} %get-tuple-element.143), channel_id=1, source_target_pairs={{0,4},{2,6},{4,0},{6,2},{1,5},{3,7},{5,1},{7,3},{8,12},{10,14},{12... | collective-permute-start | bytes 1769480 | tf_op jit(solution)/shard_map/reduce_gate_weights/ppermute | solution.py:916
  144.8 11.9 %shard_map.302 = (f32[1024,1024]{1,0:T(8,128)}, bf16[1024,128]{1,0:T(8,128)(2,1)}, f32[8,128]{1,0:T(8,128)}) custom-call(s32[10]{0:T(128)} %concatenate.30.info, bf16[784,128]{1,0:T(8,128)(2,1)} %copy-done.24, bf16[784,128]{1,0:T(8,128)(2,1)} %copy-done.25, bf16[784,128]{1,0:T(8,128)(2,1)} %copy-done.26, f32[4,768,128]{2,1,0:T(8,128)} %get-tuple-element.106.refs_3_, ...), custom_call_target="tpu_custom_call" | custom-call | flops 12099999744 | bytes 38500000 | tf_op jit(solution)/shard_map/pallas_call | solution.py:888
  156.6 21.7 %shard_map.303 = (bf16[1024,1152]{1,0:T(8,128)(2,1)}, bf16[16,1024]{1,0:T(8,128)(2,1)}, bf16[192,1152]{1,0:T(8,128)(2,1)}, bf16[192,1152]{1,0:T(8,128)(2,1)}, bf...) custom-call(s32[10]{0:T(128)} %concatenate.30.info, f32[1024,1024]{1,0:T(8,128)} %get-tuple-element.118.refs_0_, ...), custom_call_target="tpu_custom_call" | custom-call | flops 19800000512 | bytes 63000000 | tf_op jit(solution)/shard_map/pallas_call | solution.py:888
  182.3 9.3 %collective-permute-done.20 = bf16[192,1152]{1,0:T(8,128)(2,1)S(1)} collective-permute-done((bf16[192,1152]{1,0:T(8,128)(2,1)}, bf16[192,1152]{1,0:T(8,128)(2,1)S(1)}, u32[]{:S(2)}, u32[]{:S(2)}) %collective-permute-start.20) | collective-permute-done | bytes 442400 | tf_op jit(solution)/shard_map/ppermute | solution.py:916
  191.6 8.1 %shard_map.304 = (bf16[1024,768]{1,0:T(8,128)(2,1)}, f32[8,768]{1,0:T(8,128)}, f32[192,128]{1,0:T(8,128)}) custom-call(s32[10]{0:T(128)} %concatenate.30.info, bf16[1024,1152]{1,0:T(8,128)(2,1)} %get-tuple-element.131.packed, bf16[16,1024]{1,0:T(8,128)(2,1)} %get-tuple-element.132.back, f32[1024,768]{1,0:T(8,128)} %get-tuple-element.133.dnz, ...), custom_call_target="tpu_custom_call" | custom-call | flops 8800000000 | bytes 28000000 | tf_op jit(solution)/shard_map/pallas_call | solution.py:888
  199.7 2.3 collective-permute-done.21
  202.0 3.5 %collective-permute-start.38 = (bf16[48,1536]{1,0:T(8,128)(2,1)S(1)}, bf16[48,1536]{1,0:T(8,128)(2,1)S(1)}, u32[]{:S(2)}, u32[]{:S(2)}) collective-permute-start(bf16[48,1536]{1,0:T(8,128)(2,1)S(1)} %get-tuple-element.163), channel_id=1, source_target_pairs={{0,24},{8,16},{16,8},{24,0},{1,25},{9,17},{17,9},{25,1},{2,26},{10... | collective-permute-start | bytes 442376 | tf_op jit(solution)/shard_map/reduce_gate_weights/ppermute | solution.py:916
  209.1 3.9 %collective-permute-start.25 = (bf16[48,1152]{1,0:T(8,128)(2,1)S(1)}, bf16[48,1152]{1,0:T(8,128)(2,1)S(1)}, u32[]{:S(2)}, u32[]{:S(2)}) collective-permute-start(bf16[48,1152]{1,0:T(8,128)(2,1)S(1)} %get-tuple-element.166), channel_id=1, source_target_pairs={{0,24},{8,16},{16,8},{24,0},{1,25},{9,17},{17,9},{25,1},{2,26},{10... | collective-permute-start | bytes 331784 | tf_op jit(solution)/shard_map/reduce_input_weights/ppermute | solution.py:916
  214.6 3.9 %collective-permute-done.24 = bf16[48,1152]{1,0:T(8,128)(2,1)S(1)} collective-permute-done((bf16[48,1152]{1,0:T(8,128)(2,1)S(1)}, bf16[48,1152]{1,0:T(8,128)(2,1)S(1)}, u32[]{:S(2)}, u32[]{:S(2)}) %collective-permute-start.24) | collective-permute-done | bytes 110624 | tf_op jit(solution)/shard_map/reduce_input_weights/ppermute | solution.py:916
  227.9 5.6 %shard_map.305 = f32[1024,768]{1,0:T(8,128)} custom-call(s32[10]{0:T(128)} %concatenate.30.info, bf16[1024,768]{1,0:T(8,128)(2,1)} %get-tuple-element.136.own, bf16[1024,768]{1,0:T(8,128)(2,1)} %copy-done.16, f32[8,768]{1,0:T(8,128)} %copy-done.38, f32[8,768]{1,0:T(8,128)} %copy-done.39, bf16[1024,768]{1,0:T(8,128)(2,1)} %tok.3, bf16[1024,768]{1,0:T(8,128)(2,1)} %cot.3, ...), custom_call_target="tpu_custom_call" | custom-call | flops 5500000256 | bytes 17500000 | tf_op jit(solution)/shard_map/pallas_call | solution.py:888
  243.3 2.3 shard_map.306
  (193 shorter events, 63.7 us)
Async XLA Ops:
  1.6 14.5 %collective-permute-start = (bf16[48,1024]{1,0:T(8,128)(2,1)S(1)}, bf16[48,1024]{1,0:T(8,128)(2,1)S(1)}, u32[]{:S(2)}, u32[]{:S(2)}) collective-permute-start(bf16[48,1024]{1,0:T(8,128)(2,1)S(1)} %fusion.10), channel_id=1, source_target_pairs={{0,8},{8,0},{16,24},{24,16},{1,9},{9,1},{17,25},{25,17},{2,10},{10... | collective-permute-start | bytes 294920 | tf_op jit(solution)/shard_map/gather_weights/ppermute | solution.py:916
  18.0 17.4 %collective-permute-start.4 = (bf16[64,1536]{1,0:T(8,128)(2,1)S(1)}, bf16[64,1536]{1,0:T(8,128)(2,1)S(1)}, u32[]{:S(2)}, u32[]{:S(2)}) collective-permute-start(bf16[64,1536]{1,0:T(8,128)(2,1)S(1)} %fusion.8.refs_0_), channel_id=1, source_target_pairs={{0,16},{8,24},{16,0},{24,8},{1,17},{9,25},{17,1},{25,9},{2,18},{10... | collective-permute-start | bytes 589832 | tf_op jit(solution)/shard_map/gather_weights/ppermute | solution.py:916
  21.5 17.3 %collective-permute-start.5 = (bf16[64,1536]{1,0:T(8,128)(2,1)S(1)}, bf16[64,1536]{1,0:T(8,128)(2,1)S(1)}, u32[]{:S(2)}, u32[]{:S(2)}) collective-permute-start(bf16[64,1536]{1,0:T(8,128)(2,1)S(1)} %fusion.8.refs_0_), channel_id=1, source_target_pairs={{0,24},{8,16},{16,8},{24,0},{1,25},{9,17},{17,9},{25,1},{2,26},{10... | collective-permute-start | bytes 589832 | tf_op jit(solution)/shard_map/gather_weights/ppermute | solution.py:916
  21.5 22.5 %collective-permute-start.6 = (bf16[192,1024]{1,0:T(8,128)(2,1)S(1)}, bf16[192,1024]{1,0:T(8,128)(2,1)S(1)}, u32[]{:S(2)}, u32[]{:S(2)}) collective-permute-start(bf16[192,1024]{1,0:T(8,128)(2,1)S(1)} %pad_maximum_fusion.1.refs_4_), channel_id=1, source_target_pairs={{0,2},{2,0},{4,6},{6,4},{1,3},{3,1},{5,7},{7,5},{8,10},{10,8},{12,... | collective-permute-start | bytes 1179656 | tf_op jit(solution)/shard_map/gather_weights/ppermute | solution.py:916
  23.2 22.5 %collective-permute-start.7 = (bf16[192,1024]{1,0:T(8,128)(2,1)S(1)}, bf16[192,1024]{1,0:T(8,128)(2,1)S(1)}, u32[]{:S(2)}, u32[]{:S(2)}) collective-permute-start(bf16[192,1024]{1,0:T(8,128)(2,1)S(1)} %pad_maximum_fusion.1.refs_4_), channel_id=1, source_target_pairs={{0,4},{2,6},{4,0},{6,2},{1,5},{3,7},{5,1},{7,3},{8,12},{10,14},{12... | collective-permute-start | bytes 1179656 | tf_op jit(solution)/shard_map/gather_weights/ppermute | solution.py:916
  24.8 21.0 %collective-permute-start.8 = (bf16[192,1024]{1,0:T(8,128)(2,1)S(1)}, bf16[192,1024]{1,0:T(8,128)(2,1)S(1)}, u32[]{:S(2)}, u32[]{:S(2)}) collective-permute-start(bf16[192,1024]{1,0:T(8,128)(2,1)S(1)} %pad_maximum_fusion.1.refs_4_), channel_id=1, source_target_pairs={{0,6},{2,4},{4,2},{6,0},{1,7},{3,5},{5,3},{7,1},{8,14},{10,12},{12... | collective-permute-start | bytes 1179656 | tf_op jit(solution)/shard_map/gather_weights/ppermute | solution.py:916
  38.9 36.7 %collective-permute-start.13 = (bf16[192,1536]{1,0:T(8,128)(2,1)S(1)}, bf16[192,1536]{1,0:T(8,128)(2,1)S(1)}, u32[]{:S(2)}, u32[]{:S(2)}) collective-permute-start(bf16[192,1536]{1,0:T(8,128)(2,1)S(1)} %pad_maximum_fusion.refs_0_), channel_id=1, source_target_pairs={{0,2},{2,0},{4,6},{6,4},{1,3},{3,1},{5,7},{7,5},{8,10},{10,8},{12,... | collective-permute-start | bytes 1769480 | tf_op jit(solution)/shard_map/gather_weights/ppermute | solution.py:916
  41.8 35.2 %collective-permute-start.14 = (bf16[192,1536]{1,0:T(8,128)(2,1)S(1)}, bf16[192,1536]{1,0:T(8,128)(2,1)S(1)}, u32[]{:S(2)}, u32[]{:S(2)}) collective-permute-start(bf16[192,1536]{1,0:T(8,128)(2,1)S(1)} %pad_maximum_fusion.refs_0_), channel_id=1, source_target_pairs={{0,4},{2,6},{4,0},{6,2},{1,5},{3,7},{5,1},{7,3},{8,12},{10,14},{12... | collective-permute-start | bytes 1769480 | tf_op jit(solution)/shard_map/gather_weights/ppermute | solution.py:916
  44.0 32.9 %collective-permute-start.15 = (bf16[192,1536]{1,0:T(8,128)(2,1)S(1)}, bf16[192,1536]{1,0:T(8,128)(2,1)S(1)}, u32[]{:S(2)}, u32[]{:S(2)}) collective-permute-start(bf16[192,1536]{1,0:T(8,128)(2,1)S(1)} %pad_maximum_fusion.refs_0_), channel_id=1, source_target_pairs={{0,6},{2,4},{4,2},{6,0},{1,7},{3,5},{5,3},{7,1},{8,14},{10,12},{12... | collective-permute-start | bytes 1769480 | tf_op jit(solution)/shard_map/gather_weights/ppermute | solution.py:916
  70.0 15.3 %collective-permute-start.10 = (bf16[784,128]{1,0:T(8,128)(2,1)}, bf16[784,128]{1,0:T(8,128)(2,1)S(1)}, u32[]{:S(2)}, u32[]{:S(2)}) collective-permute-start(bf16[784,128]{1,0:T(8,128)(2,1)} %get-tuple-element.88), channel_id=1, source_target_pairs={{0,2},{2,4},{4,6},{1,3},{3,5},{5,7},{8,10},{10,12},{12,14},{9,11},... | collective-permute-start | bytes 602120 | tf_op jit(solution)/shard_map/ppermute | solution.py:908
  72.1 13.3 %collective-permute-start.11 = (bf16[784,128]{1,0:T(8,128)(2,1)}, bf16[784,128]{1,0:T(8,128)(2,1)S(1)}, u32[]{:S(2)}, u32[]{:S(2)}) collective-permute-start(bf16[784,128]{1,0:T(8,128)(2,1)} %get-tuple-element.88), channel_id=1, source_target_pairs={{0,4},{2,6},{1,5},{3,7},{8,12},{10,14},{9,13},{11,15},{16,20},{18,... | collective-permute-start | bytes 602120 | tf_op jit(solution)/shard_map/ppermute | solution.py:908
  114.8 29.2 %collective-permute-start.17 = (bf16[784,128]{1,0:T(8,128)(2,1)}, bf16[784,128]{1,0:T(8,128)(2,1)S(1)}, u32[]{:S(2)}, u32[]{:S(2)}) collective-permute-start(bf16[784,128]{1,0:T(8,128)(2,1)} %get-tuple-element.105), channel_id=1, source_target_pairs={{2,0},{4,2},{6,4},{3,1},{5,3},{7,5},{10,8},{12,10},{14,12},{11,9},... | collective-permute-start | bytes 602120 | tf_op jit(solution)/shard_map/ppermute | solution.py:908
  116.1 27.9 %collective-permute-start.18 = (bf16[784,128]{1,0:T(8,128)(2,1)}, bf16[784,128]{1,0:T(8,128)(2,1)S(1)}, u32[]{:S(2)}, u32[]{:S(2)}) collective-permute-start(bf16[784,128]{1,0:T(8,128)(2,1)} %get-tuple-element.105), channel_id=1, source_target_pairs={{4,0},{6,2},{5,1},{7,3},{12,8},{14,10},{13,9},{15,11},{20,16},{22,... | collective-permute-start | bytes 602120 | tf_op jit(solution)/shard_map/ppermute | solution.py:908
  117.4 26.7 %collective-permute-start.19 = (bf16[784,128]{1,0:T(8,128)(2,1)}, bf16[784,128]{1,0:T(8,128)(2,1)S(1)}, u32[]{:S(2)}, u32[]{:S(2)}) collective-permute-start(bf16[784,128]{1,0:T(8,128)(2,1)} %get-tuple-element.105), channel_id=1, source_target_pairs={{6,0},{7,1},{14,8},{15,9},{22,16},{23,17},{30,24},{31,25}} | collective-permute-start | bytes 602120 | tf_op jit(solution)/shard_map/ppermute | solution.py:908
  138.5 41.3 %collective-permute-start.33 = (bf16[192,1536]{1,0:T(8,128)(2,1)}, bf16[192,1536]{1,0:T(8,128)(2,1)S(1)}, u32[]{:S(2)}, u32[]{:S(2)}) collective-permute-start(bf16[192,1536]{1,0:T(8,128)(2,1)} %get-tuple-element.142), channel_id=1, source_target_pairs={{0,2},{2,0},{4,6},{6,4},{1,3},{3,1},{5,7},{7,5},{8,10},{10,8},{12,... | collective-permute-start | bytes 1769480 | tf_op jit(solution)/shard_map/reduce_gate_weights/ppermute | solution.py:916
  140.6 41.2 %collective-permute-start.34 = (bf16[192,1536]{1,0:T(8,128)(2,1)}, bf16[192,1536]{1,0:T(8,128)(2,1)S(1)}, u32[]{:S(2)}, u32[]{:S(2)}) collective-permute-start(bf16[192,1536]{1,0:T(8,128)(2,1)} %get-tuple-element.143), channel_id=1, source_target_pairs={{0,4},{2,6},{4,0},{6,2},{1,5},{3,7},{5,1},{7,3},{8,12},{10,14},{12... | collective-permute-start | bytes 1769480 | tf_op jit(solution)/shard_map/reduce_gate_weights/ppermute | solution.py:916
  143.9 38.0 %collective-permute-start.35 = (bf16[192,1536]{1,0:T(8,128)(2,1)}, bf16[192,1536]{1,0:T(8,128)(2,1)S(1)}, u32[]{:S(2)}, u32[]{:S(2)}) collective-permute-start(bf16[192,1536]{1,0:T(8,128)(2,1)} %get-tuple-element.144), channel_id=1, source_target_pairs={{0,6},{2,4},{4,2},{6,0},{1,7},{3,5},{5,3},{7,1},{8,14},{10,12},{12... | collective-permute-start | bytes 1769480 | tf_op jit(solution)/shard_map/reduce_gate_weights/ppermute | solution.py:916
  144.0 77.9 %collective-permute-start.16 = (bf16[1024,384]{1,0:T(8,128)(2,1)S(1)}, bf16[1024,384]{1,0:T(8,128)(2,1)S(1)}, u32[]{:S(2)}, u32[]{:S(2)}) collective-permute-start(bf16[1024,384]{1,0:T(8,128)(2,1)S(1)} %copy-done.17), channel_id=1, source_target_pairs={{0,1},{1,0},{2,3},{3,2},{4,5},{5,4},{6,7},{7,6},{8,9},{9,8},{10,11... | collective-permute-start | bytes 2359304 | tf_op jit(solution)/shard_map/layer_out/ppermute | solution.py:912
  179.9 22.2 %collective-permute-start.21 = (bf16[192,1152]{1,0:T(8,128)(2,1)}, bf16[192,1152]{1,0:T(8,128)(2,1)S(1)}, u32[]{:S(2)}, u32[]{:S(2)}) collective-permute-start(bf16[192,1152]{1,0:T(8,128)(2,1)} %get-tuple-element.129), channel_id=1, source_target_pairs={{0,4},{2,6},{4,0},{6,2},{1,5},{3,7},{5,1},{7,3},{8,12},{10,14},{12... | collective-permute-start | bytes 1327112 | tf_op jit(solution)/shard_map/ppermute | solution.py:916
  181.8 23.7 %collective-permute-start.22 = (bf16[192,1152]{1,0:T(8,128)(2,1)}, bf16[192,1152]{1,0:T(8,128)(2,1)S(1)}, u32[]{:S(2)}, u32[]{:S(2)}) collective-permute-start(bf16[192,1152]{1,0:T(8,128)(2,1)} %get-tuple-element.130), channel_id=1, source_target_pairs={{0,6},{2,4},{4,2},{6,0},{1,7},{3,5},{5,3},{7,1},{8,14},{10,12},{12... | collective-permute-start | bytes 1327112 | tf_op jit(solution)/shard_map/ppermute | solution.py:916
  182.2 24.5 %collective-permute-start.36 = (bf16[48,1536]{1,0:T(8,128)(2,1)S(1)}, bf16[48,1536]{1,0:T(8,128)(2,1)S(1)}, u32[]{:S(2)}, u32[]{:S(2)}) collective-permute-start(bf16[48,1536]{1,0:T(8,128)(2,1)S(1)} %get-tuple-element.162), channel_id=1, source_target_pairs={{0,8},{8,0},{16,24},{24,16},{1,9},{9,1},{17,25},{25,17},{2,10},{10... | collective-permute-start | bytes 442376 | tf_op jit(solution)/shard_map/reduce_gate_weights/ppermute | solution.py:916
  191.6 15.3 %collective-permute-start.37 = (bf16[48,1536]{1,0:T(8,128)(2,1)S(1)}, bf16[48,1536]{1,0:T(8,128)(2,1)S(1)}, u32[]{:S(2)}, u32[]{:S(2)}) collective-permute-start(bf16[48,1536]{1,0:T(8,128)(2,1)S(1)} %get-tuple-element.164), channel_id=1, source_target_pairs={{0,16},{8,24},{16,0},{24,8},{1,17},{9,25},{17,1},{25,9},{2,18},{10... | collective-permute-start | bytes 442376 | tf_op jit(solution)/shard_map/reduce_gate_weights/ppermute | solution.py:916
  205.6 20.5 %collective-permute-start.27 = (bf16[1024,768]{1,0:T(8,128)(2,1)}, bf16[1024,768]{1,0:T(8,128)(2,1)S(1)}, u32[]{:S(2)}, u32[]{:S(2)}) collective-permute-start(bf16[1024,768]{1,0:T(8,128)(2,1)} %get-tuple-element.136.own), channel_id=1, source_target_pairs={{0,1},{1,0},{2,3},{3,2},{4,5},{5,4},{6,7},{7,6},{8,9},{9,8},{10,11... | collective-permute-start | bytes 4718600 | tf_op jit(solution)/shard_map/ppermute | solution.py:912
  219.8 17.1 %collective-permute-start.39 = (bf16[48,1536]{1,0:T(8,128)(2,1)S(1)}, bf16[48,1536]{1,0:T(8,128)(2,1)S(1)}, u32[]{:S(2)}, u32[]{:S(2)}) collective-permute-start(bf16[48,1536]{1,0:T(8,128)(2,1)S(1)} %fusion.4.refs_0_), channel_id=1, source_target_pairs={{0,2},{2,0},{4,6},{6,4},{1,3},{3,1},{5,7},{7,5},{8,10},{10,8},{12,... | collective-permute-start | bytes 442376 | tf_op jit(solution)/shard_map/last_hop/ppermute | solution.py:916
  (58 other events, 515.5 us)

commit v6 on v4

--- a/solution.py
+++ b/solution.py
@@ -12,7 +12,7 @@
 HEAD = 64
 LANES = 128
 EPS = 1e-05
-VMEM = 56 * 1024 * 1024
+MEGA = 1024 * 1024
 F32 = jnp.float32
 BF16 = jnp.bfloat16
 
@@ -39,6 +39,10 @@
 
 def sigmoid(value):
     return 1.0 / (1.0 + jnp.exp(-value))
+
+
+def gate_sigmoid(value):
+    return 0.5 * jnp.tanh(0.5 * value) + 0.5
 
 
 def softplus(value):
@@ -349,7 +353,7 @@
     v_o[...] = v
     ext[8 : 8 + BLOCK, :] = v.astype(F32)
     pre = conv_pre(place, block, ext, par, channels)
-    act = (pre * sigmoid(pre)).astype(BF16)
+    act = (pre * gate_sigmoid(pre)).astype(BF16)
     xc = act[:, :inner]
     bq = act[:, inner : inner + state]
     cq = act[:, inner + state :]
@@ -426,7 +430,7 @@
     y = ypart[...] + expand(enter_weights(place, block, cum[...]), spread) * dot_nt(cq, low)
     y_o[...] = y
     gate = z[...].astype(F32)
-    gated = y * gate * sigmoid(gate)
+    gated = y * gate * gate_sigmoid(gate)
     squares = jnp.sum(gated * gated, axis=1, keepdims=True)
     cross = jnp.sum(par[6:7, :inner] * dn[...] * gated, axis=1, keepdims=True)
     lane = iota((BLOCK, LANES), 1)
@@ -458,7 +462,7 @@
     cross = column[:, 1:2]
     gain = par[6:7, :inner]
     gate = z[...].astype(F32)
-    sig = sigmoid(gate)
+    sig = gate_sigmoid(gate)
     silu = gate * sig
     mixed = y[...]
     gated = mixed * silu
@@ -554,22 +558,27 @@
         cut_pieces(place, dp_count, gwo, parts, slice(inner, 2 * inner))
 
 
-def state_back_kernel(counts, heads, packet_count, info, *refs):
+def state_back_kernel(counts, heads, dp_count, packet_count, part_count, info, *refs):
     packets = refs[:packet_count]
     (
-        exits, h, xc, bc, cum, pre_step, de, dxc, dcq, dbq, rows, cols, decay, dtp, spread,
-        act_o, ddt_o, small_o,
-        start, factor,
-    ) = refs[packet_count:]
+        exits, h, xc, bc, cum, pre_step, de, dxc, dcq, dbq, rows, cols, decay, v, v_tail, halo_v, halo_normed,
+        normed, small_gate, par, dtp, spread,
+        packed_o, back_o,
+    ) = refs[packet_count : -6 - part_count]
+    parts = refs[-6 - part_count : -6]
+    start, factor, ext, grad_ext, acc, small_o = refs[-6:]
     step_id = pl.program_id(0)
     block = pl.num_programs(0) - 1 - step_id
     place = Place(info, counts)
     inner = heads * HEAD
+    channels = inner + 2 * LANES
 
     @pl.when(step_id == 0)
     def _():
         start[...] = merge_packets([packet[...] for packet in packets], inner)
         factor[...] = jnp.ones_like(factor)
+        acc[...] = jnp.zeros_like(acc)
+        grad_ext[...] = jnp.zeros_like(grad_ext)
         small_o[...] = jnp.zeros_like(small_o)
 
     here = decay[0, 0:1, :]
@@ -592,10 +601,9 @@
     end_weight = end_kernel * step
     end_wide = expand(end_weight, spread)
     spread_b = dot_nt(bq, low)
-    act_o[:, :inner] = dxc[...] + end_wide * spread_b
+    grad_x = dxc[...] + end_wide * spread_b
     grad_end = reduce_heads(x_float * spread_b, spread)
-    act_o[:, inner : inner + LANES] = dbq[...] + dot((x_float * end_wide).astype(BF16), low)
-    act_o[:, inner + LANES :] = dcq[...]
+    grad_b = dbq[...] + dot((x_float * end_wide).astype(BF16), low)
     end_part = grad_end * end_weight
     last = iota((BLOCK, LANES), 0) == BLOCK - 1
     grad_cum = rows[...] - cols[...] * step - end_part + de[...] * enter_weights(place, block, cums)
@@ -608,27 +616,8 @@
     grad_step = cols[...] + grad_end * end_kernel - rates * grad_log
     heads_lane = iota((BLOCK, LANES), 1) < heads
     grad_pre_dt = jnp.where(heads_lane, grad_step * sigmoid(pre_dt), 0.0) * valid
-    ddt_o[...] = grad_pre_dt.astype(BF16)
-    small_o[0:1, :] += jnp.sum(grad_pre_dt, axis=0, keepdims=True)
-    small_o[1:2, :] += jnp.sum(grad_log * (-rates * step), axis=0, keepdims=True)
-
-
-def conv_back_kernel(counts, heads, dp_count, part_count, info, *refs):
-    act, ddt, v, v_tail, halo_v, halo_normed, normed, small_gate, small_state, par, spread = refs[:11]
-    packed_o, back_o = refs[11:13]
-    parts = refs[13 : 13 + part_count]
-    ext, grad_ext, acc, small_o = refs[13 + part_count :]
-    step_id = pl.program_id(0)
-    block = pl.num_programs(0) - 1 - step_id
-    place = Place(info, counts)
-    inner = heads * HEAD
-    channels = inner + 2 * LANES
-
-    @pl.when(step_id == 0)
-    def _():
-        acc[...] = jnp.zeros_like(acc)
-        grad_ext[...] = jnp.zeros_like(grad_ext)
-        small_o[...] = jnp.zeros_like(small_o)
+    small_o[6:7, :LANES] += jnp.sum(grad_pre_dt, axis=0, keepdims=True)
+    small_o[7:8, :LANES] += jnp.sum(grad_log * (-rates * step), axis=0, keepdims=True)
 
     ext[8 : 8 + BLOCK, :] = v[...].astype(F32)
 
@@ -641,9 +630,9 @@
         ext[0:8, :] = v_tail[...].astype(F32)[8:16, :]
 
     pre = conv_pre(place, block, ext, par, channels)
-    sig = sigmoid(pre)
+    sig = gate_sigmoid(pre)
     slope = sig * (1.0 + pre * (1.0 - sig))
-    grad_pre = act[...] * slope
+    grad_pre = jnp.concatenate([grad_x, grad_b, dcq[...]], axis=1) * slope
     small_o[4:5, :] += jnp.sum(grad_pre, axis=0, keepdims=True)
     carry = grad_ext[0:8, :]
     grad_ext[0:BLOCK, :] = jnp.zeros((BLOCK, channels), F32)
@@ -653,7 +642,7 @@
         masked = grad_pre * same_mask(place, block, tap)
         small_o[tap : tap + 1, :] += jnp.sum(masked * ext[first : first + BLOCK, :], axis=0, keepdims=True)
         grad_ext[first : first + BLOCK, :] += par[tap : tap + 1, :channels] * masked
-    packed = jnp.concatenate([grad_ext[8 : 8 + BLOCK, :].astype(BF16), ddt[...]], axis=1)
+    packed = jnp.concatenate([grad_ext[8 : 8 + BLOCK, :].astype(BF16), grad_pre_dt.astype(BF16)], axis=1)
     packed_o[...] = packed
     acc[...] += dot_tn(normed[...], packed)
 
@@ -662,8 +651,6 @@
         back = jnp.concatenate([jnp.zeros((8, channels), F32), grad_ext[0:8, :]], axis=0).astype(BF16)
         back_o[...] = back
         acc[:, :channels] += dot_tn(halo_normed[...], back)
-        small_o[6:7, :LANES] = small_state[0:1, :]
-        small_o[7:8, :LANES] = small_state[1:2, :]
         skip = reduce_heads(jnp.broadcast_to(small_gate[1:2, :], (8, inner)), spread)[0:1, :]
         acc[:, channels:] += pack_parameters(dp_count, heads, small_o, small_gate[0:1, :], skip)
         cut_pieces(place, dp_count, acc, parts, slice(0, channels + LANES))
@@ -778,7 +765,7 @@
     skip_o[...] = row[:, 2 * heads : 3 * heads]
 
 
-def call(body, steps, info, operands, outputs, scratch=(), reverse=False, micros=1):
+def call(body, steps, info, operands, outputs, scratch=(), reverse=False, micros=1, mega=20):
     def at(index):
         return steps - 1 - index if reverse else index
 
@@ -805,7 +792,7 @@
         out_shape=[shape for shape, _ in outputs],
         scratch_shapes=list(scratch),
         compiler_params=pltpu.CompilerParams(
-            dimension_semantics=("arbitrary",), vmem_limit_bytes=VMEM
+            dimension_semantics=("arbitrary",), vmem_limit_bytes=mega * MEGA
         ),
         cost_estimate=pl.CostEstimate(
             flops=micros * 1_100_000_000, bytes_accessed=micros * 3_500_000, transcendentals=0
@@ -967,6 +954,7 @@
             pltpu.VMEM((8, LANES), F32),
         ],
         micros=20,
+        mega=28,
     )
     packets = [(shifted(packet, "ctx", step), "whole") for step in range(1, ctx_count)]
     wz_spec = pl.BlockSpec((width, inner), lambda i: (0, 0))
@@ -978,6 +966,7 @@
         [(value, "whole") for value in w2_parts] + [(normed, "rows"), (cotangent, "rows")],
         [out((width, 2 * inner), BF16, "whole"), row_out(inner, BF16), row_out(inner, F32)],
         micros=7,
+        mega=20,
     )
     y, hb, h, stat = call(
         functools.partial(apply_kernel, counts, len(packets)),
@@ -1044,6 +1033,7 @@
         ],
         reverse=True,
         micros=15,
+        mega=24,
     )
     packets = [(shifted(packet, "ctx", -step), "whole") for step in range(1, ctx_count)]
     with jax.named_scope("layer_out"):
@@ -1080,11 +1070,12 @@
         + [out((width // parts, 2 * inner), BF16, "whole")] * parts,
         [pltpu.VMEM((width, inner), F32), pltpu.VMEM((LANES, BLOCK), F32)],
         micros=18,
+        mega=24,
     )
     with jax.named_scope("reduce_gate_weights"):
         total2 = ctx_sum(g2) if parts > 1 else g2[0]
-    grad_act, ddt, small_state = call(
-        functools.partial(state_back_kernel, counts, heads, len(packets)),
+    packed, back, *g1 = call(
+        functools.partial(state_back_kernel, counts, heads, dp_count, len(packets), parts),
         steps,
         info,
         packets
@@ -1102,48 +1093,36 @@
             (row_sums, "rows"),
             (col_sums, "rows"),
             (decay, "block"),
-            (dtp, "whole"),
-            (spread, "whole"),
-        ],
-        [row_out(channels, F32), row_out(LANES, BF16), out((8, LANES), F32, "whole")],
-        [pltpu.VMEM((inner, LANES), F32), pltpu.VMEM((8, LANES), F32)],
-        reverse=True,
-        micros=11,
-    )
-    with jax.named_scope("reduce_gate_weights"):
-        if parts > 1:
-            total2 = dp_sum(total2)
-        else:
-            total2 = whole_sum(total2)
-    packed, back, *g1 = call(
-        functools.partial(conv_back_kernel, counts, heads, dp_count, parts),
-        steps,
-        info,
-        [
-            (grad_act, "rows"),
-            (ddt, "rows"),
             (v, "rows"),
             (v, "tail"),
             (halo_v, "whole"),
             (halo_normed, "whole"),
             (normed, "rows"),
             (small_gate, "whole"),
-            (small_state, "whole"),
             (par, "whole"),
+            (dtp, "whole"),
             (spread, "whole"),
         ],
         [row_out(channels + LANES, BF16), out((16, channels), BF16, "whole")]
         + [out((width // parts, channels + LANES), BF16, "whole")] * parts,
         [
+            pltpu.VMEM((inner, LANES), F32),
+            pltpu.VMEM((8, LANES), F32),
             pltpu.VMEM((8 + BLOCK, channels), F32),
             pltpu.VMEM((8 + BLOCK, channels), F32),
             pltpu.VMEM((width, channels + LANES), F32),
             pltpu.VMEM((8, channels), F32),
         ],
         reverse=True,
-        micros=18,
-    )
+        micros=25,
+        mega=32,
+    )
+    with jax.named_scope("reduce_gate_weights"):
+        total2 = dp_sum(total2) if parts > 1 else whole_sum(total2)
     norm_rows = part_rows * dp_count
+    if parts > 1:
+        g1 = [g1[0]] + [partnered(g1[mask], "ctx", mask) for mask in range(1, parts)]
+        packed, g1[1] = lax.optimization_barrier((packed, g1[1]))
     partial, halo_grad, norm_part = call(
         functools.partial(input_back_kernel, counts, dp_count, parts),
         steps,
@@ -1174,7 +1153,7 @@
     with jax.named_scope("reduce_input_weights"):
         norm_part = jnp.pad(norm_part, ((0, 0), (channels, 0)))
         if parts > 1:
-            total1 = dp_sum(ctx_sum(g1) + norm_part)
+            total1 = dp_sum(sum(piece.astype(F32) for piece in g1) + norm_part)
         else:
             total1 = whole_sum((g1[0].astype(F32) + norm_part).astype(BF16))
         across = swapped(total1[:, inner:])

time: 255 us -> 249 us (0.976)
  local copies, waits for them, and re-layouts: 13 us -> 50.4 us
  Pallas kernels: 119 us -> 86.6 us
  waiting for transfers between devices: 43.3 us -> 32.9 us
    unnamed x89 -> x135, local copies, waits for them, and re-layouts: 8.44 us -> 46.6 us
    pallas_call x11 -> x10, Pallas kernels: 119 us -> 86.6 us  [call(): pl.pallas_call(body, grid=(steps,), in_specs=[pl.BlockSpec(memory_space=p...]
    ppermute x30, waiting for transfers between devices: 42 us -> 31.9 us  [partnered(): lax.ppermute(value, axis, [(one, one ^ mask) for one in range(lax.axis_si...]
  transfers between devices with their start and end apart: 42 -> 42, of which waited for: 8 -> 9; matrix products, arithmetic and copies ran while one was open for 5% -> 5% of each run, Pallas kernels for 37% -> 28%
where the time goes in v6:
time: 249 us; the launch traced here: 248 us
  Pallas kernels  86.6 us (35%)
  starting transfers between devices  63.6 us (26%)
  local copies, waits for them, and re-layouts  50.4 us (20%)
  waiting for transfers between devices  32.9 us (13%)
  other arithmetic  8.49 us (3%)
  blocking collectives  3.39 us (1%)
    pallas_call x10, Pallas kernels, call(): pl.pallas_call(body, grid=(steps,), in_specs=[pl.BlockSpec(memory_space=p...  86.6 us
    unnamed x135, local copies, waits for them, and re-layouts  46.6 us
    ppermute x30, starting transfers between devices, partnered(): lax.ppermute(value, axis, [(one, one ^ mask) for one in range(lax.axis_si...  45.1 us
    ppermute x30, waiting for transfers between devices, partnered(): lax.ppermute(value, axis, [(one, one ^ mask) for one in range(lax.axis_si...  31.9 us
    ppermute x7, starting transfers between devices, shifted(): lax.ppermute(value, axis, [(source, source + steps) for source in range(f...  14.5 us
  transfers between devices with their start and end apart: 42, of which 9 were waited for; matrix products, arithmetic and copies ran while one was open for 5% of the time, Pallas kernels for 28%

profile of v6, /device:TPU:0, one launch (start us, length us, event | category | flops | bytes accessed | tf_op | source)
XLA Modules:
  0.0 247.8 jit_solution(16825445788299288700)
XLA Ops:
  1.7 3.1 %collective-permute-start = (bf16[48,1024]{1,0:T(8,128)(2,1)S(1)}, bf16[48,1024]{1,0:T(8,128)(2,1)S(1)}, u32[]{:S(2)}, u32[]{:S(2)}) collective-permute-start(bf16[48,1024]{1,0:T(8,128)(2,1)S(1)} %fusion.10), channel_id=1, source_target_pairs={{0,8},{8,0},{16,24},{24,16},{1,9},{9,1},{17,25},{25,17},{2,10},{10... | collective-permute-start | bytes 294920 | tf_op jit(solution)/shard_map/gather_weights/ppermute | solution.py:814
  4.8 2.6 %collective-permute-start.1 = (bf16[48,1024]{1,0:T(8,128)(2,1)S(1)}, bf16[48,1024]{1,0:T(8,128)(2,1)S(1)}, u32[]{:S(2)}, u32[]{:S(2)}) collective-permute-start(bf16[48,1024]{1,0:T(8,128)(2,1)S(1)} %fusion.10), channel_id=1, source_target_pairs={{0,16},{8,24},{16,0},{24,8},{1,17},{9,25},{17,1},{25,9},{2,18},{10... | collective-permute-start | bytes 294920 | tf_op jit(solution)/shard_map/gather_weights/ppermute | solution.py:814
  17.1 3.2 %collective-permute-start.4 = (bf16[64,1536]{1,0:T(8,128)(2,1)S(1)}, bf16[64,1536]{1,0:T(8,128)(2,1)S(1)}, u32[]{:S(2)}, u32[]{:S(2)}) collective-permute-start(bf16[64,1536]{1,0:T(8,128)(2,1)S(1)} %fusion.8.refs_0_), channel_id=1, source_target_pairs={{0,16},{8,24},{16,0},{24,8},{1,17},{9,25},{17,1},{25,9},{2,18},{10... | collective-permute-start | bytes 589832 | tf_op jit(solution)/shard_map/gather_weights/ppermute | solution.py:814
  24.5 2.4 collective-permute-start.8
  27.8 6.8 %collective-permute-done.4.refs_2_ = bf16[64,1536]{1,0:T(8,128)(2,1)S(1)} collective-permute-done((bf16[64,1536]{1,0:T(8,128)(2,1)S(1)}, bf16[64,1536]{1,0:T(8,128)(2,1)S(1)}, u32[]{:S(2)}, u32[]{:S(2)}) %collective-permute-start.4) | collective-permute-done | bytes 196640 | tf_op jit(solution)/shard_map/gather_weights/ppermute | solution.py:814
  34.5 3.4 %collective-permute-start.9 = (bf16[16,768]{1,0:T(8,128)(2,1)S(1)}, bf16[16,768]{1,0:T(8,128)(2,1)S(1)}, u32[]{:S(2)}, u32[]{:S(2)}) collective-permute-start(bf16[16,768]{1,0:T(8,128)(2,1)S(1)} %constant_dynamic-slice_fusion), channel_id=1, source_target_pairs={{0,2},{2,4},{4,6},{1,3},{3,5},{5,7},{8,10},{10,12},{12,14},{9,11},... | collective-permute-start | bytes 73736 | tf_op jit(solution)/shard_map/ppermute | solution.py:806
  44.6 17.6 %shard_map.297 = (bf16[768,1152]{1,0:T(8,128)(2,1)S(1)}, f32[8,1024]{1,0:T(8,128)S(1)}, bf16[1024,768]{1,0:T(8,128)(2,1)S(1)}, bf16[16,768]{1,0:T(8,128)(2,1)S(1...) custom-call(s32[10]{0:T(128)S(1)} %concatenate.30.info, ...), custom_call_target="tpu_custom_call" | custom-call | flops 22000001024 | bytes 70000000 | tf_op jit(solution)/shard_map/pallas_call | solution.py:786
  68.0 3.8 %collective-permute-start.11 = (bf16[784,128]{1,0:T(8,128)(2,1)S(1)}, bf16[784,128]{1,0:T(8,128)(2,1)S(1)}, u32[]{:S(2)}, u32[]{:S(2)}) collective-permute-start(bf16[784,128]{1,0:T(8,128)(2,1)S(1)} %get-tuple-element.85), channel_id=1, source_target_pairs={{0,4},{2,6},{1,5},{3,7},{8,12},{10,14},{9,13},{11,15},{16,20},{18,... | collective-permute-start | bytes 602120 | tf_op jit(solution)/shard_map/ppermute | solution.py:806
  73.1 4.0 %shard_map.298 = (bf16[768,1536]{1,0:T(8,128)(2,1)S(1)}, bf16[1024,768]{1,0:T(8,128)(2,1)S(1)}, f32[1024,768]{1,0:T(8,128)S(1)}) custom-call(s32[10]{0:T(128)S(1)} %concatenate.30.info, bf16[192,1536]{1,0:T(8,128)(2,1)S(1)} %pad_maximum_fusion.refs_0_, bf16[192,1536]{1,0:T(8,128)(2,1)S(1)} %collective-permute-done.13.refs_1_, ...), custom_call_target="tpu_custom_call" | custom-call | flops 7699999744 | bytes 24500000 | tf_op jit(solution)/shard_map/pallas_call | solution.py:786
  77.2 4.2 %shard_map.299 = (f32[1024,768]{1,0:T(8,128)S(1)}, bf16[4,768,128]{2,1,0:T(8,128)(2,1)S(1)}, f32[4,768,128]{2,1,0:T(8,128)S(1)}, f32[8,1024]{1,0:T(8,128)S(1)}) custom-call(s32[10]{0:T(128)S(1)} %concatenate.30.info, bf16[784,128]{1,0:T(8,128)(2,1)S(1)} %collective-permute-done.10.refs_0_, bf16[784,128]{1,0:T(8,128)(2,1)S(1)} %collective-permute-done.11.refs_1_, ...), custom_call_target="tpu_custom_call" | custom-call | flops 8800000000 | bytes 28000000 | tf_op jit(solution)/shard_map/pallas_call | solution.py:786
  85.2 3.4 %psum.7.stat = f32[8,1024]{1,0:T(8,128)S(1)} all-reduce(f32[8,1024]{1,0:T(8,128)S(1)} %get-tuple-element.95), channel_id=1, replica_groups=mesh['dp'=4,'ctx'=4,'tp'=2] {'tp'}, use_global_device_ids=true, to_apply=%region_1.2 | all-reduce | flops 8192 | bytes 65536 | tf_op jit(solution)/shard_map/psum | solution.py:996
  103.0 11.1 %shard_map.300 = (bf16[1024,384]{1,0:T(8,128)(2,1)S(1)}, bf16[1024,384]{1,0:T(8,128)(2,1)S(1)}, bf16[768,768]{1,0:T(8,128)(2,1)S(1)}, f32[8,768]{1,0:T(8,128)S(1...) custom-call(s32[10]{0:T(128)S(1)} %concatenate.30.info, ...), custom_call_target="tpu_custom_call" | custom-call | flops 16499999744 | bytes 52500000 | tf_op jit(solution)/shard_map/pallas_call | solution.py:786
  126.1 15.1 %shard_map.301 = (f32[1024,768]{1,0:T(8,128)S(1)}, f32[1024,128]{1,0:T(8,128)S(1)}, f32[1024,128]{1,0:T(8,128)S(1)}, f32[1024,128]{1,0:T(8,128)S(1)}, f32[1024,1...) custom-call(s32[10]{0:T(128)S(1)} %concatenate.30.info, ...), custom_call_target="tpu_custom_call" | custom-call | flops 19800000512 | bytes 63000000 | tf_op jit(solution)/shard_map/pallas_call | solution.py:786
  146.4 3.1 %collective-permute-start.34 = (bf16[192,1536]{1,0:T(8,128)(2,1)S(1)}, bf16[192,1536]{1,0:T(8,128)(2,1)S(1)}, u32[]{:S(2)}, u32[]{:S(2)}) collective-permute-start(bf16[192,1536]{1,0:T(8,128)(2,1)S(1)} %get-tuple-element.137), channel_id=1, source_target_pairs={{0,4},{2,6},{4,0},{6,2},{1,5},{3,7},{5,1},{7,3},{8,12},{10,14},{12... | collective-permute-start | bytes 1769480 | tf_op jit(solution)/shard_map/reduce_gate_weights/ppermute | solution.py:814
  162.6 22.6 %shard_map.302 = (bf16[1024,1152]{1,0:T(8,128)(2,1)S(1)}, bf16[16,1024]{1,0:T(8,128)(2,1)S(1)}, bf16[192,1152]{1,0:T(8,128)(2,1)S(1)}, bf16[192,1152]{1,0:T(8,12...) custom-call(s32[10]{0:T(128)S(1)} %concatenate.30.info, ...), custom_call_target="tpu_custom_call" | custom-call | flops 27499999232 | bytes 87500000 | tf_op jit(solution)/shard_map/pallas_call | solution.py:786
  189.2 9.0 %collective-permute-done.20 = bf16[192,1152]{1,0:T(8,128)(2,1)S(1)} collective-permute-done((bf16[192,1152]{1,0:T(8,128)(2,1)S(1)}, bf16[192,1152]{1,0:T(8,128)(2,1)S(1)}, u32[]{:S(2)}, u32[]{:S(2)}) %collective-permute-start.20) | collective-permute-done | bytes 442400 | tf_op jit(solution)/shard_map/ppermute | solution.py:814
  198.3 5.0 %shard_map.303 = (bf16[1024,768]{1,0:T(8,128)(2,1)S(1)}, f32[8,768]{1,0:T(8,128)S(1)}, f32[192,128]{1,0:T(8,128)S(1)}) custom-call(s32[10]{0:T(128)S(1)} %concatenate.30.info, bf16[1024,1152]{1,0:T(8,128)(2,1)S(1)} %get-tuple-element.125.packed, bf16[16,1024]{1,0:T(8,128)(2,1)S(1)} %get-tuple-element.126.back, f32[1024,768]{1,0:T(8,128)S(1)} %get-tuple-element.127.dnz, ...), custom_call_target="tpu_custom_call" | custom-call | flops 5500000256 | bytes 17500000 | tf_op jit(solution)/shard_map/pallas_call | solution.py:786
  203.2 5.5 %collective-permute-done.21 = bf16[192,1152]{1,0:T(8,128)(2,1)S(1)} collective-permute-done((bf16[192,1152]{1,0:T(8,128)(2,1)S(1)}, bf16[192,1152]{1,0:T(8,128)(2,1)S(1)}, u32[]{:S(2)}, u32[]{:S(2)}) %collective-permute-start.21) | collective-permute-done | bytes 442400 | tf_op jit(solution)/shard_map/ppermute | solution.py:814
  208.7 3.7 %collective-permute-start.38 = (bf16[48,1536]{1,0:T(8,128)(2,1)S(1)}, bf16[48,1536]{1,0:T(8,128)(2,1)S(1)}, u32[]{:S(2)}, u32[]{:S(2)}) collective-permute-start(bf16[48,1536]{1,0:T(8,128)(2,1)S(1)} %get-tuple-element.157), channel_id=1, source_target_pairs={{0,24},{8,16},{16,8},{24,0},{1,25},{9,17},{17,9},{25,1},{2,26},{10... | collective-permute-start | bytes 442376 | tf_op jit(solution)/shard_map/reduce_gate_weights/ppermute | solution.py:814
  213.4 3.5 %collective-permute-done.38 = bf16[48,1536]{1,0:T(8,128)(2,1)S(1)} collective-permute-done((bf16[48,1536]{1,0:T(8,128)(2,1)S(1)}, bf16[48,1536]{1,0:T(8,128)(2,1)S(1)}, u32[]{:S(2)}, u32[]{:S(2)}) %collective-permute-start.38) | collective-permute-done | bytes 147488 | tf_op jit(solution)/shard_map/reduce_gate_weights/ppermute | solution.py:814
  216.9 3.9 %collective-permute-start.25 = (bf16[48,1152]{1,0:T(8,128)(2,1)S(1)}, bf16[48,1152]{1,0:T(8,128)(2,1)S(1)}, u32[]{:S(2)}, u32[]{:S(2)}) collective-permute-start(bf16[48,1152]{1,0:T(8,128)(2,1)S(1)} %get-tuple-element.160), channel_id=1, source_target_pairs={{0,24},{8,16},{16,8},{24,0},{1,25},{9,17},{17,9},{25,1},{2,26},{10... | collective-permute-start | bytes 331784 | tf_op jit(solution)/shard_map/reduce_input_weights/ppermute | solution.py:814
  228.4 2.8 %multiply_add_fusion = f32[1024,384]{1,0:T(8,128)} fusion(bf16[1024,384]{1,0:T(8,128)(2,1)} %collective-permute-done.16, bf16[1024,384]{1,0:T(8,128)(2,1)S(1)} %get-tuple-element.100, f32[1024]{0:T(1024)S(1)} %fusion.21, bf16[1024,768]{1,0:T(8,128)(2,1)S(1)} %copy-done, s32[]{:T(128)S(6)} %select_n.46), kind=kLoop, calls=%fused_computation | loop fusion | flops 2359296 | bytes 3936260 | tf_op jit(solution)/shard_map/layer_out/add | solution.py:1043
  233.1 3.7 %shard_map.304 = f32[1024,768]{1,0:T(8,128)} custom-call(s32[10]{0:T(128)S(1)} %concatenate.30.info, bf16[1024,768]{1,0:T(8,128)(2,1)S(1)} %get-tuple-element.130.own, bf16[1024,768]{1,0:T(8,128)(2,1)S(1)} %collective-permute-done.27.other, f32[8,768]{1,0:T(8,128)S(1)} %collective-permute-done.28.halo_a, f32[8,768]{1,0:T(8,128)S(1)} %collective-permute-done.29.halo_b, ...), custom_call_target="tpu_custom_call" | custom-call | flops 5500000256 | bytes 17500000 | tf_op jit(solution)/shard_map/pallas_call | solution.py:786
  241.9 2.4 collective-permute-done.31.refs_2_
  (246 shorter events, 99.7 us)
Async XLA Ops:
  1.7 13.9 %collective-permute-start = (bf16[48,1024]{1,0:T(8,128)(2,1)S(1)}, bf16[48,1024]{1,0:T(8,128)(2,1)S(1)}, u32[]{:S(2)}, u32[]{:S(2)}) collective-permute-start(bf16[48,1024]{1,0:T(8,128)(2,1)S(1)} %fusion.10), channel_id=1, source_target_pairs={{0,8},{8,0},{16,24},{24,16},{1,9},{9,1},{17,25},{25,17},{2,10},{10... | collective-permute-start | bytes 294920 | tf_op jit(solution)/shard_map/gather_weights/ppermute | solution.py:814
  17.1 17.4 %collective-permute-start.4 = (bf16[64,1536]{1,0:T(8,128)(2,1)S(1)}, bf16[64,1536]{1,0:T(8,128)(2,1)S(1)}, u32[]{:S(2)}, u32[]{:S(2)}) collective-permute-start(bf16[64,1536]{1,0:T(8,128)(2,1)S(1)} %fusion.8.refs_0_), channel_id=1, source_target_pairs={{0,16},{8,24},{16,0},{24,8},{1,17},{9,25},{17,1},{25,9},{2,18},{10... | collective-permute-start | bytes 589832 | tf_op jit(solution)/shard_map/gather_weights/ppermute | solution.py:814
  20.3 17.6 %collective-permute-start.5 = (bf16[64,1536]{1,0:T(8,128)(2,1)S(1)}, bf16[64,1536]{1,0:T(8,128)(2,1)S(1)}, u32[]{:S(2)}, u32[]{:S(2)}) collective-permute-start(bf16[64,1536]{1,0:T(8,128)(2,1)S(1)} %fusion.8.refs_0_), channel_id=1, source_target_pairs={{0,24},{8,16},{16,8},{24,0},{1,25},{9,17},{17,9},{25,1},{2,26},{10... | collective-permute-start | bytes 589832 | tf_op jit(solution)/shard_map/gather_weights/ppermute | solution.py:814
  20.3 22.7 %collective-permute-start.6 = (bf16[192,1024]{1,0:T(8,128)(2,1)S(1)}, bf16[192,1024]{1,0:T(8,128)(2,1)S(1)}, u32[]{:S(2)}, u32[]{:S(2)}) collective-permute-start(bf16[192,1024]{1,0:T(8,128)(2,1)S(1)} %pad_maximum_fusion.1.refs_4_), channel_id=1, source_target_pairs={{0,2},{2,0},{4,6},{6,4},{1,3},{3,1},{5,7},{7,5},{8,10},{10,8},{12,... | collective-permute-start | bytes 1179656 | tf_op jit(solution)/shard_map/gather_weights/ppermute | solution.py:814
  22.0 22.5 %collective-permute-start.7 = (bf16[192,1024]{1,0:T(8,128)(2,1)S(1)}, bf16[192,1024]{1,0:T(8,128)(2,1)}, u32[]{:S(2)}, u32[]{:S(2)}) collective-permute-start(bf16[192,1024]{1,0:T(8,128)(2,1)S(1)} %pad_maximum_fusion.1.refs_4_), channel_id=1, source_target_pairs={{0,4},{2,6},{4,0},{6,2},{1,5},{3,7},{5,1},{7,3},{8,12},{10,14},{12... | collective-permute-start | bytes 1179656 | tf_op jit(solution)/shard_map/gather_weights/ppermute | solution.py:814
  24.5 20.0 %collective-permute-start.8 = (bf16[192,1024]{1,0:T(8,128)(2,1)S(1)}, bf16[192,1024]{1,0:T(8,128)(2,1)}, u32[]{:S(2)}, u32[]{:S(2)}) collective-permute-start(bf16[192,1024]{1,0:T(8,128)(2,1)S(1)} %pad_maximum_fusion.1.refs_4_), channel_id=1, source_target_pairs={{0,6},{2,4},{4,2},{6,0},{1,7},{3,5},{5,3},{7,1},{8,14},{10,12},{12... | collective-permute-start | bytes 1179656 | tf_op jit(solution)/shard_map/gather_weights/ppermute | solution.py:814
  38.0 33.7 %collective-permute-start.13 = (bf16[192,1536]{1,0:T(8,128)(2,1)S(1)}, bf16[192,1536]{1,0:T(8,128)(2,1)S(1)}, u32[]{:S(2)}, u32[]{:S(2)}) collective-permute-start(bf16[192,1536]{1,0:T(8,128)(2,1)S(1)} %pad_maximum_fusion.refs_0_), channel_id=1, source_target_pairs={{0,2},{2,0},{4,6},{6,4},{1,3},{3,1},{5,7},{7,5},{8,10},{10,8},{12,... | collective-permute-start | bytes 1769480 | tf_op jit(solution)/shard_map/gather_weights/ppermute | solution.py:814
  40.6 32.5 %collective-permute-start.14 = (bf16[192,1536]{1,0:T(8,128)(2,1)S(1)}, bf16[192,1536]{1,0:T(8,128)(2,1)S(1)}, u32[]{:S(2)}, u32[]{:S(2)}) collective-permute-start(bf16[192,1536]{1,0:T(8,128)(2,1)S(1)} %pad_maximum_fusion.refs_0_), channel_id=1, source_target_pairs={{0,4},{2,6},{4,0},{6,2},{1,5},{3,7},{5,1},{7,3},{8,12},{10,14},{12... | collective-permute-start | bytes 1769480 | tf_op jit(solution)/shard_map/gather_weights/ppermute | solution.py:814
  43.0 30.1 %collective-permute-start.15 = (bf16[192,1536]{1,0:T(8,128)(2,1)S(1)}, bf16[192,1536]{1,0:T(8,128)(2,1)S(1)}, u32[]{:S(2)}, u32[]{:S(2)}) collective-permute-start(bf16[192,1536]{1,0:T(8,128)(2,1)S(1)} %pad_maximum_fusion.refs_0_), channel_id=1, source_target_pairs={{0,6},{2,4},{4,2},{6,0},{1,7},{3,5},{5,3},{7,1},{8,14},{10,12},{12... | collective-permute-start | bytes 1769480 | tf_op jit(solution)/shard_map/gather_weights/ppermute | solution.py:814
  118.2 31.3 %collective-permute-start.17 = (bf16[784,128]{1,0:T(8,128)(2,1)S(1)}, bf16[784,128]{1,0:T(8,128)(2,1)S(1)}, u32[]{:S(2)}, u32[]{:S(2)}) collective-permute-start(bf16[784,128]{1,0:T(8,128)(2,1)S(1)} %get-tuple-element.102), channel_id=1, source_target_pairs={{2,0},{4,2},{6,4},{3,1},{5,3},{7,5},{10,8},{12,10},{14,12},{11,9},... | collective-permute-start | bytes 602120 | tf_op jit(solution)/shard_map/ppermute | solution.py:806
  119.5 30.0 %collective-permute-start.18 = (bf16[784,128]{1,0:T(8,128)(2,1)S(1)}, bf16[784,128]{1,0:T(8,128)(2,1)S(1)}, u32[]{:S(2)}, u32[]{:S(2)}) collective-permute-start(bf16[784,128]{1,0:T(8,128)(2,1)S(1)} %get-tuple-element.102), channel_id=1, source_target_pairs={{4,0},{6,2},{5,1},{7,3},{12,8},{14,10},{13,9},{15,11},{20,16},{22,... | collective-permute-start | bytes 602120 | tf_op jit(solution)/shard_map/ppermute | solution.py:806
  121.0 28.6 %collective-permute-start.19 = (bf16[784,128]{1,0:T(8,128)(2,1)S(1)}, bf16[784,128]{1,0:T(8,128)(2,1)S(1)}, u32[]{:S(2)}, u32[]{:S(2)}) collective-permute-start(bf16[784,128]{1,0:T(8,128)(2,1)S(1)} %get-tuple-element.102), channel_id=1, source_target_pairs={{6,0},{7,1},{14,8},{15,9},{22,16},{23,17},{30,24},{31,25}} | collective-permute-start | bytes 602120 | tf_op jit(solution)/shard_map/ppermute | solution.py:806
  144.4 42.3 %collective-permute-start.33 = (bf16[192,1536]{1,0:T(8,128)(2,1)S(1)}, bf16[192,1536]{1,0:T(8,128)(2,1)S(1)}, u32[]{:S(2)}, u32[]{:S(2)}) collective-permute-start(bf16[192,1536]{1,0:T(8,128)(2,1)S(1)} %get-tuple-element.136), channel_id=1, source_target_pairs={{0,2},{2,0},{4,6},{6,4},{1,3},{3,1},{5,7},{7,5},{8,10},{10,8},{12,... | collective-permute-start | bytes 1769480 | tf_op jit(solution)/shard_map/reduce_gate_weights/ppermute | solution.py:814
  146.4 42.3 %collective-permute-start.34 = (bf16[192,1536]{1,0:T(8,128)(2,1)S(1)}, bf16[192,1536]{1,0:T(8,128)(2,1)S(1)}, u32[]{:S(2)}, u32[]{:S(2)}) collective-permute-start(bf16[192,1536]{1,0:T(8,128)(2,1)S(1)} %get-tuple-element.137), channel_id=1, source_target_pairs={{0,4},{2,6},{4,0},{6,2},{1,5},{3,7},{5,1},{7,3},{8,12},{10,14},{12... | collective-permute-start | bytes 1769480 | tf_op jit(solution)/shard_map/reduce_gate_weights/ppermute | solution.py:814
  149.5 39.2 %collective-permute-start.35 = (bf16[192,1536]{1,0:T(8,128)(2,1)S(1)}, bf16[192,1536]{1,0:T(8,128)(2,1)S(1)}, u32[]{:S(2)}, u32[]{:S(2)}) collective-permute-start(bf16[192,1536]{1,0:T(8,128)(2,1)S(1)} %get-tuple-element.138), channel_id=1, source_target_pairs={{0,6},{2,4},{4,2},{6,0},{1,7},{3,5},{5,3},{7,1},{8,14},{10,12},{12... | collective-permute-start | bytes 1769480 | tf_op jit(solution)/shard_map/reduce_gate_weights/ppermute | solution.py:814
  149.5 77.4 %collective-permute-start.16 = (bf16[1024,384]{1,0:T(8,128)(2,1)S(1)}, bf16[1024,384]{1,0:T(8,128)(2,1)}, u32[]{:S(2)}, u32[]{:S(2)}) collective-permute-start(bf16[1024,384]{1,0:T(8,128)(2,1)S(1)} %get-tuple-element.101), channel_id=1, source_target_pairs={{0,1},{1,0},{2,3},{3,2},{4,5},{5,4},{6,7},{7,6},{8,9},{9,8},{10,11... | collective-permute-start | bytes 2359304 | tf_op jit(solution)/shard_map/layer_out/ppermute | solution.py:810
  185.2 13.0 %collective-permute-start.20 = (bf16[192,1152]{1,0:T(8,128)(2,1)S(1)}, bf16[192,1152]{1,0:T(8,128)(2,1)S(1)}, u32[]{:S(2)}, u32[]{:S(2)}) collective-permute-start(bf16[192,1152]{1,0:T(8,128)(2,1)S(1)} %get-tuple-element.121), channel_id=1, source_target_pairs={{0,2},{2,0},{4,6},{6,4},{1,3},{3,1},{5,7},{7,5},{8,10},{10,8},{12,... | collective-permute-start | bytes 1327112 | tf_op jit(solution)/shard_map/ppermute | solution.py:814
  186.7 22.0 %collective-permute-start.21 = (bf16[192,1152]{1,0:T(8,128)(2,1)S(1)}, bf16[192,1152]{1,0:T(8,128)(2,1)S(1)}, u32[]{:S(2)}, u32[]{:S(2)}) collective-permute-start(bf16[192,1152]{1,0:T(8,128)(2,1)S(1)} %get-tuple-element.123), channel_id=1, source_target_pairs={{0,4},{2,6},{4,0},{6,2},{1,5},{3,7},{5,1},{7,3},{8,12},{10,14},{12... | collective-permute-start | bytes 1327112 | tf_op jit(solution)/shard_map/ppermute | solution.py:814
  188.7 23.7 %collective-permute-start.22 = (bf16[192,1152]{1,0:T(8,128)(2,1)S(1)}, bf16[192,1152]{1,0:T(8,128)(2,1)S(1)}, u32[]{:S(2)}, u32[]{:S(2)}) collective-permute-start(bf16[192,1152]{1,0:T(8,128)(2,1)S(1)} %get-tuple-element.124), channel_id=1, source_target_pairs={{0,6},{2,4},{4,2},{6,0},{1,7},{3,5},{5,3},{7,1},{8,14},{10,12},{12... | collective-permute-start | bytes 1327112 | tf_op jit(solution)/shard_map/ppermute | solution.py:814
  189.1 23.5 %collective-permute-start.36 = (bf16[48,1536]{1,0:T(8,128)(2,1)S(1)}, bf16[48,1536]{1,0:T(8,128)(2,1)S(1)}, u32[]{:S(2)}, u32[]{:S(2)}) collective-permute-start(bf16[48,1536]{1,0:T(8,128)(2,1)S(1)} %get-tuple-element.156), channel_id=1, source_target_pairs={{0,8},{8,0},{16,24},{24,16},{1,9},{9,1},{17,25},{25,17},{2,10},{10... | collective-permute-start | bytes 442376 | tf_op jit(solution)/shard_map/reduce_gate_weights/ppermute | solution.py:814
  198.2 14.5 %collective-permute-start.37 = (bf16[48,1536]{1,0:T(8,128)(2,1)S(1)}, bf16[48,1536]{1,0:T(8,128)(2,1)S(1)}, u32[]{:S(2)}, u32[]{:S(2)}) collective-permute-start(bf16[48,1536]{1,0:T(8,128)(2,1)S(1)} %get-tuple-element.158), channel_id=1, source_target_pairs={{0,16},{8,24},{16,0},{24,8},{1,17},{9,25},{17,1},{25,9},{2,18},{10... | collective-permute-start | bytes 442376 | tf_op jit(solution)/shard_map/reduce_gate_weights/ppermute | solution.py:814
  212.4 20.7 %collective-permute-start.27 = (bf16[1024,768]{1,0:T(8,128)(2,1)S(1)}, bf16[1024,768]{1,0:T(8,128)(2,1)S(1)}, u32[]{:S(2)}, u32[]{:S(2)}) collective-permute-start(bf16[1024,768]{1,0:T(8,128)(2,1)S(1)} %get-tuple-element.130.own), channel_id=1, source_target_pairs={{0,1},{1,0},{2,3},{3,2},{4,5},{5,4},{6,7},{7,6},{8,9},{9,8},{10,11... | collective-permute-start | bytes 4718600 | tf_op jit(solution)/shard_map/ppermute | solution.py:810
  220.9 12.1 %collective-permute-start.28 = (f32[8,768]{1,0:T(8,128)S(1)}, f32[8,768]{1,0:T(8,128)S(1)}, u32[]{:S(2)}, u32[]{:S(2)}) collective-permute-start(f32[8,768]{1,0:T(8,128)S(1)} %get-tuple-element.131), channel_id=1, source_target_pairs={{2,0},{3,1},{4,2},{5,3},{6,4},{7,5},{10,8},{11,9},{12,10},{13,11},... | collective-permute-start | bytes 73736 | tf_op jit(solution)/shard_map/ppermute | solution.py:1151
  225.7 14.6 %collective-permute-start.39 = (bf16[48,1536]{1,0:T(8,128)(2,1)S(1)}, bf16[48,1536]{1,0:T(8,128)(2,1)S(1)}, u32[]{:S(2)}, u32[]{:S(2)}) collective-permute-start(bf16[48,1536]{1,0:T(8,128)(2,1)S(1)} %fusion.4.refs_0_), channel_id=1, source_target_pairs={{0,2},{2,0},{4,6},{6,4},{1,3},{3,1},{5,7},{7,5},{8,10},{10,8},{12,... | collective-permute-start | bytes 442376 | tf_op jit(solution)/shard_map/last_hop/ppermute | solution.py:814
  (85 other events, 623.4 us)

commit v7 on v6

--- a/solution.py
+++ b/solution.py
@@ -408,7 +408,7 @@
 
     z_o[...] = dot(normed[...], w2[:, :inner]).astype(BF16)
     grad = (cot[...].astype(F32) * place.valid(block)).astype(BF16)
-    dn_o[...] = dot(grad, w2[:, inner:])
+    dn_o[...] = dot(grad, w2[:, inner:]).astype(BF16)
 
 
 def apply_kernel(counts, packet_count, info, *refs):
@@ -432,7 +432,7 @@
     gate = z[...].astype(F32)
     gated = y * gate * gate_sigmoid(gate)
     squares = jnp.sum(gated * gated, axis=1, keepdims=True)
-    cross = jnp.sum(par[6:7, :inner] * dn[...] * gated, axis=1, keepdims=True)
+    cross = jnp.sum(par[6:7, :inner] * dn[...].astype(F32) * gated, axis=1, keepdims=True)
     lane = iota((BLOCK, LANES), 1)
     both = jnp.where(lane == 0, squares, jnp.where(lane == 1, cross, 0.0))
     stat_o[...] = both.T[0:8, :]
@@ -473,7 +473,7 @@
     send_o[...] = dot_nt(normal, wo[pl.ds(other, half), :]).astype(BF16)
     grad = (cot[...].astype(F32) * place.valid(block)).astype(BF16)
     acc[...] += dot_tn(grad, normal)
-    back = dn[...]
+    back = dn[...].astype(F32)
     grad_gated = inv * (gain * back) - gated * (inv * inv * inv) * (cross / inner_all)
     dy = (grad_gated * silu).astype(BF16)
     dy_o[...] = dy
@@ -499,9 +499,9 @@
 
 
 def intra_back_kernel(counts, heads, dp_count, info, *refs):
-    dy, dz, xc, bc, cum, pre_step, hb, normed, wz, gwo, par, spread = refs[:12]
-    dxc_o, dcq_o, dbq_o, rows_o, cols_o, dnz_o = refs[12:18]
-    parts = refs[18:-2]
+    dy, dz, xc, bc, cum, pre_step, hb, normed, gwo, par, spread = refs[:11]
+    dxc_o, dcq_o, dbq_o, rows_o, cols_o = refs[11:16]
+    parts = refs[16:-2]
     acc, columns = refs[-2:]
     block = pl.program_id(0)
     place = Place(info, counts)
@@ -542,14 +542,13 @@
             columns[head : head + 1, :] = jnp.sum(part, axis=0, keepdims=True)
             sums = sums + jnp.where(lane == head, jnp.sum(part * step_row, axis=1, keepdims=True), 0.0)
         dx_pair = dot_tn(jnp.concatenate(mixing, axis=0), halves)
-        dxc_o[:, lanes] = dx_pair + par[7:8, lanes] * dy_pair.astype(F32)
+        dxc_o[:, lanes] = (dx_pair + par[7:8, lanes] * dy_pair.astype(F32)).astype(BF16)
     grad_low = grad_gram.astype(BF16)
     dq = (expand(enter_weights(place, block, cums), spread) * dy[...].astype(F32)).astype(BF16)
     dcq_o[...] = dot(grad_low, bq) + dot(dq, hb[0])
     dbq_o[...] = dot_tn(grad_low, cq)
     rows_o[...] = sums
     cols_o[...] = columns[...].T
-    dnz_o[...] = dot_nt(dz[...], wz[...])
     acc[...] += dot_tn(normed[...], dz[...])
 
     @pl.when(block == pl.num_programs(0) - 1)
@@ -601,7 +600,7 @@
     end_weight = end_kernel * step
     end_wide = expand(end_weight, spread)
     spread_b = dot_nt(bq, low)
-    grad_x = dxc[...] + end_wide * spread_b
+    grad_x = dxc[...].astype(F32) + end_wide * spread_b
     grad_end = reduce_heads(x_float * spread_b, spread)
     grad_b = dbq[...] + dot((x_float * end_wide).astype(BF16), low)
     end_part = grad_end * end_weight
@@ -657,7 +656,7 @@
 
 
 def input_back_kernel(
-    counts, dp_count, part_count, info, packed, back, dnz, tok, halo, w1, par,
+    counts, dp_count, part_count, info, packed, back, dz, wz, tok, halo, w1, par,
     dn_o, dnh_o, norm_o, total,
 ):
     block = pl.program_id(0)
@@ -675,7 +674,7 @@
             jnp.sum(halo_grad * halo_scaled, axis=0, keepdims=True), total.shape
         )
 
-    partial = dnz[...] + dot_nt(packed[...], w1[...])
+    partial = dot_nt(dz[...], wz[...]) + dot_nt(packed[...], w1[...])
     dn_o[...] = partial.astype(BF16)
     scaled, _, _ = normalise(tok[...].astype(F32), gain)
     total[0:1, :] += jnp.sum(partial * scaled, axis=0, keepdims=True)
@@ -704,15 +703,15 @@
 
 
 def unpack_gate_kernel(counts, part_count, info, *refs):
-    parts = refs[:part_count]
-    wz_o, wo_o = refs[part_count:]
+    whole, wz_o, wo_o = refs
     place = Place(info, counts)
     shard, inner = wz_o.shape
     rows = shard // part_count
     for part in range(part_count):
         first = pl.multiple_of(xor(place.ctx, part) * rows, rows) if part_count > 1 else 0
-        wz_o[pl.ds(first, rows), :] = parts[part][:, :inner].astype(F32)
-        wo_o[pl.ds(first, rows), :] = parts[part][:, inner:].astype(F32)
+        lines = slice(part * rows, (part + 1) * rows)
+        wz_o[pl.ds(first, rows), :] = whole[lines, :inner].astype(F32)
+        wo_o[pl.ds(first, rows), :] = whole[lines, inner:].astype(F32)
 
 
 def unpack_input_kernel(counts, heads, part_count, info, *refs):
@@ -781,13 +780,15 @@
             return pl.BlockSpec((16, shape[1]), lambda i: (jnp.maximum(at(i) * each - 1, 0), 0))
         if kind == "whole":
             return pl.BlockSpec(tuple(shape), lambda i: (0,) * len(shape))
+        if kind == "once":
+            return pl.BlockSpec(tuple(shape), lambda i: (0,) * len(shape), pipeline_mode=pl.Buffered(1))
         return kind
 
     return pl.pallas_call(
         body,
         grid=(steps,),
         in_specs=[pl.BlockSpec(memory_space=pltpu.SMEM)]
-        + [spec(array.shape, kind) for array, kind in operands],
+        + [spec(array.shape, "once" if kind == "whole" else kind) for array, kind in operands],
         out_specs=[spec(shape.shape, kind) for shape, kind in outputs],
         out_shape=[shape for shape, _ in outputs],
         scratch_shapes=list(scratch),
@@ -841,6 +842,29 @@
         block = total[mask * rows : (mask + 1) * rows].astype(BF16)
         own = own + partnered(block, "dp", mask).astype(F32)
     return own.astype(BF16)
+
+
+def halved_sum(total):
+    blocks = lax.axis_size("dp")
+    rows = total.shape[0] // blocks
+    total = total.reshape(blocks, rows, -1).astype(F32)
+    mask = 1
+    while mask < blocks:
+        kept = [total[block] for block in range(total.shape[0]) if block % 2 == 0]
+        sent = [total[block] for block in range(total.shape[0]) if block % 2 == 1]
+        received = partnered(jnp.concatenate(sent, axis=0).astype(BF16), "dp", mask)
+        received = received.reshape(len(sent), rows, -1).astype(F32)
+        total = jnp.stack(kept) + received
+        mask *= 2
+    return total[0].astype(BF16)
+
+
+def doubled(value):
+    mask = 1
+    while mask < lax.axis_size("ctx"):
+        value = jnp.concatenate([value, partnered(value, "ctx", mask)], axis=0)
+        mask *= 2
+    return value
 
 
 def whole_sum(value):
@@ -901,7 +925,9 @@
             w2_parts = [lax.all_gather(gate_rows, "dp", axis=0, tiled=True)]
             vectors = exchanged(vector, "dp")
     first_vector = part_rows // 16 if parts > 1 else 0
-    vector_spec = pl.BlockSpec((16, 2 * shard), lambda i: (first_vector, 0))
+    vector_spec = pl.BlockSpec(
+        (16, 2 * shard), lambda i: (first_vector, 0), pipeline_mode=pl.Buffered(1)
+    )
 
     dtp = jnp.pad(jnp.stack([dt_bias, jnp.exp(a_log), skip_d]), ((0, 5), (0, LANES - heads)))
     shape = (2 * LANES, inner)
@@ -954,19 +980,19 @@
             pltpu.VMEM((8, LANES), F32),
         ],
         micros=20,
-        mega=28,
+        mega=16,
     )
     packets = [(shifted(packet, "ctx", step), "whole") for step in range(1, ctx_count)]
-    wz_spec = pl.BlockSpec((width, inner), lambda i: (0, 0))
-    wo_spec = pl.BlockSpec((width, inner), lambda i: (0, 1))
+    wz_spec = pl.BlockSpec((width, inner), lambda i: (0, 0), pipeline_mode=pl.Buffered(1))
+    wo_spec = pl.BlockSpec((width, inner), lambda i: (0, 1), pipeline_mode=pl.Buffered(1))
     w2, z, dn = call(
         functools.partial(gate_matmul_kernel, counts, dp_count, parts),
         steps,
         info,
         [(value, "whole") for value in w2_parts] + [(normed, "rows"), (cotangent, "rows")],
-        [out((width, 2 * inner), BF16, "whole"), row_out(inner, BF16), row_out(inner, F32)],
+        [out((width, 2 * inner), BF16, "whole"), row_out(inner, BF16), row_out(inner, BF16)],
         micros=7,
-        mega=20,
+        mega=12,
     )
     y, hb, h, stat = call(
         functools.partial(apply_kernel, counts, len(packets)),
@@ -992,6 +1018,7 @@
         ],
         [pltpu.VMEM((inner, LANES), F32)],
         micros=8,
+        mega=12,
     )
     stat = lax.psum(stat, "tp")
     inner_all = inner * lax.axis_size("tp")
@@ -1033,7 +1060,7 @@
         ],
         reverse=True,
         micros=15,
-        mega=24,
+        mega=14,
     )
     packets = [(shifted(packet, "ctx", -step), "whole") for step in range(1, ctx_count)]
     with jax.named_scope("layer_out"):
@@ -1041,7 +1068,7 @@
         own_inputs = lax.dynamic_slice_in_dim(tokens, tp_index * half, half, 1).astype(F32)
         valid = (jnp.arange(rows) < fill).astype(F32)[:, None]
         layer_out = own_inputs + (keep.astype(F32) + received.astype(F32)) * valid
-    dxc, dcq, dbq, row_sums, col_sums, dnz, *g2 = call(
+    dxc, dcq, dbq, row_sums, col_sums, *g2 = call(
         functools.partial(intra_back_kernel, counts, heads, dp_count),
         steps,
         info,
@@ -1054,23 +1081,21 @@
             (pre_step, "rows"),
             (hb, "block"),
             (normed, "rows"),
-            (w2, wz_spec),
             (gwo, "whole"),
             (par, "whole"),
             (spread, "whole"),
         ],
         [
-            row_out(inner, F32),
+            row_out(inner, BF16),
             row_out(LANES, F32),
             row_out(LANES, F32),
             row_out(LANES, F32),
             row_out(LANES, F32),
-            row_out(width, F32),
         ]
         + [out((width // parts, 2 * inner), BF16, "whole")] * parts,
         [pltpu.VMEM((width, inner), F32), pltpu.VMEM((LANES, BLOCK), F32)],
         micros=18,
-        mega=24,
+        mega=14,
     )
     with jax.named_scope("reduce_gate_weights"):
         total2 = ctx_sum(g2) if parts > 1 else g2[0]
@@ -1115,10 +1140,10 @@
         ],
         reverse=True,
         micros=25,
-        mega=32,
+        mega=20,
     )
     with jax.named_scope("reduce_gate_weights"):
-        total2 = dp_sum(total2) if parts > 1 else whole_sum(total2)
+        total2 = halved_sum(total2) if parts > 1 else whole_sum(total2)
     norm_rows = part_rows * dp_count
     if parts > 1:
         g1 = [g1[0]] + [partnered(g1[mask], "ctx", mask) for mask in range(1, parts)]
@@ -1130,7 +1155,8 @@
         [
             (packed, "rows"),
             (back, "whole"),
-            (dnz, "rows"),
+            (dz, "rows"),
+            (w2, wz_spec),
             (tokens, "rows"),
             (halo, "whole"),
             (w1, "whole"),
@@ -1143,6 +1169,7 @@
         ],
         [pltpu.VMEM((8, width), F32)],
         micros=5,
+        mega=12,
     )
     other = swapped(partial)
     size = ctx_count * 2
@@ -1177,14 +1204,15 @@
         ],
         [row_out(width, F32)],
         micros=5,
+        mega=10,
     )
     with jax.named_scope("last_hop"):
         if parts > 1:
-            total2 = exchanged(total2, "ctx")
+            total2 = doubled(total2)
             total1, grad_tokens = lax.optimization_barrier((total1, grad_tokens))
             total1 = exchanged(total1, "ctx")
         else:
-            total1, total2 = [total1], [total2]
+            total1 = [total1]
     each = HEAD // dp_count
     part_bc = bias_bc.shape[0]
     tall = -(-shard // LANES) * LANES
@@ -1196,9 +1224,10 @@
         functools.partial(unpack_gate_kernel, counts, parts),
         1,
         info,
-        [(value, "whole") for value in total2],
+        [(total2, "whole")],
         [final(shard, inner), final(shard, inner)],
         micros=2,
+        mega=8,
     )
     (
         grad_wx, grad_wbc, grad_wdt, grad_norm, grad_taps, grad_bias, grad_state_taps, grad_state_bias,
@@ -1224,6 +1253,7 @@
         ],
         [pltpu.VMEM((tall, channels + LANES), F32)],
         micros=2,
+        mega=8,
     )
     return (
         layer_out,

time: 249 us -> 239 us (0.960)
  local copies, waits for them, and re-layouts: 50.4 us -> 28.2 us
  waiting for transfers between devices: 32.9 us -> 47.3 us
    unnamed x135 -> x95, local copies, waits for them, and re-layouts: 46.6 us -> 24.3 us
    ppermute x30 -> x28, waiting for transfers between devices: 31.9 us -> 46.3 us  [partnered(): lax.ppermute(value, axis, [(one, one ^ mask) for one in range(lax.axis_si...]
    ppermute x30 -> x28, starting transfers between devices: 45.1 us -> 45 us  [partnered(): lax.ppermute(value, axis, [(one, one ^ mask) for one in range(lax.axis_si...]
  transfers between devices with their start and end apart: 42 -> 40, of which waited for: 9 -> 13; matrix products, arithmetic and copies ran while one was open for 5% -> 5% of each run, Pallas kernels for 28% -> 28%
where the time goes in v7:
time: 239 us; the launch traced here: 238 us
  Pallas kernels  87.1 us (36%)
  starting transfers between devices  62.2 us (26%)
  waiting for transfers between devices  47.3 us (20%)
  local copies, waits for them, and re-layouts  28.2 us (12%)
  other arithmetic  7.31 us (3%)
  blocking collectives  3.39 us (1%)
    pallas_call x10, Pallas kernels, call(): pl.pallas_call(body, grid=(steps,), in_specs=[pl.BlockSpec(memory_space=p...  87.1 us
    ppermute x28, waiting for transfers between devices, partnered(): lax.ppermute(value, axis, [(one, one ^ mask) for one in range(lax.axis_si...  46.3 us
    ppermute x28, starting transfers between devices, partnered(): lax.ppermute(value, axis, [(one, one ^ mask) for one in range(lax.axis_si...  45 us
    unnamed x95, local copies, waits for them, and re-layouts  24.3 us
    ppermute x7, starting transfers between devices, shifted(): lax.ppermute(value, axis, [(source, source + steps) for source in range(f...  14.5 us
  transfers between devices with their start and end apart: 40, of which 13 were waited for; matrix products, arithmetic and copies ran while one was open for 5% of the time, Pallas kernels for 28%

profile of v7, /device:TPU:0, one launch (start us, length us, event | category | flops | bytes accessed | tf_op | source)
XLA Modules:
  0.0 237.9 jit_solution(2762691453994472426)
XLA Ops:
  1.7 3.1 %collective-permute-start = (bf16[48,1024]{1,0:T(8,128)(2,1)S(1)}, bf16[48,1024]{1,0:T(8,128)(2,1)S(1)}, u32[]{:S(2)}, u32[]{:S(2)}) collective-permute-start(bf16[48,1024]{1,0:T(8,128)(2,1)S(1)} %fusion.10), channel_id=1, source_target_pairs={{0,8},{8,0},{16,24},{24,16},{1,9},{9,1},{17,25},{25,17},{2,10},{10... | collective-permute-start | bytes 294920 | tf_op jit(solution)/shard_map/gather_weights/ppermute | solution.py:815
  4.8 2.6 %collective-permute-start.1 = (bf16[48,1024]{1,0:T(8,128)(2,1)S(1)}, bf16[48,1024]{1,0:T(8,128)(2,1)S(1)}, u32[]{:S(2)}, u32[]{:S(2)}) collective-permute-start(bf16[48,1024]{1,0:T(8,128)(2,1)S(1)} %fusion.10), channel_id=1, source_target_pairs={{0,16},{8,24},{16,0},{24,8},{1,17},{9,25},{17,1},{25,9},{2,18},{10... | collective-permute-start | bytes 294920 | tf_op jit(solution)/shard_map/gather_weights/ppermute | solution.py:815
  17.1 3.2 %collective-permute-start.4 = (bf16[64,1536]{1,0:T(8,128)(2,1)S(1)}, bf16[64,1536]{1,0:T(8,128)(2,1)S(1)}, u32[]{:S(2)}, u32[]{:S(2)}) collective-permute-start(bf16[64,1536]{1,0:T(8,128)(2,1)S(1)} %fusion.6.refs_0_), channel_id=1, source_target_pairs={{0,16},{8,24},{16,0},{24,8},{1,17},{9,25},{17,1},{25,9},{2,18},{10... | collective-permute-start | bytes 589832 | tf_op jit(solution)/shard_map/gather_weights/ppermute | solution.py:815
  27.8 6.8 %collective-permute-done.4.refs_2_ = bf16[64,1536]{1,0:T(8,128)(2,1)S(1)} collective-permute-done((bf16[64,1536]{1,0:T(8,128)(2,1)S(1)}, bf16[64,1536]{1,0:T(8,128)(2,1)S(1)}, u32[]{:S(2)}, u32[]{:S(2)}) %collective-permute-start.4) | collective-permute-done | bytes 196640 | tf_op jit(solution)/shard_map/gather_weights/ppermute | solution.py:815
  34.5 3.4 %collective-permute-start.9 = (bf16[16,768]{1,0:T(8,128)(2,1)S(1)}, bf16[16,768]{1,0:T(8,128)(2,1)S(1)}, u32[]{:S(2)}, u32[]{:S(2)}) collective-permute-start(bf16[16,768]{1,0:T(8,128)(2,1)S(1)} %constant_dynamic-slice_fusion), channel_id=1, source_target_pairs={{0,2},{2,4},{4,6},{1,3},{3,5},{5,7},{8,10},{10,12},{12,14},{9,11},... | collective-permute-start | bytes 73736 | tf_op jit(solution)/shard_map/ppermute | solution.py:807
  44.6 17.5 %shard_map.297 = (bf16[768,1152]{1,0:T(8,128)(2,1)S(1)}, f32[8,1024]{1,0:T(8,128)S(1)}, bf16[1024,768]{1,0:T(8,128)(2,1)S(1)}, bf16[16,768]{1,0:T(8,128)(2,1)S(1...) custom-call(s32[10]{0:T(128)S(1)} %concatenate.41.info, ...), custom_call_target="tpu_custom_call" | custom-call | flops 22000001024 | bytes 70000000 | tf_op jit(solution)/shard_map/pallas_call | solution.py:787
  68.7 3.8 %collective-permute-start.11 = (bf16[784,128]{1,0:T(8,128)(2,1)S(1)}, bf16[784,128]{1,0:T(8,128)(2,1)S(1)}, u32[]{:S(2)}, u32[]{:S(2)}) collective-permute-start(bf16[784,128]{1,0:T(8,128)(2,1)S(1)} %get-tuple-element.84), channel_id=1, source_target_pairs={{0,4},{2,6},{1,5},{3,7},{8,12},{10,14},{9,13},{11,15},{16,20},{18,... | collective-permute-start | bytes 602120 | tf_op jit(solution)/shard_map/ppermute | solution.py:807
  73.9 4.0 %shard_map.298 = (bf16[768,1536]{1,0:T(8,128)(2,1)S(1)}, bf16[1024,768]{1,0:T(8,128)(2,1)S(1)}, bf16[1024,768]{1,0:T(8,128)(2,1)S(1)}) custom-call(s32[10]{0:T(128)S(1)} %concatenate.41.info, bf16[192,1536]{1,0:T(8,128)(2,1)S(1)} %pad_maximum_fusion.refs_0_, bf16[192,1536]{1,0:T(8,128)(2,1)S(1)} %collective-permute-done.13.refs_1_, ...), custom_call_target="tpu_custom_call" | custom-call | flops 7699999744 | bytes 24500000 | tf_op jit(solution)/shard_map/pallas_call | solution.py:787
  79.3 4.2 %shard_map.299 = (f32[1024,768]{1,0:T(8,128)S(1)}, bf16[4,768,128]{2,1,0:T(8,128)(2,1)S(1)}, f32[4,768,128]{2,1,0:T(8,128)S(1)}, f32[8,1024]{1,0:T(8,128)S(1)}) custom-call(s32[10]{0:T(128)S(1)} %concatenate.41.info, bf16[784,128]{1,0:T(8,128)(2,1)S(1)} %collective-permute-done.10.refs_0_, bf16[784,128]{1,0:T(8,128)(2,1)S(1)} %collective-permute-done.11.refs_1_, ...), custom_call_target="tpu_custom_call" | custom-call | flops 8800000000 | bytes 28000000 | tf_op jit(solution)/shard_map/pallas_call | solution.py:787
  87.2 3.4 %psum.7.stat = f32[8,1024]{1,0:T(8,128)S(1)} all-reduce(f32[8,1024]{1,0:T(8,128)S(1)} %get-tuple-element.94), channel_id=1, replica_groups=mesh['dp'=4,'ctx'=4,'tp'=2] {'tp'}, use_global_device_ids=true, to_apply=%region_1.2 | all-reduce | flops 8192 | bytes 65536 | tf_op jit(solution)/shard_map/psum | solution.py:1023
  104.5 10.9 %shard_map.300 = (bf16[1024,384]{1,0:T(8,128)(2,1)S(1)}, bf16[1024,384]{1,0:T(8,128)(2,1)S(1)}, bf16[768,768]{1,0:T(8,128)(2,1)S(1)}, f32[8,768]{1,0:T(8,128)S(1...) custom-call(s32[10]{0:T(128)S(1)} %concatenate.41.info, ...), custom_call_target="tpu_custom_call" | custom-call | flops 16499999744 | bytes 52500000 | tf_op jit(solution)/shard_map/pallas_call | solution.py:787
  119.6 14.9 %shard_map.301 = (bf16[1024,768]{1,0:T(8,128)(2,1)S(1)}, f32[1024,128]{1,0:T(8,128)S(1)}, f32[1024,128]{1,0:T(8,128)S(1)}, f32[1024,128]{1,0:T(8,128)S(1)}, f32[...) custom-call(s32[10]{0:T(128)S(1)} %concatenate.41.info, ...), custom_call_target="tpu_custom_call" | custom-call | flops 19800000512 | bytes 63000000 | tf_op jit(solution)/shard_map/pallas_call | solution.py:787
  136.6 3.3 %collective-permute-start.34 = (bf16[192,1536]{1,0:T(8,128)(2,1)S(1)}, bf16[192,1536]{1,0:T(8,128)(2,1)S(1)}, u32[]{:S(2)}, u32[]{:S(2)}) collective-permute-start(bf16[192,1536]{1,0:T(8,128)(2,1)S(1)} %get-tuple-element.135), channel_id=1, source_target_pairs={{0,4},{2,6},{4,0},{6,2},{1,5},{3,7},{5,1},{7,3},{8,12},{10,14},{12... | collective-permute-start | bytes 1769480 | tf_op jit(solution)/shard_map/reduce_gate_weights/ppermute | solution.py:815
  140.0 22.7 %shard_map.302 = (bf16[1024,1152]{1,0:T(8,128)(2,1)S(1)}, bf16[16,1024]{1,0:T(8,128)(2,1)S(1)}, bf16[192,1152]{1,0:T(8,128)(2,1)S(1)}, bf16[192,1152]{1,0:T(8,12...) custom-call(s32[10]{0:T(128)S(1)} %concatenate.41.info, ...), custom_call_target="tpu_custom_call" | custom-call | flops 27499999232 | bytes 87500000 | tf_op jit(solution)/shard_map/pallas_call | solution.py:787
  167.5 8.2 %collective-permute-done.20 = bf16[192,1152]{1,0:T(8,128)(2,1)S(1)} collective-permute-done((bf16[192,1152]{1,0:T(8,128)(2,1)S(1)}, bf16[192,1152]{1,0:T(8,128)(2,1)S(1)}, u32[]{:S(2)}, u32[]{:S(2)}) %collective-permute-start.20) | collective-permute-done | bytes 442400 | tf_op jit(solution)/shard_map/ppermute | solution.py:815
  175.8 6.0 %shard_map.303 = (bf16[1024,768]{1,0:T(8,128)(2,1)S(1)}, f32[8,768]{1,0:T(8,128)S(1)}, f32[192,128]{1,0:T(8,128)S(1)}) custom-call(s32[10]{0:T(128)S(1)} %concatenate.41.info, bf16[1024,1152]{1,0:T(8,128)(2,1)S(1)} %get-tuple-element.124.packed, bf16[16,1024]{1,0:T(8,128)(2,1)S(1)} %get-tuple-element.125.back, ...), custom_call_target="tpu_custom_call" | custom-call | flops 5500000256 | bytes 17500000 | tf_op jit(solution)/shard_map/pallas_call | solution.py:787
  183.1 3.2 %collective-permute-done.21 = bf16[192,1152]{1,0:T(8,128)(2,1)S(1)} collective-permute-done((bf16[192,1152]{1,0:T(8,128)(2,1)S(1)}, bf16[192,1152]{1,0:T(8,128)(2,1)S(1)}, u32[]{:S(2)}, u32[]{:S(2)}) %collective-permute-start.21) | collective-permute-done | bytes 442400 | tf_op jit(solution)/shard_map/ppermute | solution.py:815
  186.6 4.2 %collective-permute-start.24 = (bf16[48,1152]{1,0:T(8,128)(2,1)S(1)}, bf16[48,1152]{1,0:T(8,128)(2,1)S(1)}, u32[]{:S(2)}, u32[]{:S(2)}) collective-permute-start(bf16[48,1152]{1,0:T(8,128)(2,1)S(1)} %get-tuple-element.160), channel_id=1, source_target_pairs={{0,16},{8,24},{16,0},{24,8},{1,17},{9,25},{17,1},{25,9},{2,18},{10... | collective-permute-start | bytes 331784 | tf_op jit(solution)/shard_map/reduce_input_weights/ppermute | solution.py:815
  193.8 5.5 %collective-permute-done.24 = bf16[48,1152]{1,0:T(8,128)(2,1)S(1)} collective-permute-done((bf16[48,1152]{1,0:T(8,128)(2,1)S(1)}, bf16[48,1152]{1,0:T(8,128)(2,1)S(1)}, u32[]{:S(2)}, u32[]{:S(2)}) %collective-permute-start.24) | collective-permute-done | bytes 110624 | tf_op jit(solution)/shard_map/reduce_input_weights/ppermute | solution.py:815
  199.3 2.7 %collective-permute-start.37 = (bf16[48,1536]{1,0:T(8,128)(2,1)S(1)}, bf16[48,1536]{1,0:T(8,128)(2,1)S(1)}, u32[]{:S(2)}, u32[]{:S(2)}) collective-permute-start(bf16[48,1536]{1,0:T(8,128)(2,1)S(1)} %fusion.8), channel_id=1, source_target_pairs={{0,16},{8,24},{16,0},{24,8},{1,17},{9,25},{17,1},{25,9},{2,18},{10... | collective-permute-start | bytes 442376 | tf_op jit(solution)/shard_map/reduce_gate_weights/ppermute | solution.py:815
  202.1 7.3 %collective-permute-done.37 = bf16[48,1536]{1,0:T(8,128)(2,1)S(1)} collective-permute-done((bf16[48,1536]{1,0:T(8,128)(2,1)S(1)}, bf16[48,1536]{1,0:T(8,128)(2,1)S(1)}, u32[]{:S(2)}, u32[]{:S(2)}) %collective-permute-start.37) | collective-permute-done | bytes 147488 | tf_op jit(solution)/shard_map/reduce_gate_weights/ppermute | solution.py:815
  212.7 3.1 %collective-permute-done.38 = bf16[48,1536]{1,0:T(8,128)(2,1)S(1)} collective-permute-done((bf16[48,1536]{1,0:T(8,128)(2,1)S(1)}, bf16[48,1536]{1,0:T(8,128)(2,1)S(1)}, u32[]{:S(2)}, u32[]{:S(2)}) %collective-permute-start.38) | collective-permute-done | bytes 147488 | tf_op jit(solution)/shard_map/last_hop/ppermute | solution.py:815
  217.5 7.0 %collective-permute-done.39 = bf16[96,1536]{1,0:T(8,128)(2,1)S(1)} collective-permute-done((bf16[96,1536]{1,0:T(8,128)(2,1)S(1)}, bf16[96,1536]{1,0:T(8,128)(2,1)S(1)}, u32[]{:S(2)}, u32[]{:S(2)}) %collective-permute-start.39) | collective-permute-done | bytes 294944 | tf_op jit(solution)/shard_map/last_hop/ppermute | solution.py:815
  224.5 3.6 %shard_map.304 = f32[1024,768]{1,0:T(8,128)} custom-call(s32[10]{0:T(128)S(1)} %concatenate.41.info, bf16[1024,768]{1,0:T(8,128)(2,1)S(1)} %get-tuple-element.128.own, bf16[1024,768]{1,0:T(8,128)(2,1)S(1)} %collective-permute-done.27.other, f32[8,768]{1,0:T(8,128)S(1)} %collective-permute-done.28.halo_a, f32[8,768]{1,0:T(8,128)S(1)} %collective-permute-done.29.halo_b, ...), custom_call_target="tpu_custom_call" | custom-call | flops 5500000256 | bytes 17500000 | tf_op jit(solution)/shard_map/pallas_call | solution.py:787
  (208 shorter events, 81.1 us)
Async XLA Ops:
  1.7 13.9 %collective-permute-start = (bf16[48,1024]{1,0:T(8,128)(2,1)S(1)}, bf16[48,1024]{1,0:T(8,128)(2,1)S(1)}, u32[]{:S(2)}, u32[]{:S(2)}) collective-permute-start(bf16[48,1024]{1,0:T(8,128)(2,1)S(1)} %fusion.10), channel_id=1, source_target_pairs={{0,8},{8,0},{16,24},{24,16},{1,9},{9,1},{17,25},{25,17},{2,10},{10... | collective-permute-start | bytes 294920 | tf_op jit(solution)/shard_map/gather_weights/ppermute | solution.py:815
  17.1 17.4 %collective-permute-start.4 = (bf16[64,1536]{1,0:T(8,128)(2,1)S(1)}, bf16[64,1536]{1,0:T(8,128)(2,1)S(1)}, u32[]{:S(2)}, u32[]{:S(2)}) collective-permute-start(bf16[64,1536]{1,0:T(8,128)(2,1)S(1)} %fusion.6.refs_0_), channel_id=1, source_target_pairs={{0,16},{8,24},{16,0},{24,8},{1,17},{9,25},{17,1},{25,9},{2,18},{10... | collective-permute-start | bytes 589832 | tf_op jit(solution)/shard_map/gather_weights/ppermute | solution.py:815
  20.3 17.6 %collective-permute-start.5 = (bf16[64,1536]{1,0:T(8,128)(2,1)S(1)}, bf16[64,1536]{1,0:T(8,128)(2,1)S(1)}, u32[]{:S(2)}, u32[]{:S(2)}) collective-permute-start(bf16[64,1536]{1,0:T(8,128)(2,1)S(1)} %fusion.6.refs_0_), channel_id=1, source_target_pairs={{0,24},{8,16},{16,8},{24,0},{1,25},{9,17},{17,9},{25,1},{2,26},{10... | collective-permute-start | bytes 589832 | tf_op jit(solution)/shard_map/gather_weights/ppermute | solution.py:815
  20.3 22.7 %collective-permute-start.6 = (bf16[192,1024]{1,0:T(8,128)(2,1)S(1)}, bf16[192,1024]{1,0:T(8,128)(2,1)S(1)}, u32[]{:S(2)}, u32[]{:S(2)}) collective-permute-start(bf16[192,1024]{1,0:T(8,128)(2,1)S(1)} %pad_maximum_fusion.2.refs_4_), channel_id=1, source_target_pairs={{0,2},{2,0},{4,6},{6,4},{1,3},{3,1},{5,7},{7,5},{8,10},{10,8},{12,... | collective-permute-start | bytes 1179656 | tf_op jit(solution)/shard_map/gather_weights/ppermute | solution.py:815
  22.0 22.5 %collective-permute-start.7 = (bf16[192,1024]{1,0:T(8,128)(2,1)S(1)}, bf16[192,1024]{1,0:T(8,128)(2,1)}, u32[]{:S(2)}, u32[]{:S(2)}) collective-permute-start(bf16[192,1024]{1,0:T(8,128)(2,1)S(1)} %pad_maximum_fusion.2.refs_4_), channel_id=1, source_target_pairs={{0,4},{2,6},{4,0},{6,2},{1,5},{3,7},{5,1},{7,3},{8,12},{10,14},{12... | collective-permute-start | bytes 1179656 | tf_op jit(solution)/shard_map/gather_weights/ppermute | solution.py:815
  24.5 20.0 %collective-permute-start.8 = (bf16[192,1024]{1,0:T(8,128)(2,1)S(1)}, bf16[192,1024]{1,0:T(8,128)(2,1)}, u32[]{:S(2)}, u32[]{:S(2)}) collective-permute-start(bf16[192,1024]{1,0:T(8,128)(2,1)S(1)} %pad_maximum_fusion.2.refs_4_), channel_id=1, source_target_pairs={{0,6},{2,4},{4,2},{6,0},{1,7},{3,5},{5,3},{7,1},{8,14},{10,12},{12... | collective-permute-start | bytes 1179656 | tf_op jit(solution)/shard_map/gather_weights/ppermute | solution.py:815
  38.0 34.5 %collective-permute-start.13 = (bf16[192,1536]{1,0:T(8,128)(2,1)S(1)}, bf16[192,1536]{1,0:T(8,128)(2,1)S(1)}, u32[]{:S(2)}, u32[]{:S(2)}) collective-permute-start(bf16[192,1536]{1,0:T(8,128)(2,1)S(1)} %pad_maximum_fusion.refs_0_), channel_id=1, source_target_pairs={{0,2},{2,0},{4,6},{6,4},{1,3},{3,1},{5,7},{7,5},{8,10},{10,8},{12,... | collective-permute-start | bytes 1769480 | tf_op jit(solution)/shard_map/gather_weights/ppermute | solution.py:815
  40.6 33.2 %collective-permute-start.14 = (bf16[192,1536]{1,0:T(8,128)(2,1)S(1)}, bf16[192,1536]{1,0:T(8,128)(2,1)S(1)}, u32[]{:S(2)}, u32[]{:S(2)}) collective-permute-start(bf16[192,1536]{1,0:T(8,128)(2,1)S(1)} %pad_maximum_fusion.refs_0_), channel_id=1, source_target_pairs={{0,4},{2,6},{4,0},{6,2},{1,5},{3,7},{5,1},{7,3},{8,12},{10,14},{12... | collective-permute-start | bytes 1769480 | tf_op jit(solution)/shard_map/gather_weights/ppermute | solution.py:815
  43.0 30.8 %collective-permute-start.15 = (bf16[192,1536]{1,0:T(8,128)(2,1)S(1)}, bf16[192,1536]{1,0:T(8,128)(2,1)S(1)}, u32[]{:S(2)}, u32[]{:S(2)}) collective-permute-start(bf16[192,1536]{1,0:T(8,128)(2,1)S(1)} %pad_maximum_fusion.refs_0_), channel_id=1, source_target_pairs={{0,6},{2,4},{4,2},{6,0},{1,7},{3,5},{5,3},{7,1},{8,14},{10,12},{12... | collective-permute-start | bytes 1769480 | tf_op jit(solution)/shard_map/gather_weights/ppermute | solution.py:815
  115.4 24.4 %collective-permute-start.17 = (bf16[784,128]{1,0:T(8,128)(2,1)S(1)}, bf16[784,128]{1,0:T(8,128)(2,1)S(1)}, u32[]{:S(2)}, u32[]{:S(2)}) collective-permute-start(bf16[784,128]{1,0:T(8,128)(2,1)S(1)} %get-tuple-element.101), channel_id=1, source_target_pairs={{2,0},{4,2},{6,4},{3,1},{5,3},{7,5},{10,8},{12,10},{14,12},{11,9},... | collective-permute-start | bytes 602120 | tf_op jit(solution)/shard_map/ppermute | solution.py:807
  116.7 23.1 %collective-permute-start.18 = (bf16[784,128]{1,0:T(8,128)(2,1)S(1)}, bf16[784,128]{1,0:T(8,128)(2,1)S(1)}, u32[]{:S(2)}, u32[]{:S(2)}) collective-permute-start(bf16[784,128]{1,0:T(8,128)(2,1)S(1)} %get-tuple-element.101), channel_id=1, source_target_pairs={{4,0},{6,2},{5,1},{7,3},{12,8},{14,10},{13,9},{15,11},{20,16},{22,... | collective-permute-start | bytes 602120 | tf_op jit(solution)/shard_map/ppermute | solution.py:807
  118.2 21.7 %collective-permute-start.19 = (bf16[784,128]{1,0:T(8,128)(2,1)S(1)}, bf16[784,128]{1,0:T(8,128)(2,1)S(1)}, u32[]{:S(2)}, u32[]{:S(2)}) collective-permute-start(bf16[784,128]{1,0:T(8,128)(2,1)S(1)} %get-tuple-element.101), channel_id=1, source_target_pairs={{6,0},{7,1},{14,8},{15,9},{22,16},{23,17},{30,24},{31,25}} | collective-permute-start | bytes 602120 | tf_op jit(solution)/shard_map/ppermute | solution.py:807
  134.5 29.7 %collective-permute-start.33 = (bf16[192,1536]{1,0:T(8,128)(2,1)S(1)}, bf16[192,1536]{1,0:T(8,128)(2,1)S(1)}, u32[]{:S(2)}, u32[]{:S(2)}) collective-permute-start(bf16[192,1536]{1,0:T(8,128)(2,1)S(1)} %get-tuple-element.134), channel_id=1, source_target_pairs={{0,2},{2,0},{4,6},{6,4},{1,3},{3,1},{5,7},{7,5},{8,10},{10,8},{12,... | collective-permute-start | bytes 1769480 | tf_op jit(solution)/shard_map/reduce_gate_weights/ppermute | solution.py:815
  136.6 29.6 %collective-permute-start.34 = (bf16[192,1536]{1,0:T(8,128)(2,1)S(1)}, bf16[192,1536]{1,0:T(8,128)(2,1)S(1)}, u32[]{:S(2)}, u32[]{:S(2)}) collective-permute-start(bf16[192,1536]{1,0:T(8,128)(2,1)S(1)} %get-tuple-element.135), channel_id=1, source_target_pairs={{0,4},{2,6},{4,0},{6,2},{1,5},{3,7},{5,1},{7,3},{8,12},{10,14},{12... | collective-permute-start | bytes 1769480 | tf_op jit(solution)/shard_map/reduce_gate_weights/ppermute | solution.py:815
  139.9 27.2 %collective-permute-start.35 = (bf16[192,1536]{1,0:T(8,128)(2,1)S(1)}, bf16[192,1536]{1,0:T(8,128)(2,1)S(1)}, u32[]{:S(2)}, u32[]{:S(2)}) collective-permute-start(bf16[192,1536]{1,0:T(8,128)(2,1)S(1)} %get-tuple-element.136), channel_id=1, source_target_pairs={{0,6},{2,4},{4,2},{6,0},{1,7},{3,5},{5,3},{7,1},{8,14},{10,12},{12... | collective-permute-start | bytes 1769480 | tf_op jit(solution)/shard_map/reduce_gate_weights/ppermute | solution.py:815
  139.9 69.7 %collective-permute-start.16 = (bf16[1024,384]{1,0:T(8,128)(2,1)S(1)}, bf16[1024,384]{1,0:T(8,128)(2,1)S(1)}, u32[]{:S(2)}, u32[]{:S(2)}) collective-permute-start(bf16[1024,384]{1,0:T(8,128)(2,1)S(1)} %get-tuple-element.100), channel_id=1, source_target_pairs={{0,1},{1,0},{2,3},{3,2},{4,5},{5,4},{6,7},{7,6},{8,9},{9,8},{10,11... | collective-permute-start | bytes 2359304 | tf_op jit(solution)/shard_map/layer_out/ppermute | solution.py:811
  162.7 13.0 %collective-permute-start.20 = (bf16[192,1152]{1,0:T(8,128)(2,1)S(1)}, bf16[192,1152]{1,0:T(8,128)(2,1)S(1)}, u32[]{:S(2)}, u32[]{:S(2)}) collective-permute-start(bf16[192,1152]{1,0:T(8,128)(2,1)S(1)} %get-tuple-element.120), channel_id=1, source_target_pairs={{0,2},{2,0},{4,6},{6,4},{1,3},{3,1},{5,7},{7,5},{8,10},{10,8},{12,... | collective-permute-start | bytes 1327112 | tf_op jit(solution)/shard_map/ppermute | solution.py:815
  164.2 22.0 %collective-permute-start.21 = (bf16[192,1152]{1,0:T(8,128)(2,1)S(1)}, bf16[192,1152]{1,0:T(8,128)(2,1)S(1)}, u32[]{:S(2)}, u32[]{:S(2)}) collective-permute-start(bf16[192,1152]{1,0:T(8,128)(2,1)S(1)} %get-tuple-element.122), channel_id=1, source_target_pairs={{0,4},{2,6},{4,0},{6,2},{1,5},{3,7},{5,1},{7,3},{8,12},{10,14},{12... | collective-permute-start | bytes 1327112 | tf_op jit(solution)/shard_map/ppermute | solution.py:815
  166.2 20.0 %collective-permute-start.22 = (bf16[192,1152]{1,0:T(8,128)(2,1)S(1)}, bf16[192,1152]{1,0:T(8,128)(2,1)S(1)}, u32[]{:S(2)}, u32[]{:S(2)}) collective-permute-start(bf16[192,1152]{1,0:T(8,128)(2,1)S(1)} %get-tuple-element.123), channel_id=1, source_target_pairs={{0,6},{2,4},{4,2},{6,0},{1,7},{3,5},{5,3},{7,1},{8,14},{10,12},{12... | collective-permute-start | bytes 1327112 | tf_op jit(solution)/shard_map/ppermute | solution.py:815
  167.4 23.4 %collective-permute-start.36 = (bf16[96,1536]{1,0:T(8,128)(2,1)S(1)}, bf16[96,1536]{1,0:T(8,128)(2,1)S(1)}, u32[]{:S(2)}, u32[]{:S(2)}) collective-permute-start(bf16[96,1536]{1,0:T(8,128)(2,1)S(1)} %pad_maximum_fusion.3), channel_id=1, source_target_pairs={{0,8},{8,0},{16,24},{24,16},{1,9},{9,1},{17,25},{25,17},{2,10},{10... | collective-permute-start | bytes 884744 | tf_op jit(solution)/shard_map/reduce_gate_weights/ppermute | solution.py:815
  181.8 42.7 %collective-permute-start.28 = (f32[8,768]{1,0:T(8,128)S(1)}, f32[8,768]{1,0:T(8,128)S(1)}, u32[]{:S(2)}, u32[]{:S(2)}) collective-permute-start(f32[8,768]{1,0:T(8,128)S(1)} %get-tuple-element.129), channel_id=1, source_target_pairs={{2,0},{3,1},{4,2},{5,3},{6,4},{7,5},{10,8},{11,9},{12,10},{13,11},... | collective-permute-start | bytes 73736 | tf_op jit(solution)/shard_map/ppermute | solution.py:1178
  186.6 12.7 %collective-permute-start.24 = (bf16[48,1152]{1,0:T(8,128)(2,1)S(1)}, bf16[48,1152]{1,0:T(8,128)(2,1)S(1)}, u32[]{:S(2)}, u32[]{:S(2)}) collective-permute-start(bf16[48,1152]{1,0:T(8,128)(2,1)S(1)} %get-tuple-element.160), channel_id=1, source_target_pairs={{0,16},{8,24},{16,0},{24,8},{1,17},{9,25},{17,1},{25,9},{2,18},{10... | collective-permute-start | bytes 331784 | tf_op jit(solution)/shard_map/reduce_input_weights/ppermute | solution.py:815
  192.5 32.0 %collective-permute-start.29 = (f32[8,768]{1,0:T(8,128)S(1)}, f32[8,768]{1,0:T(8,128)S(1)}, u32[]{:S(2)}, u32[]{:S(2)}) collective-permute-start(f32[8,768]{1,0:T(8,128)S(1)} %get-tuple-element.129), channel_id=1, source_target_pairs={{2,1},{3,0},{4,3},{5,2},{6,5},{7,4},{10,9},{11,8},{12,11},{13,10},... | collective-permute-start | bytes 73736 | tf_op jit(solution)/shard_map/ppermute | solution.py:1179
  199.3 25.2 %collective-permute-start.27 = (bf16[1024,768]{1,0:T(8,128)(2,1)S(1)}, bf16[1024,768]{1,0:T(8,128)(2,1)S(1)}, u32[]{:S(2)}, u32[]{:S(2)}) collective-permute-start(bf16[1024,768]{1,0:T(8,128)(2,1)S(1)} %get-tuple-element.128.own), channel_id=1, source_target_pairs={{0,1},{1,0},{2,3},{3,2},{4,5},{5,4},{6,7},{7,6},{8,9},{9,8},{10,11... | collective-permute-start | bytes 4718600 | tf_op jit(solution)/shard_map/ppermute | solution.py:811
  (63 other events, 566.6 us)

commit v8 on v7

--- a/solution.py
+++ b/solution.py
@@ -439,7 +439,7 @@
 
 
 def gate_back_kernel(
-    counts, inner_all, info, stat, y, z, dn, cot, cum, bc, xc, hb, decay, wo, par, spread,
+    counts, inner_all, info, stat, other_stat, y, z, dn, cot, cum, bc, xc, hb, decay, wo, par, spread,
     keep_o, send_o, gwo_o, small_o, dy_o, dz_o, de_o, exit_o, packet_o,
     acc, run, factor,
 ):
@@ -457,7 +457,7 @@
         factor[...] = jnp.ones_like(factor)
         small_o[...] = jnp.zeros_like(small_o)
 
-    column = jnp.concatenate([stat[...], jnp.zeros((LANES - 8, BLOCK), F32)], axis=0).T
+    column = jnp.concatenate([stat[...] + other_stat[...], jnp.zeros((LANES - 8, BLOCK), F32)], axis=0).T
     inv = lax.rsqrt(column[:, 0:1] / inner_all + EPS)
     cross = column[:, 1:2]
     gain = par[6:7, :inner]
@@ -979,7 +979,7 @@
             pltpu.VMEM((inner, LANES), F32),
             pltpu.VMEM((8, LANES), F32),
         ],
-        micros=20,
+        micros=40,
         mega=16,
     )
     packets = [(shifted(packet, "ctx", step), "whole") for step in range(1, ctx_count)]
@@ -1020,7 +1020,7 @@
         micros=8,
         mega=12,
     )
-    stat = lax.psum(stat, "tp")
+    other_stat = swapped(stat)
     inner_all = inner * lax.axis_size("tp")
     half = width // 2
     keep, send, gwo, small_gate, dy, dz, de, exits, packet = call(
@@ -1029,6 +1029,7 @@
         info,
         [
             (stat, "lanes"),
+            (other_stat, "lanes"),
             (y, "rows"),
             (z, "rows"),
             (dn, "rows"),
@@ -1180,7 +1181,11 @@
     with jax.named_scope("reduce_input_weights"):
         norm_part = jnp.pad(norm_part, ((0, 0), (channels, 0)))
         if parts > 1:
-            total1 = dp_sum(sum(piece.astype(F32) for piece in g1) + norm_part)
+            total1 = sum(piece.astype(F32) for piece in g1) + norm_part
+            total1, total2 = lax.optimization_barrier((total1, total2))
+            total1 = dp_sum(total1)
+            total2 = doubled(total2)
+            total1, total2 = lax.optimization_barrier((total1, total2))
         else:
             total1 = whole_sum((g1[0].astype(F32) + norm_part).astype(BF16))
         across = swapped(total1[:, inner:])
@@ -1208,9 +1213,8 @@
     )
     with jax.named_scope("last_hop"):
         if parts > 1:
-            total2 = doubled(total2)
-            total1, grad_tokens = lax.optimization_barrier((total1, grad_tokens))
             total1 = exchanged(total1, "ctx")
+            total1[-1], grad_tokens = lax.optimization_barrier((total1[-1], grad_tokens))
         else:
             total1 = [total1]
     each = HEAD // dp_count

time: 239 us -> 229 us (0.958)
  waiting for transfers between devices: 47.3 us -> 36 us
  starting transfers between devices: 62.2 us -> 66.5 us
  blocking collectives: 3.39 us -> 0 us
    ppermute x28, waiting for transfers between devices: 46.3 us -> 34.8 us  [partnered(): lax.ppermute(value, axis, [(one, one ^ mask) for one in range(lax.axis_si...]
    psum x1 -> x0, blocking collectives: 3.39 us -> none  [body(): stat = lax.psum(stat, 'tp')]
    ppermute x28, starting transfers between devices: 45 us -> 47.9 us  [partnered(): lax.ppermute(value, axis, [(one, one ^ mask) for one in range(lax.axis_si...]
  transfers between devices with their start and end apart: 40 -> 41, of which waited for: 13 -> 13; matrix products, arithmetic and copies ran while one was open for 5% -> 5% of each run, Pallas kernels for 28% -> 31%
where the time goes in v8:
time: 229 us; the launch traced here: 228 us
  Pallas kernels  87.7 us (38%)
  starting transfers between devices  66.5 us (29%)
  waiting for transfers between devices  36 us (16%)
  local copies, waits for them, and re-layouts  27.6 us (12%)
  other arithmetic  8.01 us (3%)
    pallas_call x10, Pallas kernels, call(): pl.pallas_call(body, grid=(steps,), in_specs=[pl.BlockSpec(memory_space=p...  87.7 us
    ppermute x28, starting transfers between devices, partnered(): lax.ppermute(value, axis, [(one, one ^ mask) for one in range(lax.axis_si...  47.9 us
    ppermute x28, waiting for transfers between devices, partnered(): lax.ppermute(value, axis, [(one, one ^ mask) for one in range(lax.axis_si...  34.8 us
    unnamed x95, local copies, waits for them, and re-layouts  24.3 us
    ppermute x7, starting transfers between devices, shifted(): lax.ppermute(value, axis, [(source, source + steps) for source in range(f...  15.7 us
  transfers between devices with their start and end apart: 41, of which 13 were waited for; matrix products, arithmetic and copies ran while one was open for 5% of the time, Pallas kernels for 31%

profile of v8, /device:TPU:0, one launch (start us, length us, event | category | flops | bytes accessed | tf_op | source)
XLA Modules:
  0.0 228.1 jit_solution(5834383220943296999)
XLA Ops:
  1.7 5.1 %collective-permute-start.2 = (bf16[48,1024]{1,0:T(8,128)(2,1)S(1)}, bf16[48,1024]{1,0:T(8,128)(2,1)S(1)}, u32[]{:S(2)}, u32[]{:S(2)}) collective-permute-start(bf16[48,1024]{1,0:T(8,128)(2,1)S(1)} %fusion.7), channel_id=1, source_target_pairs={{0,24},{8,16},{16,8},{24,0},{1,25},{9,17},{17,9},{25,1},{2,26},{10... | collective-permute-start | bytes 294920 | tf_op jit(solution)/shard_map/gather_weights/ppermute | solution.py:815
  15.2 3.8 %collective-permute-start.5 = (bf16[64,1536]{1,0:T(8,128)(2,1)S(1)}, bf16[64,1536]{1,0:T(8,128)(2,1)S(1)}, u32[]{:S(2)}, u32[]{:S(2)}) collective-permute-start(bf16[64,1536]{1,0:T(8,128)(2,1)S(1)} %fusion.3.refs_0_), channel_id=1, source_target_pairs={{0,24},{8,16},{16,8},{24,0},{1,25},{9,17},{17,9},{25,1},{2,26},{10... | collective-permute-start | bytes 589832 | tf_op jit(solution)/shard_map/gather_weights/ppermute | solution.py:815
  28.9 5.8 %collective-permute-done.4.refs_2_ = bf16[64,1536]{1,0:T(8,128)(2,1)S(1)} collective-permute-done((bf16[64,1536]{1,0:T(8,128)(2,1)S(1)}, bf16[64,1536]{1,0:T(8,128)(2,1)S(1)}, u32[]{:S(2)}, u32[]{:S(2)}) %collective-permute-start.4) | collective-permute-done | bytes 196640 | tf_op jit(solution)/shard_map/gather_weights/ppermute | solution.py:815
  34.8 3.4 %collective-permute-start.9 = (bf16[16,768]{1,0:T(8,128)(2,1)S(1)}, bf16[16,768]{1,0:T(8,128)(2,1)S(1)}, u32[]{:S(2)}, u32[]{:S(2)}) collective-permute-start(bf16[16,768]{1,0:T(8,128)(2,1)S(1)} %constant_dynamic-slice_fusion), channel_id=1, source_target_pairs={{0,2},{2,4},{4,6},{1,3},{3,5},{5,7},{8,10},{10,12},{12,14},{9,11},... | collective-permute-start | bytes 73736 | tf_op jit(solution)/shard_map/ppermute | solution.py:807
  39.9 3.4 %collective-permute-start.14 = (bf16[192,1536]{1,0:T(8,128)(2,1)S(1)}, bf16[192,1536]{1,0:T(8,128)(2,1)S(1)}, u32[]{:S(2)}, u32[]{:S(2)}) collective-permute-start(bf16[192,1536]{1,0:T(8,128)(2,1)S(1)} %pad_maximum_fusion.refs_0_), channel_id=1, source_target_pairs={{0,4},{2,6},{4,0},{6,2},{1,5},{3,7},{5,1},{7,3},{8,12},{10,14},{12... | collective-permute-start | bytes 1769480 | tf_op jit(solution)/shard_map/gather_weights/ppermute | solution.py:815
  43.6 17.6 %shard_map.297 = (bf16[768,1152]{1,0:T(8,128)(2,1)S(1)}, f32[8,1024]{1,0:T(8,128)S(1)}, bf16[1024,768]{1,0:T(8,128)(2,1)S(1)}, bf16[16,768]{1,0:T(8,128)(2,1)S(1...) custom-call(s32[10]{0:T(128)S(1)} %concatenate.41.info, ...), custom_call_target="tpu_custom_call" | custom-call | flops 44000002048 | bytes 140000000 | tf_op jit(solution)/shard_map/pallas_call | solution.py:787
  65.9 3.1 %collective-permute-start.10 = (bf16[784,128]{1,0:T(8,128)(2,1)S(1)}, bf16[784,128]{1,0:T(8,128)(2,1)S(1)}, u32[]{:S(2)}, u32[]{:S(2)}) collective-permute-start(bf16[784,128]{1,0:T(8,128)(2,1)S(1)} %get-tuple-element.88), channel_id=1, source_target_pairs={{0,2},{2,4},{4,6},{1,3},{3,5},{5,7},{8,10},{10,12},{12,14},{9,11},... | collective-permute-start | bytes 602120 | tf_op jit(solution)/shard_map/ppermute | solution.py:807
  69.0 3.9 %collective-permute-start.11 = (bf16[784,128]{1,0:T(8,128)(2,1)S(1)}, bf16[784,128]{1,0:T(8,128)(2,1)S(1)}, u32[]{:S(2)}, u32[]{:S(2)}) collective-permute-start(bf16[784,128]{1,0:T(8,128)(2,1)S(1)} %get-tuple-element.88), channel_id=1, source_target_pairs={{0,4},{2,6},{1,5},{3,7},{8,12},{10,14},{9,13},{11,15},{16,20},{18,... | collective-permute-start | bytes 602120 | tf_op jit(solution)/shard_map/ppermute | solution.py:807
  74.2 4.0 %shard_map.298 = (bf16[768,1536]{1,0:T(8,128)(2,1)S(1)}, bf16[1024,768]{1,0:T(8,128)(2,1)S(1)}, bf16[1024,768]{1,0:T(8,128)(2,1)S(1)}) custom-call(s32[10]{0:T(128)S(1)} %concatenate.41.info, bf16[192,1536]{1,0:T(8,128)(2,1)S(1)} %pad_maximum_fusion.refs_0_, bf16[192,1536]{1,0:T(8,128)(2,1)S(1)} %collective-permute-done.13.refs_1_, ...), custom_call_target="tpu_custom_call" | custom-call | flops 7699999744 | bytes 24500000 | tf_op jit(solution)/shard_map/pallas_call | solution.py:787
  79.7 4.2 %shard_map.299 = (f32[1024,768]{1,0:T(8,128)S(1)}, bf16[4,768,128]{2,1,0:T(8,128)(2,1)S(1)}, f32[4,768,128]{2,1,0:T(8,128)S(1)}, f32[8,1024]{1,0:T(8,128)S(1)}) custom-call(s32[10]{0:T(128)S(1)} %concatenate.41.info, bf16[784,128]{1,0:T(8,128)(2,1)S(1)} %collective-permute-done.10.refs_0_, bf16[784,128]{1,0:T(8,128)(2,1)S(1)} %collective-permute-done.11.refs_1_, ...), custom_call_target="tpu_custom_call" | custom-call | flops 8800000000 | bytes 28000000 | tf_op jit(solution)/shard_map/pallas_call | solution.py:787
  102.7 11.1 %shard_map.300 = (bf16[1024,384]{1,0:T(8,128)(2,1)S(1)}, bf16[1024,384]{1,0:T(8,128)(2,1)S(1)}, bf16[768,768]{1,0:T(8,128)(2,1)S(1)}, f32[8,768]{1,0:T(8,128)S(1...) custom-call(s32[10]{0:T(128)S(1)} %concatenate.41.info, ...), custom_call_target="tpu_custom_call" | custom-call | flops 16499999744 | bytes 52500000 | tf_op jit(solution)/shard_map/pallas_call | solution.py:787
  118.2 15.0 %shard_map.301 = (bf16[1024,768]{1,0:T(8,128)(2,1)S(1)}, f32[1024,128]{1,0:T(8,128)S(1)}, f32[1024,128]{1,0:T(8,128)S(1)}, f32[1024,128]{1,0:T(8,128)S(1)}, f32[...) custom-call(s32[10]{0:T(128)S(1)} %concatenate.41.info, ...), custom_call_target="tpu_custom_call" | custom-call | flops 19800000512 | bytes 63000000 | tf_op jit(solution)/shard_map/pallas_call | solution.py:787
  133.3 4.7 %collective-permute-start.26 = (bf16[192,1536]{1,0:T(8,128)(2,1)S(1)}, bf16[192,1536]{1,0:T(8,128)(2,1)S(1)}, u32[]{:S(2)}, u32[]{:S(2)}) collective-permute-start(bf16[192,1536]{1,0:T(8,128)(2,1)S(1)} %get-tuple-element.135), channel_id=1, source_target_pairs={{0,6},{2,4},{4,2},{6,0},{1,7},{3,5},{5,3},{7,1},{8,14},{10,12},{12... | collective-permute-start | bytes 1769480 | tf_op jit(solution)/shard_map/reduce_gate_weights/ppermute | solution.py:815
  138.6 22.8 %shard_map.302 = (bf16[1024,1152]{1,0:T(8,128)(2,1)S(1)}, bf16[16,1024]{1,0:T(8,128)(2,1)S(1)}, bf16[192,1152]{1,0:T(8,128)(2,1)S(1)}, bf16[192,1152]{1,0:T(8,12...) custom-call(s32[10]{0:T(128)S(1)} %concatenate.41.info, ...), custom_call_target="tpu_custom_call" | custom-call | flops 27499999232 | bytes 87500000 | tf_op jit(solution)/shard_map/pallas_call | solution.py:787
  165.4 4.0 %collective-permute-start.27 = (bf16[96,1536]{1,0:T(8,128)(2,1)S(1)}, bf16[96,1536]{1,0:T(8,128)(2,1)S(1)}, u32[]{:S(2)}, u32[]{:S(2)}) collective-permute-start(bf16[96,1536]{1,0:T(8,128)(2,1)S(1)} %pad_maximum_fusion.3), channel_id=1, source_target_pairs={{0,8},{8,0},{16,24},{24,16},{1,9},{9,1},{17,25},{25,17},{2,10},{10... | collective-permute-start | bytes 884744 | tf_op jit(solution)/shard_map/reduce_gate_weights/ppermute | solution.py:815
  169.4 5.2 %collective-permute-done.21 = bf16[192,1152]{1,0:T(8,128)(2,1)S(1)} collective-permute-done((bf16[192,1152]{1,0:T(8,128)(2,1)S(1)}, bf16[192,1152]{1,0:T(8,128)(2,1)S(1)}, u32[]{:S(2)}, u32[]{:S(2)}) %collective-permute-start.21) | collective-permute-done | bytes 442400 | tf_op jit(solution)/shard_map/ppermute | solution.py:815
  174.5 6.0 %shard_map.303 = (bf16[1024,768]{1,0:T(8,128)(2,1)S(1)}, f32[8,768]{1,0:T(8,128)S(1)}, f32[192,128]{1,0:T(8,128)S(1)}) custom-call(s32[10]{0:T(128)S(1)} %concatenate.41.info, bf16[1024,1152]{1,0:T(8,128)(2,1)S(1)} %get-tuple-element.128.packed, bf16[16,1024]{1,0:T(8,128)(2,1)S(1)} %get-tuple-element.129.back, ...), custom_call_target="tpu_custom_call" | custom-call | flops 5500000256 | bytes 17500000 | tf_op jit(solution)/shard_map/pallas_call | solution.py:787
  180.6 3.3 %collective-permute-done.23 = bf16[192,1152]{1,0:T(8,128)(2,1)S(1)} collective-permute-done((bf16[192,1152]{1,0:T(8,128)(2,1)S(1)}, bf16[192,1152]{1,0:T(8,128)(2,1)S(1)}, u32[]{:S(2)}, u32[]{:S(2)}) %collective-permute-start.23) | collective-permute-done | bytes 442400 | tf_op jit(solution)/shard_map/ppermute | solution.py:815
  188.2 4.4 %collective-permute-done.28 = bf16[48,1536]{1,0:T(8,128)(2,1)S(1)} collective-permute-done((bf16[48,1536]{1,0:T(8,128)(2,1)S(1)}, bf16[48,1536]{1,0:T(8,128)(2,1)S(1)}, u32[]{:S(2)}, u32[]{:S(2)}) %collective-permute-start.28) | collective-permute-done | bytes 147488 | tf_op jit(solution)/shard_map/reduce_gate_weights/ppermute | solution.py:815
  192.6 3.4 %collective-permute-start.32 = (bf16[48,1536]{1,0:T(8,128)(2,1)S(1)}, bf16[48,1536]{1,0:T(8,128)(2,1)S(1)}, u32[]{:S(2)}, u32[]{:S(2)}) collective-permute-start(bf16[48,1536]{1,0:T(8,128)(2,1)S(1)} %fusion.4), channel_id=1, source_target_pairs={{0,2},{2,0},{4,6},{6,4},{1,3},{3,1},{5,7},{7,5},{8,10},{10,8},{12,... | collective-permute-start | bytes 442376 | tf_op jit(solution)/shard_map/reduce_input_weights/ppermute | solution.py:815
  196.0 2.7 %collective-permute-start.31 = (bf16[48,1152]{1,0:T(8,128)(2,1)S(1)}, bf16[48,1152]{1,0:T(8,128)(2,1)S(1)}, u32[]{:S(2)}, u32[]{:S(2)}) collective-permute-start(bf16[48,1152]{1,0:T(8,128)(2,1)S(1)} %get-tuple-element.165), channel_id=1, source_target_pairs={{0,24},{8,16},{16,8},{24,0},{1,25},{9,17},{17,9},{25,1},{2,26},{10... | collective-permute-start | bytes 331784 | tf_op jit(solution)/shard_map/reduce_input_weights/ppermute | solution.py:815
  204.3 3.2 %collective-permute-done.30 = bf16[48,1152]{1,0:T(8,128)(2,1)S(1)} collective-permute-done((bf16[48,1152]{1,0:T(8,128)(2,1)S(1)}, bf16[48,1152]{1,0:T(8,128)(2,1)S(1)}, u32[]{:S(2)}, u32[]{:S(2)}) %collective-permute-start.30) | collective-permute-done | bytes 110624 | tf_op jit(solution)/shard_map/reduce_input_weights/ppermute | solution.py:815
  208.6 6.9 %collective-permute-done.33 = bf16[96,1536]{1,0:T(8,128)(2,1)S(1)} collective-permute-done((bf16[96,1536]{1,0:T(8,128)(2,1)S(1)}, bf16[96,1536]{1,0:T(8,128)(2,1)S(1)}, u32[]{:S(2)}, u32[]{:S(2)}) %collective-permute-start.33) | collective-permute-done | bytes 294944 | tf_op jit(solution)/shard_map/reduce_input_weights/ppermute | solution.py:815
  220.9 3.6 %shard_map.304 = f32[1024,768]{1,0:T(8,128)} custom-call(s32[10]{0:T(128)S(1)} %concatenate.41.info, bf16[1024,768]{1,0:T(8,128)(2,1)S(1)} %get-tuple-element.139.own, bf16[1024,768]{1,0:T(8,128)(2,1)S(1)} %collective-permute-done.36.other, f32[8,768]{1,0:T(8,128)S(1)} %collective-permute-done.37.halo_a, f32[8,768]{1,0:T(8,128)S(1)} %collective-permute-done.38.halo_b, ...), custom_call_target="tpu_custom_call" | custom-call | flops 5500000256 | bytes 17500000 | tf_op jit(solution)/shard_map/pallas_call | solution.py:787
  (210 shorter events, 75.4 us)
Async XLA Ops:
  1.7 13.4 %collective-permute-start.2 = (bf16[48,1024]{1,0:T(8,128)(2,1)S(1)}, bf16[48,1024]{1,0:T(8,128)(2,1)S(1)}, u32[]{:S(2)}, u32[]{:S(2)}) collective-permute-start(bf16[48,1024]{1,0:T(8,128)(2,1)S(1)} %fusion.7), channel_id=1, source_target_pairs={{0,24},{8,16},{16,8},{24,0},{1,25},{9,17},{17,9},{25,1},{2,26},{10... | collective-permute-start | bytes 294920 | tf_op jit(solution)/shard_map/gather_weights/ppermute | solution.py:815
  19.0 19.2 %collective-permute-start.3 = (bf16[64,1536]{1,0:T(8,128)(2,1)S(1)}, bf16[64,1536]{1,0:T(8,128)(2,1)S(1)}, u32[]{:S(2)}, u32[]{:S(2)}) collective-permute-start(bf16[64,1536]{1,0:T(8,128)(2,1)S(1)} %fusion.3.refs_0_), channel_id=1, source_target_pairs={{0,8},{8,0},{16,24},{24,16},{1,9},{9,1},{17,25},{25,17},{2,10},{10... | collective-permute-start | bytes 589832 | tf_op jit(solution)/shard_map/gather_weights/ppermute | solution.py:815
  19.0 15.8 %collective-permute-start.4 = (bf16[64,1536]{1,0:T(8,128)(2,1)S(1)}, bf16[64,1536]{1,0:T(8,128)(2,1)S(1)}, u32[]{:S(2)}, u32[]{:S(2)}) collective-permute-start(bf16[64,1536]{1,0:T(8,128)(2,1)S(1)} %fusion.3.refs_0_), channel_id=1, source_target_pairs={{0,16},{8,24},{16,0},{24,8},{1,17},{9,25},{17,1},{25,9},{2,18},{10... | collective-permute-start | bytes 589832 | tf_op jit(solution)/shard_map/gather_weights/ppermute | solution.py:815
  19.7 23.6 %collective-permute-start.6 = (bf16[192,1024]{1,0:T(8,128)(2,1)S(1)}, bf16[192,1024]{1,0:T(8,128)(2,1)S(1)}, u32[]{:S(2)}, u32[]{:S(2)}) collective-permute-start(bf16[192,1024]{1,0:T(8,128)(2,1)S(1)} %pad_maximum_fusion.2.refs_4_), channel_id=1, source_target_pairs={{0,2},{2,0},{4,6},{6,4},{1,3},{3,1},{5,7},{7,5},{8,10},{10,8},{12,... | collective-permute-start | bytes 1179656 | tf_op jit(solution)/shard_map/gather_weights/ppermute | solution.py:815
  21.3 22.4 %collective-permute-start.7 = (bf16[192,1024]{1,0:T(8,128)(2,1)S(1)}, bf16[192,1024]{1,0:T(8,128)(2,1)}, u32[]{:S(2)}, u32[]{:S(2)}) collective-permute-start(bf16[192,1024]{1,0:T(8,128)(2,1)S(1)} %pad_maximum_fusion.2.refs_4_), channel_id=1, source_target_pairs={{0,4},{2,6},{4,0},{6,2},{1,5},{3,7},{5,1},{7,3},{8,12},{10,14},{12... | collective-permute-start | bytes 1179656 | tf_op jit(solution)/shard_map/gather_weights/ppermute | solution.py:815
  24.9 18.8 %collective-permute-start.8 = (bf16[192,1024]{1,0:T(8,128)(2,1)S(1)}, bf16[192,1024]{1,0:T(8,128)(2,1)}, u32[]{:S(2)}, u32[]{:S(2)}) collective-permute-start(bf16[192,1024]{1,0:T(8,128)(2,1)S(1)} %pad_maximum_fusion.2.refs_4_), channel_id=1, source_target_pairs={{0,6},{2,4},{4,2},{6,0},{1,7},{3,5},{5,3},{7,1},{8,14},{10,12},{12... | collective-permute-start | bytes 1179656 | tf_op jit(solution)/shard_map/gather_weights/ppermute | solution.py:815
  38.3 34.6 %collective-permute-start.13 = (bf16[192,1536]{1,0:T(8,128)(2,1)S(1)}, bf16[192,1536]{1,0:T(8,128)(2,1)S(1)}, u32[]{:S(2)}, u32[]{:S(2)}) collective-permute-start(bf16[192,1536]{1,0:T(8,128)(2,1)S(1)} %pad_maximum_fusion.refs_0_), channel_id=1, source_target_pairs={{0,2},{2,0},{4,6},{6,4},{1,3},{3,1},{5,7},{7,5},{8,10},{10,8},{12,... | collective-permute-start | bytes 1769480 | tf_op jit(solution)/shard_map/gather_weights/ppermute | solution.py:815
  39.9 34.3 %collective-permute-start.14 = (bf16[192,1536]{1,0:T(8,128)(2,1)S(1)}, bf16[192,1536]{1,0:T(8,128)(2,1)S(1)}, u32[]{:S(2)}, u32[]{:S(2)}) collective-permute-start(bf16[192,1536]{1,0:T(8,128)(2,1)S(1)} %pad_maximum_fusion.refs_0_), channel_id=1, source_target_pairs={{0,4},{2,6},{4,0},{6,2},{1,5},{3,7},{5,1},{7,3},{8,12},{10,14},{12... | collective-permute-start | bytes 1769480 | tf_op jit(solution)/shard_map/gather_weights/ppermute | solution.py:815
  43.2 31.0 %collective-permute-start.15 = (bf16[192,1536]{1,0:T(8,128)(2,1)S(1)}, bf16[192,1536]{1,0:T(8,128)(2,1)S(1)}, u32[]{:S(2)}, u32[]{:S(2)}) collective-permute-start(bf16[192,1536]{1,0:T(8,128)(2,1)S(1)} %pad_maximum_fusion.refs_0_), channel_id=1, source_target_pairs={{0,6},{2,4},{4,2},{6,0},{1,7},{3,5},{5,3},{7,1},{8,14},{10,12},{12... | collective-permute-start | bytes 1769480 | tf_op jit(solution)/shard_map/gather_weights/ppermute | solution.py:815
  65.9 13.7 %collective-permute-start.10 = (bf16[784,128]{1,0:T(8,128)(2,1)S(1)}, bf16[784,128]{1,0:T(8,128)(2,1)S(1)}, u32[]{:S(2)}, u32[]{:S(2)}) collective-permute-start(bf16[784,128]{1,0:T(8,128)(2,1)S(1)} %get-tuple-element.88), channel_id=1, source_target_pairs={{0,2},{2,4},{4,6},{1,3},{3,5},{5,7},{8,10},{10,12},{12,14},{9,11},... | collective-permute-start | bytes 602120 | tf_op jit(solution)/shard_map/ppermute | solution.py:807
  113.8 24.1 %collective-permute-start.18 = (bf16[784,128]{1,0:T(8,128)(2,1)S(1)}, bf16[784,128]{1,0:T(8,128)(2,1)S(1)}, u32[]{:S(2)}, u32[]{:S(2)}) collective-permute-start(bf16[784,128]{1,0:T(8,128)(2,1)S(1)} %get-tuple-element.105), channel_id=1, source_target_pairs={{2,0},{4,2},{6,4},{3,1},{5,3},{7,5},{10,8},{12,10},{14,12},{11,9},... | collective-permute-start | bytes 602120 | tf_op jit(solution)/shard_map/ppermute | solution.py:807
  115.1 22.8 %collective-permute-start.19 = (bf16[784,128]{1,0:T(8,128)(2,1)S(1)}, bf16[784,128]{1,0:T(8,128)(2,1)S(1)}, u32[]{:S(2)}, u32[]{:S(2)}) collective-permute-start(bf16[784,128]{1,0:T(8,128)(2,1)S(1)} %get-tuple-element.105), channel_id=1, source_target_pairs={{4,0},{6,2},{5,1},{7,3},{12,8},{14,10},{13,9},{15,11},{20,16},{22,... | collective-permute-start | bytes 602120 | tf_op jit(solution)/shard_map/ppermute | solution.py:807
  116.4 22.2 %collective-permute-start.20 = (bf16[784,128]{1,0:T(8,128)(2,1)S(1)}, bf16[784,128]{1,0:T(8,128)(2,1)S(1)}, u32[]{:S(2)}, u32[]{:S(2)}) collective-permute-start(bf16[784,128]{1,0:T(8,128)(2,1)S(1)} %get-tuple-element.105), channel_id=1, source_target_pairs={{6,0},{7,1},{14,8},{15,9},{22,16},{23,17},{30,24},{31,25}} | collective-permute-start | bytes 602120 | tf_op jit(solution)/shard_map/ppermute | solution.py:807
  117.9 68.8 %collective-permute-start.17 = (bf16[1024,384]{1,0:T(8,128)(2,1)S(1)}, bf16[1024,384]{1,0:T(8,128)(2,1)S(1)}, u32[]{:S(2)}, u32[]{:S(2)}) collective-permute-start(bf16[1024,384]{1,0:T(8,128)(2,1)S(1)} %get-tuple-element.104), channel_id=1, source_target_pairs={{0,1},{1,0},{2,3},{3,2},{4,5},{5,4},{6,7},{7,6},{8,9},{9,8},{10,11... | collective-permute-start | bytes 2359304 | tf_op jit(solution)/shard_map/layer_out/ppermute | solution.py:811
  133.3 29.7 %collective-permute-start.26 = (bf16[192,1536]{1,0:T(8,128)(2,1)S(1)}, bf16[192,1536]{1,0:T(8,128)(2,1)S(1)}, u32[]{:S(2)}, u32[]{:S(2)}) collective-permute-start(bf16[192,1536]{1,0:T(8,128)(2,1)S(1)} %get-tuple-element.135), channel_id=1, source_target_pairs={{0,6},{2,4},{4,2},{6,0},{1,7},{3,5},{5,3},{7,1},{8,14},{10,12},{12... | collective-permute-start | bytes 1769480 | tf_op jit(solution)/shard_map/reduce_gate_weights/ppermute | solution.py:815
  137.9 26.6 %collective-permute-start.25 = (bf16[192,1536]{1,0:T(8,128)(2,1)S(1)}, bf16[192,1536]{1,0:T(8,128)(2,1)S(1)}, u32[]{:S(2)}, u32[]{:S(2)}) collective-permute-start(bf16[192,1536]{1,0:T(8,128)(2,1)S(1)} %get-tuple-element.134), channel_id=1, source_target_pairs={{0,4},{2,6},{4,0},{6,2},{1,5},{3,7},{5,1},{7,3},{8,12},{10,14},{12... | collective-permute-start | bytes 1769480 | tf_op jit(solution)/shard_map/reduce_gate_weights/ppermute | solution.py:815
  137.9 27.1 %collective-permute-start.24 = (bf16[192,1536]{1,0:T(8,128)(2,1)S(1)}, bf16[192,1536]{1,0:T(8,128)(2,1)S(1)}, u32[]{:S(2)}, u32[]{:S(2)}) collective-permute-start(bf16[192,1536]{1,0:T(8,128)(2,1)S(1)} %get-tuple-element.133), channel_id=1, source_target_pairs={{0,2},{2,0},{4,6},{6,4},{1,3},{3,1},{5,7},{7,5},{8,10},{10,8},{12,... | collective-permute-start | bytes 1769480 | tf_op jit(solution)/shard_map/reduce_gate_weights/ppermute | solution.py:815
  161.4 13.1 %collective-permute-start.21 = (bf16[192,1152]{1,0:T(8,128)(2,1)S(1)}, bf16[192,1152]{1,0:T(8,128)(2,1)S(1)}, u32[]{:S(2)}, u32[]{:S(2)}) collective-permute-start(bf16[192,1152]{1,0:T(8,128)(2,1)S(1)} %get-tuple-element.124), channel_id=1, source_target_pairs={{0,2},{2,0},{4,6},{6,4},{1,3},{3,1},{5,7},{7,5},{8,10},{10,8},{12,... | collective-permute-start | bytes 1327112 | tf_op jit(solution)/shard_map/ppermute | solution.py:815
  162.9 20.9 %collective-permute-start.23 = (bf16[192,1152]{1,0:T(8,128)(2,1)S(1)}, bf16[192,1152]{1,0:T(8,128)(2,1)S(1)}, u32[]{:S(2)}, u32[]{:S(2)}) collective-permute-start(bf16[192,1152]{1,0:T(8,128)(2,1)S(1)} %get-tuple-element.127), channel_id=1, source_target_pairs={{0,6},{2,4},{4,2},{6,0},{1,7},{3,5},{5,3},{7,1},{8,14},{10,12},{12... | collective-permute-start | bytes 1327112 | tf_op jit(solution)/shard_map/ppermute | solution.py:815
  164.5 21.6 %collective-permute-start.22 = (bf16[192,1152]{1,0:T(8,128)(2,1)S(1)}, bf16[192,1152]{1,0:T(8,128)(2,1)S(1)}, u32[]{:S(2)}, u32[]{:S(2)}) collective-permute-start(bf16[192,1152]{1,0:T(8,128)(2,1)S(1)} %get-tuple-element.126), channel_id=1, source_target_pairs={{0,4},{2,6},{4,0},{6,2},{1,5},{3,7},{5,1},{7,3},{8,12},{10,14},{12... | collective-permute-start | bytes 1327112 | tf_op jit(solution)/shard_map/ppermute | solution.py:815
  165.4 21.0 %collective-permute-start.27 = (bf16[96,1536]{1,0:T(8,128)(2,1)S(1)}, bf16[96,1536]{1,0:T(8,128)(2,1)S(1)}, u32[]{:S(2)}, u32[]{:S(2)}) collective-permute-start(bf16[96,1536]{1,0:T(8,128)(2,1)S(1)} %pad_maximum_fusion.3), channel_id=1, source_target_pairs={{0,8},{8,0},{16,24},{24,16},{1,9},{9,1},{17,25},{25,17},{2,10},{10... | collective-permute-start | bytes 884744 | tf_op jit(solution)/shard_map/reduce_gate_weights/ppermute | solution.py:815
  180.5 40.4 %collective-permute-start.36 = (bf16[1024,768]{1,0:T(8,128)(2,1)S(1)}, bf16[1024,768]{1,0:T(8,128)(2,1)S(1)}, u32[]{:S(2)}, u32[]{:S(2)}) collective-permute-start(bf16[1024,768]{1,0:T(8,128)(2,1)S(1)} %get-tuple-element.139.own), channel_id=1, source_target_pairs={{0,1},{1,0},{2,3},{3,2},{4,5},{5,4},{6,7},{7,6},{8,9},{9,8},{10,11... | collective-permute-start | bytes 4718600 | tf_op jit(solution)/shard_map/ppermute | solution.py:811
  183.9 35.5 %collective-permute-start.37 = (f32[8,768]{1,0:T(8,128)S(1)}, f32[8,768]{1,0:T(8,128)S(1)}, u32[]{:S(2)}, u32[]{:S(2)}) collective-permute-start(f32[8,768]{1,0:T(8,128)S(1)} %get-tuple-element.140), channel_id=1, source_target_pairs={{2,0},{3,1},{4,2},{5,3},{6,4},{7,5},{10,8},{11,9},{12,10},{13,11},... | collective-permute-start | bytes 73736 | tf_op jit(solution)/shard_map/ppermute | solution.py:1179
  203.0 17.8 %collective-permute-start.38 = (f32[8,768]{1,0:T(8,128)S(1)}, f32[8,768]{1,0:T(8,128)S(1)}, u32[]{:S(2)}, u32[]{:S(2)}) collective-permute-start(f32[8,768]{1,0:T(8,128)S(1)} %get-tuple-element.140), channel_id=1, source_target_pairs={{2,1},{3,0},{4,3},{5,2},{6,5},{7,4},{10,9},{11,8},{12,11},{13,10},... | collective-permute-start | bytes 73736 | tf_op jit(solution)/shard_map/ppermute | solution.py:1180
  (64 other events, 578.4 us)

commit v9 on v8

--- a/solution.py
+++ b/solution.py
@@ -2,6 +2,7 @@
 
 import jax
 import jax.numpy as jnp
+import numpy as np
 from jax import lax
 from jax.experimental import pallas as pl
 from jax.experimental.pallas import tpu as pltpu
@@ -685,7 +686,7 @@
         norm_o[...] = pack_norm(place, dp_count, part_count, total[0:1, :], rows)
 
 
-def finish_kernel(counts, info, own, other, halo_a, halo_b, tok, cot, par, grad_o):
+def finish_kernel(counts, info, own, other, halo_a, halo_b, keep, received, tok, cot, par, grad_o, out_o):
     block = pl.program_id(0)
     place = Place(info, counts)
     width = tok.shape[1]
@@ -697,6 +698,9 @@
     inv = lax.rsqrt(jnp.mean(inputs * inputs, axis=1, keepdims=True) + EPS)
     scaled = par[5:6, :width] * grad
     inner_dot = jnp.sum(scaled * inputs, axis=1, keepdims=True)
+    half = width // 2
+    branch = (keep[...].astype(F32) + received[...].astype(F32)) * place.valid(block)
+    out_o[...] = jnp.where(place.tp == 0, inputs[:, :half], inputs[:, half:]) + branch
     grad_o[...] = (
         inv * scaled - inputs * (inv * inv * inv) * (inner_dot / width) + cot[...].astype(F32)
     )
@@ -844,27 +848,15 @@
     return own.astype(BF16)
 
 
-def halved_sum(total):
-    blocks = lax.axis_size("dp")
-    rows = total.shape[0] // blocks
-    total = total.reshape(blocks, rows, -1).astype(F32)
-    mask = 1
-    while mask < blocks:
-        kept = [total[block] for block in range(total.shape[0]) if block % 2 == 0]
-        sent = [total[block] for block in range(total.shape[0]) if block % 2 == 1]
-        received = partnered(jnp.concatenate(sent, axis=0).astype(BF16), "dp", mask)
-        received = received.reshape(len(sent), rows, -1).astype(F32)
-        total = jnp.stack(kept) + received
-        mask *= 2
-    return total[0].astype(BF16)
-
-
-def doubled(value):
-    mask = 1
-    while mask < lax.axis_size("ctx"):
-        value = jnp.concatenate([value, partnered(value, "ctx", mask)], axis=0)
-        mask *= 2
-    return value
+def halved(blocks, mask):
+    count, rows = blocks.shape[:2]
+    sent = jnp.concatenate([blocks[block] for block in range(1, count, 2)], axis=0).astype(BF16)
+    received = partnered(sent, "dp", mask).reshape(count // 2, rows, -1).astype(F32)
+    return jnp.stack([blocks[block] for block in range(0, count, 2)]) + received
+
+
+def doubled(value, mask):
+    return jnp.concatenate([value, partnered(value, "ctx", mask)], axis=0)
 
 
 def whole_sum(value):
@@ -979,7 +971,7 @@
             pltpu.VMEM((inner, LANES), F32),
             pltpu.VMEM((8, LANES), F32),
         ],
-        micros=40,
+        micros=20,
         mega=16,
     )
     packets = [(shifted(packet, "ctx", step), "whole") for step in range(1, ctx_count)]
@@ -1064,11 +1056,7 @@
         mega=14,
     )
     packets = [(shifted(packet, "ctx", -step), "whole") for step in range(1, ctx_count)]
-    with jax.named_scope("layer_out"):
-        received = swapped(send)
-        own_inputs = lax.dynamic_slice_in_dim(tokens, tp_index * half, half, 1).astype(F32)
-        valid = (jnp.arange(rows) < fill).astype(F32)[:, None]
-        layer_out = own_inputs + (keep.astype(F32) + received.astype(F32)) * valid
+    received = swapped(send)
     dxc, dcq, dbq, row_sums, col_sums, *g2 = call(
         functools.partial(intra_back_kernel, counts, heads, dp_count),
         steps,
@@ -1144,11 +1132,20 @@
         mega=20,
     )
     with jax.named_scope("reduce_gate_weights"):
-        total2 = halved_sum(total2) if parts > 1 else whole_sum(total2)
+        if parts > 1:
+            total2 = total2.reshape(dp_count, part_rows, 2 * inner)
+            total2 = halved(total2, 1) if dp_count > 1 else total2
+        else:
+            total2 = whole_sum(total2)
     norm_rows = part_rows * dp_count
     if parts > 1:
         g1 = [g1[0]] + [partnered(g1[mask], "ctx", mask) for mask in range(1, parts)]
-        packed, g1[1] = lax.optimization_barrier((packed, g1[1]))
+        packed, g1[1], total2 = lax.optimization_barrier((packed, g1[1], total2))
+        mask = 2
+        while mask < dp_count:
+            total2 = halved(total2, mask)
+            mask *= 2
+        total2 = total2[0].astype(BF16)
     partial, halo_grad, norm_part = call(
         functools.partial(input_back_kernel, counts, dp_count, parts),
         steps,
@@ -1184,17 +1181,21 @@
             total1 = sum(piece.astype(F32) for piece in g1) + norm_part
             total1, total2 = lax.optimization_barrier((total1, total2))
             total1 = dp_sum(total1)
-            total2 = doubled(total2)
+            total2 = doubled(total2, 1)
             total1, total2 = lax.optimization_barrier((total1, total2))
+            mask = 2
+            while mask < ctx_count:
+                total2 = doubled(total2, mask)
+                mask *= 2
         else:
             total1 = whole_sum((g1[0].astype(F32) + norm_part).astype(BF16))
         across = swapped(total1[:, inner:])
-        lane = jnp.arange(3 * LANES) - 2 * LANES
+        lane = np.arange(3 * LANES) - 2 * LANES
         both = (lane < 0) | ((lane >= STATE_TAPS) & (lane < BY_HEAD))
         both = both | ((lane >= NORM) & (lane < NORM + shard // part_rows))
         summed = total1[:, inner:] + jnp.where(both[None, :], across, 0)
         total1 = jnp.concatenate([total1[:, :inner], summed], axis=1)
-    (grad_tokens,) = call(
+    grad_tokens, layer_out = call(
         functools.partial(finish_kernel, counts),
         steps,
         info,
@@ -1203,11 +1204,13 @@
             (other, "rows"),
             (halo_a, "whole"),
             (halo_b, "whole"),
+            (keep, "rows"),
+            (received, "rows"),
             (tokens, "rows"),
             (cotangent, "rows"),
             (par, "whole"),
         ],
-        [row_out(width, F32)],
+        [row_out(width, F32), row_out(half, F32)],
         micros=5,
         mega=10,
     )

time: 229 us -> 197 us (0.86)
  local copies, waits for them, and re-layouts: 27.6 us -> 3.33 us
  other arithmetic: 8.01 us -> 5.18 us
  starting transfers between devices: 66.5 us -> 63.8 us
    unnamed x95 -> x17, local copies, waits for them, and re-layouts: 24.3 us -> 0.75 us
    ppermute x28, waiting for transfers between devices: 34.8 us -> 31.9 us  [partnered(): lax.ppermute(value, axis, [(one, one ^ mask) for one in range(lax.axis_si...]
  transfers between devices with their start and end apart: 41 -> 41, of which waited for: 13 -> 11; matrix products, arithmetic and copies ran while one was open for 5% -> 4% of each run, Pallas kernels for 31% -> 36%
where the time goes in v9:
time: 197 us; the launch traced here: 196 us
  Pallas kernels  87.5 us (44%)
  starting transfers between devices  63.8 us (32%)
  waiting for transfers between devices  34.3 us (17%)
  other arithmetic  5.18 us (3%)
  local copies, waits for them, and re-layouts  3.33 us (2%)
  between operations  2.02 us (1%)
    pallas_call x10, Pallas kernels, call(): pl.pallas_call(body, grid=(steps,), in_specs=[pl.BlockSpec(memory_space=p...  87.5 us
    ppermute x28, starting transfers between devices, partnered(): lax.ppermute(value, axis, [(one, one ^ mask) for one in range(lax.axis_si...  46.1 us
    ppermute x28, waiting for transfers between devices, partnered(): lax.ppermute(value, axis, [(one, one ^ mask) for one in range(lax.axis_si...  31.9 us
    ppermute x7, starting transfers between devices, shifted(): lax.ppermute(value, axis, [(source, source + steps) for source in range(f...  14.6 us
  transfers between devices with their start and end apart: 41, of which 11 were waited for; matrix products, arithmetic and copies ran while one was open for 4% of the time, Pallas kernels for 36%

profile of v9, /device:TPU:0, one launch (start us, length us, event | category | flops | bytes accessed | tf_op | source)
XLA Modules:
  0.0 196.1 jit_solution(16656083841219813651)
XLA Ops:
  1.7 3.1 %collective-permute-start = (bf16[48,1024]{1,0:T(8,128)(2,1)S(1)}, bf16[48,1024]{1,0:T(8,128)(2,1)S(1)}, u32[]{:S(2)}, u32[]{:S(2)}) collective-permute-start(bf16[48,1024]{1,0:T(8,128)(2,1)S(1)} %fusion.7), channel_id=1, source_target_pairs={{0,8},{8,0},{16,24},{24,16},{1,9},{9,1},{17,25},{25,17},{2,10},{10... | collective-permute-start | bytes 294920 | tf_op jit(solution)/shard_map/gather_weights/ppermute | solution.py:819
  4.8 2.6 %collective-permute-start.1 = (bf16[48,1024]{1,0:T(8,128)(2,1)S(1)}, bf16[48,1024]{1,0:T(8,128)(2,1)S(1)}, u32[]{:S(2)}, u32[]{:S(2)}) collective-permute-start(bf16[48,1024]{1,0:T(8,128)(2,1)S(1)} %fusion.7), channel_id=1, source_target_pairs={{0,16},{8,24},{16,0},{24,8},{1,17},{9,25},{17,1},{25,9},{2,18},{10... | collective-permute-start | bytes 294920 | tf_op jit(solution)/shard_map/gather_weights/ppermute | solution.py:819
  23.5 2.4 %collective-permute-start.8 = (bf16[192,1024]{1,0:T(8,128)(2,1)S(1)}, bf16[192,1024]{1,0:T(8,128)(2,1)}, u32[]{:S(2)}, u32[]{:S(2)}) collective-permute-start(bf16[192,1024]{1,0:T(8,128)(2,1)S(1)} %pad_maximum_fusion.2.refs_4_), channel_id=1, source_target_pairs={{0,6},{2,4},{4,2},{6,0},{1,7},{3,5},{5,3},{7,1},{8,14},{10,12},{12... | collective-permute-start | bytes 1179656 | tf_op jit(solution)/shard_map/gather_weights/ppermute | solution.py:819
  26.8 6.8 %collective-permute-done.4.refs_2_ = bf16[64,1536]{1,0:T(8,128)(2,1)S(1)} collective-permute-done((bf16[64,1536]{1,0:T(8,128)(2,1)S(1)}, bf16[64,1536]{1,0:T(8,128)(2,1)S(1)}, u32[]{:S(2)}, u32[]{:S(2)}) %collective-permute-start.4) | collective-permute-done | bytes 196640 | tf_op jit(solution)/shard_map/gather_weights/ppermute | solution.py:819
  33.6 3.4 %collective-permute-start.9 = (bf16[16,768]{1,0:T(8,128)(2,1)S(1)}, bf16[16,768]{1,0:T(8,128)(2,1)S(1)}, u32[]{:S(2)}, u32[]{:S(2)}) collective-permute-start(bf16[16,768]{1,0:T(8,128)(2,1)S(1)} %constant_dynamic-slice_fusion), channel_id=1, source_target_pairs={{0,2},{2,4},{4,6},{1,3},{3,5},{5,7},{8,10},{10,12},{12,14},{9,11},... | collective-permute-start | bytes 73736 | tf_op jit(solution)/shard_map/ppermute | solution.py:811
  39.8 2.4 %collective-permute-start.14 = (bf16[192,1536]{1,0:T(8,128)(2,1)S(1)}, bf16[192,1536]{1,0:T(8,128)(2,1)S(1)}, u32[]{:S(2)}, u32[]{:S(2)}) collective-permute-start(bf16[192,1536]{1,0:T(8,128)(2,1)S(1)} %pad_maximum_fusion.refs_0_), channel_id=1, source_target_pairs={{0,4},{2,6},{4,0},{6,2},{1,5},{3,7},{5,1},{7,3},{8,12},{10,14},{12... | collective-permute-start | bytes 1769480 | tf_op jit(solution)/shard_map/gather_weights/ppermute | solution.py:819
  43.8 17.5 %shard_map.306 = (bf16[768,1152]{1,0:T(8,128)(2,1)S(1)}, f32[8,1024]{1,0:T(8,128)S(1)}, bf16[1024,768]{1,0:T(8,128)(2,1)S(1)}, bf16[16,768]{1,0:T(8,128)(2,1)S(1...) custom-call(s32[10]{0:T(128)S(1)} %concatenate.40.info, ...), custom_call_target="tpu_custom_call" | custom-call | flops 22000001024 | bytes 70000000 | tf_op jit(solution)/shard_map/pallas_call | solution.py:791
  63.2 3.9 %collective-permute-start.11 = (bf16[784,128]{1,0:T(8,128)(2,1)S(1)}, bf16[784,128]{1,0:T(8,128)(2,1)S(1)}, u32[]{:S(2)}, u32[]{:S(2)}) collective-permute-start(bf16[784,128]{1,0:T(8,128)(2,1)S(1)} %get-tuple-element.91), channel_id=1, source_target_pairs={{0,4},{2,6},{1,5},{3,7},{8,12},{10,14},{9,13},{11,15},{16,20},{18,... | collective-permute-start | bytes 602120 | tf_op jit(solution)/shard_map/ppermute | solution.py:811
  68.5 4.0 %shard_map.307 = (bf16[768,1536]{1,0:T(8,128)(2,1)S(1)}, bf16[1024,768]{1,0:T(8,128)(2,1)S(1)}, bf16[1024,768]{1,0:T(8,128)(2,1)S(1)}) custom-call(s32[10]{0:T(128)S(1)} %concatenate.40.info, bf16[192,1536]{1,0:T(8,128)(2,1)S(1)} %pad_maximum_fusion.refs_0_, bf16[192,1536]{1,0:T(8,128)(2,1)S(1)} %collective-permute-done.13.refs_1_, ...), custom_call_target="tpu_custom_call" | custom-call | flops 7699999744 | bytes 24500000 | tf_op jit(solution)/shard_map/pallas_call | solution.py:791
  72.5 4.2 %shard_map.308 = (f32[1024,768]{1,0:T(8,128)S(1)}, bf16[4,768,128]{2,1,0:T(8,128)(2,1)S(1)}, f32[4,768,128]{2,1,0:T(8,128)S(1)}, f32[8,1024]{1,0:T(8,128)S(1)}) custom-call(s32[10]{0:T(128)S(1)} %concatenate.40.info, bf16[784,128]{1,0:T(8,128)(2,1)S(1)} %collective-permute-done.10.refs_0_, bf16[784,128]{1,0:T(8,128)(2,1)S(1)} %collective-permute-done.11.refs_1_, ...), custom_call_target="tpu_custom_call" | custom-call | flops 8800000000 | bytes 28000000 | tf_op jit(solution)/shard_map/pallas_call | solution.py:791
  78.0 10.9 %shard_map.309 = (bf16[1024,384]{1,0:T(8,128)(2,1)S(1)}, bf16[1024,384]{1,0:T(8,128)(2,1)S(1)}, bf16[768,768]{1,0:T(8,128)(2,1)S(1)}, f32[8,768]{1,0:T(8,128)S(1...) custom-call(s32[10]{0:T(128)S(1)} %concatenate.40.info, ...), custom_call_target="tpu_custom_call" | custom-call | flops 16499999744 | bytes 52500000 | tf_op jit(solution)/shard_map/pallas_call | solution.py:791
  93.0 15.2 %shard_map.310 = (bf16[1024,768]{1,0:T(8,128)(2,1)S(1)}, f32[1024,128]{1,0:T(8,128)S(1)}, f32[1024,128]{1,0:T(8,128)S(1)}, f32[1024,128]{1,0:T(8,128)S(1)}, f32[...) custom-call(s32[10]{0:T(128)S(1)} %concatenate.40.info, ...), custom_call_target="tpu_custom_call" | custom-call | flops 19800000512 | bytes 63000000 | tf_op jit(solution)/shard_map/pallas_call | solution.py:791
  108.2 2.1 %collective-permute-start.21 = (bf16[192,1536]{1,0:T(8,128)(2,1)S(1)}, bf16[192,1536]{1,0:T(8,128)(2,1)S(1)}, u32[]{:S(2)}, u32[]{:S(2)}) collective-permute-start(bf16[192,1536]{1,0:T(8,128)(2,1)S(1)} %get-tuple-element.126), channel_id=1, source_target_pairs={{0,2},{2,0},{4,6},{6,4},{1,3},{3,1},{5,7},{7,5},{8,10},{10,8},{12,... | collective-permute-start | bytes 1769480 | tf_op jit(solution)/shard_map/reduce_gate_weights/ppermute | solution.py:819
  110.3 3.3 %collective-permute-start.22 = (bf16[192,1536]{1,0:T(8,128)(2,1)S(1)}, bf16[192,1536]{1,0:T(8,128)(2,1)S(1)}, u32[]{:S(2)}, u32[]{:S(2)}) collective-permute-start(bf16[192,1536]{1,0:T(8,128)(2,1)S(1)} %get-tuple-element.127), channel_id=1, source_target_pairs={{0,4},{2,6},{4,0},{6,2},{1,5},{3,7},{5,1},{7,3},{8,12},{10,14},{12... | collective-permute-start | bytes 1769480 | tf_op jit(solution)/shard_map/reduce_gate_weights/ppermute | solution.py:819
  113.6 22.6 %shard_map.311 = (bf16[1024,1152]{1,0:T(8,128)(2,1)S(1)}, bf16[16,1024]{1,0:T(8,128)(2,1)S(1)}, bf16[192,1152]{1,0:T(8,128)(2,1)S(1)}, bf16[192,1152]{1,0:T(8,12...) custom-call(s32[10]{0:T(128)S(1)} %concatenate.40.info, ...), custom_call_target="tpu_custom_call" | custom-call | flops 27499999232 | bytes 87500000 | tf_op jit(solution)/shard_map/pallas_call | solution.py:791
  137.6 2.0 %collective-permute-start.29 = (bf16[192,1152]{1,0:T(8,128)(2,1)S(1)}, bf16[192,1152]{1,0:T(8,128)(2,1)S(1)}, u32[]{:S(2)}, u32[]{:S(2)}) collective-permute-start(bf16[192,1152]{1,0:T(8,128)(2,1)S(1)} %get-tuple-element.139), channel_id=1, source_target_pairs={{0,4},{2,6},{4,0},{6,2},{1,5},{3,7},{5,1},{7,3},{8,12},{10,14},{12... | collective-permute-start | bytes 1327112 | tf_op jit(solution)/shard_map/ppermute | solution.py:819
  140.9 6.4 %collective-permute-done.24 = bf16[96,1536]{1,0:T(8,128)(2,1)S(1)} collective-permute-done((bf16[96,1536]{1,0:T(8,128)(2,1)S(1)}, bf16[96,1536]{1,0:T(8,128)(2,1)S(1)}, u32[]{:S(2)}, u32[]{:S(2)}) %collective-permute-start.24) | collective-permute-done | bytes 294944 | tf_op jit(solution)/shard_map/reduce_gate_weights/ppermute | solution.py:819
  151.1 5.7 %shard_map.312 = (bf16[1024,768]{1,0:T(8,128)(2,1)S(1)}, f32[8,768]{1,0:T(8,128)S(1)}, f32[192,128]{1,0:T(8,128)S(1)}) custom-call(s32[10]{0:T(128)S(1)} %concatenate.40.info, bf16[1024,1152]{1,0:T(8,128)(2,1)S(1)} %get-tuple-element.129.packed, bf16[16,1024]{1,0:T(8,128)(2,1)S(1)} %get-tuple-element.130.back, ...), custom_call_target="tpu_custom_call" | custom-call | flops 5500000256 | bytes 17500000 | tf_op jit(solution)/shard_map/pallas_call | solution.py:791
  159.2 2.9 %collective-permute-start.33 = (bf16[48,1152]{1,0:T(8,128)(2,1)S(1)}, bf16[48,1152]{1,0:T(8,128)(2,1)S(1)}, u32[]{:S(2)}, u32[]{:S(2)}) collective-permute-start(bf16[48,1152]{1,0:T(8,128)(2,1)S(1)} %get-tuple-element.172), channel_id=1, source_target_pairs={{0,16},{8,24},{16,0},{24,8},{1,17},{9,25},{17,1},{25,9},{2,18},{10... | collective-permute-start | bytes 331784 | tf_op jit(solution)/shard_map/reduce_input_weights/ppermute | solution.py:819
  164.2 4.9 %collective-permute-done.33 = bf16[48,1152]{1,0:T(8,128)(2,1)S(1)} collective-permute-done((bf16[48,1152]{1,0:T(8,128)(2,1)S(1)}, bf16[48,1152]{1,0:T(8,128)(2,1)S(1)}, u32[]{:S(2)}, u32[]{:S(2)}) %collective-permute-start.33) | collective-permute-done | bytes 110624 | tf_op jit(solution)/shard_map/reduce_input_weights/ppermute | solution.py:819
  172.5 4.2 %collective-permute-start.40 = (bf16[96,1536]{1,0:T(8,128)(2,1)S(1)}, bf16[96,1536]{1,0:T(8,128)(2,1)S(1)}, u32[]{:S(2)}, u32[]{:S(2)}) collective-permute-start(bf16[96,1536]{1,0:T(8,128)(2,1)S(1)} %pad_maximum_fusion.4), channel_id=1, source_target_pairs={{0,4},{2,6},{4,0},{6,2},{1,5},{3,7},{5,1},{7,3},{8,12},{10,14},{12... | collective-permute-start | bytes 884744 | tf_op jit(solution)/shard_map/reduce_input_weights/ppermute | solution.py:819
  176.7 7.8 %collective-permute-done.40 = bf16[96,1536]{1,0:T(8,128)(2,1)S(1)} collective-permute-done((bf16[96,1536]{1,0:T(8,128)(2,1)S(1)}, bf16[96,1536]{1,0:T(8,128)(2,1)S(1)}, u32[]{:S(2)}, u32[]{:S(2)}) %collective-permute-start.40) | collective-permute-done | bytes 294944 | tf_op jit(solution)/shard_map/reduce_input_weights/ppermute | solution.py:819
  184.5 2.6 %collective-permute-start.37 = (bf16[48,1152]{1,0:T(8,128)(2,1)S(1)}, bf16[48,1152]{1,0:T(8,128)(2,1)S(1)}, u32[]{:S(2)}, u32[]{:S(2)}) collective-permute-start(bf16[48,1152]{1,0:T(8,128)(2,1)S(1)} %pad_maximum_fusion.5.refs_0_), channel_id=1, source_target_pairs={{0,6},{2,4},{4,2},{6,0},{1,7},{3,5},{5,3},{7,1},{8,14},{10,12},{12... | collective-permute-start | bytes 331784 | tf_op jit(solution)/shard_map/last_hop/ppermute | solution.py:819
  189.7 3.9 %shard_map.313 = (f32[1024,768]{1,0:T(8,128)}, f32[1024,384]{1,0:T(8,128)}) custom-call(s32[10]{0:T(128)S(1)} %concatenate.40.info, bf16[1024,768]{1,0:T(8,128)(2,1)S(1)} %get-tuple-element.132.own, bf16[1024,768]{1,0:T(8,128)(2,1)S(1)} %collective-permute-done.25.other, f32[8,768]{1,0:T(8,128)S(1)} %collective-permute-done.26.halo_a, ...), custom_call_target="tpu_custom_call" | custom-call | flops 5500000256 | bytes 17500000 | tf_op jit(solution)/shard_map/pallas_call | solution.py:791
  (129 shorter events, 49.2 us)
Async XLA Ops:
  1.7 12.0 %collective-permute-start = (bf16[48,1024]{1,0:T(8,128)(2,1)S(1)}, bf16[48,1024]{1,0:T(8,128)(2,1)S(1)}, u32[]{:S(2)}, u32[]{:S(2)}) collective-permute-start(bf16[48,1024]{1,0:T(8,128)(2,1)S(1)} %fusion.7), channel_id=1, source_target_pairs={{0,8},{8,0},{16,24},{24,16},{1,9},{9,1},{17,25},{25,17},{2,10},{10... | collective-permute-start | bytes 294920 | tf_op jit(solution)/shard_map/gather_weights/ppermute | solution.py:819
  17.0 16.7 %collective-permute-start.4 = (bf16[64,1536]{1,0:T(8,128)(2,1)S(1)}, bf16[64,1536]{1,0:T(8,128)(2,1)S(1)}, u32[]{:S(2)}, u32[]{:S(2)}) collective-permute-start(bf16[64,1536]{1,0:T(8,128)(2,1)S(1)} %fusion.3.refs_0_), channel_id=1, source_target_pairs={{0,16},{8,24},{16,0},{24,8},{1,17},{9,25},{17,1},{25,9},{2,18},{10... | collective-permute-start | bytes 589832 | tf_op jit(solution)/shard_map/gather_weights/ppermute | solution.py:819
  18.4 18.6 %collective-permute-start.5 = (bf16[64,1536]{1,0:T(8,128)(2,1)S(1)}, bf16[64,1536]{1,0:T(8,128)(2,1)S(1)}, u32[]{:S(2)}, u32[]{:S(2)}) collective-permute-start(bf16[64,1536]{1,0:T(8,128)(2,1)S(1)} %fusion.3.refs_0_), channel_id=1, source_target_pairs={{0,24},{8,16},{16,8},{24,0},{1,25},{9,17},{17,9},{25,1},{2,26},{10... | collective-permute-start | bytes 589832 | tf_op jit(solution)/shard_map/gather_weights/ppermute | solution.py:819
  19.7 22.5 %collective-permute-start.6 = (bf16[192,1024]{1,0:T(8,128)(2,1)S(1)}, bf16[192,1024]{1,0:T(8,128)(2,1)S(1)}, u32[]{:S(2)}, u32[]{:S(2)}) collective-permute-start(bf16[192,1024]{1,0:T(8,128)(2,1)S(1)} %pad_maximum_fusion.2.refs_4_), channel_id=1, source_target_pairs={{0,2},{2,0},{4,6},{6,4},{1,3},{3,1},{5,7},{7,5},{8,10},{10,8},{12,... | collective-permute-start | bytes 1179656 | tf_op jit(solution)/shard_map/gather_weights/ppermute | solution.py:819
  21.2 22.5 %collective-permute-start.7 = (bf16[192,1024]{1,0:T(8,128)(2,1)S(1)}, bf16[192,1024]{1,0:T(8,128)(2,1)}, u32[]{:S(2)}, u32[]{:S(2)}) collective-permute-start(bf16[192,1024]{1,0:T(8,128)(2,1)S(1)} %pad_maximum_fusion.2.refs_4_), channel_id=1, source_target_pairs={{0,4},{2,6},{4,0},{6,2},{1,5},{3,7},{5,1},{7,3},{8,12},{10,14},{12... | collective-permute-start | bytes 1179656 | tf_op jit(solution)/shard_map/gather_weights/ppermute | solution.py:819
  23.5 20.2 %collective-permute-start.8 = (bf16[192,1024]{1,0:T(8,128)(2,1)S(1)}, bf16[192,1024]{1,0:T(8,128)(2,1)}, u32[]{:S(2)}, u32[]{:S(2)}) collective-permute-start(bf16[192,1024]{1,0:T(8,128)(2,1)S(1)} %pad_maximum_fusion.2.refs_4_), channel_id=1, source_target_pairs={{0,6},{2,4},{4,2},{6,0},{1,7},{3,5},{5,3},{7,1},{8,14},{10,12},{12... | collective-permute-start | bytes 1179656 | tf_op jit(solution)/shard_map/gather_weights/ppermute | solution.py:819
  37.1 30.0 %collective-permute-start.13 = (bf16[192,1536]{1,0:T(8,128)(2,1)S(1)}, bf16[192,1536]{1,0:T(8,128)(2,1)S(1)}, u32[]{:S(2)}, u32[]{:S(2)}) collective-permute-start(bf16[192,1536]{1,0:T(8,128)(2,1)S(1)} %pad_maximum_fusion.refs_0_), channel_id=1, source_target_pairs={{0,2},{2,0},{4,6},{6,4},{1,3},{3,1},{5,7},{7,5},{8,10},{10,8},{12,... | collective-permute-start | bytes 1769480 | tf_op jit(solution)/shard_map/gather_weights/ppermute | solution.py:819
  39.8 28.6 %collective-permute-start.14 = (bf16[192,1536]{1,0:T(8,128)(2,1)S(1)}, bf16[192,1536]{1,0:T(8,128)(2,1)S(1)}, u32[]{:S(2)}, u32[]{:S(2)}) collective-permute-start(bf16[192,1536]{1,0:T(8,128)(2,1)S(1)} %pad_maximum_fusion.refs_0_), channel_id=1, source_target_pairs={{0,4},{2,6},{4,0},{6,2},{1,5},{3,7},{5,1},{7,3},{8,12},{10,14},{12... | collective-permute-start | bytes 1769480 | tf_op jit(solution)/shard_map/gather_weights/ppermute | solution.py:819
  42.3 26.2 %collective-permute-start.15 = (bf16[192,1536]{1,0:T(8,128)(2,1)S(1)}, bf16[192,1536]{1,0:T(8,128)(2,1)S(1)}, u32[]{:S(2)}, u32[]{:S(2)}) collective-permute-start(bf16[192,1536]{1,0:T(8,128)(2,1)S(1)} %pad_maximum_fusion.refs_0_), channel_id=1, source_target_pairs={{0,6},{2,4},{4,2},{6,0},{1,7},{3,5},{5,3},{7,1},{8,14},{10,12},{12... | collective-permute-start | bytes 1769480 | tf_op jit(solution)/shard_map/gather_weights/ppermute | solution.py:819
  61.3 11.2 %collective-permute-start.10 = (bf16[784,128]{1,0:T(8,128)(2,1)S(1)}, bf16[784,128]{1,0:T(8,128)(2,1)S(1)}, u32[]{:S(2)}, u32[]{:S(2)}) collective-permute-start(bf16[784,128]{1,0:T(8,128)(2,1)S(1)} %get-tuple-element.91), channel_id=1, source_target_pairs={{0,2},{2,4},{4,6},{1,3},{3,5},{5,7},{8,10},{10,12},{12,14},{9,11},... | collective-permute-start | bytes 602120 | tf_op jit(solution)/shard_map/ppermute | solution.py:811
  88.9 24.6 %collective-permute-start.17 = (bf16[784,128]{1,0:T(8,128)(2,1)S(1)}, bf16[784,128]{1,0:T(8,128)(2,1)S(1)}, u32[]{:S(2)}, u32[]{:S(2)}) collective-permute-start(bf16[784,128]{1,0:T(8,128)(2,1)S(1)} %get-tuple-element.106), channel_id=1, source_target_pairs={{2,0},{4,2},{6,4},{3,1},{5,3},{7,5},{10,8},{12,10},{14,12},{11,9},... | collective-permute-start | bytes 602120 | tf_op jit(solution)/shard_map/ppermute | solution.py:811
  90.2 23.3 %collective-permute-start.18 = (bf16[784,128]{1,0:T(8,128)(2,1)S(1)}, bf16[784,128]{1,0:T(8,128)(2,1)S(1)}, u32[]{:S(2)}, u32[]{:S(2)}) collective-permute-start(bf16[784,128]{1,0:T(8,128)(2,1)S(1)} %get-tuple-element.106), channel_id=1, source_target_pairs={{4,0},{6,2},{5,1},{7,3},{12,8},{14,10},{13,9},{15,11},{20,16},{22,... | collective-permute-start | bytes 602120 | tf_op jit(solution)/shard_map/ppermute | solution.py:811
  91.5 22.0 %collective-permute-start.19 = (bf16[784,128]{1,0:T(8,128)(2,1)S(1)}, bf16[784,128]{1,0:T(8,128)(2,1)S(1)}, u32[]{:S(2)}, u32[]{:S(2)}) collective-permute-start(bf16[784,128]{1,0:T(8,128)(2,1)S(1)} %get-tuple-element.106), channel_id=1, source_target_pairs={{6,0},{7,1},{14,8},{15,9},{22,16},{23,17},{30,24},{31,25}} | collective-permute-start | bytes 602120 | tf_op jit(solution)/shard_map/ppermute | solution.py:811
  108.2 31.5 %collective-permute-start.21 = (bf16[192,1536]{1,0:T(8,128)(2,1)S(1)}, bf16[192,1536]{1,0:T(8,128)(2,1)S(1)}, u32[]{:S(2)}, u32[]{:S(2)}) collective-permute-start(bf16[192,1536]{1,0:T(8,128)(2,1)S(1)} %get-tuple-element.126), channel_id=1, source_target_pairs={{0,2},{2,0},{4,6},{6,4},{1,3},{3,1},{5,7},{7,5},{8,10},{10,8},{12,... | collective-permute-start | bytes 1769480 | tf_op jit(solution)/shard_map/reduce_gate_weights/ppermute | solution.py:819
  110.3 29.5 %collective-permute-start.22 = (bf16[192,1536]{1,0:T(8,128)(2,1)S(1)}, bf16[192,1536]{1,0:T(8,128)(2,1)S(1)}, u32[]{:S(2)}, u32[]{:S(2)}) collective-permute-start(bf16[192,1536]{1,0:T(8,128)(2,1)S(1)} %get-tuple-element.127), channel_id=1, source_target_pairs={{0,4},{2,6},{4,0},{6,2},{1,5},{3,7},{5,1},{7,3},{8,12},{10,14},{12... | collective-permute-start | bytes 1769480 | tf_op jit(solution)/shard_map/reduce_gate_weights/ppermute | solution.py:819
  113.5 26.2 %collective-permute-start.23 = (bf16[192,1536]{1,0:T(8,128)(2,1)S(1)}, bf16[192,1536]{1,0:T(8,128)(2,1)S(1)}, u32[]{:S(2)}, u32[]{:S(2)}) collective-permute-start(bf16[192,1536]{1,0:T(8,128)(2,1)S(1)} %get-tuple-element.128), channel_id=1, source_target_pairs={{0,6},{2,4},{4,2},{6,0},{1,7},{3,5},{5,3},{7,1},{8,14},{10,12},{12... | collective-permute-start | bytes 1769480 | tf_op jit(solution)/shard_map/reduce_gate_weights/ppermute | solution.py:819
  136.2 13.2 %collective-permute-start.20 = (bf16[192,1152]{1,0:T(8,128)(2,1)S(1)}, bf16[192,1152]{1,0:T(8,128)(2,1)S(1)}, u32[]{:S(2)}, u32[]{:S(2)}) collective-permute-start(bf16[192,1152]{1,0:T(8,128)(2,1)S(1)} %get-tuple-element.124), channel_id=1, source_target_pairs={{0,2},{2,0},{4,6},{6,4},{1,3},{3,1},{5,7},{7,5},{8,10},{10,8},{12,... | collective-permute-start | bytes 1327112 | tf_op jit(solution)/shard_map/ppermute | solution.py:819
  137.6 20.3 %collective-permute-start.29 = (bf16[192,1152]{1,0:T(8,128)(2,1)S(1)}, bf16[192,1152]{1,0:T(8,128)(2,1)S(1)}, u32[]{:S(2)}, u32[]{:S(2)}) collective-permute-start(bf16[192,1152]{1,0:T(8,128)(2,1)S(1)} %get-tuple-element.139), channel_id=1, source_target_pairs={{0,4},{2,6},{4,0},{6,2},{1,5},{3,7},{5,1},{7,3},{8,12},{10,14},{12... | collective-permute-start | bytes 1327112 | tf_op jit(solution)/shard_map/ppermute | solution.py:819
  139.6 18.3 %collective-permute-start.30 = (bf16[192,1152]{1,0:T(8,128)(2,1)S(1)}, bf16[192,1152]{1,0:T(8,128)(2,1)S(1)}, u32[]{:S(2)}, u32[]{:S(2)}) collective-permute-start(bf16[192,1152]{1,0:T(8,128)(2,1)S(1)} %get-tuple-element.140), channel_id=1, source_target_pairs={{0,6},{2,4},{4,2},{6,0},{1,7},{3,5},{5,3},{7,1},{8,14},{10,12},{12... | collective-permute-start | bytes 1327112 | tf_op jit(solution)/shard_map/ppermute | solution.py:819
  162.8 26.9 %collective-permute-start.25 = (bf16[1024,768]{1,0:T(8,128)(2,1)S(1)}, bf16[1024,768]{1,0:T(8,128)(2,1)S(1)}, u32[]{:S(2)}, u32[]{:S(2)}) collective-permute-start(bf16[1024,768]{1,0:T(8,128)(2,1)S(1)} %get-tuple-element.132.own), channel_id=1, source_target_pairs={{0,1},{1,0},{2,3},{3,2},{4,5},{5,4},{6,7},{7,6},{8,9},{9,8},{10,11... | collective-permute-start | bytes 4718600 | tf_op jit(solution)/shard_map/ppermute | solution.py:815
  169.4 19.4 %collective-permute-start.28 = (bf16[1024,384]{1,0:T(8,128)(2,1)S(1)}, bf16[1024,384]{1,0:T(8,128)(2,1)S(1)}, u32[]{:S(2)}, u32[]{:S(2)}) collective-permute-start(bf16[1024,384]{1,0:T(8,128)(2,1)S(1)} %get-tuple-element.135), channel_id=1, source_target_pairs={{0,1},{1,0},{2,3},{3,2},{4,5},{5,4},{6,7},{7,6},{8,9},{9,8},{10,11... | collective-permute-start | bytes 2359304 | tf_op jit(solution)/shard_map/ppermute | solution.py:815
  169.8 19.6 %collective-permute-start.26 = (f32[8,768]{1,0:T(8,128)S(1)}, f32[8,768]{1,0:T(8,128)S(1)}, u32[]{:S(2)}, u32[]{:S(2)}) collective-permute-start(f32[8,768]{1,0:T(8,128)S(1)} %get-tuple-element.133), channel_id=1, source_target_pairs={{2,0},{3,1},{4,2},{5,3},{6,4},{7,5},{10,8},{11,9},{12,10},{13,11},... | collective-permute-start | bytes 73736 | tf_op jit(solution)/shard_map/ppermute | solution.py:1176
  171.1 18.5 %collective-permute-start.27 = (f32[8,768]{1,0:T(8,128)S(1)}, f32[8,768]{1,0:T(8,128)S(1)}, u32[]{:S(2)}, u32[]{:S(2)}) collective-permute-start(f32[8,768]{1,0:T(8,128)S(1)} %get-tuple-element.133), channel_id=1, source_target_pairs={{2,1},{3,0},{4,3},{5,2},{6,5},{7,4},{10,9},{11,8},{12,11},{13,10},... | collective-permute-start | bytes 73736 | tf_op jit(solution)/shard_map/ppermute | solution.py:1177
  172.5 12.0 %collective-permute-start.40 = (bf16[96,1536]{1,0:T(8,128)(2,1)S(1)}, bf16[96,1536]{1,0:T(8,128)(2,1)S(1)}, u32[]{:S(2)}, u32[]{:S(2)}) collective-permute-start(bf16[96,1536]{1,0:T(8,128)(2,1)S(1)} %pad_maximum_fusion.4), channel_id=1, source_target_pairs={{0,4},{2,6},{4,0},{6,2},{1,5},{3,7},{5,1},{7,3},{8,12},{10,14},{12... | collective-permute-start | bytes 884744 | tf_op jit(solution)/shard_map/reduce_input_weights/ppermute | solution.py:819
  (25 other events, 285.6 us)

commit v10 on v9

--- a/solution.py
+++ b/solution.py
@@ -147,6 +147,19 @@
 
 def decay_kernel(keep, cum, cum_rows, head):
     return jnp.exp(jnp.where(keep, cum[:, head : head + 1] - cum_rows[head : head + 1, :], -1e30))
+
+
+TILES = ((0, 0), (LANES, 0), (LANES, LANES))
+
+
+def tile_slices(tile):
+    return slice(tile[0], tile[0] + LANES), slice(tile[1], tile[1] + LANES)
+
+
+def decay_tile(neg, cum, cum_rows, head, tile):
+    rows, columns = tile_slices(tile)
+    diff = cum[rows, head : head + 1] - cum_rows[head : head + 1, columns]
+    return jnp.exp(diff + neg[rows, columns])
 
 
 def both_halves(pair):
@@ -305,19 +318,19 @@
     (
         tok, halo, dtp, spread,
         w1, par, normed_o, halo_normed_o, halo_v_o, v_o, xc_o, bc_o, ypart_o, pre_o, cum_o, entry_o, decay_o,
-        packet_o, ext, run, factor,
+        packet_o, ext, run, factor, gram, neg, mix,
     ) = refs[dp_count + part_count :]
     forward_block(
         counts, heads, info, vectors, parts, tok, halo, w1, par, dtp, spread,
         normed_o, halo_normed_o, halo_v_o, v_o, xc_o, bc_o, ypart_o, pre_o, cum_o, entry_o, decay_o, packet_o,
-        ext, run, factor,
+        ext, run, factor, gram, neg, mix,
     )
 
 
 def forward_block(
     counts, heads, info, vectors, parts, tok, halo, w1, par, dtp, spread,
     normed_o, halo_normed_o, halo_v_o, v_o, xc_o, bc_o, ypart_o, pre_o, cum_o, entry_o, decay_o, packet_o,
-    ext, run, factor,
+    ext, run, factor, gram, neg, mix,
 ):
     block = pl.program_id(0)
     place = Place(info, counts)
@@ -368,16 +381,25 @@
     cum_o[...] = cum
     cum_rows = cum.T
     step_rows = step.T
-    gram = dot_nt(cq, bq)
-    keep = place.keep(block)
+    gram[...] = dot_nt(cq, bq)
+    neg[...] = jnp.where(place.keep(block), 0.0, -1e30)
+
+    @pl.when(block == 0)
+    def _():
+        mix[...] = jnp.zeros_like(mix)
+
     for pair in range(heads // 2):
         lanes = slice(pair * LANES, (pair + 1) * LANES)
-        mixing = []
-        for head in (2 * pair, 2 * pair + 1):
-            weight = decay_kernel(keep, cum, cum_rows, head) * step_rows[head : head + 1, :]
-            mixing.append((gram * weight).astype(BF16))
+        slot = pair % 2
+        for side in range(2):
+            head = 2 * pair + side
+            for tile in TILES:
+                rows, columns = tile_slices(tile)
+                weight = decay_tile(neg, cum, cum_rows, head, tile) * step_rows[head : head + 1, columns]
+                first = side * BLOCK + columns.start
+                mix[slot, rows, first : first + LANES] = (gram[rows, columns] * weight).astype(BF16)
         x_pair = xc[:, lanes]
-        y_pair = dot(jnp.concatenate(mixing, axis=1), jnp.concatenate(both_halves(x_pair), axis=0))
+        y_pair = dot(mix[slot], jnp.concatenate(both_halves(x_pair), axis=0))
         ypart_o[:, lanes] = y_pair + par[7:8, lanes] * x_pair.astype(F32)
     weighted = (expand(end_weights(place, block, cum) * step, spread) * xc.astype(F32)).astype(BF16)
     block_state = dot_tn(weighted, bq)
@@ -502,8 +524,8 @@
 def intra_back_kernel(counts, heads, dp_count, info, *refs):
     dy, dz, xc, bc, cum, pre_step, hb, normed, gwo, par, spread = refs[:11]
     dxc_o, dcq_o, dbq_o, rows_o, cols_o = refs[11:16]
-    parts = refs[16:-2]
-    acc, columns = refs[-2:]
+    parts = refs[16:-6]
+    acc, columns, neg, gram, grad_gram, mix = refs[-6:]
     block = pl.program_id(0)
     place = Place(info, counts)
     inner = heads * HEAD
@@ -511,6 +533,7 @@
     @pl.when(block == 0)
     def _():
         acc[...] = jnp.zeros_like(acc)
+        mix[...] = jnp.zeros_like(mix)
         columns[...] = jnp.zeros_like(columns)
 
     bq = bc[:, :LANES]
@@ -519,36 +542,44 @@
     step = step_sizes(place, block, pre_step[...], heads)
     cum_rows = cums.T
     step_rows = step.T
-    gram = dot_nt(cq, bq)
-    keep = place.keep(block)
-    lane = iota((BLOCK, LANES), 1)
-    grad_gram = jnp.zeros((BLOCK, BLOCK), F32)
-    sums = jnp.zeros((BLOCK, LANES), F32)
+    gram[...] = dot_nt(cq, bq)
+    neg[...] = jnp.where(place.keep(block), 0.0, -1e30)
+    lane = iota((LANES, LANES), 1)
+    grad_gram[...] = jnp.zeros_like(grad_gram)
+    rows_o[...] = jnp.zeros_like(rows_o)
     for pair in range(heads // 2):
-        lanes = slice(pair * LANES, (pair + 1) * LANES)
-        dy_pair = dy[:, lanes]
-        x_pair = xc[:, lanes]
+        lanes_here = slice(pair * LANES, (pair + 1) * LANES)
+        slot = pair % 2
+        dy_pair = dy[:, lanes_here]
+        x_pair = xc[:, lanes_here]
         halves = jnp.concatenate(both_halves(dy_pair), axis=0)
         grad_mixing = dot_nt(halves, x_pair)
-        mixing = []
         for side in range(2):
             head = 2 * pair + side
-            grad_m = grad_mixing[side * BLOCK : (side + 1) * BLOCK, :]
-            kernel = decay_kernel(keep, cums, cum_rows, head)
-            step_row = step_rows[head : head + 1, :]
-            weight = kernel * step_row
-            mixing.append((gram * weight).astype(BF16))
-            grad_gram = grad_gram + grad_m * weight
-            part = grad_m * gram * kernel
-            columns[head : head + 1, :] = jnp.sum(part, axis=0, keepdims=True)
-            sums = sums + jnp.where(lane == head, jnp.sum(part * step_row, axis=1, keepdims=True), 0.0)
-        dx_pair = dot_tn(jnp.concatenate(mixing, axis=0), halves)
-        dxc_o[:, lanes] = (dx_pair + par[7:8, lanes] * dy_pair.astype(F32)).astype(BF16)
-    grad_low = grad_gram.astype(BF16)
+            row_sums, column_sums = [0.0, 0.0], [0.0, 0.0]
+            for tile in TILES:
+                rows, across = tile_slices(tile)
+                first = side * BLOCK + rows.start
+                grad_m = grad_mixing[first : first + LANES, across]
+                kernel = decay_tile(neg, cums, cum_rows, head, tile)
+                step_row = step_rows[head : head + 1, across]
+                weighted = gram[rows, across] * kernel
+                mixing = weighted * step_row
+                mix[slot, first : first + LANES, across] = mixing.astype(BF16)
+                grad_gram[rows, across] += grad_m * (kernel * step_row)
+                row, column = rows.start // LANES, across.start // LANES
+                column_sums[column] = column_sums[column] + jnp.sum(grad_m * weighted, axis=0, keepdims=True)
+                row_sums[row] = row_sums[row] + grad_m * mixing
+            columns[head : head + 1, :] = jnp.concatenate(column_sums, axis=1)
+            for row in range(2):
+                total = jnp.sum(row_sums[row], axis=1, keepdims=True)
+                rows_o[row * LANES : (row + 1) * LANES, :] += jnp.where(lane == head, total, 0.0)
+        dx_pair = dot_tn(mix[slot], halves)
+        dxc_o[:, lanes_here] = (dx_pair + par[7:8, lanes_here] * dy_pair.astype(F32)).astype(BF16)
+    grad_low = grad_gram[...].astype(BF16)
     dq = (expand(enter_weights(place, block, cums), spread) * dy[...].astype(F32)).astype(BF16)
     dcq_o[...] = dot(grad_low, bq) + dot(dq, hb[0])
     dbq_o[...] = dot_tn(grad_low, cq)
-    rows_o[...] = sums
     cols_o[...] = columns[...].T
     acc[...] += dot_tn(normed[...], dz[...])
 
@@ -880,6 +911,9 @@
 
     parts = ctx_count if shard % (16 * ctx_count) == 0 else 1
     part_rows = shard // parts
+
+    fill = jnp.sum(jnp.where(jnp.arange(ctx_count) == lax.axis_index("ctx"), device_fill[0], 0)) * BLOCK
+    halo = shifted(lax.dynamic_slice_in_dim(tokens, fill - 16, 16, 0), "ctx", 1)
 
     with jax.named_scope("gather_weights"):
         vector = jnp.concatenate(
@@ -908,7 +942,7 @@
             w1_parts = joined_rows(exchanged(own_rows(input_rows, part_rows), "dp"))
             vector = jnp.pad(vector, ((0, 0), (0, 2 * inner - 2 * shard)))
             block = jnp.concatenate([own_rows(gate_rows, part_rows), vector], axis=0)
-            block, _ = lax.optimization_barrier((block, w1_parts))
+            block, _, halo = lax.optimization_barrier((block, w1_parts, halo))
             vectors = exchanged(block, "dp")
             w2_parts = exchanged(joined_rows([value[:part_rows] for value in vectors]), "ctx")
             w1_parts = exchanged(w1_parts, "ctx")
@@ -931,8 +965,6 @@
             jnp.stack([lax.axis_index("ctx"), tp_index, lax.axis_index("dp")]).astype(jnp.int32),
         ]
     )
-    fill = jnp.sum(jnp.where(jnp.arange(ctx_count) == lax.axis_index("ctx"), device_fill[0], 0)) * BLOCK
-    halo = shifted(lax.dynamic_slice_in_dim(tokens, fill - 16, 16, 0), "ctx", 1)
 
     def out(shape, dtype, kind):
         return (jax.ShapeDtypeStruct(shape, dtype), kind)
@@ -970,6 +1002,9 @@
             pltpu.VMEM((8 + BLOCK, channels), F32),
             pltpu.VMEM((inner, LANES), F32),
             pltpu.VMEM((8, LANES), F32),
+            pltpu.VMEM((BLOCK, BLOCK), F32),
+            pltpu.VMEM((BLOCK, BLOCK), F32),
+            pltpu.VMEM((2, BLOCK, 2 * BLOCK), BF16),
         ],
         micros=20,
         mega=16,
@@ -1056,7 +1091,6 @@
         mega=14,
     )
     packets = [(shifted(packet, "ctx", -step), "whole") for step in range(1, ctx_count)]
-    received = swapped(send)
     dxc, dcq, dbq, row_sums, col_sums, *g2 = call(
         functools.partial(intra_back_kernel, counts, heads, dp_count),
         steps,
@@ -1082,9 +1116,16 @@
             row_out(LANES, F32),
         ]
         + [out((width // parts, 2 * inner), BF16, "whole")] * parts,
-        [pltpu.VMEM((width, inner), F32), pltpu.VMEM((LANES, BLOCK), F32)],
+        [
+            pltpu.VMEM((width, inner), F32),
+            pltpu.VMEM((LANES, BLOCK), F32),
+            pltpu.VMEM((BLOCK, BLOCK), F32),
+            pltpu.VMEM((BLOCK, BLOCK), F32),
+            pltpu.VMEM((BLOCK, BLOCK), F32),
+            pltpu.VMEM((2, 2 * BLOCK, BLOCK), BF16),
+        ],
         micros=18,
-        mega=14,
+        mega=16,
     )
     with jax.named_scope("reduce_gate_weights"):
         total2 = ctx_sum(g2) if parts > 1 else g2[0]
@@ -1170,11 +1211,6 @@
         mega=12,
     )
     other = swapped(partial)
-    size = ctx_count * 2
-    back = [(s, s - 2) for s in range(2, size)]
-    cross = [(s, (s - 2) ^ 1) for s in range(2, size)]
-    halo_a = lax.ppermute(halo_grad, ("ctx", "tp"), back)
-    halo_b = lax.ppermute(halo_grad, ("ctx", "tp"), cross)
     with jax.named_scope("reduce_input_weights"):
         norm_part = jnp.pad(norm_part, ((0, 0), (channels, 0)))
         if parts > 1:
@@ -1190,11 +1226,18 @@
         else:
             total1 = whole_sum((g1[0].astype(F32) + norm_part).astype(BF16))
         across = swapped(total1[:, inner:])
+        across, halo_grad, send = lax.optimization_barrier((across, halo_grad, send))
         lane = np.arange(3 * LANES) - 2 * LANES
         both = (lane < 0) | ((lane >= STATE_TAPS) & (lane < BY_HEAD))
         both = both | ((lane >= NORM) & (lane < NORM + shard // part_rows))
         summed = total1[:, inner:] + jnp.where(both[None, :], across, 0)
         total1 = jnp.concatenate([total1[:, :inner], summed], axis=1)
+    size = ctx_count * 2
+    back = [(s, s - 2) for s in range(2, size)]
+    cross = [(s, (s - 2) ^ 1) for s in range(2, size)]
+    halo_a = lax.ppermute(halo_grad, ("ctx", "tp"), back)
+    halo_b = lax.ppermute(halo_grad, ("ctx", "tp"), cross)
+    received = swapped(send)
     grad_tokens, layer_out = call(
         functools.partial(finish_kernel, counts),
         steps,

time: 197 us -> 196 us (level)
  starting transfers between devices: 63.8 us -> 54.1 us
  waiting for transfers between devices: 34.3 us -> 37.5 us
  Pallas kernels: 87.5 us -> 89.9 us
    ppermute x28, starting transfers between devices: 46.1 us -> 36.3 us  [partnered(): lax.ppermute(value, axis, [(one, one ^ mask) for one in range(lax.axis_si...]
    ppermute x28, waiting for transfers between devices: 31.9 us -> 36.3 us  [partnered(): lax.ppermute(value, axis, [(one, one ^ mask) for one in range(lax.axis_si...]
    pallas_call x10, Pallas kernels: 87.5 us -> 89.9 us  [call(): pl.pallas_call(body, grid=(steps,), in_specs=[pl.BlockSpec(memory_space=p...]
  transfers between devices with their start and end apart: 41 -> 41, of which waited for: 11 -> 10; matrix products, arithmetic and copies ran while one was open for 4% -> 5% of each run, Pallas kernels for 36% -> 37%
where the time goes in v10:
time: 196 us; the launch traced here: 195 us
  Pallas kernels  89.9 us (46%)
  starting transfers between devices  54.1 us (28%)
  waiting for transfers between devices  37.5 us (19%)
  other arithmetic  6.42 us (3%)
  local copies, waits for them, and re-layouts  5.2 us (3%)
  between operations  2.04 us (1%)
    pallas_call x10, Pallas kernels, call(): pl.pallas_call(body, grid=(steps,), in_specs=[pl.BlockSpec(memory_space=p...  89.9 us
    ppermute x28, starting transfers between devices, partnered(): lax.ppermute(value, axis, [(one, one ^ mask) for one in range(lax.axis_si...  36.3 us
    ppermute x28, waiting for transfers between devices, partnered(): lax.ppermute(value, axis, [(one, one ^ mask) for one in range(lax.axis_si...  36.3 us
    ppermute x7, starting transfers between devices, shifted(): lax.ppermute(value, axis, [(source, source + steps) for source in range(f...  14.8 us
  transfers between devices with their start and end apart: 41, of which 10 were waited for; matrix products, arithmetic and copies ran while one was open for 5% of the time, Pallas kernels for 37%

profile of v10, /device:TPU:0, one launch (start us, length us, event | category | flops | bytes accessed | tf_op | source)
XLA Modules:
  0.0 195.1 jit_solution(17873614308532048232)
XLA Ops:
  1.6 3.1 %collective-permute-start = (bf16[48,1024]{1,0:T(8,128)(2,1)S(1)}, bf16[48,1024]{1,0:T(8,128)(2,1)S(1)}, u32[]{:S(2)}, u32[]{:S(2)}) collective-permute-start(bf16[48,1024]{1,0:T(8,128)(2,1)S(1)} %fusion.7), channel_id=1, source_target_pairs={{0,8},{8,0},{16,24},{24,16},{1,9},{9,1},{17,25},{25,17},{2,10},{10... | collective-permute-start | bytes 294920 | tf_op jit(solution)/shard_map/gather_weights/ppermute | solution.py:850
  4.7 2.6 %collective-permute-start.1 = (bf16[48,1024]{1,0:T(8,128)(2,1)S(1)}, bf16[48,1024]{1,0:T(8,128)(2,1)S(1)}, u32[]{:S(2)}, u32[]{:S(2)}) collective-permute-start(bf16[48,1024]{1,0:T(8,128)(2,1)S(1)} %fusion.7), channel_id=1, source_target_pairs={{0,16},{8,24},{16,0},{24,8},{1,17},{9,25},{17,1},{25,9},{2,18},{10... | collective-permute-start | bytes 294920 | tf_op jit(solution)/shard_map/gather_weights/ppermute | solution.py:850
  10.0 3.6 %collective-permute-start.3 = (bf16[16,768]{1,0:T(8,128)(2,1)S(1)}, bf16[16,768]{1,0:T(8,128)(2,1)S(1)}, u32[]{:S(2)}, u32[]{:S(2)}) collective-permute-start(bf16[16,768]{1,0:T(8,128)(2,1)S(1)} %constant_dynamic-slice_fusion), channel_id=1, source_target_pairs={{0,2},{2,4},{4,6},{1,3},{3,5},{5,7},{8,10},{10,12},{12,14},{9,11},... | collective-permute-start | bytes 73736 | tf_op jit(solution)/shard_map/ppermute | solution.py:842
  20.7 3.6 %collective-permute-start.5 = (bf16[64,1536]{1,0:T(8,128)(2,1)S(1)}, bf16[64,1536]{1,0:T(8,128)(2,1)S(1)}, u32[]{:S(2)}, u32[]{:S(2)}) collective-permute-start(bf16[64,1536]{1,0:T(8,128)(2,1)S(1)} %fusion.3.refs_0_), channel_id=1, source_target_pairs={{0,16},{8,24},{16,0},{24,8},{1,17},{9,25},{17,1},{25,9},{2,18},{10... | collective-permute-start | bytes 589832 | tf_op jit(solution)/shard_map/gather_weights/ppermute | solution.py:850
  26.0 2.2 %collective-permute-done.4.refs_1_ = bf16[64,1536]{1,0:T(8,128)(2,1)S(1)} collective-permute-done((bf16[64,1536]{1,0:T(8,128)(2,1)S(1)}, bf16[64,1536]{1,0:T(8,128)(2,1)S(1)}, u32[]{:S(2)}, u32[]{:S(2)}) %collective-permute-start.4) | collective-permute-done | bytes 196640 | tf_op jit(solution)/shard_map/gather_weights/ppermute | solution.py:850
  30.1 8.1 %collective-permute-done.5.refs_2_ = bf16[64,1536]{1,0:T(8,128)(2,1)S(1)} collective-permute-done((bf16[64,1536]{1,0:T(8,128)(2,1)S(1)}, bf16[64,1536]{1,0:T(8,128)(2,1)S(1)}, u32[]{:S(2)}, u32[]{:S(2)}) %collective-permute-start.5) | collective-permute-done | bytes 196640 | tf_op jit(solution)/shard_map/gather_weights/ppermute | solution.py:850
  41.8 4.2 %collective-permute-done.9.refs_7_ = bf16[192,1024]{1,0:T(8,128)(2,1)} collective-permute-done((bf16[192,1024]{1,0:T(8,128)(2,1)S(1)}, bf16[192,1024]{1,0:T(8,128)(2,1)}, u32[]{:S(2)}, u32[]{:S(2)}) %collective-permute-start.9) | collective-permute-done | bytes 393248 | tf_op jit(solution)/shard_map/gather_weights/ppermute | solution.py:850
  46.1 19.9 %shard_map.306 = (bf16[768,1152]{1,0:T(8,128)(2,1)S(1)}, f32[8,1024]{1,0:T(8,128)S(1)}, bf16[1024,768]{1,0:T(8,128)(2,1)S(1)}, bf16[16,768]{1,0:T(8,128)(2,1)S(1...) custom-call(s32[10]{0:T(128)S(1)} %concatenate.40.info, ...), custom_call_target="tpu_custom_call" | custom-call | flops 22000001024 | bytes 70000000 | tf_op jit(solution)/shard_map/pallas_call | solution.py:822
  67.9 3.9 %collective-permute-start.11 = (bf16[784,128]{1,0:T(8,128)(2,1)S(1)}, bf16[784,128]{1,0:T(8,128)(2,1)S(1)}, u32[]{:S(2)}, u32[]{:S(2)}) collective-permute-start(bf16[784,128]{1,0:T(8,128)(2,1)S(1)} %get-tuple-element.96), channel_id=1, source_target_pairs={{0,4},{2,6},{1,5},{3,7},{8,12},{10,14},{9,13},{11,15},{16,20},{18,... | collective-permute-start | bytes 602120 | tf_op jit(solution)/shard_map/ppermute | solution.py:842
  73.2 4.0 %shard_map.307 = (bf16[768,1536]{1,0:T(8,128)(2,1)S(1)}, bf16[1024,768]{1,0:T(8,128)(2,1)S(1)}, bf16[1024,768]{1,0:T(8,128)(2,1)S(1)}) custom-call(s32[10]{0:T(128)S(1)} %concatenate.40.info, bf16[192,1536]{1,0:T(8,128)(2,1)S(1)} %pad_maximum_fusion.refs_0_, bf16[192,1536]{1,0:T(8,128)(2,1)S(1)} %collective-permute-done.13.refs_1_, ...), custom_call_target="tpu_custom_call" | custom-call | flops 7699999744 | bytes 24500000 | tf_op jit(solution)/shard_map/pallas_call | solution.py:822
  77.2 4.2 %shard_map.308 = (f32[1024,768]{1,0:T(8,128)S(1)}, bf16[4,768,128]{2,1,0:T(8,128)(2,1)S(1)}, f32[4,768,128]{2,1,0:T(8,128)S(1)}, f32[8,1024]{1,0:T(8,128)S(1)}) custom-call(s32[10]{0:T(128)S(1)} %concatenate.40.info, bf16[784,128]{1,0:T(8,128)(2,1)S(1)} %collective-permute-done.10.refs_0_, bf16[784,128]{1,0:T(8,128)(2,1)S(1)} %collective-permute-done.11.refs_1_, ...), custom_call_target="tpu_custom_call" | custom-call | flops 8800000000 | bytes 28000000 | tf_op jit(solution)/shard_map/pallas_call | solution.py:822
  82.7 11.1 %shard_map.309 = (bf16[1024,384]{1,0:T(8,128)(2,1)S(1)}, bf16[1024,384]{1,0:T(8,128)(2,1)S(1)}, bf16[768,768]{1,0:T(8,128)(2,1)S(1)}, f32[8,768]{1,0:T(8,128)S(1...) custom-call(s32[10]{0:T(128)S(1)} %concatenate.40.info, ...), custom_call_target="tpu_custom_call" | custom-call | flops 16499999744 | bytes 52500000 | tf_op jit(solution)/shard_map/pallas_call | solution.py:822
  97.9 14.9 %shard_map.310 = (bf16[1024,768]{1,0:T(8,128)(2,1)S(1)}, f32[1024,128]{1,0:T(8,128)S(1)}, f32[1024,128]{1,0:T(8,128)S(1)}, f32[1024,128]{1,0:T(8,128)S(1)}, f32[...) custom-call(s32[10]{0:T(128)S(1)} %concatenate.40.info, ...), custom_call_target="tpu_custom_call" | custom-call | flops 19800000512 | bytes 63000000 | tf_op jit(solution)/shard_map/pallas_call | solution.py:822
  112.7 2.1 %collective-permute-start.21 = (bf16[192,1536]{1,0:T(8,128)(2,1)S(1)}, bf16[192,1536]{1,0:T(8,128)(2,1)S(1)}, u32[]{:S(2)}, u32[]{:S(2)}) collective-permute-start(bf16[192,1536]{1,0:T(8,128)(2,1)S(1)} %get-tuple-element.131), channel_id=1, source_target_pairs={{0,2},{2,0},{4,6},{6,4},{1,3},{3,1},{5,7},{7,5},{8,10},{10,8},{12,... | collective-permute-start | bytes 1769480 | tf_op jit(solution)/shard_map/reduce_gate_weights/ppermute | solution.py:850
  114.8 3.3 %collective-permute-start.22 = (bf16[192,1536]{1,0:T(8,128)(2,1)S(1)}, bf16[192,1536]{1,0:T(8,128)(2,1)S(1)}, u32[]{:S(2)}, u32[]{:S(2)}) collective-permute-start(bf16[192,1536]{1,0:T(8,128)(2,1)S(1)} %get-tuple-element.132), channel_id=1, source_target_pairs={{0,4},{2,6},{4,0},{6,2},{1,5},{3,7},{5,1},{7,3},{8,12},{10,14},{12... | collective-permute-start | bytes 1769480 | tf_op jit(solution)/shard_map/reduce_gate_weights/ppermute | solution.py:850
  118.1 22.8 %shard_map.311 = (bf16[1024,1152]{1,0:T(8,128)(2,1)S(1)}, bf16[16,1024]{1,0:T(8,128)(2,1)S(1)}, bf16[192,1152]{1,0:T(8,128)(2,1)S(1)}, bf16[192,1152]{1,0:T(8,12...) custom-call(s32[10]{0:T(128)S(1)} %concatenate.40.info, ...), custom_call_target="tpu_custom_call" | custom-call | flops 27499999232 | bytes 87500000 | tf_op jit(solution)/shard_map/pallas_call | solution.py:822
  142.3 2.0 %collective-permute-start.26 = (bf16[192,1152]{1,0:T(8,128)(2,1)S(1)}, bf16[192,1152]{1,0:T(8,128)(2,1)S(1)}, u32[]{:S(2)}, u32[]{:S(2)}) collective-permute-start(bf16[192,1152]{1,0:T(8,128)(2,1)S(1)} %get-tuple-element.140), channel_id=1, source_target_pairs={{0,4},{2,6},{4,0},{6,2},{1,5},{3,7},{5,1},{7,3},{8,12},{10,14},{12... | collective-permute-start | bytes 1327112 | tf_op jit(solution)/shard_map/ppermute | solution.py:850
  145.0 7.0 %collective-permute-done.24 = bf16[96,1536]{1,0:T(8,128)(2,1)S(1)} collective-permute-done((bf16[96,1536]{1,0:T(8,128)(2,1)S(1)}, bf16[96,1536]{1,0:T(8,128)(2,1)S(1)}, u32[]{:S(2)}, u32[]{:S(2)}) %collective-permute-start.24) | collective-permute-done | bytes 294944 | tf_op jit(solution)/shard_map/reduce_gate_weights/ppermute | solution.py:850
  154.6 5.8 %shard_map.312 = (bf16[1024,768]{1,0:T(8,128)(2,1)S(1)}, f32[8,768]{1,0:T(8,128)S(1)}, f32[192,128]{1,0:T(8,128)S(1)}) custom-call(s32[10]{0:T(128)S(1)} %concatenate.40.info, bf16[1024,1152]{1,0:T(8,128)(2,1)S(1)} %get-tuple-element.134.packed, bf16[16,1024]{1,0:T(8,128)(2,1)S(1)} %get-tuple-element.135.back, ...), custom_call_target="tpu_custom_call" | custom-call | flops 5500000256 | bytes 17500000 | tf_op jit(solution)/shard_map/pallas_call | solution.py:822
  160.4 2.3 %collective-permute-done.26 = bf16[192,1152]{1,0:T(8,128)(2,1)S(1)} collective-permute-done((bf16[192,1152]{1,0:T(8,128)(2,1)S(1)}, bf16[192,1152]{1,0:T(8,128)(2,1)S(1)}, u32[]{:S(2)}, u32[]{:S(2)}) %collective-permute-start.26) | collective-permute-done | bytes 442400 | tf_op jit(solution)/shard_map/ppermute | solution.py:850
  164.6 2.7 %collective-permute-start.30 = (bf16[48,1152]{1,0:T(8,128)(2,1)S(1)}, bf16[48,1152]{1,0:T(8,128)(2,1)S(1)}, u32[]{:S(2)}, u32[]{:S(2)}) collective-permute-start(bf16[48,1152]{1,0:T(8,128)(2,1)S(1)} %get-tuple-element.180), channel_id=1, source_target_pairs={{0,16},{8,24},{16,0},{24,8},{1,17},{9,25},{17,1},{25,9},{2,18},{10... | collective-permute-start | bytes 331784 | tf_op jit(solution)/shard_map/reduce_input_weights/ppermute | solution.py:850
  168.9 5.2 %collective-permute-done.30 = bf16[48,1152]{1,0:T(8,128)(2,1)S(1)} collective-permute-done((bf16[48,1152]{1,0:T(8,128)(2,1)S(1)}, bf16[48,1152]{1,0:T(8,128)(2,1)S(1)}, u32[]{:S(2)}, u32[]{:S(2)}) %collective-permute-start.30) | collective-permute-done | bytes 110624 | tf_op jit(solution)/shard_map/reduce_input_weights/ppermute | solution.py:850
  178.8 4.9 %collective-permute-done.40 = bf16[96,1536]{1,0:T(8,128)(2,1)S(1)} collective-permute-done((bf16[96,1536]{1,0:T(8,128)(2,1)S(1)}, bf16[96,1536]{1,0:T(8,128)(2,1)S(1)}, u32[]{:S(2)}, u32[]{:S(2)}) %collective-permute-start.40) | collective-permute-done | bytes 294944 | tf_op jit(solution)/shard_map/reduce_input_weights/ppermute | solution.py:850
  188.9 3.9 %shard_map.313 = (f32[1024,768]{1,0:T(8,128)}, f32[1024,384]{1,0:T(8,128)}) custom-call(s32[10]{0:T(128)S(1)} %concatenate.40.info, bf16[1024,768]{1,0:T(8,128)(2,1)S(1)} %get-tuple-element.137.own, bf16[1024,768]{1,0:T(8,128)(2,1)S(1)} %collective-permute-done.25.other, f32[8,768]{1,0:T(8,128)S(1)} %collective-permute-done.34.halo_a, ...), custom_call_target="tpu_custom_call" | custom-call | flops 5500000256 | bytes 17500000 | tf_op jit(solution)/shard_map/pallas_call | solution.py:822
  (131 shorter events, 45.8 us)
Async XLA Ops:
  1.6 17.5 %collective-permute-start = (bf16[48,1024]{1,0:T(8,128)(2,1)S(1)}, bf16[48,1024]{1,0:T(8,128)(2,1)S(1)}, u32[]{:S(2)}, u32[]{:S(2)}) collective-permute-start(bf16[48,1024]{1,0:T(8,128)(2,1)S(1)} %fusion.7), channel_id=1, source_target_pairs={{0,8},{8,0},{16,24},{24,16},{1,9},{9,1},{17,25},{25,17},{2,10},{10... | collective-permute-start | bytes 294920 | tf_op jit(solution)/shard_map/gather_weights/ppermute | solution.py:850
  4.7 14.4 %collective-permute-start.1 = (bf16[48,1024]{1,0:T(8,128)(2,1)S(1)}, bf16[48,1024]{1,0:T(8,128)(2,1)S(1)}, u32[]{:S(2)}, u32[]{:S(2)}) collective-permute-start(bf16[48,1024]{1,0:T(8,128)(2,1)S(1)} %fusion.7), channel_id=1, source_target_pairs={{0,16},{8,24},{16,0},{24,8},{1,17},{9,25},{17,1},{25,9},{2,18},{10... | collective-permute-start | bytes 294920 | tf_op jit(solution)/shard_map/gather_weights/ppermute | solution.py:850
  7.3 11.9 %collective-permute-start.2 = (bf16[48,1024]{1,0:T(8,128)(2,1)S(1)}, bf16[48,1024]{1,0:T(8,128)(2,1)S(1)}, u32[]{:S(2)}, u32[]{:S(2)}) collective-permute-start(bf16[48,1024]{1,0:T(8,128)(2,1)S(1)} %fusion.7), channel_id=1, source_target_pairs={{0,24},{8,16},{16,8},{24,0},{1,25},{9,17},{17,9},{25,1},{2,26},{10... | collective-permute-start | bytes 294920 | tf_op jit(solution)/shard_map/gather_weights/ppermute | solution.py:850
  20.7 17.5 %collective-permute-start.5 = (bf16[64,1536]{1,0:T(8,128)(2,1)S(1)}, bf16[64,1536]{1,0:T(8,128)(2,1)S(1)}, u32[]{:S(2)}, u32[]{:S(2)}) collective-permute-start(bf16[64,1536]{1,0:T(8,128)(2,1)S(1)} %fusion.3.refs_0_), channel_id=1, source_target_pairs={{0,16},{8,24},{16,0},{24,8},{1,17},{9,25},{17,1},{25,9},{2,18},{10... | collective-permute-start | bytes 589832 | tf_op jit(solution)/shard_map/gather_weights/ppermute | solution.py:850
  24.2 14.0 %collective-permute-start.6 = (bf16[64,1536]{1,0:T(8,128)(2,1)S(1)}, bf16[64,1536]{1,0:T(8,128)(2,1)S(1)}, u32[]{:S(2)}, u32[]{:S(2)}) collective-permute-start(bf16[64,1536]{1,0:T(8,128)(2,1)S(1)} %fusion.3.refs_0_), channel_id=1, source_target_pairs={{0,24},{8,16},{16,8},{24,0},{1,25},{9,17},{17,9},{25,1},{2,26},{10... | collective-permute-start | bytes 589832 | tf_op jit(solution)/shard_map/gather_weights/ppermute | solution.py:850
  24.5 15.5 %collective-permute-start.7 = (bf16[192,1024]{1,0:T(8,128)(2,1)S(1)}, bf16[192,1024]{1,0:T(8,128)(2,1)S(1)}, u32[]{:S(2)}, u32[]{:S(2)}) collective-permute-start(bf16[192,1024]{1,0:T(8,128)(2,1)S(1)} %pad_maximum_fusion.2.refs_4_), channel_id=1, source_target_pairs={{0,2},{2,0},{4,6},{6,4},{1,3},{3,1},{5,7},{7,5},{8,10},{10,8},{12,... | collective-permute-start | bytes 1179656 | tf_op jit(solution)/shard_map/gather_weights/ppermute | solution.py:850
  26.0 15.9 %collective-permute-start.8 = (bf16[192,1024]{1,0:T(8,128)(2,1)S(1)}, bf16[192,1024]{1,0:T(8,128)(2,1)}, u32[]{:S(2)}, u32[]{:S(2)}) collective-permute-start(bf16[192,1024]{1,0:T(8,128)(2,1)S(1)} %pad_maximum_fusion.2.refs_4_), channel_id=1, source_target_pairs={{0,4},{2,6},{4,0},{6,2},{1,5},{3,7},{5,1},{7,3},{8,12},{10,14},{12... | collective-permute-start | bytes 1179656 | tf_op jit(solution)/shard_map/gather_weights/ppermute | solution.py:850
  28.2 17.9 %collective-permute-start.9 = (bf16[192,1024]{1,0:T(8,128)(2,1)S(1)}, bf16[192,1024]{1,0:T(8,128)(2,1)}, u32[]{:S(2)}, u32[]{:S(2)}) collective-permute-start(bf16[192,1024]{1,0:T(8,128)(2,1)S(1)} %pad_maximum_fusion.2.refs_4_), channel_id=1, source_target_pairs={{0,6},{2,4},{4,2},{6,0},{1,7},{3,5},{5,3},{7,1},{8,14},{10,12},{12... | collective-permute-start | bytes 1179656 | tf_op jit(solution)/shard_map/gather_weights/ppermute | solution.py:850
  38.3 33.6 %collective-permute-start.13 = (bf16[192,1536]{1,0:T(8,128)(2,1)S(1)}, bf16[192,1536]{1,0:T(8,128)(2,1)S(1)}, u32[]{:S(2)}, u32[]{:S(2)}) collective-permute-start(bf16[192,1536]{1,0:T(8,128)(2,1)S(1)} %pad_maximum_fusion.refs_0_), channel_id=1, source_target_pairs={{0,2},{2,0},{4,6},{6,4},{1,3},{3,1},{5,7},{7,5},{8,10},{10,8},{12,... | collective-permute-start | bytes 1769480 | tf_op jit(solution)/shard_map/gather_weights/ppermute | solution.py:850
  39.8 33.3 %collective-permute-start.14 = (bf16[192,1536]{1,0:T(8,128)(2,1)S(1)}, bf16[192,1536]{1,0:T(8,128)(2,1)S(1)}, u32[]{:S(2)}, u32[]{:S(2)}) collective-permute-start(bf16[192,1536]{1,0:T(8,128)(2,1)S(1)} %pad_maximum_fusion.refs_0_), channel_id=1, source_target_pairs={{0,4},{2,6},{4,0},{6,2},{1,5},{3,7},{5,1},{7,3},{8,12},{10,14},{12... | collective-permute-start | bytes 1769480 | tf_op jit(solution)/shard_map/gather_weights/ppermute | solution.py:850
  40.0 33.2 %collective-permute-start.15 = (bf16[192,1536]{1,0:T(8,128)(2,1)S(1)}, bf16[192,1536]{1,0:T(8,128)(2,1)S(1)}, u32[]{:S(2)}, u32[]{:S(2)}) collective-permute-start(bf16[192,1536]{1,0:T(8,128)(2,1)S(1)} %pad_maximum_fusion.refs_0_), channel_id=1, source_target_pairs={{0,6},{2,4},{4,2},{6,0},{1,7},{3,5},{5,3},{7,1},{8,14},{10,12},{12... | collective-permute-start | bytes 1769480 | tf_op jit(solution)/shard_map/gather_weights/ppermute | solution.py:850
  66.0 11.2 %collective-permute-start.10 = (bf16[784,128]{1,0:T(8,128)(2,1)S(1)}, bf16[784,128]{1,0:T(8,128)(2,1)S(1)}, u32[]{:S(2)}, u32[]{:S(2)}) collective-permute-start(bf16[784,128]{1,0:T(8,128)(2,1)S(1)} %get-tuple-element.96), channel_id=1, source_target_pairs={{0,2},{2,4},{4,6},{1,3},{3,5},{5,7},{8,10},{10,12},{12,14},{9,11},... | collective-permute-start | bytes 602120 | tf_op jit(solution)/shard_map/ppermute | solution.py:842
  93.8 24.3 %collective-permute-start.17 = (bf16[784,128]{1,0:T(8,128)(2,1)S(1)}, bf16[784,128]{1,0:T(8,128)(2,1)S(1)}, u32[]{:S(2)}, u32[]{:S(2)}) collective-permute-start(bf16[784,128]{1,0:T(8,128)(2,1)S(1)} %get-tuple-element.111), channel_id=1, source_target_pairs={{2,0},{4,2},{6,4},{3,1},{5,3},{7,5},{10,8},{12,10},{14,12},{11,9},... | collective-permute-start | bytes 602120 | tf_op jit(solution)/shard_map/ppermute | solution.py:842
  95.1 23.0 %collective-permute-start.18 = (bf16[784,128]{1,0:T(8,128)(2,1)S(1)}, bf16[784,128]{1,0:T(8,128)(2,1)S(1)}, u32[]{:S(2)}, u32[]{:S(2)}) collective-permute-start(bf16[784,128]{1,0:T(8,128)(2,1)S(1)} %get-tuple-element.111), channel_id=1, source_target_pairs={{4,0},{6,2},{5,1},{7,3},{12,8},{14,10},{13,9},{15,11},{20,16},{22,... | collective-permute-start | bytes 602120 | tf_op jit(solution)/shard_map/ppermute | solution.py:842
  96.4 21.7 %collective-permute-start.19 = (bf16[784,128]{1,0:T(8,128)(2,1)S(1)}, bf16[784,128]{1,0:T(8,128)(2,1)S(1)}, u32[]{:S(2)}, u32[]{:S(2)}) collective-permute-start(bf16[784,128]{1,0:T(8,128)(2,1)S(1)} %get-tuple-element.111), channel_id=1, source_target_pairs={{6,0},{7,1},{14,8},{15,9},{22,16},{23,17},{30,24},{31,25}} | collective-permute-start | bytes 602120 | tf_op jit(solution)/shard_map/ppermute | solution.py:842
  112.7 31.6 %collective-permute-start.21 = (bf16[192,1536]{1,0:T(8,128)(2,1)S(1)}, bf16[192,1536]{1,0:T(8,128)(2,1)S(1)}, u32[]{:S(2)}, u32[]{:S(2)}) collective-permute-start(bf16[192,1536]{1,0:T(8,128)(2,1)S(1)} %get-tuple-element.131), channel_id=1, source_target_pairs={{0,2},{2,0},{4,6},{6,4},{1,3},{3,1},{5,7},{7,5},{8,10},{10,8},{12,... | collective-permute-start | bytes 1769480 | tf_op jit(solution)/shard_map/reduce_gate_weights/ppermute | solution.py:850
  114.8 29.7 %collective-permute-start.22 = (bf16[192,1536]{1,0:T(8,128)(2,1)S(1)}, bf16[192,1536]{1,0:T(8,128)(2,1)S(1)}, u32[]{:S(2)}, u32[]{:S(2)}) collective-permute-start(bf16[192,1536]{1,0:T(8,128)(2,1)S(1)} %get-tuple-element.132), channel_id=1, source_target_pairs={{0,4},{2,6},{4,0},{6,2},{1,5},{3,7},{5,1},{7,3},{8,12},{10,14},{12... | collective-permute-start | bytes 1769480 | tf_op jit(solution)/shard_map/reduce_gate_weights/ppermute | solution.py:850
  118.1 26.4 %collective-permute-start.23 = (bf16[192,1536]{1,0:T(8,128)(2,1)S(1)}, bf16[192,1536]{1,0:T(8,128)(2,1)S(1)}, u32[]{:S(2)}, u32[]{:S(2)}) collective-permute-start(bf16[192,1536]{1,0:T(8,128)(2,1)S(1)} %get-tuple-element.133), channel_id=1, source_target_pairs={{0,6},{2,4},{4,2},{6,0},{1,7},{3,5},{5,3},{7,1},{8,14},{10,12},{12... | collective-permute-start | bytes 1769480 | tf_op jit(solution)/shard_map/reduce_gate_weights/ppermute | solution.py:850
  140.9 13.2 %collective-permute-start.20 = (bf16[192,1152]{1,0:T(8,128)(2,1)S(1)}, bf16[192,1152]{1,0:T(8,128)(2,1)S(1)}, u32[]{:S(2)}, u32[]{:S(2)}) collective-permute-start(bf16[192,1152]{1,0:T(8,128)(2,1)S(1)} %get-tuple-element.129), channel_id=1, source_target_pairs={{0,2},{2,0},{4,6},{6,4},{1,3},{3,1},{5,7},{7,5},{8,10},{10,8},{12,... | collective-permute-start | bytes 1327112 | tf_op jit(solution)/shard_map/ppermute | solution.py:850
  142.3 20.3 %collective-permute-start.26 = (bf16[192,1152]{1,0:T(8,128)(2,1)S(1)}, bf16[192,1152]{1,0:T(8,128)(2,1)S(1)}, u32[]{:S(2)}, u32[]{:S(2)}) collective-permute-start(bf16[192,1152]{1,0:T(8,128)(2,1)S(1)} %get-tuple-element.140), channel_id=1, source_target_pairs={{0,4},{2,6},{4,0},{6,2},{1,5},{3,7},{5,1},{7,3},{8,12},{10,14},{12... | collective-permute-start | bytes 1327112 | tf_op jit(solution)/shard_map/ppermute | solution.py:850
  144.4 18.3 %collective-permute-start.27 = (bf16[192,1152]{1,0:T(8,128)(2,1)S(1)}, bf16[192,1152]{1,0:T(8,128)(2,1)S(1)}, u32[]{:S(2)}, u32[]{:S(2)}) collective-permute-start(bf16[192,1152]{1,0:T(8,128)(2,1)S(1)} %get-tuple-element.141), channel_id=1, source_target_pairs={{0,6},{2,4},{4,2},{6,0},{1,7},{3,5},{5,3},{7,1},{8,14},{10,12},{12... | collective-permute-start | bytes 1327112 | tf_op jit(solution)/shard_map/ppermute | solution.py:850
  167.5 21.4 %collective-permute-start.25 = (bf16[1024,768]{1,0:T(8,128)(2,1)S(1)}, bf16[1024,768]{1,0:T(8,128)(2,1)S(1)}, u32[]{:S(2)}, u32[]{:S(2)}) collective-permute-start(bf16[1024,768]{1,0:T(8,128)(2,1)S(1)} %get-tuple-element.137.own), channel_id=1, source_target_pairs={{0,1},{1,0},{2,3},{3,2},{4,5},{5,4},{6,7},{7,6},{8,9},{9,8},{10,11... | collective-permute-start | bytes 4718600 | tf_op jit(solution)/shard_map/ppermute | solution.py:846
  175.9 11.4 %collective-permute-start.34 = (f32[8,768]{1,0:T(8,128)S(1)}, f32[8,768]{1,0:T(8,128)S(1)}, u32[]{:S(2)}, u32[]{:S(2)}) collective-permute-start(f32[8,768]{1,0:T(8,128)S(1)} %get-tuple-element.149), channel_id=1, source_target_pairs={{2,0},{3,1},{4,2},{5,3},{6,4},{7,5},{10,8},{11,9},{12,10},{13,11},... | collective-permute-start | bytes 73736 | tf_op jit(solution)/shard_map/ppermute | solution.py:1238
  177.2 11.2 %collective-permute-start.35 = (f32[8,768]{1,0:T(8,128)S(1)}, f32[8,768]{1,0:T(8,128)S(1)}, u32[]{:S(2)}, u32[]{:S(2)}) collective-permute-start(f32[8,768]{1,0:T(8,128)S(1)} %get-tuple-element.149), channel_id=1, source_target_pairs={{2,1},{3,0},{4,3},{5,2},{6,5},{7,4},{10,9},{11,8},{12,11},{13,10},... | collective-permute-start | bytes 73736 | tf_op jit(solution)/shard_map/ppermute | solution.py:1239
  (26 other events, 328.2 us)

commit v11 on v9

--- a/solution.py
+++ b/solution.py
@@ -1056,7 +1056,6 @@
         mega=14,
     )
     packets = [(shifted(packet, "ctx", -step), "whole") for step in range(1, ctx_count)]
-    received = swapped(send)
     dxc, dcq, dbq, row_sums, col_sums, *g2 = call(
         functools.partial(intra_back_kernel, counts, heads, dp_count),
         steps,
@@ -1170,11 +1169,6 @@
         mega=12,
     )
     other = swapped(partial)
-    size = ctx_count * 2
-    back = [(s, s - 2) for s in range(2, size)]
-    cross = [(s, (s - 2) ^ 1) for s in range(2, size)]
-    halo_a = lax.ppermute(halo_grad, ("ctx", "tp"), back)
-    halo_b = lax.ppermute(halo_grad, ("ctx", "tp"), cross)
     with jax.named_scope("reduce_input_weights"):
         norm_part = jnp.pad(norm_part, ((0, 0), (channels, 0)))
         if parts > 1:
@@ -1190,11 +1184,18 @@
         else:
             total1 = whole_sum((g1[0].astype(F32) + norm_part).astype(BF16))
         across = swapped(total1[:, inner:])
+        across, halo_grad, send = lax.optimization_barrier((across, halo_grad, send))
         lane = np.arange(3 * LANES) - 2 * LANES
         both = (lane < 0) | ((lane >= STATE_TAPS) & (lane < BY_HEAD))
         both = both | ((lane >= NORM) & (lane < NORM + shard // part_rows))
         summed = total1[:, inner:] + jnp.where(both[None, :], across, 0)
         total1 = jnp.concatenate([total1[:, :inner], summed], axis=1)
+    size = ctx_count * 2
+    back = [(s, s - 2) for s in range(2, size)]
+    cross = [(s, (s - 2) ^ 1) for s in range(2, size)]
+    halo_a = lax.ppermute(halo_grad, ("ctx", "tp"), back)
+    halo_b = lax.ppermute(halo_grad, ("ctx", "tp"), cross)
+    received = swapped(send)
     grad_tokens, layer_out = call(
         functools.partial(finish_kernel, counts),
         steps,

time: 197 us -> 191 us (0.970)
  waiting for transfers between devices: 34.3 us -> 31.2 us
  starting transfers between devices: 63.8 us -> 61 us
    ppermute x28, waiting for transfers between devices: 31.9 us -> 28.8 us  [partnered(): lax.ppermute(value, axis, [(one, one ^ mask) for one in range(lax.axis_si...]
    ppermute x28, starting transfers between devices: 46.1 us -> 43.5 us  [partnered(): lax.ppermute(value, axis, [(one, one ^ mask) for one in range(lax.axis_si...]
  transfers between devices with their start and end apart: 41 -> 41, of which waited for: 11 -> 11; matrix products, arithmetic and copies ran while one was open for 4% -> 4% of each run, Pallas kernels for 36% -> 37%
where the time goes in v11:
time: 191 us; the launch traced here: 190 us
  Pallas kernels  87.5 us (46%)
  starting transfers between devices  61 us (32%)
  waiting for transfers between devices  31.2 us (16%)
  other arithmetic  5.18 us (3%)
  local copies, waits for them, and re-layouts  3.33 us (2%)
  between operations  2.01 us (1%)
    pallas_call x10, Pallas kernels, call(): pl.pallas_call(body, grid=(steps,), in_specs=[pl.BlockSpec(memory_space=p...  87.5 us
    ppermute x28, starting transfers between devices, partnered(): lax.ppermute(value, axis, [(one, one ^ mask) for one in range(lax.axis_si...  43.5 us
    ppermute x28, waiting for transfers between devices, partnered(): lax.ppermute(value, axis, [(one, one ^ mask) for one in range(lax.axis_si...  28.8 us
    ppermute x7, starting transfers between devices, shifted(): lax.ppermute(value, axis, [(source, source + steps) for source in range(f...  14.6 us
  transfers between devices with their start and end apart: 41, of which 11 were waited for; matrix products, arithmetic and copies ran while one was open for 4% of the time, Pallas kernels for 37%

profile of v11, /device:TPU:0, one launch (start us, length us, event | category | flops | bytes accessed | tf_op | source)
XLA Modules:
  0.0 190.1 jit_solution(14166043815942473522)
XLA Ops:
  1.7 3.1 %collective-permute-start = (bf16[48,1024]{1,0:T(8,128)(2,1)S(1)}, bf16[48,1024]{1,0:T(8,128)(2,1)S(1)}, u32[]{:S(2)}, u32[]{:S(2)}) collective-permute-start(bf16[48,1024]{1,0:T(8,128)(2,1)S(1)} %fusion.7), channel_id=1, source_target_pairs={{0,8},{8,0},{16,24},{24,16},{1,9},{9,1},{17,25},{25,17},{2,10},{10... | collective-permute-start | bytes 294920 | tf_op jit(solution)/shard_map/gather_weights/ppermute | solution.py:819
  4.8 2.6 %collective-permute-start.1 = (bf16[48,1024]{1,0:T(8,128)(2,1)S(1)}, bf16[48,1024]{1,0:T(8,128)(2,1)S(1)}, u32[]{:S(2)}, u32[]{:S(2)}) collective-permute-start(bf16[48,1024]{1,0:T(8,128)(2,1)S(1)} %fusion.7), channel_id=1, source_target_pairs={{0,16},{8,24},{16,0},{24,8},{1,17},{9,25},{17,1},{25,9},{2,18},{10... | collective-permute-start | bytes 294920 | tf_op jit(solution)/shard_map/gather_weights/ppermute | solution.py:819
  23.5 2.4 %collective-permute-start.8 = (bf16[192,1024]{1,0:T(8,128)(2,1)S(1)}, bf16[192,1024]{1,0:T(8,128)(2,1)}, u32[]{:S(2)}, u32[]{:S(2)}) collective-permute-start(bf16[192,1024]{1,0:T(8,128)(2,1)S(1)} %pad_maximum_fusion.2.refs_4_), channel_id=1, source_target_pairs={{0,6},{2,4},{4,2},{6,0},{1,7},{3,5},{5,3},{7,1},{8,14},{10,12},{12... | collective-permute-start | bytes 1179656 | tf_op jit(solution)/shard_map/gather_weights/ppermute | solution.py:819
  26.8 6.8 %collective-permute-done.4.refs_2_ = bf16[64,1536]{1,0:T(8,128)(2,1)S(1)} collective-permute-done((bf16[64,1536]{1,0:T(8,128)(2,1)S(1)}, bf16[64,1536]{1,0:T(8,128)(2,1)S(1)}, u32[]{:S(2)}, u32[]{:S(2)}) %collective-permute-start.4) | collective-permute-done | bytes 196640 | tf_op jit(solution)/shard_map/gather_weights/ppermute | solution.py:819
  33.6 3.4 %collective-permute-start.9 = (bf16[16,768]{1,0:T(8,128)(2,1)S(1)}, bf16[16,768]{1,0:T(8,128)(2,1)S(1)}, u32[]{:S(2)}, u32[]{:S(2)}) collective-permute-start(bf16[16,768]{1,0:T(8,128)(2,1)S(1)} %constant_dynamic-slice_fusion), channel_id=1, source_target_pairs={{0,2},{2,4},{4,6},{1,3},{3,5},{5,7},{8,10},{10,12},{12,14},{9,11},... | collective-permute-start | bytes 73736 | tf_op jit(solution)/shard_map/ppermute | solution.py:811
  39.8 2.4 %collective-permute-start.14 = (bf16[192,1536]{1,0:T(8,128)(2,1)S(1)}, bf16[192,1536]{1,0:T(8,128)(2,1)S(1)}, u32[]{:S(2)}, u32[]{:S(2)}) collective-permute-start(bf16[192,1536]{1,0:T(8,128)(2,1)S(1)} %pad_maximum_fusion.refs_0_), channel_id=1, source_target_pairs={{0,4},{2,6},{4,0},{6,2},{1,5},{3,7},{5,1},{7,3},{8,12},{10,14},{12... | collective-permute-start | bytes 1769480 | tf_op jit(solution)/shard_map/gather_weights/ppermute | solution.py:819
  43.8 17.5 %shard_map.306 = (bf16[768,1152]{1,0:T(8,128)(2,1)S(1)}, f32[8,1024]{1,0:T(8,128)S(1)}, bf16[1024,768]{1,0:T(8,128)(2,1)S(1)}, bf16[16,768]{1,0:T(8,128)(2,1)S(1...) custom-call(s32[10]{0:T(128)S(1)} %concatenate.40.info, ...), custom_call_target="tpu_custom_call" | custom-call | flops 22000001024 | bytes 70000000 | tf_op jit(solution)/shard_map/pallas_call | solution.py:791
  61.3 2.0 %collective-permute-start.10 = (bf16[784,128]{1,0:T(8,128)(2,1)S(1)}, bf16[784,128]{1,0:T(8,128)(2,1)S(1)}, u32[]{:S(2)}, u32[]{:S(2)}) collective-permute-start(bf16[784,128]{1,0:T(8,128)(2,1)S(1)} %get-tuple-element.94), channel_id=1, source_target_pairs={{0,2},{2,4},{4,6},{1,3},{3,5},{5,7},{8,10},{10,12},{12,14},{9,11},... | collective-permute-start | bytes 602120 | tf_op jit(solution)/shard_map/ppermute | solution.py:811
  63.2 3.9 %collective-permute-start.11 = (bf16[784,128]{1,0:T(8,128)(2,1)S(1)}, bf16[784,128]{1,0:T(8,128)(2,1)S(1)}, u32[]{:S(2)}, u32[]{:S(2)}) collective-permute-start(bf16[784,128]{1,0:T(8,128)(2,1)S(1)} %get-tuple-element.94), channel_id=1, source_target_pairs={{0,4},{2,6},{1,5},{3,7},{8,12},{10,14},{9,13},{11,15},{16,20},{18,... | collective-permute-start | bytes 602120 | tf_op jit(solution)/shard_map/ppermute | solution.py:811
  68.5 4.0 %shard_map.307 = (bf16[768,1536]{1,0:T(8,128)(2,1)S(1)}, bf16[1024,768]{1,0:T(8,128)(2,1)S(1)}, bf16[1024,768]{1,0:T(8,128)(2,1)S(1)}) custom-call(s32[10]{0:T(128)S(1)} %concatenate.40.info, bf16[192,1536]{1,0:T(8,128)(2,1)S(1)} %pad_maximum_fusion.refs_0_, bf16[192,1536]{1,0:T(8,128)(2,1)S(1)} %collective-permute-done.13.refs_1_, ...), custom_call_target="tpu_custom_call" | custom-call | flops 7699999744 | bytes 24500000 | tf_op jit(solution)/shard_map/pallas_call | solution.py:791
  72.5 4.2 %shard_map.308 = (f32[1024,768]{1,0:T(8,128)S(1)}, bf16[4,768,128]{2,1,0:T(8,128)(2,1)S(1)}, f32[4,768,128]{2,1,0:T(8,128)S(1)}, f32[8,1024]{1,0:T(8,128)S(1)}) custom-call(s32[10]{0:T(128)S(1)} %concatenate.40.info, bf16[784,128]{1,0:T(8,128)(2,1)S(1)} %collective-permute-done.10.refs_0_, bf16[784,128]{1,0:T(8,128)(2,1)S(1)} %collective-permute-done.11.refs_1_, ...), custom_call_target="tpu_custom_call" | custom-call | flops 8800000000 | bytes 28000000 | tf_op jit(solution)/shard_map/pallas_call | solution.py:791
  78.0 10.9 %shard_map.309 = (bf16[1024,384]{1,0:T(8,128)(2,1)S(1)}, bf16[1024,384]{1,0:T(8,128)(2,1)S(1)}, bf16[768,768]{1,0:T(8,128)(2,1)S(1)}, f32[8,768]{1,0:T(8,128)S(1...) custom-call(s32[10]{0:T(128)S(1)} %concatenate.40.info, ...), custom_call_target="tpu_custom_call" | custom-call | flops 16499999744 | bytes 52500000 | tf_op jit(solution)/shard_map/pallas_call | solution.py:791
  93.0 15.2 %shard_map.310 = (bf16[1024,768]{1,0:T(8,128)(2,1)S(1)}, f32[1024,128]{1,0:T(8,128)S(1)}, f32[1024,128]{1,0:T(8,128)S(1)}, f32[1024,128]{1,0:T(8,128)S(1)}, f32[...) custom-call(s32[10]{0:T(128)S(1)} %concatenate.40.info, ...), custom_call_target="tpu_custom_call" | custom-call | flops 19800000512 | bytes 63000000 | tf_op jit(solution)/shard_map/pallas_call | solution.py:791
  108.2 2.1 %collective-permute-start.21 = (bf16[192,1536]{1,0:T(8,128)(2,1)S(1)}, bf16[192,1536]{1,0:T(8,128)(2,1)S(1)}, u32[]{:S(2)}, u32[]{:S(2)}) collective-permute-start(bf16[192,1536]{1,0:T(8,128)(2,1)S(1)} %get-tuple-element.129), channel_id=1, source_target_pairs={{0,2},{2,0},{4,6},{6,4},{1,3},{3,1},{5,7},{7,5},{8,10},{10,8},{12,... | collective-permute-start | bytes 1769480 | tf_op jit(solution)/shard_map/reduce_gate_weights/ppermute | solution.py:819
  110.3 3.3 %collective-permute-start.22 = (bf16[192,1536]{1,0:T(8,128)(2,1)S(1)}, bf16[192,1536]{1,0:T(8,128)(2,1)S(1)}, u32[]{:S(2)}, u32[]{:S(2)}) collective-permute-start(bf16[192,1536]{1,0:T(8,128)(2,1)S(1)} %get-tuple-element.130), channel_id=1, source_target_pairs={{0,4},{2,6},{4,0},{6,2},{1,5},{3,7},{5,1},{7,3},{8,12},{10,14},{12... | collective-permute-start | bytes 1769480 | tf_op jit(solution)/shard_map/reduce_gate_weights/ppermute | solution.py:819
  113.6 22.6 %shard_map.311 = (bf16[1024,1152]{1,0:T(8,128)(2,1)S(1)}, bf16[16,1024]{1,0:T(8,128)(2,1)S(1)}, bf16[192,1152]{1,0:T(8,128)(2,1)S(1)}, bf16[192,1152]{1,0:T(8,12...) custom-call(s32[10]{0:T(128)S(1)} %concatenate.40.info, ...), custom_call_target="tpu_custom_call" | custom-call | flops 27499999232 | bytes 87500000 | tf_op jit(solution)/shard_map/pallas_call | solution.py:791
  137.6 2.0 %collective-permute-start.26 = (bf16[192,1152]{1,0:T(8,128)(2,1)S(1)}, bf16[192,1152]{1,0:T(8,128)(2,1)S(1)}, u32[]{:S(2)}, u32[]{:S(2)}) collective-permute-start(bf16[192,1152]{1,0:T(8,128)(2,1)S(1)} %get-tuple-element.138), channel_id=1, source_target_pairs={{0,4},{2,6},{4,0},{6,2},{1,5},{3,7},{5,1},{7,3},{8,12},{10,14},{12... | collective-permute-start | bytes 1327112 | tf_op jit(solution)/shard_map/ppermute | solution.py:819
  140.9 6.4 %collective-permute-done.24 = bf16[96,1536]{1,0:T(8,128)(2,1)S(1)} collective-permute-done((bf16[96,1536]{1,0:T(8,128)(2,1)S(1)}, bf16[96,1536]{1,0:T(8,128)(2,1)S(1)}, u32[]{:S(2)}, u32[]{:S(2)}) %collective-permute-start.24) | collective-permute-done | bytes 294944 | tf_op jit(solution)/shard_map/reduce_gate_weights/ppermute | solution.py:819
  147.3 2.0 %collective-permute-done.20 = bf16[192,1152]{1,0:T(8,128)(2,1)S(1)} collective-permute-done((bf16[192,1152]{1,0:T(8,128)(2,1)S(1)}, bf16[192,1152]{1,0:T(8,128)(2,1)S(1)}, u32[]{:S(2)}, u32[]{:S(2)}) %collective-permute-start.20) | collective-permute-done | bytes 442400 | tf_op jit(solution)/shard_map/ppermute | solution.py:819
  151.1 5.7 %shard_map.312 = (bf16[1024,768]{1,0:T(8,128)(2,1)S(1)}, f32[8,768]{1,0:T(8,128)S(1)}, f32[192,128]{1,0:T(8,128)S(1)}) custom-call(s32[10]{0:T(128)S(1)} %concatenate.40.info, bf16[1024,1152]{1,0:T(8,128)(2,1)S(1)} %get-tuple-element.132.packed, bf16[16,1024]{1,0:T(8,128)(2,1)S(1)} %get-tuple-element.133.back, ...), custom_call_target="tpu_custom_call" | custom-call | flops 5500000256 | bytes 17500000 | tf_op jit(solution)/shard_map/pallas_call | solution.py:791
  159.2 2.9 %collective-permute-start.30 = (bf16[48,1152]{1,0:T(8,128)(2,1)S(1)}, bf16[48,1152]{1,0:T(8,128)(2,1)S(1)}, u32[]{:S(2)}, u32[]{:S(2)}) collective-permute-start(bf16[48,1152]{1,0:T(8,128)(2,1)S(1)} %get-tuple-element.178), channel_id=1, source_target_pairs={{0,16},{8,24},{16,0},{24,8},{1,17},{9,25},{17,1},{25,9},{2,18},{10... | collective-permute-start | bytes 331784 | tf_op jit(solution)/shard_map/reduce_input_weights/ppermute | solution.py:819
  164.2 4.9 %collective-permute-done.30 = bf16[48,1152]{1,0:T(8,128)(2,1)S(1)} collective-permute-done((bf16[48,1152]{1,0:T(8,128)(2,1)S(1)}, bf16[48,1152]{1,0:T(8,128)(2,1)S(1)}, u32[]{:S(2)}, u32[]{:S(2)}) %collective-permute-start.30) | collective-permute-done | bytes 110624 | tf_op jit(solution)/shard_map/reduce_input_weights/ppermute | solution.py:819
  173.8 5.0 %collective-permute-done.40 = bf16[96,1536]{1,0:T(8,128)(2,1)S(1)} collective-permute-done((bf16[96,1536]{1,0:T(8,128)(2,1)S(1)}, bf16[96,1536]{1,0:T(8,128)(2,1)S(1)}, u32[]{:S(2)}, u32[]{:S(2)}) %collective-permute-start.40) | collective-permute-done | bytes 294944 | tf_op jit(solution)/shard_map/reduce_input_weights/ppermute | solution.py:819
  184.0 3.9 %shard_map.313 = (f32[1024,768]{1,0:T(8,128)}, f32[1024,384]{1,0:T(8,128)}) custom-call(s32[10]{0:T(128)S(1)} %concatenate.40.info, bf16[1024,768]{1,0:T(8,128)(2,1)S(1)} %get-tuple-element.135.own, bf16[1024,768]{1,0:T(8,128)(2,1)S(1)} %collective-permute-done.25.other, f32[8,768]{1,0:T(8,128)S(1)} %collective-permute-done.34.halo_a, ...), custom_call_target="tpu_custom_call" | custom-call | flops 5500000256 | bytes 17500000 | tf_op jit(solution)/shard_map/pallas_call | solution.py:791
  (129 shorter events, 48.8 us)
Async XLA Ops:
  1.7 12.0 %collective-permute-start = (bf16[48,1024]{1,0:T(8,128)(2,1)S(1)}, bf16[48,1024]{1,0:T(8,128)(2,1)S(1)}, u32[]{:S(2)}, u32[]{:S(2)}) collective-permute-start(bf16[48,1024]{1,0:T(8,128)(2,1)S(1)} %fusion.7), channel_id=1, source_target_pairs={{0,8},{8,0},{16,24},{24,16},{1,9},{9,1},{17,25},{25,17},{2,10},{10... | collective-permute-start | bytes 294920 | tf_op jit(solution)/shard_map/gather_weights/ppermute | solution.py:819
  4.8 10.4 %collective-permute-start.1 = (bf16[48,1024]{1,0:T(8,128)(2,1)S(1)}, bf16[48,1024]{1,0:T(8,128)(2,1)S(1)}, u32[]{:S(2)}, u32[]{:S(2)}) collective-permute-start(bf16[48,1024]{1,0:T(8,128)(2,1)S(1)} %fusion.7), channel_id=1, source_target_pairs={{0,16},{8,24},{16,0},{24,8},{1,17},{9,25},{17,1},{25,9},{2,18},{10... | collective-permute-start | bytes 294920 | tf_op jit(solution)/shard_map/gather_weights/ppermute | solution.py:819
  17.0 16.7 %collective-permute-start.4 = (bf16[64,1536]{1,0:T(8,128)(2,1)S(1)}, bf16[64,1536]{1,0:T(8,128)(2,1)S(1)}, u32[]{:S(2)}, u32[]{:S(2)}) collective-permute-start(bf16[64,1536]{1,0:T(8,128)(2,1)S(1)} %fusion.3.refs_0_), channel_id=1, source_target_pairs={{0,16},{8,24},{16,0},{24,8},{1,17},{9,25},{17,1},{25,9},{2,18},{10... | collective-permute-start | bytes 589832 | tf_op jit(solution)/shard_map/gather_weights/ppermute | solution.py:819
  18.4 18.6 %collective-permute-start.5 = (bf16[64,1536]{1,0:T(8,128)(2,1)S(1)}, bf16[64,1536]{1,0:T(8,128)(2,1)S(1)}, u32[]{:S(2)}, u32[]{:S(2)}) collective-permute-start(bf16[64,1536]{1,0:T(8,128)(2,1)S(1)} %fusion.3.refs_0_), channel_id=1, source_target_pairs={{0,24},{8,16},{16,8},{24,0},{1,25},{9,17},{17,9},{25,1},{2,26},{10... | collective-permute-start | bytes 589832 | tf_op jit(solution)/shard_map/gather_weights/ppermute | solution.py:819
  19.7 22.5 %collective-permute-start.6 = (bf16[192,1024]{1,0:T(8,128)(2,1)S(1)}, bf16[192,1024]{1,0:T(8,128)(2,1)S(1)}, u32[]{:S(2)}, u32[]{:S(2)}) collective-permute-start(bf16[192,1024]{1,0:T(8,128)(2,1)S(1)} %pad_maximum_fusion.2.refs_4_), channel_id=1, source_target_pairs={{0,2},{2,0},{4,6},{6,4},{1,3},{3,1},{5,7},{7,5},{8,10},{10,8},{12,... | collective-permute-start | bytes 1179656 | tf_op jit(solution)/shard_map/gather_weights/ppermute | solution.py:819
  21.2 22.5 %collective-permute-start.7 = (bf16[192,1024]{1,0:T(8,128)(2,1)S(1)}, bf16[192,1024]{1,0:T(8,128)(2,1)}, u32[]{:S(2)}, u32[]{:S(2)}) collective-permute-start(bf16[192,1024]{1,0:T(8,128)(2,1)S(1)} %pad_maximum_fusion.2.refs_4_), channel_id=1, source_target_pairs={{0,4},{2,6},{4,0},{6,2},{1,5},{3,7},{5,1},{7,3},{8,12},{10,14},{12... | collective-permute-start | bytes 1179656 | tf_op jit(solution)/shard_map/gather_weights/ppermute | solution.py:819
  23.5 20.2 %collective-permute-start.8 = (bf16[192,1024]{1,0:T(8,128)(2,1)S(1)}, bf16[192,1024]{1,0:T(8,128)(2,1)}, u32[]{:S(2)}, u32[]{:S(2)}) collective-permute-start(bf16[192,1024]{1,0:T(8,128)(2,1)S(1)} %pad_maximum_fusion.2.refs_4_), channel_id=1, source_target_pairs={{0,6},{2,4},{4,2},{6,0},{1,7},{3,5},{5,3},{7,1},{8,14},{10,12},{12... | collective-permute-start | bytes 1179656 | tf_op jit(solution)/shard_map/gather_weights/ppermute | solution.py:819
  37.1 30.0 %collective-permute-start.13 = (bf16[192,1536]{1,0:T(8,128)(2,1)S(1)}, bf16[192,1536]{1,0:T(8,128)(2,1)S(1)}, u32[]{:S(2)}, u32[]{:S(2)}) collective-permute-start(bf16[192,1536]{1,0:T(8,128)(2,1)S(1)} %pad_maximum_fusion.refs_0_), channel_id=1, source_target_pairs={{0,2},{2,0},{4,6},{6,4},{1,3},{3,1},{5,7},{7,5},{8,10},{10,8},{12,... | collective-permute-start | bytes 1769480 | tf_op jit(solution)/shard_map/gather_weights/ppermute | solution.py:819
  39.8 28.6 %collective-permute-start.14 = (bf16[192,1536]{1,0:T(8,128)(2,1)S(1)}, bf16[192,1536]{1,0:T(8,128)(2,1)S(1)}, u32[]{:S(2)}, u32[]{:S(2)}) collective-permute-start(bf16[192,1536]{1,0:T(8,128)(2,1)S(1)} %pad_maximum_fusion.refs_0_), channel_id=1, source_target_pairs={{0,4},{2,6},{4,0},{6,2},{1,5},{3,7},{5,1},{7,3},{8,12},{10,14},{12... | collective-permute-start | bytes 1769480 | tf_op jit(solution)/shard_map/gather_weights/ppermute | solution.py:819
  42.3 26.2 %collective-permute-start.15 = (bf16[192,1536]{1,0:T(8,128)(2,1)S(1)}, bf16[192,1536]{1,0:T(8,128)(2,1)S(1)}, u32[]{:S(2)}, u32[]{:S(2)}) collective-permute-start(bf16[192,1536]{1,0:T(8,128)(2,1)S(1)} %pad_maximum_fusion.refs_0_), channel_id=1, source_target_pairs={{0,6},{2,4},{4,2},{6,0},{1,7},{3,5},{5,3},{7,1},{8,14},{10,12},{12... | collective-permute-start | bytes 1769480 | tf_op jit(solution)/shard_map/gather_weights/ppermute | solution.py:819
  61.3 11.2 %collective-permute-start.10 = (bf16[784,128]{1,0:T(8,128)(2,1)S(1)}, bf16[784,128]{1,0:T(8,128)(2,1)S(1)}, u32[]{:S(2)}, u32[]{:S(2)}) collective-permute-start(bf16[784,128]{1,0:T(8,128)(2,1)S(1)} %get-tuple-element.94), channel_id=1, source_target_pairs={{0,2},{2,4},{4,6},{1,3},{3,5},{5,7},{8,10},{10,12},{12,14},{9,11},... | collective-permute-start | bytes 602120 | tf_op jit(solution)/shard_map/ppermute | solution.py:811
  88.9 24.6 %collective-permute-start.17 = (bf16[784,128]{1,0:T(8,128)(2,1)S(1)}, bf16[784,128]{1,0:T(8,128)(2,1)S(1)}, u32[]{:S(2)}, u32[]{:S(2)}) collective-permute-start(bf16[784,128]{1,0:T(8,128)(2,1)S(1)} %get-tuple-element.109), channel_id=1, source_target_pairs={{2,0},{4,2},{6,4},{3,1},{5,3},{7,5},{10,8},{12,10},{14,12},{11,9},... | collective-permute-start | bytes 602120 | tf_op jit(solution)/shard_map/ppermute | solution.py:811
  90.2 23.3 %collective-permute-start.18 = (bf16[784,128]{1,0:T(8,128)(2,1)S(1)}, bf16[784,128]{1,0:T(8,128)(2,1)S(1)}, u32[]{:S(2)}, u32[]{:S(2)}) collective-permute-start(bf16[784,128]{1,0:T(8,128)(2,1)S(1)} %get-tuple-element.109), channel_id=1, source_target_pairs={{4,0},{6,2},{5,1},{7,3},{12,8},{14,10},{13,9},{15,11},{20,16},{22,... | collective-permute-start | bytes 602120 | tf_op jit(solution)/shard_map/ppermute | solution.py:811
  91.5 22.0 %collective-permute-start.19 = (bf16[784,128]{1,0:T(8,128)(2,1)S(1)}, bf16[784,128]{1,0:T(8,128)(2,1)S(1)}, u32[]{:S(2)}, u32[]{:S(2)}) collective-permute-start(bf16[784,128]{1,0:T(8,128)(2,1)S(1)} %get-tuple-element.109), channel_id=1, source_target_pairs={{6,0},{7,1},{14,8},{15,9},{22,16},{23,17},{30,24},{31,25}} | collective-permute-start | bytes 602120 | tf_op jit(solution)/shard_map/ppermute | solution.py:811
  108.2 31.5 %collective-permute-start.21 = (bf16[192,1536]{1,0:T(8,128)(2,1)S(1)}, bf16[192,1536]{1,0:T(8,128)(2,1)S(1)}, u32[]{:S(2)}, u32[]{:S(2)}) collective-permute-start(bf16[192,1536]{1,0:T(8,128)(2,1)S(1)} %get-tuple-element.129), channel_id=1, source_target_pairs={{0,2},{2,0},{4,6},{6,4},{1,3},{3,1},{5,7},{7,5},{8,10},{10,8},{12,... | collective-permute-start | bytes 1769480 | tf_op jit(solution)/shard_map/reduce_gate_weights/ppermute | solution.py:819
  110.3 29.5 %collective-permute-start.22 = (bf16[192,1536]{1,0:T(8,128)(2,1)S(1)}, bf16[192,1536]{1,0:T(8,128)(2,1)S(1)}, u32[]{:S(2)}, u32[]{:S(2)}) collective-permute-start(bf16[192,1536]{1,0:T(8,128)(2,1)S(1)} %get-tuple-element.130), channel_id=1, source_target_pairs={{0,4},{2,6},{4,0},{6,2},{1,5},{3,7},{5,1},{7,3},{8,12},{10,14},{12... | collective-permute-start | bytes 1769480 | tf_op jit(solution)/shard_map/reduce_gate_weights/ppermute | solution.py:819
  113.5 26.2 %collective-permute-start.23 = (bf16[192,1536]{1,0:T(8,128)(2,1)S(1)}, bf16[192,1536]{1,0:T(8,128)(2,1)S(1)}, u32[]{:S(2)}, u32[]{:S(2)}) collective-permute-start(bf16[192,1536]{1,0:T(8,128)(2,1)S(1)} %get-tuple-element.131), channel_id=1, source_target_pairs={{0,6},{2,4},{4,2},{6,0},{1,7},{3,5},{5,3},{7,1},{8,14},{10,12},{12... | collective-permute-start | bytes 1769480 | tf_op jit(solution)/shard_map/reduce_gate_weights/ppermute | solution.py:819
  136.2 13.2 %collective-permute-start.20 = (bf16[192,1152]{1,0:T(8,128)(2,1)S(1)}, bf16[192,1152]{1,0:T(8,128)(2,1)S(1)}, u32[]{:S(2)}, u32[]{:S(2)}) collective-permute-start(bf16[192,1152]{1,0:T(8,128)(2,1)S(1)} %get-tuple-element.127), channel_id=1, source_target_pairs={{0,2},{2,0},{4,6},{6,4},{1,3},{3,1},{5,7},{7,5},{8,10},{10,8},{12,... | collective-permute-start | bytes 1327112 | tf_op jit(solution)/shard_map/ppermute | solution.py:819
  137.6 20.3 %collective-permute-start.26 = (bf16[192,1152]{1,0:T(8,128)(2,1)S(1)}, bf16[192,1152]{1,0:T(8,128)(2,1)S(1)}, u32[]{:S(2)}, u32[]{:S(2)}) collective-permute-start(bf16[192,1152]{1,0:T(8,128)(2,1)S(1)} %get-tuple-element.138), channel_id=1, source_target_pairs={{0,4},{2,6},{4,0},{6,2},{1,5},{3,7},{5,1},{7,3},{8,12},{10,14},{12... | collective-permute-start | bytes 1327112 | tf_op jit(solution)/shard_map/ppermute | solution.py:819
  139.6 18.3 %collective-permute-start.27 = (bf16[192,1152]{1,0:T(8,128)(2,1)S(1)}, bf16[192,1152]{1,0:T(8,128)(2,1)S(1)}, u32[]{:S(2)}, u32[]{:S(2)}) collective-permute-start(bf16[192,1152]{1,0:T(8,128)(2,1)S(1)} %get-tuple-element.139), channel_id=1, source_target_pairs={{0,6},{2,4},{4,2},{6,0},{1,7},{3,5},{5,3},{7,1},{8,14},{10,12},{12... | collective-permute-start | bytes 1327112 | tf_op jit(solution)/shard_map/ppermute | solution.py:819
  162.8 21.2 %collective-permute-start.25 = (bf16[1024,768]{1,0:T(8,128)(2,1)S(1)}, bf16[1024,768]{1,0:T(8,128)(2,1)S(1)}, u32[]{:S(2)}, u32[]{:S(2)}) collective-permute-start(bf16[1024,768]{1,0:T(8,128)(2,1)S(1)} %get-tuple-element.135.own), channel_id=1, source_target_pairs={{0,1},{1,0},{2,3},{3,2},{4,5},{5,4},{6,7},{7,6},{8,9},{9,8},{10,11... | collective-permute-start | bytes 4718600 | tf_op jit(solution)/shard_map/ppermute | solution.py:815
  171.0 11.1 %collective-permute-start.34 = (f32[8,768]{1,0:T(8,128)S(1)}, f32[8,768]{1,0:T(8,128)S(1)}, u32[]{:S(2)}, u32[]{:S(2)}) collective-permute-start(f32[8,768]{1,0:T(8,128)S(1)} %get-tuple-element.147), channel_id=1, source_target_pairs={{2,0},{3,1},{4,2},{5,3},{6,4},{7,5},{10,8},{11,9},{12,10},{13,11},... | collective-permute-start | bytes 73736 | tf_op jit(solution)/shard_map/ppermute | solution.py:1196
  172.2 11.2 %collective-permute-start.35 = (f32[8,768]{1,0:T(8,128)S(1)}, f32[8,768]{1,0:T(8,128)S(1)}, u32[]{:S(2)}, u32[]{:S(2)}) collective-permute-start(f32[8,768]{1,0:T(8,128)S(1)} %get-tuple-element.147), channel_id=1, source_target_pairs={{2,1},{3,0},{4,3},{5,2},{6,5},{7,4},{10,9},{11,8},{12,11},{13,10},... | collective-permute-start | bytes 73736 | tf_op jit(solution)/shard_map/ppermute | solution.py:1197
  173.6 10.4 %collective-permute-start.36 = (bf16[1024,384]{1,0:T(8,128)(2,1)S(1)}, bf16[1024,384]{1,0:T(8,128)(2,1)S(1)}, u32[]{:S(2)}, u32[]{:S(2)}) collective-permute-start(bf16[1024,384]{1,0:T(8,128)(2,1)S(1)} %get-tuple-element.149), channel_id=1, source_target_pairs={{0,1},{1,0},{2,3},{3,2},{4,5},{5,4},{6,7},{7,6},{8,9},{9,8},{10,11... | collective-permute-start | bytes 2359304 | tf_op jit(solution)/shard_map/ppermute | solution.py:815
  (25 other events, 281.3 us)
